TPU v7x, 512 devices: a whole 4x4x16 slice. The times are simulated.
512 devices in a mesh: seq: 32 (over z, core), head: 16 (over x, y).
Axes of the slice: x: 4, y: 4, z: 16, core: 2. Of those that a mesh axis runs over, the one named last changes fastest.
Arguments:
- queries: bfloat16 [16384, 8192], P('seq', 'head'), may hold values from -6 to 6
- keys: bfloat16 [16384, 8192], P('seq', 'head'), may hold values from -6 to 6
- values: bfloat16 [16384, 8192], P('seq', 'head'), may hold values from -6 to 6
- rates: float32 [64], P('head'), as said below
- gain: float32 [8192], P('head'), may hold values from 0.1 to 1.9
- cotangent: bfloat16 [16384, 8192], P('seq', 'head'), may hold values from -6 to 6
Outputs:
- attended: bfloat16 [16384, 8192], P('seq', 'head')
- query_grad: bfloat16 [16384, 8192], P('seq', 'head')
- key_grad: bfloat16 [16384, 8192], P('seq', 'head')
- value_grad: bfloat16 [16384, 8192], P('seq', 'head')
- gain_grad: float32 [8192], P('head')
Inputs may be any that keep to these rules, and one draw needn't show every extreme that they name: `rates`: every rate is positive.
All inputs are finite; a program needn't handle non-finite values.
Results may differ from a plain program's by a relative error of at most 0.0051.
Values sent between devices are 32-bit elements; how exact they have to be, the bound alone decides.
No kernel may reach another device: no remote copies, remote signals or barrier semaphores. Data moves between devices by JAX's collectives and lax.ppermute only.
A program may use at most 64 MiB of HBM per device.

v0:
```python
import jax
import jax.numpy as jnp
from jax import lax
from jax.sharding import PartitionSpec as P

epsilon = 1e-06
HIGH = lax.Precision.HIGHEST


def carried_in(x, axis, combine, identity, reverse):
    count, position = (lax.axis_size(axis), lax.axis_index(axis))
    everything = jax.tree.map(lambda part: lax.all_gather(part, axis), x)
    start = jax.tree.map(
        lambda part, zero: jnp.broadcast_to(jnp.asarray(zero, part.dtype), part.shape), x, identity
    )

    def lap(k, before):
        at = count - 1 - k if reverse else k
        reached = at > position if reverse else at < position
        new = combine(before, jax.tree.map(lambda part: part[at], everything))
        return jax.tree.map(lambda a, b: jnp.where(reached, a, b), new, before)

    return lax.fori_loop(0, count, lap, start)


def decay_parts(rates, length):
    position = jnp.arange(length, dtype=jnp.float32)
    distance = position[:, None] - position[None, :]
    weight = jnp.where(
        distance[None] >= 0, jnp.exp(-rates[:, None, None] * jnp.maximum(distance, 0.0)[None]), 0.0
    )
    head_in = jnp.exp(-rates[None, :] * (position[:, None] + 1.0))
    tail_out = jnp.exp(-rates[None, :] * (length - 1.0 - position[:, None]))
    return (weight, head_in, tail_out)


def chain_combine(earlier, later):
    return (earlier[0] * later[0], later[0][:, None, None] * earlier[1] + later[1])


def body(queries, keys, values, rates, gain, cotangent):
    length, channels = queries.shape
    head_count = rates.shape[0]
    head_size = channels // head_count
    query_rows = queries.reshape(length, head_count, head_size)
    key_rows = keys.reshape(length, head_count, head_size)
    value_rows = values.reshape(length, head_count, head_size)
    query_wide = query_rows.astype(jnp.float32)
    key_wide = key_rows.astype(jnp.float32)
    value_wide = value_rows.astype(jnp.float32)
    weight, head_in, tail_out = decay_parts(rates, length)
    factor = jnp.exp(-rates * length)
    empty_state = jnp.zeros((head_count, head_size, head_size), jnp.float32)
    identity = (jnp.ones_like(factor), empty_state)
    block_total = jnp.einsum(
        "shd,she->hde", key_wide * tail_out[:, :, None], value_wide, precision=HIGH
    )
    carried, state_in = carried_in((factor, block_total), "seq", chain_combine, identity, False)
    scores = jnp.einsum("thd,shd->hts", query_rows, key_rows, preferred_element_type=jnp.float32)
    weights_bf = (scores * weight).astype(jnp.bfloat16)
    mixed = jnp.einsum("hts,shd->thd", weights_bf, value_rows, preferred_element_type=jnp.float32)
    mixed = mixed + head_in[:, :, None] * jnp.einsum(
        "thd,hde->the", query_wide, state_in, precision=HIGH
    )
    total_channels = channels * lax.axis_size("head")
    gain_heads = gain.reshape(head_count, head_size)
    upstream = cotangent.reshape(length, head_count, head_size).astype(jnp.float32)
    scaled_up = upstream * gain_heads
    square, inner = lax.psum(
        (jnp.sum(mixed * mixed, axis=(1, 2)), jnp.sum(scaled_up * mixed, axis=(1, 2))), "head"
    )
    inv_rms = lax.rsqrt(square / total_channels + epsilon)
    normed = mixed * inv_rms[:, None, None]
    attended = (normed * gain_heads).astype(jnp.bfloat16).reshape(length, channels)
    gain_grad = lax.psum(jnp.sum(upstream * normed, axis=0).reshape(channels), "seq")
    mixed_grad = (
        inv_rms[:, None, None] * scaled_up
        - mixed * (inv_rms**3 * inner / total_channels)[:, None, None]
    ).astype(jnp.bfloat16)
    grad_wide = mixed_grad.astype(jnp.float32)
    back_total = jnp.einsum(
        "thd,the->hde", query_wide * head_in[:, :, None], grad_wide, precision=HIGH
    )
    carried_back, back_in = carried_in((factor, back_total), "seq", chain_combine, identity, True)
    grad_weights = (
        jnp.einsum("the,she->hts", mixed_grad, value_rows, preferred_element_type=jnp.float32)
        * weight
    ).astype(jnp.bfloat16)
    query_grad = jnp.einsum(
        "hts,shd->thd", grad_weights, key_rows, preferred_element_type=jnp.float32
    )
    query_grad = query_grad + head_in[:, :, None] * jnp.einsum(
        "the,hde->thd", grad_wide, state_in, precision=HIGH
    )
    key_grad = jnp.einsum(
        "hts,thd->shd", grad_weights, query_rows, preferred_element_type=jnp.float32
    )
    key_grad = key_grad + tail_out[:, :, None] * jnp.einsum(
        "she,hde->shd", value_wide, back_in, precision=HIGH
    )
    value_grad = jnp.einsum(
        "hts,the->she", weights_bf, mixed_grad, preferred_element_type=jnp.float32
    )
    value_grad = value_grad + tail_out[:, :, None] * jnp.einsum(
        "shd,hde->she", key_wide, back_in, precision=HIGH
    )
    return (
        attended,
        query_grad.astype(jnp.bfloat16).reshape(length, channels),
        key_grad.astype(jnp.bfloat16).reshape(length, channels),
        value_grad.astype(jnp.bfloat16).reshape(length, channels),
        gain_grad,
    )


def solution(mesh):
    placed = (
        P("seq", "head"),
        P("seq", "head"),
        P("seq", "head"),
        P("head"),
        P("head"),
        P("seq", "head"),
    )
    return jax.shard_map(
        body,
        mesh=mesh,
        in_specs=placed,
        out_specs=(
            P("seq", "head"),
            P("seq", "head"),
            P("seq", "head"),
            P("seq", "head"),
            P("head"),
        ),
        check_vma=False,
    )
```

profile of v0, /device:TPU:1, one launch (start us, length us, event | category | flops | bytes accessed | tf_op | source)
XLA Modules:
  0.0 334.0 jit_solution(18096123085216300833)
XLA Ops:
  8.6 1.3 dynamic-slice
  11.4 1.4 fusion.16
  12.9 54.7 %all-reduce = f32[128]{0:T(128)S(1)} all-reduce(f32[128]{0:T(128)S(1)} %get-tuple-element.310), channel_id=2, replica_groups=mesh['seq'=32,'head'=16] {'seq'}, use_global_device_ids=true, to_apply=%add | all-reduce | flops 128 | bytes 1024
  68.9 1.4 copy.59
  71.8 1.4 multiply_convert_fusion.1
  73.2 1.3 copy-done.1
  74.6 1.8 convolution_bitcast_fusion.3
  76.4 21.9 %all-gather.6.cloned.1.call-done = f32[128,128,128]{2,1,0:T(8,128)} async-done(((f32[4,128,128]{2,1,0:T(8,128)}), f32[128,128,128]{2,1,0:T(8,128)}) %all-gather.6.cloned.1.call-update) | async-done | bytes 8388624 | tf_op jit(solution)/shard_map/all_gather | solution.py:12
  98.3 35.1 %while.30 = (s32[]{:T(128)}, f32[4,128,128]{2,1,0:T(8,128)S(1)}, s32[]{:T(128)}, f32[32,4]{1,0:T(8,128)S(1)}, f32[32,4,128,128]{3,2,1,0:T(8,128)}, /*index=5*/s32[]{:T(128)}, s32[]{:T(128)}) while((s32[]{:T(128)}, f32[4,128,128]{2,1,0:T(8,128)S(1)}, s32[]{:T(128)}, f32[32,4]{1,0:T(8,128)S(1)}, f32[32,4,128,128]{3,2,1,0:T(8,128)}, ...), condition=%wide.region_1.2_spmd.clone, body=%wide.region_0.1_spmd.clone.sunk | while | flops 262148 | bytes 786593 | solution.py:23
  133.4 1.9 multiply_reduce_fusion.2
  135.3 33.1 %psum.21 = f32[512]{0:T(512)S(1)} all-reduce(f32[512]{0:T(512)S(1)} %get-tuple-element.312), channel_id=1, replica_groups=mesh['seq'=32,'head'=16] {'head'}, use_global_device_ids=true, to_apply=%region_3.4 | all-reduce | flops 512 | bytes 4096 | tf_op jit(solution)/shard_map/psum | solution.py:69
  168.7 28.5 %psum.22 = f32[512]{0:T(512)S(1)} all-reduce(f32[512]{0:T(512)S(1)} %get-tuple-element.285), channel_id=1, replica_groups=mesh['seq'=32,'head'=16] {'head'}, use_global_device_ids=true, to_apply=%region_5.6 | all-reduce | flops 512 | bytes 4096 | tf_op jit(solution)/shard_map/psum | solution.py:69
  199.1 1.4 fusion.13
  200.6 2.0 copy.67
  202.6 2.8 multiply_convert_fusion
  205.5 2.4 convolution_bitcast_fusion.2
  207.9 1.4 fusion.10
  209.3 2.0 copy.68
  211.4 62.2 %psum.23 = f32[512]{0:T(512)} all-reduce(f32[512]{0:T(512)S(1)} %bitcast.127), channel_id=1, replica_groups=mesh['seq'=32,'head'=16] {'seq'}, use_global_device_ids=true, to_apply=%region_9.10 | all-reduce | flops 512 | bytes 4096 | tf_op jit(solution)/shard_map/psum | solution.py:75
  273.5 2.7 convolution_bitcast_fusion.1
  276.2 1.5 convolution_bitcast_fusion
  277.8 9.6 %all-gather.8.cloned.1.call-done = f32[128,128,128]{2,1,0:T(8,128)} async-done(((f32[4,128,128]{2,1,0:T(8,128)}), f32[128,128,128]{2,1,0:T(8,128)}) %all-gather.8.cloned.1.call-update) | async-done | bytes 8388624 | tf_op jit(solution)/shard_map/all_gather | solution.py:12
  287.4 35.3 %while.31 = (s32[]{:T(128)}, f32[4,128,128]{2,1,0:T(8,128)S(1)}, s32[]{:T(128)}, f32[32,4]{1,0:T(8,128)S(1)}, f32[32,4,128,128]{3,2,1,0:T(8,128)}, /*index=5*/s32[]{:T(128)}, s32[]{:T(128)}, s32[]{:T(128)}, s32[]{:T(128)}) while((s32[]{:T(128)}, f32[4,128,128]{2,1,0:T(8,128)S(1)}, s32[]{:T(128)}, f32[32,4]{1,0:T(8,128)S(1)}, ...), condition=%wide.region_7.8_spmd.clone, body=%wide.region_6.7_spmd.clone.sunk | while | flops 262152 | bytes 786655 | solution.py:23
  322.7 1.9 fusion.12
  (175 shorter events, 78.1 us)
Async XLA Ops:
  7.2 4.2 %copy-start = (bf16[512,512]{1,0:T(8,128)(2,1)S(1)}, bf16[512,512]{1,0:T(8,128)(2,1)}, u32[]{:S(2)}) copy-start(bf16[512,512]{1,0:T(8,128)(2,1)} %param.12) | copy-start | bytes 1572868
  7.2 91.1 %all-gather.6.cloned.1.call-start = ((), (), s32[]{:S(2)}) async-start(), calls=%async_computation | async-start | bytes 8650752 | tf_op jit(solution)/shard_map/all_gather | solution.py:12
  8.5 64.7 %copy-start.8 = (bf16[512,512]{0,1:T(8,128)(2,1)}, bf16[512,512]{0,1:T(8,128)(2,1)S(1)}, u32[]{:S(2)}) copy-start(bf16[512,512]{0,1:T(8,128)(2,1)S(1)} %copy.52) | copy-start | bytes 1572868
  12.8 274.6 %all-gather.8.cloned.1.call-start = ((), (), s32[]{:S(2)}) async-start(), calls=%async_computation.1 | async-start | bytes 8650752 | tf_op jit(solution)/shard_map/all_gather | solution.py:12
  68.9 129.4 %copy-start.5 = (bf16[512,512]{0,1:T(8,128)(2,1)}, bf16[512,512]{0,1:T(8,128)(2,1)S(1)}, u32[]{:S(2)}) copy-start(bf16[512,512]{0,1:T(8,128)(2,1)S(1)} %copy.51) | copy-start | bytes 1572868
  70.6 2.6 copy-start.11
  70.8 1.0 copy-start.10
  73.2 1.4 copy-start.1
  76.4 92.0 %copy-start.12 = (f32[512]{0:T(512)S(1)}, f32[512]{0:T(512)}, u32[]{:S(2)}) copy-start(f32[512]{0:T(512)} %param.14) | copy-start | bytes 6148
  198.3 0.8 copy-start.6
  202.6 5.3 %copy-start.7 = (bf16[512,4,128]{0,2,1:T(8,128)(2,1)S(1)}, bf16[512,4,128]{0,2,1:T(8,128)(2,1)}, u32[]{:S(2)}) copy-start(bf16[512,4,128]{0,2,1:T(8,128)(2,1)} %copy-done.6) | copy-start | bytes 1572868
  205.5 3.8 %copy-start.3 = (bf16[4,512,512]{2,1,0:T(8,128)(2,1)}, bf16[4,512,512]{2,1,0:T(8,128)(2,1)S(1)}, u32[]{:S(2)}) copy-start(bf16[4,512,512]{2,1,0:T(8,128)(2,1)S(1)} %multiply_convert_fusion) | copy-start | bytes 6291460
  205.5 68.0 %copy-start.2 = (bf16[4,512,512]{2,1,0:T(8,128)(2,1)S(1)}, bf16[4,512,512]{2,1,0:T(8,128)(2,1)}, u32[]{:S(2)}) copy-start(bf16[4,512,512]{2,1,0:T(8,128)(2,1)} %copy-done.1) | copy-start | bytes 6291460
  273.5 2.7 copy-start.4
  276.2 46.4 %copy-start.9 = (bf16[512,512]{0,1:T(8,128)(2,1)S(1)}, bf16[512,512]{0,1:T(8,128)(2,1)}, u32[]{:S(2)}) copy-start(bf16[512,512]{0,1:T(8,128)(2,1)} %copy-done.8) | copy-start | bytes 1572868
Sparse Core Ops, SparseCore 0:
  12.9 85.3 all-gather.5
  200.7 86.6 all-gather.7
where the time goes:
time: 337 us; the launch traced here: 334 us
  blocking collectives  178 us (53%)
  other arithmetic  70.3 us (21%)
  waiting for transfers between devices  31.5 us (9%)
  matrix products  21.3 us (6%)
  local copies, waits for them, and re-layouts  15.3 us (5%)
  between operations  15 us (4%)
    select_n x64, other arithmetic, lap(): return jax.tree.map(lambda a, b: jnp.where(reached, a, b), new, before)  67.6 us
    psum x1, blocking collectives, body(): lax.psum(jnp.sum(upstream * normed, axis=0).reshape(channels), 'seq')  62.2 us
    psum x2, blocking collectives, body(): lax.psum((jnp.sum(mixed * mixed, axis=(1, 2)), jnp.sum(scaled_up * mixed,...  61.6 us
    unnamed x1, blocking collectives  54.7 us
    all_gather x2, waiting for transfers between devices, carried_in(): everything = jax.tree.map(lambda part: lax.all_gather(part, axis), x)  31.5 us
    unnamed x34, local copies, waits for them, and re-layouts  13.1 us
  transfers between devices with their start and end apart: 2, of which 2 were waited for; matrix products, arithmetic and copies ran while one was open for 6% of the time, Pallas kernels for 0%

commit v1 on v0

v1 whole, which is shorter than its diff:
```python
import jax
import jax.numpy as jnp
from jax import lax
from jax.experimental import pallas as pl
from jax.experimental.pallas import tpu as pltpu
from jax.sharding import PartitionSpec as P

epsilon = 1e-06
F32, BF16 = jnp.float32, jnp.bfloat16
GROUP = 8
EXTRA = 8


def dot(a, b, over_a, over_b):
    return lax.dot_general(a, b, (((over_a,), (over_b,)), ((), ())), preferred_element_type=F32)


def split(x):
    high = x.astype(BF16)
    return high, (x - high.astype(F32)).astype(BF16)


def dot_split_left(x, b, over_a, over_b):
    high, low = split(x)
    return dot(high, b, over_a, over_b) + dot(low, b, over_a, over_b)


def dot_split_right(a, x, over_a, over_b):
    high, low = split(x)
    return dot(a, high, over_a, over_b) + dot(a, low, over_a, over_b)


def rows_of(length, width=128):
    return lax.broadcasted_iota(jnp.int32, (length, width), 0).astype(F32)


def head_in_of(rate, length):
    return jnp.exp(-rate * (rows_of(length) + 1.0))


def tail_out_of(rate, length):
    return jnp.exp(-rate * (length - 1.0 - rows_of(length)))


def tile_weights(rate, half):
    distance = (
        lax.broadcasted_iota(jnp.int32, (half, half), 0) - lax.broadcasted_iota(jnp.int32, (half, half), 1)
    ).astype(F32)
    same = jnp.where(distance >= 0, jnp.exp(-rate * jnp.maximum(distance, 0.0)), 0.0)
    return same, jnp.exp(-rate * (distance + half))


def block_sum_kernel(rates, keys, values, out):
    rate = rates[pl.program_id(0)]
    length, size = keys.shape
    scaled = keys[...].astype(F32) * tail_out_of(rate, length)
    out[...] = dot_split_left(scaled, values[...], 0, 0).reshape(2, size // 2, size)


def intra_kernel(rates, queries, keys, values, out):
    rate = rates[pl.program_id(0)]
    half = queries.shape[0] // 2
    same, across = tile_weights(rate, half)
    first, second = pl.ds(0, half), pl.ds(half, half)

    def probs(t, s, weight):
        return (dot(queries[t, :], keys[s, :], 1, 1) * weight).astype(BF16)

    out[first, :] = dot(probs(first, first, same), values[first, :], 1, 0)
    out[second, :] = dot(probs(second, first, across), values[first, :], 1, 0) + dot(
        probs(second, second, same), values[second, :], 1, 0
    )


def mixed_kernel(rates, queries, state, intra, gain, cotangent, mixed, stats, square, inner):
    head = pl.program_id(0)
    rate = rates[head]
    length, size = queries.shape
    state_in = state[...].reshape(size, size)
    value = intra[...] + head_in_of(rate, length) * dot_split_right(queries[...], state_in, 1, 0)
    mixed[...] = value
    first = head == 0
    square[...] = jnp.where(first, 0.0, square[...]) + value * value
    inner[...] = jnp.where(first, 0.0, inner[...]) + cotangent[...].astype(F32) * gain[...] * value

    @pl.when(head == pl.num_programs(0) - 1)
    def _():
        pieces = []
        for ref in (square, inner):
            for start in range(0, length, 128):
                pieces.append(jnp.sum(ref[pl.ds(start, 128), :].T, axis=0, keepdims=True))
        tile = jnp.concatenate(pieces, axis=0)
        stats[...] = jnp.broadcast_to(tile[None], stats.shape)


def token_scales(received, channels, inv_out, coef_out):
    total = jnp.sum(received[...], axis=0)
    chunks = total.shape[0] // 2
    inv = lax.rsqrt(total[:chunks] / channels + epsilon)
    coef = inv * inv * inv * total[chunks:] / channels
    for chunk in range(chunks):
        rows = pl.ds(chunk * 128, 128)
        inv_out[rows, :] = jnp.broadcast_to(inv[chunk : chunk + 1], (128, 128)).T
        if coef_out is not None:
            coef_out[rows, :] = jnp.broadcast_to(coef[chunk : chunk + 1], (128, 128)).T


def back_sum_kernel(channels, rates, received, mixed, gain, cotangent, queries, grad, sums, inv, coef):
    head = pl.program_id(0)
    rate = rates[head]
    length, size = queries.shape

    @pl.when(head == 0)
    def _():
        token_scales(received, channels, inv, coef)

    upstream = cotangent[...].astype(F32)
    value = mixed[...]
    mixed_grad = (inv[...] * (upstream * gain[...]) - value * coef[...]).astype(BF16)
    grad[...] = mixed_grad
    scaled = queries[...].astype(F32) * head_in_of(rate, length)
    sums[:, pl.ds(0, size // 2), :] = dot_split_left(scaled, mixed_grad, 0, 0).reshape(2, size // 2, size)
    gain_grad = jnp.sum(upstream * (value * inv[...]), axis=0, keepdims=True)
    sums[:, pl.ds(size // 2, EXTRA), :] = jnp.broadcast_to(gain_grad[None], (2, EXTRA, size))


def grads_kernel(
    channels, rates, received, mixed, gain, queries, keys, values, grad, state,
    attended, query_grad, key_part, value_part, inv,
):
    head = pl.program_id(0)
    rate = rates[head]
    length, size = queries.shape
    half = length // 2

    @pl.when(head == 0)
    def _():
        token_scales(received, channels, inv, None)

    attended[...] = (mixed[...] * inv[...] * gain[...]).astype(BF16)
    same, across = tile_weights(rate, half)
    first, second = pl.ds(0, half), pl.ds(half, half)
    state_part = head_in_of(rate, length) * dot_split_right(grad[...], state[...].reshape(size, size), 1, 1)

    def weighted(a, b, t, s, weight):
        return (dot(a[t, :], b[s, :], 1, 1) * weight).astype(BF16)

    grads = [weighted(grad, values, *pair) for pair in ((first, first, same), (second, first, across), (second, second, same))]
    query_grad[first, :] = (dot(grads[0], keys[first, :], 1, 0) + state_part[:half]).astype(BF16)
    query_grad[second, :] = (
        dot(grads[1], keys[first, :], 1, 0) + dot(grads[2], keys[second, :], 1, 0) + state_part[half:]
    ).astype(BF16)
    key_part[first, :] = dot(grads[0], queries[first, :], 0, 0) + dot(grads[1], queries[second, :], 0, 0)
    key_part[second, :] = dot(grads[2], queries[second, :], 0, 0)
    probs = [weighted(queries, keys, *pair) for pair in ((first, first, same), (second, first, across), (second, second, same))]
    value_part[first, :] = dot(probs[0], grad[first, :], 0, 0) + dot(probs[1], grad[second, :], 0, 0)
    value_part[second, :] = dot(probs[2], grad[second, :], 0, 0)


def finish_kernel(rates, back, keys, values, key_part, value_part, key_grad, value_grad, gain_grad):
    rate = rates[pl.program_id(0)]
    length, size = keys.shape
    half = size // 2
    back_in = back[:, pl.ds(0, half), :].reshape(size, size)
    gain_grad[...] = back[0, pl.ds(half, 1), :]
    tail = tail_out_of(rate, length)
    key_grad[...] = (key_part[...] + tail * dot_split_right(values[...], back_in, 1, 1)).astype(BF16)
    value_grad[...] = (value_part[...] + tail * dot_split_right(keys[...], back_in, 1, 0)).astype(BF16)


def shift(x, groups, by):
    count = groups * GROUP
    return lax.ppermute(x, "seq", [(i, (i + by * GROUP) % count) for i in range(count)])


def scan_seq(x, rates, length, reverse, has_extra):
    count = lax.axis_size("seq")
    groups = count // GROUP
    members = [[g * GROUP + j for j in range(GROUP)] for g in range(groups)]
    position = lax.axis_index("seq")
    group, member = position // GROUP, position % GROUP
    rate = lax.dynamic_index_in_dim(rates, member * rates.shape[0] // GROUP, 0, False)
    factor, group_factor = jnp.exp(-rate * length), jnp.exp(-rate * (length * GROUP))
    parts = lax.all_to_all(x, "seq", 0, 0, axis_index_groups=members)
    rows = parts.shape[1] - (EXTRA if has_extra else 0)
    states = parts[:, :rows]
    order = range(GROUP - 1, -1, -1) if reverse else range(GROUP)
    total = jnp.zeros(states.shape[1:], F32)
    for k in order:
        total = factor * total + states[k]
    if has_extra:
        extra = jnp.sum(parts[:, rows:], axis=0)
        total = jnp.concatenate([total, extra], axis=0)
    sign = -1 if reverse else 1
    arrived = [shift(total, groups, sign * by) for by in range(1, groups)]
    carry = jnp.zeros(states.shape[1:], F32)
    for by in range(groups - 1, 0, -1):
        inside = group + by < groups if reverse else group - by >= 0
        carry = group_factor * carry + jnp.where(inside, arrived[by - 1][:rows], 0.0)
    before = [None] * GROUP
    for k in order:
        before[k] = carry
        carry = factor * carry + states[k]
    out = jnp.stack(before)
    if has_extra:
        extra = extra + sum(a[rows:] for a in arrived)
        out = jnp.concatenate([out, jnp.broadcast_to(extra[None], (GROUP,) + extra.shape)], axis=1)
    return lax.all_to_all(out, "seq", 0, 0, axis_index_groups=members)


def body(queries, keys, values, rates, gain, cotangent):
    length, channels = queries.shape
    heads = rates.shape[0]
    size = channels // heads
    head_devices = lax.axis_size("head")
    total_channels = channels * head_devices
    gain_row = gain.reshape(1, channels)

    smem = pl.BlockSpec(memory_space=pltpu.SMEM)
    tokens = pl.BlockSpec((length, size), lambda h: (0, h))
    row = pl.BlockSpec((1, size), lambda h: (0, h))
    shards = pl.BlockSpec((2, size // 2, size), lambda h: (h, 0, 0))
    shards_extra = pl.BlockSpec((2, size // 2 + EXTRA, size), lambda h: (h, 0, 0))
    stats_shape = (head_devices, 2 * length // 128, 128)
    stats_spec = pl.BlockSpec(stats_shape, lambda h: (0, 0, 0))
    column = pltpu.VMEM((length, size), F32)

    def array(kind, *shape):
        return jax.ShapeDtypeStruct(shape, kind)

    def call(kernel, in_specs, out_specs, out_shape, flops, nbytes, scratch=()):
        return pl.pallas_call(
            kernel,
            grid=(heads,),
            in_specs=in_specs,
            out_specs=out_specs,
            out_shape=out_shape,
            scratch_shapes=list(scratch),
            compiler_params=pltpu.CompilerParams(vmem_limit_bytes=32 * 1024 * 1024),
            cost_estimate=pl.CostEstimate(flops=flops, bytes_accessed=nbytes, transcendentals=0),
        )

    square = 2 * heads * length * length * size
    wide = array(F32, length, channels)
    narrow = array(BF16, length, channels)

    sums = call(
        block_sum_kernel, [smem, tokens, tokens], shards,
        array(F32, 2 * heads, size // 2, size), square // 2, 2 << 20,
    )(rates, keys, values)
    intra = call(intra_kernel, [smem, tokens, tokens, tokens], tokens, wide, 2 * square, 4 << 20)(
        rates, queries, keys, values
    )
    state_in = scan_seq(sums, rates, length, False, False)
    mixed, stats = call(
        mixed_kernel, [smem, tokens, shards, tokens, row, tokens], [tokens, stats_spec],
        [wide, array(F32, *stats_shape)], square // 2, 4 << 20, [column, column],
    )(rates, queries, state_in, intra, gain_row, cotangent)
    received = lax.all_to_all(stats, "head", 0, 0)
    grad, back_sums = call(
        lambda *refs: back_sum_kernel(total_channels, *refs),
        [smem, stats_spec, tokens, row, tokens, tokens], [tokens, shards_extra],
        [narrow, array(F32, 2 * heads, size // 2 + EXTRA, size)], square // 2, 4 << 20, [column, column],
    )(rates, received, mixed, gain_row, cotangent, queries)
    attended, query_grad, key_part, value_part = call(
        lambda *refs: grads_kernel(total_channels, *refs),
        [smem, stats_spec, tokens, row, tokens, tokens, tokens, tokens, shards],
        [tokens, tokens, tokens, tokens], [narrow, narrow, wide, wide], 6 * square, 6 << 20, [column],
    )(rates, received, mixed, gain_row, queries, keys, values, grad, state_in)
    back_in = scan_seq(back_sums, rates, length, True, True)
    key_grad, value_grad, gain_grad = call(
        finish_kernel, [smem, shards_extra, tokens, tokens, tokens, tokens], [tokens, tokens, row],
        [narrow, narrow, array(F32, 1, channels)], square, 4 << 20,
    )(rates, back_in, keys, values, key_part, value_part)
    return attended, query_grad, key_grad, value_grad, gain_grad.reshape(channels)


def solution(mesh):
    placed = (
        P("seq", "head"),
        P("seq", "head"),
        P("seq", "head"),
        P("head"),
        P("head"),
        P("seq", "head"),
    )
    return jax.shard_map(
        body,
        mesh=mesh,
        in_specs=placed,
        out_specs=(
            P("seq", "head"),
            P("seq", "head"),
            P("seq", "head"),
            P("seq", "head"),
            P("head"),
        ),
        check_vma=False,
    )
```

time: 337 us -> 146 us (0.43)
  blocking collectives: 178 us -> 27.6 us
  other arithmetic: 70.3 us -> 9.01 us
  starting transfers between devices: 0.08 us -> 58.2 us
  matrix products: 21.3 us -> 0 us
  Pallas kernels: 0 us -> 20 us
  between operations: 15 us -> 1.63 us
  waiting for transfers between devices: 31.5 us -> 18.8 us
  local copies, waits for them, and re-layouts: 15.3 us -> 9.46 us
    psum x3 -> x0, blocking collectives: 124 us -> none  [the longest x1 62.2 us: body(): lax.psum(jnp.sum(upstream * normed, axis=0).reshape(channels), 'seq')]
    select_n x64 -> x0, other arithmetic: 67.6 us -> none  [lap(): return jax.tree.map(lambda a, b: jnp.where(reached, a, b), new, before)]
    unnamed x1 -> x0, blocking collectives: 54.7 us -> none
    ppermute x0 -> x6, starting transfers between devices: none -> 35.7 us  [shift(): lax.ppermute(x, 'seq', [(i, (i + by * GROUP) % count) for i in range(coun...]
    all_gather x2 -> x0, waiting for transfers between devices: 31.5 us -> none  [carried_in(): everything = jax.tree.map(lambda part: lax.all_gather(part, axis), x)]
    all_to_all x0 -> x2, blocking collectives: none -> 27.6 us  [the longest x1 14.7 us: scan_seq(): parts = lax.all_to_all(x, 'seq', 0, 0, axis_index_groups=members)]
    all_to_all x0 -> x3, starting transfers between devices: none -> 22.5 us  [the longest x2 12.3 us: scan_seq(): return lax.all_to_all(out, 'seq', 0, 0, axis_index_groups=members)]
    dot_general x12 -> x0, matrix products: 21.3 us -> none  [the longest x1 2.83 us: body(): jnp.einsum('the,she->hts', mixed_grad, value_rows, preferred_element_type...]
  transfers between devices with their start and end apart: 2 -> 9, of which waited for: 2 -> 6; matrix products, arithmetic and copies ran while one was open for 6% -> 0% of each run, Pallas kernels for 0% -> 6%
where the time goes in v1:
time: 146 us; the launch traced here: 145 us
  starting transfers between devices  58.2 us (40%)
  blocking collectives  27.6 us (19%)
  Pallas kernels  20 us (14%)
  waiting for transfers between devices  18.8 us (13%)
  local copies, waits for them, and re-layouts  9.46 us (6%)
  other arithmetic  9.01 us (6%)
  between operations  1.63 us (1%)
    ppermute x6, starting transfers between devices, shift(): lax.ppermute(x, 'seq', [(i, (i + by * GROUP) % count) for i in range(coun...  35.7 us
    all_to_all x1, blocking collectives, scan_seq(): parts = lax.all_to_all(x, 'seq', 0, 0, axis_index_groups=members)  14.7 us
    all_to_all x1, blocking collectives, body(): received = lax.all_to_all(stats, 'head', 0, 0)  12.9 us
    all_to_all x2, starting transfers between devices, scan_seq(): return lax.all_to_all(out, 'seq', 0, 0, axis_index_groups=members)  12.3 us
    all_to_all x1, starting transfers between devices, scan_seq(): parts = lax.all_to_all(x, 'seq', 0, 0, axis_index_groups=members)  10.2 us
    unnamed x38, local copies, waits for them, and re-layouts  8.87 us
    unnamed x12, other arithmetic  7.58 us
    all_to_all x1, waiting for transfers between devices, scan_seq(): parts = lax.all_to_all(x, 'seq', 0, 0, axis_index_groups=members)  6.79 us
  transfers between devices with their start and end apart: 9, of which 6 were waited for; matrix products, arithmetic and copies ran while one was open for 0% of the time, Pallas kernels for 6%

profile of v1, /device:TPU:1, one launch (start us, length us, event | category | flops | bytes accessed | tf_op | source)
XLA Modules:
  0.0 144.6 jit_solution(15974863644242079793)
XLA Ops:
  3.4 2.9 %shard_map.101 = f32[8,64,128]{2,1,0:T(8,128)} custom-call(f32[4]{0:T(128)S(1)} %copy-done.12, bf16[512,512]{1,0:T(8,128)(2,1)S(1)} %copy-done, bf16[512,512]{1,0:T(8,128)(2,1)S(1)} %copy-done.2), custom_call_target="tpu_custom_call" | custom-call | flops 134217728 | bytes 2097152 | tf_op jit(solution)/shard_map/pallas_call | solution.py:247
  6.3 10.2 %all-to-all-start = ((f32[8,64,128]{2,1,0:T(8,128)}), f32[8,64,128]{2,1,0:T(8,128)S(1)}, u32[]{:S(2)}, u32[]{:S(2)}) async-start(f32[8,64,128]{2,1,0:T(8,128)} %shard_map.101), calls=%async_computation | async-start | bytes 524288 | tf_op jit(solution)/shard_map/all_to_all | solution.py:184
  18.4 6.8 %all-to-all-done = f32[8,64,128]{2,1,0:T(8,128)S(1)} async-done(((f32[8,64,128]{2,1,0:T(8,128)}), f32[8,64,128]{2,1,0:T(8,128)S(1)}, u32[]{:S(2)}, u32[]{:S(2)}) %all-to-all-start) | async-done | bytes 262176 | tf_op jit(solution)/shard_map/all_to_all | solution.py:184
  25.2 6.0 %collective-permute-start.2 = (f32[64,128]{1,0:T(8,128)S(1)}, f32[64,128]{1,0:T(8,128)S(1)}, u32[]{:S(2)}, u32[]{:S(2)}) collective-permute-start(f32[64,128]{1,0:T(8,128)S(1)} %fusion.6), channel_id=1, source_target_pairs={{0,128},{16,144},{32,160},{48,176},{64,192},{80,208},{96,224},{112... | collective-permute-start | bytes 98312 | tf_op jit(solution)/shard_map/ppermute | solution.py:173
  31.3 8.1 %collective-permute-start.1 = (f32[64,128]{1,0:T(8,128)S(1)}, f32[64,128]{1,0:T(8,128)S(1)}, u32[]{:S(2)}, u32[]{:S(2)}) collective-permute-start(f32[64,128]{1,0:T(8,128)S(1)} %fusion.6), channel_id=1, source_target_pairs={{0,256},{16,272},{32,288},{48,304},{64,320},{80,336},{96,352},{112... | collective-permute-start | bytes 98312 | tf_op jit(solution)/shard_map/ppermute | solution.py:173
  39.3 5.2 %collective-permute-start = (f32[64,128]{1,0:T(8,128)S(1)}, f32[64,128]{1,0:T(8,128)S(1)}, u32[]{:S(2)}, u32[]{:S(2)}) collective-permute-start(f32[64,128]{1,0:T(8,128)S(1)} %fusion.6), channel_id=1, source_target_pairs={{0,384},{16,400},{32,416},{48,432},{64,448},{80,464},{96,480},{112... | collective-permute-start | bytes 98312 | tf_op jit(solution)/shard_map/ppermute | solution.py:173
  45.0 3.1 %collective-permute-done = f32[64,128]{1,0:T(8,128)S(1)} collective-permute-done((f32[64,128]{1,0:T(8,128)S(1)}, f32[64,128]{1,0:T(8,128)S(1)}, u32[]{:S(2)}, u32[]{:S(2)}) %collective-permute-start) | collective-permute-done | bytes 32800 | tf_op jit(solution)/shard_map/ppermute | solution.py:173
  53.1 6.0 %all-to-all-start.1 = ((f32[8,64,128]{2,1,0:T(8,128)}), f32[8,64,128]{2,1,0:T(8,128)S(1)}, u32[]{:S(2)}, u32[]{:S(2)}) async-start(f32[8,64,128]{2,1,0:T(8,128)} %constant_dynamic-update-slice_fusion), calls=%async_computation.1 | async-start | bytes 524288 | tf_op jit(solution)/shard_map/all_to_all | solution.py:208
  59.2 3.1 %shard_map.102.intra = f32[512,512]{1,0:T(8,128)S(1)} custom-call(f32[4]{0:T(128)S(1)} %copy-done.13, bf16[512,512]{1,0:T(8,128)(2,1)S(1)} %copy-done.4, bf16[512,512]{1,0:T(8,128)(2,1)S(1)} %copy-done.1, bf16[512,512]{1,0:T(8,128)(2,1)S(1)} %copy-done.3), custom_call_target="tpu_custom_call" | custom-call | flops 536870912 | bytes 4194304 | tf_op jit(solution)/shard_map/pallas_call | solution.py:251
  62.3 5.6 %all-to-all-done.1.state.refs_8_ = f32[8,64,128]{2,1,0:T(8,128)S(1)} async-done(((f32[8,64,128]{2,1,0:T(8,128)}), f32[8,64,128]{2,1,0:T(8,128)S(1)}, u32[]{:S(2)}, u32[]{:S(2)}) %all-to-all-start.1) | async-done | bytes 262176 | tf_op jit(solution)/shard_map/all_to_all | solution.py:208
  67.9 2.1 %shard_map.103 = (f32[512,512]{1,0:T(8,128)S(1)}, f32[16,8,128]{2,1,0:T(8,128)S(1)}) custom-call(f32[4]{0:T(128)S(1)} %copy-done.13, bf16[512,512]{1,0:T(8,128)(2,1)S(1)} %copy-done.4, f32[8,64,128]{2,1,0:T(8,128)S(1)} %all-to-all-done.1.state.refs_8_, f32[512,512]{1,0:T(8,128)S(1)} %shard_map.102.intra, f32[1,512]{1,0:T(1,128)S(1)} %bitcast.176, ...), custom_call_target="tpu_custom_call" | custom-call | flops 134217728 | bytes 4194304 | tf_op jit(solution)/shard_map/pallas_call | solution.py:255
  70.0 12.9 %all_to_all.25.refs_1_ = f32[16,8,128]{2,1,0:T(8,128)S(1)} all-to-all(f32[16,8,128]{2,1,0:T(8,128)S(1)} %get-tuple-element.16), channel_id=1, replica_groups=mesh['seq'=32,'head'=16] {'head'}, dimensions={0} | all-to-all | bytes 131072 | tf_op jit(solution)/shard_map/all_to_all | solution.py:259
  82.9 2.6 %shard_map.104 = (bf16[512,512]{1,0:T(8,128)(2,1)S(1)}, f32[8,72,128]{2,1,0:T(8,128)S(1)}) custom-call(f32[4]{0:T(128)S(1)} %copy-done.13, f32[16,8,128]{2,1,0:T(8,128)S(1)} %all_to_all.25.refs_1_, f32[512,512]{1,0:T(8,128)S(1)} %get-tuple-element.17.refs_2_, f32[1,512]{1,0:T(1,128)S(1)} %bitcast.177, bf16[512,512]{1,0:T(8,128)(2,1)S(1)} %copy-done.5, ...), custom_call_target="tpu_custom_call" | custom-call | flops 134217728 | bytes 4194304 | tf_op jit(solution)/shard_map/pallas_call | solution.py:260
  85.5 14.7 %all_to_all.26 = f32[8,72,128]{2,1,0:T(8,128)S(1)} all-to-all(f32[8,72,128]{2,1,0:T(8,128)S(1)} %get-tuple-element.21), channel_id=1, replica_groups={{0,16,32,48,64,80,96,112},{128,144,160,176,192,208,224,240},{256,272,28..., dimensions={0} | all-to-all | bytes 589824 | tf_op jit(solution)/shard_map/all_to_all | solution.py:184
  100.3 5.2 %collective-permute-start.5 = (f32[72,128]{1,0:T(8,128)S(1)}, f32[72,128]{1,0:T(8,128)S(1)}, u32[]{:S(2)}, u32[]{:S(2)}) collective-permute-start(f32[72,128]{1,0:T(8,128)S(1)} %pad_maximum_fusion.1), channel_id=1, source_target_pairs={{0,384},{16,400},{32,416},{48,432},{64,448},{80,464},{96,480},{112... | collective-permute-start | bytes 110600 | tf_op jit(solution)/shard_map/ppermute | solution.py:173
  105.5 4.7 %collective-permute-start.4 = (f32[72,128]{1,0:T(8,128)S(1)}, f32[72,128]{1,0:T(8,128)S(1)}, u32[]{:S(2)}, u32[]{:S(2)}) collective-permute-start(f32[72,128]{1,0:T(8,128)S(1)} %pad_maximum_fusion.1), channel_id=1, source_target_pairs={{0,256},{16,272},{32,288},{48,304},{64,320},{80,336},{96,352},{112... | collective-permute-start | bytes 110600 | tf_op jit(solution)/shard_map/ppermute | solution.py:173
  110.2 6.5 %collective-permute-start.3 = (f32[72,128]{1,0:T(8,128)S(1)}, f32[72,128]{1,0:T(8,128)S(1)}, u32[]{:S(2)}, u32[]{:S(2)}) collective-permute-start(f32[72,128]{1,0:T(8,128)S(1)} %pad_maximum_fusion.1), channel_id=1, source_target_pairs={{0,128},{16,144},{32,160},{48,176},{64,192},{80,208},{96,224},{112... | collective-permute-start | bytes 110600 | tf_op jit(solution)/shard_map/ppermute | solution.py:173
  116.7 2.7 %collective-permute-done.4 = f32[72,128]{1,0:T(8,128)S(1)} collective-permute-done((f32[72,128]{1,0:T(8,128)S(1)}, f32[72,128]{1,0:T(8,128)S(1)}, u32[]{:S(2)}, u32[]{:S(2)}) %collective-permute-start.4) | collective-permute-done | bytes 36896 | tf_op jit(solution)/shard_map/ppermute | solution.py:173
  123.4 6.3 %all-to-all-start.4 = ((f32[8,72,128]{2,1,0:T(8,128)}), f32[8,72,128]{2,1,0:T(8,128)S(1)}, u32[]{:S(2)}, u32[]{:S(2)}) async-start(f32[8,72,128]{2,1,0:T(8,128)} %pad_maximum_fusion), calls=%async_computation.4 | async-start | bytes 589824 | tf_op jit(solution)/shard_map/all_to_all | solution.py:208
  129.7 1.0 copy-done.16
  130.8 6.1 %shard_map.105 = (bf16[512,512]{1,0:T(8,128)(2,1)}, bf16[512,512]{1,0:T(8,128)(2,1)}, f32[512,512]{1,0:T(8,128)S(1)}, f32[512,512]{1,0:T(8,128)S(1)}) custom-call(f32[4]{0:T(128)S(1)} %copy-done.13, f32[16,8,128]{2,1,0:T(8,128)S(1)} %all_to_all.25.refs_1_, f32[512,512]{1,0:T(8,128)S(1)} %copy-done.7, f32[1,512]{1,0:T(1,128)S(1)} %bitcast.178, ...), custom_call_target="tpu_custom_call" | custom-call | flops 1610612736 | bytes 6291456 | tf_op jit(solution)/shard_map/pallas_call | solution.py:265
  139.1 1.2 copy-done.9
  140.3 1.2 copy-done.11
  141.5 3.1 %shard_map.106 = (bf16[512,512]{1,0:T(8,128)(2,1)}, bf16[512,512]{1,0:T(8,128)(2,1)}, f32[1,512]{1,0:T(1,128)}) custom-call(f32[4]{0:T(128)S(1)} %copy-done.13, f32[8,72,128]{2,1,0:T(8,128)S(1)} %all-to-all-done.4.back, bf16[512,512]{1,0:T(8,128)(2,1)S(1)} %copy-done.1, bf16[512,512]{1,0:T(8,128)(2,1)S(1)} %copy-done.3, f32[512,512]{1,0:T(8,128)S(1)} %copy-done.9, ...), custom_call_target="tpu_custom_call" | custom-call | flops 268435456 | bytes 4194304 | tf_op jit(solution)/shard_map/pallas_call | solution.py:271
  (62 shorter events, 15.6 us)
Async XLA Ops:
  0.6 1.0 copy-start
  1.7 1.0 copy-start.2
  6.3 18.9 %all-to-all-start = ((f32[8,64,128]{2,1,0:T(8,128)}), f32[8,64,128]{2,1,0:T(8,128)S(1)}, u32[]{:S(2)}, u32[]{:S(2)}) async-start(f32[8,64,128]{2,1,0:T(8,128)} %shard_map.101), calls=%async_computation | async-start | bytes 524288 | tf_op jit(solution)/shard_map/all_to_all | solution.py:184
  25.2 19.4 %collective-permute-start.2 = (f32[64,128]{1,0:T(8,128)S(1)}, f32[64,128]{1,0:T(8,128)S(1)}, u32[]{:S(2)}, u32[]{:S(2)}) collective-permute-start(f32[64,128]{1,0:T(8,128)S(1)} %fusion.6), channel_id=1, source_target_pairs={{0,128},{16,144},{32,160},{48,176},{64,192},{80,208},{96,224},{112... | collective-permute-start | bytes 98312 | tf_op jit(solution)/shard_map/ppermute | solution.py:173
  31.3 13.7 %collective-permute-start.1 = (f32[64,128]{1,0:T(8,128)S(1)}, f32[64,128]{1,0:T(8,128)S(1)}, u32[]{:S(2)}, u32[]{:S(2)}) collective-permute-start(f32[64,128]{1,0:T(8,128)S(1)} %fusion.6), channel_id=1, source_target_pairs={{0,256},{16,272},{32,288},{48,304},{64,320},{80,336},{96,352},{112... | collective-permute-start | bytes 98312 | tf_op jit(solution)/shard_map/ppermute | solution.py:173
  39.3 8.8 %collective-permute-start = (f32[64,128]{1,0:T(8,128)S(1)}, f32[64,128]{1,0:T(8,128)S(1)}, u32[]{:S(2)}, u32[]{:S(2)}) collective-permute-start(f32[64,128]{1,0:T(8,128)S(1)} %fusion.6), channel_id=1, source_target_pairs={{0,384},{16,400},{32,416},{48,432},{64,448},{80,464},{96,480},{112... | collective-permute-start | bytes 98312 | tf_op jit(solution)/shard_map/ppermute | solution.py:173
  48.1 11.0 %copy-start.4 = (bf16[512,512]{1,0:T(8,128)(2,1)S(1)}, bf16[512,512]{1,0:T(8,128)(2,1)}, u32[]{:S(2)}) copy-start(bf16[512,512]{1,0:T(8,128)(2,1)} %refs_4_.3) | copy-start | bytes 1572868
  50.6 8.5 %copy-start.1 = (bf16[512,512]{1,0:T(8,128)(2,1)S(1)}, bf16[512,512]{1,0:T(8,128)(2,1)}, u32[]{:S(2)}) copy-start(bf16[512,512]{1,0:T(8,128)(2,1)} %keys.5) | copy-start | bytes 1572868
  50.6 8.5 %copy-start.3 = (bf16[512,512]{1,0:T(8,128)(2,1)S(1)}, bf16[512,512]{1,0:T(8,128)(2,1)}, u32[]{:S(2)}) copy-start(bf16[512,512]{1,0:T(8,128)(2,1)} %values.5) | copy-start | bytes 1572868
  53.1 14.8 %all-to-all-start.1 = ((f32[8,64,128]{2,1,0:T(8,128)}), f32[8,64,128]{2,1,0:T(8,128)S(1)}, u32[]{:S(2)}, u32[]{:S(2)}) async-start(f32[8,64,128]{2,1,0:T(8,128)} %constant_dynamic-update-slice_fusion), calls=%async_computation.1 | async-start | bytes 524288 | tf_op jit(solution)/shard_map/all_to_all | solution.py:208
  59.2 8.7 %copy-start.5 = (bf16[512,512]{1,0:T(8,128)(2,1)S(1)}, bf16[512,512]{1,0:T(8,128)(2,1)}, u32[]{:S(2)}) copy-start(bf16[512,512]{1,0:T(8,128)(2,1)} %refs_4_.2) | copy-start | bytes 1572868
  59.2 8.7 %copy-start.14 = (f32[512]{0:T(512)S(1)}, f32[512]{0:T(512)}, u32[]{:S(2)}) copy-start(f32[512]{0:T(512)} %param.10) | copy-start | bytes 6148
  70.0 15.5 %copy-start.6 = (f32[512,512]{1,0:T(8,128)}, f32[512,512]{1,0:T(8,128)S(1)}, u32[]{:S(2)}) copy-start(f32[512,512]{1,0:T(8,128)S(1)} %get-tuple-element.17.refs_2_) | copy-start | bytes 3145732
  85.5 33.9 %copy-start.15 = (bf16[512,512]{1,0:T(8,128)(2,1)}, bf16[512,512]{1,0:T(8,128)(2,1)S(1)}, u32[]{:S(2)}) copy-start(bf16[512,512]{1,0:T(8,128)(2,1)S(1)} %get-tuple-element.18.refs_7_) | copy-start | bytes 1572868
  100.2 19.2 %copy-start.17 = (f32[8,72,128]{2,1,0:T(8,128)}, f32[8,72,128]{2,1,0:T(8,128)S(1)}, u32[]{:S(2)}) copy-start(f32[8,72,128]{2,1,0:T(8,128)S(1)} %all_to_all.26) | copy-start | bytes 884740
  100.3 16.4 %collective-permute-start.5 = (f32[72,128]{1,0:T(8,128)S(1)}, f32[72,128]{1,0:T(8,128)S(1)}, u32[]{:S(2)}, u32[]{:S(2)}) collective-permute-start(f32[72,128]{1,0:T(8,128)S(1)} %pad_maximum_fusion.1), channel_id=1, source_target_pairs={{0,384},{16,400},{32,416},{48,432},{64,448},{80,464},{96,480},{112... | collective-permute-start | bytes 110600 | tf_op jit(solution)/shard_map/ppermute | solution.py:173
  105.5 13.9 %collective-permute-start.4 = (f32[72,128]{1,0:T(8,128)S(1)}, f32[72,128]{1,0:T(8,128)S(1)}, u32[]{:S(2)}, u32[]{:S(2)}) collective-permute-start(f32[72,128]{1,0:T(8,128)S(1)} %pad_maximum_fusion.1), channel_id=1, source_target_pairs={{0,256},{16,272},{32,288},{48,304},{64,320},{80,336},{96,352},{112... | collective-permute-start | bytes 110600 | tf_op jit(solution)/shard_map/ppermute | solution.py:173
  110.2 9.2 %collective-permute-start.3 = (f32[72,128]{1,0:T(8,128)S(1)}, f32[72,128]{1,0:T(8,128)S(1)}, u32[]{:S(2)}, u32[]{:S(2)}) collective-permute-start(f32[72,128]{1,0:T(8,128)S(1)} %pad_maximum_fusion.1), channel_id=1, source_target_pairs={{0,128},{16,144},{32,160},{48,176},{64,192},{80,208},{96,224},{112... | collective-permute-start | bytes 110600 | tf_op jit(solution)/shard_map/ppermute | solution.py:173
  119.5 10.3 %copy-start.7 = (f32[512,512]{1,0:T(8,128)S(1)}, f32[512,512]{1,0:T(8,128)}, u32[]{:S(2)}) copy-start(f32[512,512]{1,0:T(8,128)} %copy-done.6) | copy-start | bytes 3145732
  123.4 15.6 %all-to-all-start.4 = ((f32[8,72,128]{2,1,0:T(8,128)}), f32[8,72,128]{2,1,0:T(8,128)S(1)}, u32[]{:S(2)}, u32[]{:S(2)}) async-start(f32[8,72,128]{2,1,0:T(8,128)} %pad_maximum_fusion), calls=%async_computation.4 | async-start | bytes 589824 | tf_op jit(solution)/shard_map/all_to_all | solution.py:208
  129.7 1.0 copy-start.16
  136.9 1.0 copy-start.8
  139.1 1.2 copy-start.9
  140.3 1.2 copy-start.11
  (3 other events, 2.3 us)

commit v2 on v1

v2 whole, which is shorter than its diff:
```python
import jax
import jax.numpy as jnp
from jax import lax
from jax.experimental import pallas as pl
from jax.experimental.pallas import tpu as pltpu
from jax.sharding import PartitionSpec as P

epsilon = 1e-06
F32, BF16 = jnp.float32, jnp.bfloat16
GROUP = 8
EXTRA = 8
VMEM_LIMIT = 16 * 1024 * 1024


def dot(a, b, over_a, over_b):
    return lax.dot_general(a, b, (((over_a,), (over_b,)), ((), ())), preferred_element_type=F32)


def split(x):
    high = x.astype(BF16)
    return high, (x - high.astype(F32)).astype(BF16)


def dot_split(a, x, over_a, over_x):
    parts = jnp.concatenate(split(x), axis=1 - over_x)
    both = dot(a, parts, over_a, over_x)
    return both[:, : both.shape[1] // 2] + both[:, both.shape[1] // 2 :]


def rows_of(length, width=128):
    return lax.broadcasted_iota(jnp.int32, (length, width), 0).astype(F32)


def exp_scalar(x):
    return jnp.exp(jnp.full((8, 128), x, F32))[:1]


def head_in_of(rate, length):
    base = jnp.exp(-rate * (rows_of(128) + 1.0))
    return jnp.concatenate([base * exp_scalar(-rate * start) for start in range(0, length, 128)], axis=0)


def tail_out_of(rate, length):
    base = jnp.exp(-rate * (127.0 - rows_of(128)))
    return jnp.concatenate([base * exp_scalar(-rate * (length - 128 - start)) for start in range(0, length, 128)], axis=0)


def tile_weights(rate, half):
    distance = (
        lax.broadcasted_iota(jnp.int32, (half, half), 0) - lax.broadcasted_iota(jnp.int32, (half, half), 1)
    ).astype(F32)
    same = jnp.where(distance >= 0, jnp.exp(-rate * jnp.maximum(distance, 0.0)), 0.0)
    column = jnp.exp(-rate * (rows_of(half) + 1.0))
    row = jnp.exp(-rate * (half - 1.0 - lax.broadcasted_iota(jnp.int32, (8, half), 1).astype(F32)))[:1]
    return same, jnp.concatenate([column] * (half // 128), axis=1) * row


def block_sum_kernel(rates, keys, values, out):
    rate = rates[pl.program_id(0)]
    length, size = keys.shape
    scaled = values[...].astype(F32) * tail_out_of(rate, length)
    out[...] = dot_split(keys[...], scaled, 0, 0).reshape(2, size // 2, size)


def intra_kernel(rates, queries, keys, values, out):
    rate = rates[pl.program_id(0)]
    half = queries.shape[0] // 2
    same, across = tile_weights(rate, half)
    first, second = pl.ds(0, half), pl.ds(half, half)

    def probs(t, s, weight):
        return (dot(queries[t, :], keys[s, :], 1, 1) * weight).astype(BF16)

    out[first, :] = dot(probs(first, first, same), values[first, :], 1, 0)
    out[second, :] = dot(probs(second, first, across), values[first, :], 1, 0) + dot(
        probs(second, second, same), values[second, :], 1, 0
    )


def column(h, size):
    return pl.ds(h * size, size)


def mixed_kernel(rates, queries, state, intra, gain, cotangent, mixed, stats, square, inner):
    length = queries.shape[0]
    heads = rates.shape[0]
    size = queries.shape[1] // heads
    for h in range(heads):
        cols = column(h, size)
        state_in = state[pl.ds(2 * h, 2)].reshape(size, size)
        value = intra[:, cols] + head_in_of(rates[h], length) * dot_split(queries[:, cols], state_in, 1, 0)
        mixed[:, cols] = value
        new_square, new_inner = value * value, cotangent[:, cols].astype(F32) * gain[:, cols] * value
        if h > 0:
            new_square, new_inner = new_square + square[...], new_inner + inner[...]
        square[...] = new_square
        inner[...] = new_inner
    pieces = []
    for ref in (square, inner):
        for start in range(0, length, 128):
            pieces.append(jnp.sum(ref[pl.ds(start, 128), :].T, axis=0, keepdims=True))
    tile = jnp.concatenate(pieces, axis=0)
    stats[...] = jnp.broadcast_to(tile[None], stats.shape)


def token_scales(received, channels, inv_out, coef_out):
    total = jnp.sum(received[...], axis=0)
    chunks = total.shape[0] // 2
    inv = lax.rsqrt(total[:chunks] / channels + epsilon)
    coef = inv * inv * inv * total[chunks:] / channels
    for chunk in range(chunks):
        rows = pl.ds(chunk * 128, 128)
        inv_out[rows, :] = jnp.broadcast_to(inv[chunk : chunk + 1], (128, 128)).T
        if coef_out is not None:
            coef_out[rows, :] = jnp.broadcast_to(coef[chunk : chunk + 1], (128, 128)).T


def back_sum_kernel(channels, rates, received, mixed, gain, cotangent, queries, grad, sums, inv, coef):
    length = queries.shape[0]
    heads = rates.shape[0]
    size = queries.shape[1] // heads
    token_scales(received, channels, inv, coef)
    for h in range(heads):
        cols = column(h, size)
        upstream = cotangent[:, cols].astype(F32)
        value = mixed[:, cols]
        mixed_grad = (inv[...] * (upstream * gain[:, cols]) - value * coef[...]).astype(BF16)
        grad[:, cols] = mixed_grad
        scaled = mixed_grad.astype(F32) * head_in_of(rates[h], length)
        shards = pl.ds(2 * h, 2)
        sums[shards, pl.ds(0, size // 2), :] = dot_split(queries[:, cols], scaled, 0, 0).reshape(2, size // 2, size)
        gain_grad = jnp.sum(upstream * (value * inv[...]), axis=0, keepdims=True)
        sums[shards, pl.ds(size // 2, EXTRA), :] = jnp.broadcast_to(gain_grad[None], (2, EXTRA, size))


def grads_kernel(
    channels, rates, received, mixed, gain, queries, keys, values, grad, state,
    attended, query_grad, key_part, value_part, inv,
):
    head = pl.program_id(0)
    rate = rates[head]
    length, size = queries.shape
    half = length // 2

    @pl.when(head == 0)
    def _():
        token_scales(received, channels, inv, None)

    attended[...] = (mixed[...] * inv[...] * gain[...]).astype(BF16)
    same, across = tile_weights(rate, half)
    first, second = pl.ds(0, half), pl.ds(half, half)
    state_part = head_in_of(rate, length) * dot_split(grad[...], state[...].reshape(size, size), 1, 1)

    def weighted(a, b, t, s, weight):
        return (dot(a[t, :], b[s, :], 1, 1) * weight).astype(BF16)

    grads = [weighted(grad, values, *pair) for pair in ((first, first, same), (second, first, across), (second, second, same))]
    query_grad[first, :] = (dot(grads[0], keys[first, :], 1, 0) + state_part[:half]).astype(BF16)
    query_grad[second, :] = (
        dot(grads[1], keys[first, :], 1, 0) + dot(grads[2], keys[second, :], 1, 0) + state_part[half:]
    ).astype(BF16)
    key_part[first, :] = dot(grads[0], queries[first, :], 0, 0) + dot(grads[1], queries[second, :], 0, 0)
    key_part[second, :] = dot(grads[2], queries[second, :], 0, 0)
    probs = [weighted(queries, keys, *pair) for pair in ((first, first, same), (second, first, across), (second, second, same))]
    value_part[first, :] = dot(probs[0], grad[first, :], 0, 0) + dot(probs[1], grad[second, :], 0, 0)
    value_part[second, :] = dot(probs[2], grad[second, :], 0, 0)


def finish_kernel(rates, back, keys, values, key_part, value_part, key_grad, value_grad, gain_grad):
    rate = rates[pl.program_id(0)]
    length, size = keys.shape
    half = size // 2
    back_in = back[:, pl.ds(0, half), :].reshape(size, size)
    gain_grad[...] = back[0, pl.ds(half, 1), :]
    tail = tail_out_of(rate, length)
    key_grad[...] = (key_part[...] + tail * dot_split(values[...], back_in, 1, 1)).astype(BF16)
    value_grad[...] = (value_part[...] + tail * dot_split(keys[...], back_in, 1, 0)).astype(BF16)


def fold_factors(rates, length):
    member = lax.axis_index("seq") % GROUP
    rate = rates[member * rates.shape[0] // GROUP]
    return exp_scalar(-rate * length), exp_scalar(-rate * (length * GROUP))


def totals_kernel(length, rates, parts, out):
    factor, _ = fold_factors(rates, length)
    rows = parts.shape[1] - EXTRA
    total = parts[GROUP - 1, :rows]
    for k in range(GROUP - 2, -1, -1):
        total = factor * total + parts[k, :rows]
    extra = sum(parts[k, rows:] for k in range(GROUP))
    for g in range(out.shape[0]):
        out[g, :rows] = total
        out[g, rows:] = extra


def fold_forward_kernel(length, rates, parts, *refs):
    factor, group_factor = fold_factors(rates, length)
    *arrived, out = refs
    carry = arrived[-1][...]
    for ref in arrived[-2::-1]:
        carry = group_factor * carry + ref[...]
    for k in range(GROUP):
        out[k] = carry
        carry = factor * carry + parts[k]


def fold_back_kernel(length, rates, parts, arrived, out):
    factor, group_factor = fold_factors(rates, length)
    rows = parts.shape[1] - EXTRA
    group = lax.axis_index("seq") // GROUP
    carry = jnp.zeros((rows, parts.shape[2]), F32)
    for g in range(arrived.shape[0] - 1, 0, -1):
        carry = jnp.where(group < g, group_factor * carry + arrived[g, :rows], carry)
    extra = sum(arrived[g, rows:] for g in range(arrived.shape[0]))
    for k in range(GROUP - 1, -1, -1):
        out[k, :rows] = carry
        out[k, rows:] = extra
        carry = factor * carry + parts[k, :rows]


def whole_call(kernel, out_shape, operands, **rest):
    return pl.pallas_call(
        kernel,
        in_specs=[pl.BlockSpec(memory_space=pltpu.SMEM)] + [pl.BlockSpec(memory_space=pltpu.VMEM)] * (len(operands) - 1),
        out_specs=jax.tree.map(lambda _: pl.BlockSpec(memory_space=pltpu.VMEM), out_shape),
        out_shape=out_shape,
        compiler_params=pltpu.CompilerParams(vmem_limit_bytes=VMEM_LIMIT),
        **rest,
    )(*operands)


def scan_forward(x, rates, length):
    count = lax.axis_size("seq")
    groups = count // GROUP
    members = [[g * GROUP + j for j in range(GROUP)] for g in range(groups)]
    parts = lax.all_to_all(x, "seq", 0, 0, axis_index_groups=members)
    rate = lax.dynamic_index_in_dim(rates, lax.axis_index("seq") % GROUP * rates.shape[0] // GROUP, 0, False)
    factor = jnp.exp(-rate * length)
    total = parts[0]
    for k in range(1, GROUP):
        total = factor * total + parts[k]
    arrived = [
        lax.ppermute(total, "seq", [(i, i + by * GROUP) for i in range(count - by * GROUP)]) for by in range(1, groups)
    ]
    out = whole_call(lambda *refs: fold_forward_kernel(length, *refs), like(x), [rates, parts, *arrived])
    return lax.all_to_all(out, "seq", 0, 0, axis_index_groups=members)


def scan_back(x, rates, length):
    groups = lax.axis_size("seq") // GROUP
    members = [[g * GROUP + j for j in range(GROUP)] for g in range(groups)]
    across = [[g * GROUP + j for g in range(groups)] for j in range(GROUP)]
    parts = lax.all_to_all(x, "seq", 0, 0, axis_index_groups=members)
    totals = whole_call(
        lambda *refs: totals_kernel(length, *refs), jax.ShapeDtypeStruct((groups,) + x.shape[1:], F32), [rates, parts]
    )
    arrived = lax.all_to_all(totals, "seq", 0, 0, axis_index_groups=across)
    out = whole_call(lambda *refs: fold_back_kernel(length, *refs), like(x), [rates, parts, arrived])
    return lax.all_to_all(out, "seq", 0, 0, axis_index_groups=members)


def like(x):
    return jax.ShapeDtypeStruct(x.shape, x.dtype)


def body(queries, keys, values, rates, gain, cotangent):
    length, channels = queries.shape
    heads = rates.shape[0]
    size = channels // heads
    head_devices = lax.axis_size("head")
    total_channels = channels * head_devices
    gain_row = gain.reshape(1, channels)

    smem = pl.BlockSpec(memory_space=pltpu.SMEM)
    tokens = pl.BlockSpec((length, size), lambda h: (0, h))
    row = pl.BlockSpec((1, size), lambda h: (0, h))
    shards = pl.BlockSpec((2, size // 2, size), lambda h: (h, 0, 0))
    shards_extra = pl.BlockSpec((2, size // 2 + EXTRA, size), lambda h: (h, 0, 0))
    stats_shape = (head_devices, 2 * length // 128, 128)
    stats_spec = pl.BlockSpec(stats_shape, lambda h: (0, 0, 0))
    scratch = pltpu.VMEM((length, size), F32)

    def array(kind, *shape):
        return jax.ShapeDtypeStruct(shape, kind)

    def call(kernel, in_specs, out_specs, out_shape, flops, nbytes, scratches=()):
        return pl.pallas_call(
            kernel,
            grid=(heads,),
            in_specs=in_specs,
            out_specs=out_specs,
            out_shape=out_shape,
            scratch_shapes=list(scratches),
            compiler_params=pltpu.CompilerParams(vmem_limit_bytes=VMEM_LIMIT),
            cost_estimate=pl.CostEstimate(flops=flops, bytes_accessed=nbytes, transcendentals=0),
        )

    square = 2 * heads * length * length * size
    wide = array(F32, length, channels)
    narrow = array(BF16, length, channels)

    hbm = lambda x: pltpu.with_memory_space_constraint(x, pltpu.HBM)
    sums = call(
        block_sum_kernel, [smem, tokens, tokens], shards,
        array(F32, 2 * heads, size // 2, size), square // 2, 2 << 20,
    )(hbm(rates), hbm(keys), hbm(values))
    intra = call(intra_kernel, [smem, tokens, tokens, tokens], tokens, wide, 2 * square, 4 << 20)(
        rates, queries, keys, values
    )
    state_in = scan_forward(sums, rates, length)
    mixed, stats = whole_call(
        mixed_kernel, [wide, array(F32, *stats_shape)],
        [rates, queries, state_in, intra, gain_row, cotangent], scratch_shapes=[scratch, scratch],
    )
    received = lax.all_to_all(stats, "head", 0, 0)
    grad, back_sums = whole_call(
        lambda *refs: back_sum_kernel(total_channels, *refs),
        [narrow, array(F32, 2 * heads, size // 2 + EXTRA, size)],
        [rates, received, mixed, gain_row, cotangent, queries], scratch_shapes=[scratch, scratch],
    )
    attended, query_grad, key_part, value_part = call(
        lambda *refs: grads_kernel(total_channels, *refs),
        [smem, stats_spec, tokens, row, tokens, tokens, tokens, tokens, shards],
        [tokens, tokens, tokens, tokens], [narrow, narrow, wide, wide], 6 * square, 6 << 20, [scratch],
    )(rates, received, mixed, gain_row, queries, keys, values, grad, state_in)
    back_in = scan_back(back_sums, rates, length)
    key_grad, value_grad, gain_grad = call(
        finish_kernel, [smem, shards_extra, tokens, tokens, tokens, tokens], [tokens, tokens, row],
        [narrow, narrow, array(F32, 1, channels)], square, 4 << 20,
    )(rates, back_in, keys, values, key_part, value_part)
    return attended, query_grad, key_grad, value_grad, gain_grad.reshape(channels)


def solution(mesh):
    placed = (
        P("seq", "head"),
        P("seq", "head"),
        P("seq", "head"),
        P("head"),
        P("head"),
        P("seq", "head"),
    )
    return jax.shard_map(
        body,
        mesh=mesh,
        in_specs=placed,
        out_specs=(
            P("seq", "head"),
            P("seq", "head"),
            P("seq", "head"),
            P("seq", "head"),
            P("head"),
        ),
        check_vma=False,
    )
```

time: 146 us -> 132 us (0.904)
  blocking collectives: 27.6 us -> 48.5 us
  starting transfers between devices: 58.2 us -> 38.2 us
  other arithmetic: 9.01 us -> 0.02 us
  waiting for transfers between devices: 18.8 us -> 13.6 us
  local copies, waits for them, and re-layouts: 9.46 us -> 7.53 us
  Pallas kernels: 20 us -> 21.8 us
    all_to_all x1 -> x2, blocking collectives: 14.7 us -> 35.5 us  [the longest x1 20.8 us: scan_back(): arrived = lax.all_to_all(totals, 'seq', 0, 0, axis_index_groups=across)]
    ppermute x6 -> x3, starting transfers between devices: 35.7 us -> 15.5 us  [scan_forward(): lax.ppermute(total, 'seq', [(i, i + by * GROUP) for i in range(count - by...]
    unnamed x12 -> x0, other arithmetic: 7.58 us -> none
    ppermute x6 -> x3, waiting for transfers between devices: 6.18 us -> 0.99 us  [scan_forward(): lax.ppermute(total, 'seq', [(i, i + by * GROUP) for i in range(count - by...]
    unnamed x38 -> x28, local copies, waits for them, and re-layouts: 8.87 us -> 6.95 us
    pallas_call x2 -> x5, Pallas kernels: 4.69 us -> 5.8 us  [whole_call(): pl.pallas_call(kernel, in_specs=[pl.BlockSpec(memory_space=pltpu.SMEM)] +...]
  transfers between devices with their start and end apart: 9 -> 6, of which waited for: 6 -> 4; matrix products, arithmetic and copies ran while one was open for 0% -> 0% of each run, Pallas kernels for 6% -> 7%
where the time goes in v2:
time: 132 us; the launch traced here: 131 us
  blocking collectives  48.5 us (37%)
  starting transfers between devices  38.2 us (29%)
  Pallas kernels  21.8 us (17%)
  waiting for transfers between devices  13.6 us (10%)
  local copies, waits for them, and re-layouts  7.53 us (6%)
  between operations  1.48 us (1%)
    all_to_all x1, blocking collectives, scan_back(): arrived = lax.all_to_all(totals, 'seq', 0, 0, axis_index_groups=across)  20.8 us
    ppermute x3, starting transfers between devices, scan_forward(): lax.ppermute(total, 'seq', [(i, i + by * GROUP) for i in range(count - by...  15.5 us
    all_to_all x1, blocking collectives, scan_back(): parts = lax.all_to_all(x, 'seq', 0, 0, axis_index_groups=members)  14.7 us
    all_to_all x1, blocking collectives, body(): received = lax.all_to_all(stats, 'head', 0, 0)  13.1 us
    all_to_all x1, starting transfers between devices, scan_forward(): parts = lax.all_to_all(x, 'seq', 0, 0, axis_index_groups=members)  10.3 us
    unnamed x28, local copies, waits for them, and re-layouts  6.95 us
    all_to_all x1, starting transfers between devices, scan_back(): return lax.all_to_all(out, 'seq', 0, 0, axis_index_groups=members)  6.93 us
    all_to_all x1, waiting for transfers between devices, scan_forward(): parts = lax.all_to_all(x, 'seq', 0, 0, axis_index_groups=members)  6.8 us
  transfers between devices with their start and end apart: 6, of which 4 were waited for; matrix products, arithmetic and copies ran while one was open for 0% of the time, Pallas kernels for 7%

profile of v2, /device:TPU:1, one launch (start us, length us, event | category | flops | bytes accessed | tf_op | source)
XLA Modules:
  0.0 131.3 jit_solution(18273870229966494220)
XLA Ops:
  0.6 3.7 %shard_map.101 = f32[8,64,128]{2,1,0:T(8,128)} custom-call(f32[4]{0:T(128)} %rates.7, bf16[512,512]{1,0:T(8,128)(2,1)} %keys.5, bf16[512,512]{1,0:T(8,128)(2,1)} %values.5), custom_call_target="tpu_custom_call" | custom-call | flops 134217728 | bytes 2097152 | tf_op jit(solution)/shard_map/pallas_call | solution.py:305
  4.4 10.3 %all-to-all-start = ((f32[8,64,128]{2,1,0:T(8,128)}), f32[8,64,128]{2,1,0:T(8,128)S(1)}, u32[]{:S(2)}, u32[]{:S(2)}) async-start(f32[8,64,128]{2,1,0:T(8,128)} %shard_map.101), calls=%async_computation | async-start | bytes 524288 | tf_op jit(solution)/shard_map/all_to_all | solution.py:238
  16.6 6.8 %all-to-all-done.refs_1_ = f32[8,64,128]{2,1,0:T(8,128)S(1)} async-done(((f32[8,64,128]{2,1,0:T(8,128)}), f32[8,64,128]{2,1,0:T(8,128)S(1)}, u32[]{:S(2)}, u32[]{:S(2)}) %all-to-all-start) | async-done | bytes 262176 | tf_op jit(solution)/shard_map/all_to_all | solution.py:238
  23.5 7.2 %collective-permute-start.2 = (f32[64,128]{1,0:T(8,128)S(1)}, f32[64,128]{1,0:T(8,128)S(1)}, u32[]{:S(2)}, u32[]{:S(2)}) collective-permute-start(f32[64,128]{1,0:T(8,128)S(1)} %fusion), channel_id=1, source_target_pairs={{0,384},{16,400},{32,416},{48,432},{64,448},{80,464},{96,480},{112... | collective-permute-start | bytes 98312 | tf_op jit(solution)/shard_map/ppermute | solution.py:245
  30.7 3.7 %collective-permute-start.1 = (f32[64,128]{1,0:T(8,128)S(1)}, f32[64,128]{1,0:T(8,128)S(1)}, u32[]{:S(2)}, u32[]{:S(2)}) collective-permute-start(f32[64,128]{1,0:T(8,128)S(1)} %fusion), channel_id=1, source_target_pairs={{0,256},{16,272},{32,288},{48,304},{64,320},{80,336},{96,352},{112... | collective-permute-start | bytes 98312 | tf_op jit(solution)/shard_map/ppermute | solution.py:245
  34.3 4.6 %collective-permute-start = (f32[64,128]{1,0:T(8,128)S(1)}, f32[64,128]{1,0:T(8,128)S(1)}, u32[]{:S(2)}, u32[]{:S(2)}) collective-permute-start(f32[64,128]{1,0:T(8,128)S(1)} %fusion), channel_id=1, source_target_pairs={{0,128},{16,144},{32,160},{48,176},{64,192},{80,208},{96,224},{112... | collective-permute-start | bytes 98312 | tf_op jit(solution)/shard_map/ppermute | solution.py:245
  39.0 1.0 collective-permute-done.refs_2_
  40.0 1.3 shard_map.102
  41.3 5.5 %all-to-all-start.1 = ((f32[8,64,128]{2,1,0:T(8,128)}), f32[8,64,128]{2,1,0:T(8,128)S(1)}, u32[]{:S(2)}, u32[]{:S(2)}) async-start(f32[8,64,128]{2,1,0:T(8,128)} %shard_map.102), calls=%async_computation.1 | async-start | bytes 524288 | tf_op jit(solution)/shard_map/all_to_all | solution.py:248
  46.8 3.1 %shard_map.103.intra = f32[512,512]{1,0:T(8,128)S(1)} custom-call(f32[4]{0:T(128)S(1)} %copy-done.10, bf16[512,512]{1,0:T(8,128)(2,1)S(1)} %copy-done.2, bf16[512,512]{1,0:T(8,128)(2,1)S(1)} %copy-done, bf16[512,512]{1,0:T(8,128)(2,1)S(1)} %copy-done.1), custom_call_target="tpu_custom_call" | custom-call | flops 536870912 | bytes 4194304 | tf_op jit(solution)/shard_map/pallas_call | solution.py:309
  49.9 5.6 %all-to-all-done.1.state.refs_8_ = f32[8,64,128]{2,1,0:T(8,128)S(1)} async-done(((f32[8,64,128]{2,1,0:T(8,128)}), f32[8,64,128]{2,1,0:T(8,128)S(1)}, u32[]{:S(2)}, u32[]{:S(2)}) %all-to-all-start.1) | async-done | bytes 262176 | tf_op jit(solution)/shard_map/all_to_all | solution.py:248
  55.5 1.2 shard_map.104
  56.7 13.1 %all_to_all.30.refs_1_ = f32[16,8,128]{2,1,0:T(8,128)S(1)} all-to-all(f32[16,8,128]{2,1,0:T(8,128)S(1)} %get-tuple-element.16), channel_id=1, replica_groups=mesh['seq'=32,'head'=16] {'head'}, dimensions={0} | all-to-all | bytes 131072 | tf_op jit(solution)/shard_map/all_to_all | solution.py:317
  69.8 1.4 %shard_map.105 = (bf16[512,512]{1,0:T(8,128)(2,1)S(1)}, f32[8,72,128]{2,1,0:T(8,128)S(1)}) custom-call(f32[4]{0:T(128)S(1)} %copy-done.10, f32[16,8,128]{2,1,0:T(8,128)S(1)} %all_to_all.30.refs_1_, f32[512,512]{1,0:T(8,128)S(1)} %get-tuple-element.17.refs_2_, f32[1,512]{1,0:T(1,128)S(1)} %bitcast.6, bf16[512,512]{1,0:T(8,128)(2,1)S(1)} %copy-done.3, ...), custom_call_target="tpu_custom_call" | custom-call | tf_op jit(solution)/shard_map/pallas_call | solution.py:224
  72.0 14.7 %all_to_all.31.refs_1_ = f32[8,72,128]{2,1,0:T(8,128)S(1)} all-to-all(f32[8,72,128]{2,1,0:T(8,128)S(1)} %get-tuple-element.21), channel_id=1, replica_groups={{0,16,32,48,64,80,96,112},{128,144,160,176,192,208,224,240},{256,272,28..., dimensions={0} | all-to-all | bytes 589824 | tf_op jit(solution)/shard_map/all_to_all | solution.py:255
  87.3 20.8 %all_to_all.32.refs_2_ = f32[4,72,128]{2,1,0:T(8,128)S(1)} all-to-all(f32[4,72,128]{2,1,0:T(8,128)S(1)} %shard_map.107), channel_id=1, replica_groups={{0,128,256,384},{16,144,272,400},{32,160,288,416},{48,176,304,432},{64,..., dimensions={0} | all-to-all | bytes 294912 | tf_op jit(solution)/shard_map/all_to_all | solution.py:259
  108.1 1.3 %shard_map.108 = f32[8,72,128]{2,1,0:T(8,128)} custom-call(f32[4]{0:T(128)S(1)} %copy-done.10, f32[8,72,128]{2,1,0:T(8,128)S(1)} %all_to_all.31.refs_1_, f32[4,72,128]{2,1,0:T(8,128)S(1)} %all_to_all.32.refs_2_), custom_call_target="tpu_custom_call" | custom-call | tf_op jit(solution)/shard_map/pallas_call | solution.py:224
  109.4 6.9 %all-to-all-start.5 = ((f32[8,72,128]{2,1,0:T(8,128)}), f32[8,72,128]{2,1,0:T(8,128)S(1)}, u32[]{:S(2)}, u32[]{:S(2)}) async-start(f32[8,72,128]{2,1,0:T(8,128)} %shard_map.108), calls=%async_computation.5 | async-start | bytes 589824 | tf_op jit(solution)/shard_map/all_to_all | solution.py:261
  116.3 1.0 copy-done.13
  117.4 6.1 %shard_map.106 = (bf16[512,512]{1,0:T(8,128)(2,1)}, bf16[512,512]{1,0:T(8,128)(2,1)}, f32[512,512]{1,0:T(8,128)S(1)}, f32[512,512]{1,0:T(8,128)S(1)}) custom-call(f32[4]{0:T(128)S(1)} %copy-done.10, f32[16,8,128]{2,1,0:T(8,128)S(1)} %all_to_all.30.refs_1_, f32[512,512]{1,0:T(8,128)S(1)} %copy-done.5, f32[1,512]{1,0:T(1,128)S(1)} %bitcast.7, ...), custom_call_target="tpu_custom_call" | custom-call | flops 1610612736 | bytes 6291456 | tf_op jit(solution)/shard_map/pallas_call | solution.py:323
  123.5 1.0 copy-done.6
  125.7 1.2 copy-done.7
  126.9 1.2 copy-done.9
  128.2 3.1 %shard_map.109 = (bf16[512,512]{1,0:T(8,128)(2,1)}, bf16[512,512]{1,0:T(8,128)(2,1)}, f32[1,512]{1,0:T(1,128)}) custom-call(f32[4]{0:T(128)S(1)} %copy-done.10, f32[8,72,128]{2,1,0:T(8,128)S(1)} %all-to-all-done.5.back, bf16[512,512]{1,0:T(8,128)(2,1)S(1)} %copy-done, bf16[512,512]{1,0:T(8,128)(2,1)S(1)} %copy-done.1, f32[512,512]{1,0:T(8,128)S(1)} %copy-done.7, ...), custom_call_target="tpu_custom_call" | custom-call | flops 268435456 | bytes 4194304 | tf_op jit(solution)/shard_map/pallas_call | solution.py:329
  (30 shorter events, 3.9 us)
Async XLA Ops:
  4.4 42.4 %copy-start.2 = (bf16[512,512]{1,0:T(8,128)(2,1)S(1)}, bf16[512,512]{1,0:T(8,128)(2,1)}, u32[]{:S(2)}) copy-start(bf16[512,512]{1,0:T(8,128)(2,1)} %refs_4_.3) | copy-start | bytes 1572868
  4.4 19.1 %all-to-all-start = ((f32[8,64,128]{2,1,0:T(8,128)}), f32[8,64,128]{2,1,0:T(8,128)S(1)}, u32[]{:S(2)}, u32[]{:S(2)}) async-start(f32[8,64,128]{2,1,0:T(8,128)} %shard_map.101), calls=%async_computation | async-start | bytes 524288 | tf_op jit(solution)/shard_map/all_to_all | solution.py:238
  14.7 0.7 copy-start.10
  23.4 23.3 %copy-start = (bf16[512,512]{1,0:T(8,128)(2,1)S(1)}, bf16[512,512]{1,0:T(8,128)(2,1)}, u32[]{:S(2)}) copy-start(bf16[512,512]{1,0:T(8,128)(2,1)} %keys.5) | copy-start | bytes 1572868
  23.5 23.3 %copy-start.1 = (bf16[512,512]{1,0:T(8,128)(2,1)S(1)}, bf16[512,512]{1,0:T(8,128)(2,1)}, u32[]{:S(2)}) copy-start(bf16[512,512]{1,0:T(8,128)(2,1)} %values.5) | copy-start | bytes 1572868
  23.5 15.5 %collective-permute-start.2 = (f32[64,128]{1,0:T(8,128)S(1)}, f32[64,128]{1,0:T(8,128)S(1)}, u32[]{:S(2)}, u32[]{:S(2)}) collective-permute-start(f32[64,128]{1,0:T(8,128)S(1)} %fusion), channel_id=1, source_target_pairs={{0,384},{16,400},{32,416},{48,432},{64,448},{80,464},{96,480},{112... | collective-permute-start | bytes 98312 | tf_op jit(solution)/shard_map/ppermute | solution.py:245
  30.7 8.3 %collective-permute-start.1 = (f32[64,128]{1,0:T(8,128)S(1)}, f32[64,128]{1,0:T(8,128)S(1)}, u32[]{:S(2)}, u32[]{:S(2)}) collective-permute-start(f32[64,128]{1,0:T(8,128)S(1)} %fusion), channel_id=1, source_target_pairs={{0,256},{16,272},{32,288},{48,304},{64,320},{80,336},{96,352},{112... | collective-permute-start | bytes 98312 | tf_op jit(solution)/shard_map/ppermute | solution.py:245
  34.3 5.7 %collective-permute-start = (f32[64,128]{1,0:T(8,128)S(1)}, f32[64,128]{1,0:T(8,128)S(1)}, u32[]{:S(2)}, u32[]{:S(2)}) collective-permute-start(f32[64,128]{1,0:T(8,128)S(1)} %fusion), channel_id=1, source_target_pairs={{0,128},{16,144},{32,160},{48,176},{64,192},{80,208},{96,224},{112... | collective-permute-start | bytes 98312 | tf_op jit(solution)/shard_map/ppermute | solution.py:245
  41.3 14.2 %all-to-all-start.1 = ((f32[8,64,128]{2,1,0:T(8,128)}), f32[8,64,128]{2,1,0:T(8,128)S(1)}, u32[]{:S(2)}, u32[]{:S(2)}) async-start(f32[8,64,128]{2,1,0:T(8,128)} %shard_map.102), calls=%async_computation.1 | async-start | bytes 524288 | tf_op jit(solution)/shard_map/all_to_all | solution.py:248
  46.8 8.7 %copy-start.3 = (bf16[512,512]{1,0:T(8,128)(2,1)S(1)}, bf16[512,512]{1,0:T(8,128)(2,1)}, u32[]{:S(2)}) copy-start(bf16[512,512]{1,0:T(8,128)(2,1)} %refs_4_.2) | copy-start | bytes 1572868
  46.8 8.7 %copy-start.11 = (f32[512]{0:T(512)S(1)}, f32[512]{0:T(512)}, u32[]{:S(2)}) copy-start(f32[512]{0:T(512)} %param.10) | copy-start | bytes 6148
  56.7 14.5 %copy-start.4 = (f32[512,512]{1,0:T(8,128)}, f32[512,512]{1,0:T(8,128)S(1)}, u32[]{:S(2)}) copy-start(f32[512,512]{1,0:T(8,128)S(1)} %get-tuple-element.17.refs_2_) | copy-start | bytes 3145732
  71.2 0.8 copy-start.12
  86.7 29.6 %copy-start.5 = (f32[512,512]{1,0:T(8,128)S(1)}, f32[512,512]{1,0:T(8,128)}, u32[]{:S(2)}) copy-start(f32[512,512]{1,0:T(8,128)} %copy-done.4) | copy-start | bytes 3145732
  109.4 16.3 %all-to-all-start.5 = ((f32[8,72,128]{2,1,0:T(8,128)}), f32[8,72,128]{2,1,0:T(8,128)S(1)}, u32[]{:S(2)}, u32[]{:S(2)}) async-start(f32[8,72,128]{2,1,0:T(8,128)} %shard_map.108), calls=%async_computation.5 | async-start | bytes 589824 | tf_op jit(solution)/shard_map/all_to_all | solution.py:261
  116.3 1.0 copy-start.13
  123.5 1.0 copy-start.6
  124.5 1.0 copy-start.8
  125.7 1.2 copy-start.7
  126.9 1.2 copy-start.9

commit v3 on v2

--- a/solution.py
+++ b/solution.py
@@ -55,11 +55,32 @@
     return same, jnp.concatenate([column] * (half // 128), axis=1) * row
 
 
-def block_sum_kernel(rates, keys, values, out):
-    rate = rates[pl.program_id(0)]
-    length, size = keys.shape
-    scaled = values[...].astype(F32) * tail_out_of(rate, length)
-    out[...] = dot_split(keys[...], scaled, 0, 0).reshape(2, size // 2, size)
+def column(h, size):
+    return pl.ds(h * size, size)
+
+
+def block_sum_kernel(rates, keys, values, out, key_rows, value_rows, arrived):
+    length = keys.shape[0]
+    heads = rates.shape[0]
+    size = keys.shape[1] // heads
+    copies = []
+    for h in range(heads):
+        cols = column(h, size)
+        copies.append(
+            [
+                pltpu.make_async_copy(source.at[:, cols], rows.at[:, cols], arrived.at[2 * h + i])
+                for i, (source, rows) in enumerate(((values, value_rows), (keys, key_rows)))
+            ]
+        )
+        for copy in copies[-1]:
+            copy.start()
+    for h in range(heads):
+        cols = column(h, size)
+        tail = tail_out_of(rates[h], length)
+        for copy in copies[h]:
+            copy.wait()
+        scaled = value_rows[:, cols].astype(F32) * tail
+        out[pl.ds(2 * h, 2)] = dot_split(key_rows[:, cols], scaled, 0, 0).reshape(2, size // 2, size)
 
 
 def intra_kernel(rates, queries, keys, values, out):
@@ -75,10 +96,6 @@
     out[second, :] = dot(probs(second, first, across), values[first, :], 1, 0) + dot(
         probs(second, second, same), values[second, :], 1, 0
     )
-
-
-def column(h, size):
-    return pl.ds(h * size, size)
 
 
 def mixed_kernel(rates, queries, state, intra, gain, cotangent, mixed, stats, square, inner):
@@ -133,9 +150,25 @@
         sums[shards, pl.ds(size // 2, EXTRA), :] = jnp.broadcast_to(gain_grad[None], (2, EXTRA, size))
 
 
+def weighted(a, b, t, s, weight):
+    return (dot(a[t, :], b[s, :], 1, 1) * weight).astype(BF16)
+
+
+def value_part_kernel(rates, queries, keys, grad, value_part, token):
+    half = queries.shape[0] // 2
+    same, across = tile_weights(rates[pl.program_id(0)], half)
+    first, second = pl.ds(0, half), pl.ds(half, half)
+    lower = weighted(queries, keys, second, first, across)
+    value_part[first, :] = dot(weighted(queries, keys, first, first, same), grad[first, :], 0, 0) + dot(
+        lower, grad[second, :], 0, 0
+    )
+    value_part[second, :] = dot(weighted(queries, keys, second, second, same), grad[second, :], 0, 0)
+    token[...] = jnp.zeros_like(token)
+
+
 def grads_kernel(
     channels, rates, received, mixed, gain, queries, keys, values, grad, state,
-    attended, query_grad, key_part, value_part, inv,
+    attended, query_grad, key_part, token, inv,
 ):
     head = pl.program_id(0)
     rate = rates[head]
@@ -150,31 +183,39 @@
     same, across = tile_weights(rate, half)
     first, second = pl.ds(0, half), pl.ds(half, half)
     state_part = head_in_of(rate, length) * dot_split(grad[...], state[...].reshape(size, size), 1, 1)
-
-    def weighted(a, b, t, s, weight):
-        return (dot(a[t, :], b[s, :], 1, 1) * weight).astype(BF16)
-
-    grads = [weighted(grad, values, *pair) for pair in ((first, first, same), (second, first, across), (second, second, same))]
-    query_grad[first, :] = (dot(grads[0], keys[first, :], 1, 0) + state_part[:half]).astype(BF16)
+    upper = weighted(grad, values, first, first, same)
+    lower = weighted(grad, values, second, first, across)
+    final = weighted(grad, values, second, second, same)
+    query_grad[first, :] = (dot(upper, keys[first, :], 1, 0) + state_part[:half]).astype(BF16)
     query_grad[second, :] = (
-        dot(grads[1], keys[first, :], 1, 0) + dot(grads[2], keys[second, :], 1, 0) + state_part[half:]
+        dot(lower, keys[first, :], 1, 0) + dot(final, keys[second, :], 1, 0) + state_part[half:]
     ).astype(BF16)
-    key_part[first, :] = dot(grads[0], queries[first, :], 0, 0) + dot(grads[1], queries[second, :], 0, 0)
-    key_part[second, :] = dot(grads[2], queries[second, :], 0, 0)
-    probs = [weighted(queries, keys, *pair) for pair in ((first, first, same), (second, first, across), (second, second, same))]
-    value_part[first, :] = dot(probs[0], grad[first, :], 0, 0) + dot(probs[1], grad[second, :], 0, 0)
-    value_part[second, :] = dot(probs[2], grad[second, :], 0, 0)
-
-
-def finish_kernel(rates, back, keys, values, key_part, value_part, key_grad, value_grad, gain_grad):
-    rate = rates[pl.program_id(0)]
-    length, size = keys.shape
+    key_part[first, :] = dot(upper, queries[first, :], 0, 0) + dot(lower, queries[second, :], 0, 0)
+    key_part[second, :] = dot(final, queries[second, :], 0, 0)
+    token[...] = jnp.zeros_like(token)
+
+
+def finish_kernel(
+    rates, back, keys, values, key_part, value_part, key_grad, value_grad, gain_grad, key_rows, value_rows, sent
+):
+    length = keys.shape[0]
+    heads = rates.shape[0]
+    size = keys.shape[1] // heads
     half = size // 2
-    back_in = back[:, pl.ds(0, half), :].reshape(size, size)
-    gain_grad[...] = back[0, pl.ds(half, 1), :]
-    tail = tail_out_of(rate, length)
-    key_grad[...] = (key_part[...] + tail * dot_split(values[...], back_in, 1, 1)).astype(BF16)
-    value_grad[...] = (value_part[...] + tail * dot_split(keys[...], back_in, 1, 0)).astype(BF16)
+    copies = []
+    for h in range(heads):
+        cols = column(h, size)
+        back_in = back[pl.ds(2 * h, 2), pl.ds(0, half), :].reshape(size, size)
+        gain_grad[:, cols] = back[2 * h, pl.ds(half, 1), :]
+        tail = tail_out_of(rates[h], length)
+        key_rows[:, cols] = (key_part[:, cols] + tail * dot_split(values[:, cols], back_in, 1, 1)).astype(BF16)
+        value_rows[:, cols] = (value_part[:, cols] + tail * dot_split(keys[:, cols], back_in, 1, 0)).astype(BF16)
+        for i, (rows, target) in enumerate(((key_rows, key_grad), (value_rows, value_grad))):
+            copy = pltpu.make_async_copy(rows.at[:, cols], target.at[:, cols], sent.at[2 * h + i])
+            copy.start()
+            copies.append(copy)
+    for copy in copies:
+        copy.wait()
 
 
 def fold_factors(rates, length):
@@ -183,7 +224,7 @@
     return exp_scalar(-rate * length), exp_scalar(-rate * (length * GROUP))
 
 
-def totals_kernel(length, rates, parts, out):
+def totals_kernel(length, rates, parts, token, out):
     factor, _ = fold_factors(rates, length)
     rows = parts.shape[1] - EXTRA
     total = parts[GROUP - 1, :rows]
@@ -206,7 +247,7 @@
         carry = factor * carry + parts[k]
 
 
-def fold_back_kernel(length, rates, parts, arrived, out):
+def fold_back_kernel(length, rates, parts, arrived, token, out):
     factor, group_factor = fold_factors(rates, length)
     rows = parts.shape[1] - EXTRA
     group = lax.axis_index("seq") // GROUP
@@ -220,11 +261,16 @@
         carry = factor * carry + parts[k, :rows]
 
 
-def whole_call(kernel, out_shape, operands, **rest):
+def whole_call(kernel, out_shape, operands, in_specs=None, out_specs=None, **rest):
+    vmem = pl.BlockSpec(memory_space=pltpu.VMEM)
+    if in_specs is None:
+        in_specs = [pl.BlockSpec(memory_space=pltpu.SMEM)] + [vmem] * (len(operands) - 1)
+    if out_specs is None:
+        out_specs = jax.tree.map(lambda _: vmem, out_shape)
     return pl.pallas_call(
         kernel,
-        in_specs=[pl.BlockSpec(memory_space=pltpu.SMEM)] + [pl.BlockSpec(memory_space=pltpu.VMEM)] * (len(operands) - 1),
-        out_specs=jax.tree.map(lambda _: pl.BlockSpec(memory_space=pltpu.VMEM), out_shape),
+        in_specs=in_specs,
+        out_specs=out_specs,
         out_shape=out_shape,
         compiler_params=pltpu.CompilerParams(vmem_limit_bytes=VMEM_LIMIT),
         **rest,
@@ -248,16 +294,17 @@
     return lax.all_to_all(out, "seq", 0, 0, axis_index_groups=members)
 
 
-def scan_back(x, rates, length):
+def scan_back(x, rates, length, first_token, second_token):
     groups = lax.axis_size("seq") // GROUP
     members = [[g * GROUP + j for j in range(GROUP)] for g in range(groups)]
     across = [[g * GROUP + j for g in range(groups)] for j in range(GROUP)]
     parts = lax.all_to_all(x, "seq", 0, 0, axis_index_groups=members)
     totals = whole_call(
-        lambda *refs: totals_kernel(length, *refs), jax.ShapeDtypeStruct((groups,) + x.shape[1:], F32), [rates, parts]
+        lambda *refs: totals_kernel(length, *refs), jax.ShapeDtypeStruct((groups,) + x.shape[1:], F32),
+        [rates, parts, first_token],
     )
     arrived = lax.all_to_all(totals, "seq", 0, 0, axis_index_groups=across)
-    out = whole_call(lambda *refs: fold_back_kernel(length, *refs), like(x), [rates, parts, arrived])
+    out = whole_call(lambda *refs: fold_back_kernel(length, *refs), like(x), [rates, parts, arrived, second_token])
     return lax.all_to_all(out, "seq", 0, 0, axis_index_groups=members)
 
 
@@ -302,10 +349,15 @@
     narrow = array(BF16, length, channels)
 
     hbm = lambda x: pltpu.with_memory_space_constraint(x, pltpu.HBM)
-    sums = call(
-        block_sum_kernel, [smem, tokens, tokens], shards,
-        array(F32, 2 * heads, size // 2, size), square // 2, 2 << 20,
-    )(hbm(rates), hbm(keys), hbm(values))
+    vmem = lambda x: pltpu.with_memory_space_constraint(x, pltpu.VMEM)
+    anywhere = pl.BlockSpec(memory_space=pl.ANY)
+    in_vmem = pl.BlockSpec(memory_space=pltpu.VMEM)
+    rows_scratch = pltpu.VMEM((length, channels), BF16)
+    copies = pltpu.SemaphoreType.DMA((2 * heads,))
+    sums = whole_call(
+        block_sum_kernel, array(F32, 2 * heads, size // 2, size), [hbm(rates), hbm(keys), hbm(values)],
+        in_specs=[smem, anywhere, anywhere], scratch_shapes=[rows_scratch, rows_scratch, copies],
+    )
     intra = call(intra_kernel, [smem, tokens, tokens, tokens], tokens, wide, 2 * square, 4 << 20)(
         rates, queries, keys, values
     )
@@ -320,16 +372,24 @@
         [narrow, array(F32, 2 * heads, size // 2 + EXTRA, size)],
         [rates, received, mixed, gain_row, cotangent, queries], scratch_shapes=[scratch, scratch],
     )
-    attended, query_grad, key_part, value_part = call(
+    token = array(F32, 8, 128)
+    token_spec = pl.BlockSpec((8, 128), lambda h: (0, 0))
+    part = pltpu.VMEM((length, channels), F32)
+    value_part, first_token = call(
+        value_part_kernel, [smem, tokens, tokens, tokens], [tokens, token_spec],
+        [part, token], 2 * square, 4 << 20,
+    )(rates, queries, keys, grad)
+    attended, query_grad, key_part, second_token = call(
         lambda *refs: grads_kernel(total_channels, *refs),
         [smem, stats_spec, tokens, row, tokens, tokens, tokens, tokens, shards],
-        [tokens, tokens, tokens, tokens], [narrow, narrow, wide, wide], 6 * square, 6 << 20, [scratch],
+        [tokens, tokens, tokens, token_spec], [narrow, narrow, part, token], 4 * square, 6 << 20, [scratch],
     )(rates, received, mixed, gain_row, queries, keys, values, grad, state_in)
-    back_in = scan_back(back_sums, rates, length)
-    key_grad, value_grad, gain_grad = call(
-        finish_kernel, [smem, shards_extra, tokens, tokens, tokens, tokens], [tokens, tokens, row],
-        [narrow, narrow, array(F32, 1, channels)], square, 4 << 20,
-    )(rates, back_in, keys, values, key_part, value_part)
+    back_in = scan_back(back_sums, rates, length, first_token, second_token)
+    key_grad, value_grad, gain_grad = whole_call(
+        finish_kernel, [narrow, narrow, array(F32, 1, channels)],
+        [rates, back_in, keys, values, vmem(key_part), vmem(value_part)],
+        out_specs=[anywhere, anywhere, in_vmem], scratch_shapes=[rows_scratch, rows_scratch, copies],
+    )
     return attended, query_grad, key_grad, value_grad, gain_grad.reshape(channels)
 
 

time: 132 us -> 130 us (0.985)
  blocking collectives: 48.5 us -> 29.3 us
  waiting for transfers between devices: 13.6 us -> 22.8 us
  starting transfers between devices: 38.2 us -> 45.6 us
  Pallas kernels: 21.8 us -> 24 us
    all_to_all x2 -> x1, blocking collectives: 35.5 us -> 16.2 us  [scan_back(): return lax.all_to_all(out, 'seq', 0, 0, axis_index_groups=members)]
    all_to_all x1 -> x2, waiting for transfers between devices: 0.22 us -> 9.43 us  [the longest x1 4.98 us: scan_back(): arrived = lax.all_to_all(totals, 'seq', 0, 0, axis_index_groups=across)]
    all_to_all x1 -> x2, starting transfers between devices: 6.93 us -> 14.2 us  [the longest x1 8.45 us: scan_back(): arrived = lax.all_to_all(totals, 'seq', 0, 0, axis_index_groups=across)]
    pallas_call x7 -> x8, Pallas kernels: 12.6 us -> 16.3 us  [the longest x7 12.5 us: whole_call(): pl.pallas_call(kernel, in_specs=in_specs, out_specs=out_specs, out_shape=...]
    pallas_call x1, Pallas kernels: 6.13 us -> 4.59 us  [body(): call(lambda *refs: grads_kernel(total_channels, *refs), [smem, stats_spec...]
    unnamed x28 -> x26, local copies, waits for them, and re-layouts: 6.95 us -> 5.8 us
  transfers between devices with their start and end apart: 6 -> 7, of which waited for: 4 -> 5; matrix products, arithmetic and copies ran while one was open for 0% -> 0% of each run, Pallas kernels for 7% -> 9%
where the time goes in v3:
time: 130 us
  starting transfers between devices  45.6 us (35%)
  blocking collectives  29.3 us (23%)
  Pallas kernels  24 us (18%)
  waiting for transfers between devices  22.8 us (18%)
  local copies, waits for them, and re-layouts  6.39 us (5%)
  between operations  1.48 us (1%)
    all_to_all x1, blocking collectives, scan_back(): return lax.all_to_all(out, 'seq', 0, 0, axis_index_groups=members)  16.2 us
    ppermute x3, starting transfers between devices, scan_forward(): lax.ppermute(total, 'seq', [(i, i + by * GROUP) for i in range(count - by...  15.5 us
    all_to_all x1, blocking collectives, body(): received = lax.all_to_all(stats, 'head', 0, 0)  13.1 us
    pallas_call x7, Pallas kernels, whole_call(): pl.pallas_call(kernel, in_specs=in_specs, out_specs=out_specs, out_shape=...  12.5 us
    all_to_all x1, starting transfers between devices, scan_forward(): parts = lax.all_to_all(x, 'seq', 0, 0, axis_index_groups=members)  10.3 us
    all_to_all x1, starting transfers between devices, scan_back(): arrived = lax.all_to_all(totals, 'seq', 0, 0, axis_index_groups=across)  8.45 us
    all_to_all x1, waiting for transfers between devices, scan_forward(): parts = lax.all_to_all(x, 'seq', 0, 0, axis_index_groups=members)  6.8 us
    unnamed x26, local copies, waits for them, and re-layouts  5.8 us
  transfers between devices with their start and end apart: 7, of which 5 were waited for; matrix products, arithmetic and copies ran while one was open for 0% of the time, Pallas kernels for 9%

profile of v3, /device:TPU:1, one launch (start us, length us, event | category | flops | bytes accessed | tf_op | source)
XLA Modules:
  0.0 129.6 jit_solution(15131949135146875953)
XLA Ops:
  0.6 3.4 %shard_map.101 = f32[8,64,128]{2,1,0:T(8,128)} custom-call(f32[4]{0:T(128)} %rates.9, bf16[512,512]{1,0:T(8,128)(2,1)} %keys.7, bf16[512,512]{1,0:T(8,128)(2,1)} %values.5), custom_call_target="tpu_custom_call" | custom-call | tf_op jit(solution)/shard_map/pallas_call | solution.py:270
  4.1 10.3 %all-to-all-start = ((f32[8,64,128]{2,1,0:T(8,128)}), f32[8,64,128]{2,1,0:T(8,128)S(1)}, u32[]{:S(2)}, u32[]{:S(2)}) async-start(f32[8,64,128]{2,1,0:T(8,128)} %shard_map.101), calls=%async_computation | async-start | bytes 524288 | tf_op jit(solution)/shard_map/all_to_all | solution.py:284
  16.3 6.8 %all-to-all-done.refs_1_ = f32[8,64,128]{2,1,0:T(8,128)S(1)} async-done(((f32[8,64,128]{2,1,0:T(8,128)}), f32[8,64,128]{2,1,0:T(8,128)S(1)}, u32[]{:S(2)}, u32[]{:S(2)}) %all-to-all-start) | async-done | bytes 262176 | tf_op jit(solution)/shard_map/all_to_all | solution.py:284
  23.2 7.2 %collective-permute-start.2 = (f32[64,128]{1,0:T(8,128)S(1)}, f32[64,128]{1,0:T(8,128)S(1)}, u32[]{:S(2)}, u32[]{:S(2)}) collective-permute-start(f32[64,128]{1,0:T(8,128)S(1)} %fusion), channel_id=1, source_target_pairs={{0,384},{16,400},{32,416},{48,432},{64,448},{80,464},{96,480},{112... | collective-permute-start | bytes 98312 | tf_op jit(solution)/shard_map/ppermute | solution.py:291
  30.4 3.6 %collective-permute-start.1 = (f32[64,128]{1,0:T(8,128)S(1)}, f32[64,128]{1,0:T(8,128)S(1)}, u32[]{:S(2)}, u32[]{:S(2)}) collective-permute-start(f32[64,128]{1,0:T(8,128)S(1)} %fusion), channel_id=1, source_target_pairs={{0,256},{16,272},{32,288},{48,304},{64,320},{80,336},{96,352},{112... | collective-permute-start | bytes 98312 | tf_op jit(solution)/shard_map/ppermute | solution.py:291
  34.0 4.6 %collective-permute-start = (f32[64,128]{1,0:T(8,128)S(1)}, f32[64,128]{1,0:T(8,128)S(1)}, u32[]{:S(2)}, u32[]{:S(2)}) collective-permute-start(f32[64,128]{1,0:T(8,128)S(1)} %fusion), channel_id=1, source_target_pairs={{0,128},{16,144},{32,160},{48,176},{64,192},{80,208},{96,224},{112... | collective-permute-start | bytes 98312 | tf_op jit(solution)/shard_map/ppermute | solution.py:291
  39.7 1.3 %shard_map.102 = f32[8,64,128]{2,1,0:T(8,128)} custom-call(f32[4]{0:T(128)S(1)} %copy-done.8, f32[8,64,128]{2,1,0:T(8,128)S(1)} %all-to-all-done.refs_1_, f32[64,128]{1,0:T(8,128)S(1)} %collective-permute-done.refs_2_, f32[64,128]{1,0:T(8,128)S(1)} %collective-permute-done.1.refs_3_, f32[64,128]{1,0:T(8,128)S(1)} %collective-permute-done.2.refs_4_), custom_call_target="tpu_custom_call" | custom-call | tf_op jit(solution)/shard_map/pallas_call | solution.py:270
  41.0 5.5 %all-to-all-start.1 = ((f32[8,64,128]{2,1,0:T(8,128)}), f32[8,64,128]{2,1,0:T(8,128)S(1)}, u32[]{:S(2)}, u32[]{:S(2)}) async-start(f32[8,64,128]{2,1,0:T(8,128)} %shard_map.102), calls=%async_computation.1 | async-start | bytes 524288 | tf_op jit(solution)/shard_map/all_to_all | solution.py:294
  46.5 3.1 %shard_map.103.intra = f32[512,512]{1,0:T(8,128)S(1)} custom-call(f32[4]{0:T(128)S(1)} %copy-done.8, bf16[512,512]{1,0:T(8,128)(2,1)S(1)} %copy-done.2, bf16[512,512]{1,0:T(8,128)(2,1)S(1)} %copy-done, bf16[512,512]{1,0:T(8,128)(2,1)S(1)} %copy-done.1), custom_call_target="tpu_custom_call" | custom-call | flops 536870912 | bytes 4194304 | tf_op jit(solution)/shard_map/pallas_call | solution.py:361
  49.6 5.6 %all-to-all-done.1.state.refs_8_ = f32[8,64,128]{2,1,0:T(8,128)S(1)} async-done(((f32[8,64,128]{2,1,0:T(8,128)}), f32[8,64,128]{2,1,0:T(8,128)S(1)}, u32[]{:S(2)}, u32[]{:S(2)}) %all-to-all-start.1) | async-done | bytes 262176 | tf_op jit(solution)/shard_map/all_to_all | solution.py:294
  55.2 1.2 shard_map.104
  56.4 13.1 %all_to_all.30.refs_1_ = f32[16,8,128]{2,1,0:T(8,128)S(1)} all-to-all(f32[16,8,128]{2,1,0:T(8,128)S(1)} %get-tuple-element.18), channel_id=1, replica_groups=mesh['seq'=32,'head'=16] {'head'}, dimensions={0} | all-to-all | bytes 131072 | tf_op jit(solution)/shard_map/all_to_all | solution.py:369
  69.5 2.1 %shard_map.105 = (bf16[512,512]{1,0:T(8,128)(2,1)S(1)}, f32[8,72,128]{2,1,0:T(8,128)}) custom-call(f32[4]{0:T(128)S(1)} %copy-done.8, f32[16,8,128]{2,1,0:T(8,128)S(1)} %all_to_all.30.refs_1_, f32[512,512]{1,0:T(8,128)S(1)} %get-tuple-element.19.refs_2_, f32[1,512]{1,0:T(1,128)S(1)} %bitcast.6, bf16[512,512]{1,0:T(8,128)(2,1)S(1)} %copy-done.3, ...), custom_call_target="tpu_custom_call" | custom-call | tf_op jit(solution)/shard_map/pallas_call | solution.py:270
  72.4 5.8 %all-to-all-start.3 = ((f32[8,72,128]{2,1,0:T(8,128)}), f32[8,72,128]{2,1,0:T(8,128)S(1)}, u32[]{:S(2)}, u32[]{:S(2)}) async-start(f32[8,72,128]{2,1,0:T(8,128)} %get-tuple-element.23), calls=%async_computation.3 | async-start | bytes 589824 | tf_op jit(solution)/shard_map/all_to_all | solution.py:301
  78.2 1.0 copy-done.11
  79.2 3.9 %shard_map.107 = (f32[512,512]{1,0:T(8,128)S(1)}, f32[8,128]{1,0:T(8,128)S(1)}) custom-call(f32[4]{0:T(128)S(1)} %copy-done.8, bf16[512,512]{1,0:T(8,128)(2,1)S(1)} %copy-done.2, bf16[512,512]{1,0:T(8,128)(2,1)S(1)} %copy-done, bf16[512,512]{1,0:T(8,128)(2,1)S(1)} %copy-done.11), custom_call_target="tpu_custom_call" | custom-call | flops 536870912 | bytes 4194304 | tf_op jit(solution)/shard_map/pallas_call | solution.py:378
  83.1 4.5 %all-to-all-done.3.refs_1_ = f32[8,72,128]{2,1,0:T(8,128)S(1)} async-done(((f32[8,72,128]{2,1,0:T(8,128)}), f32[8,72,128]{2,1,0:T(8,128)S(1)}, u32[]{:S(2)}, u32[]{:S(2)}) %all-to-all-start.3) | async-done | bytes 294944 | tf_op jit(solution)/shard_map/all_to_all | solution.py:301
  87.6 1.3 shard_map.108
  88.8 8.4 %all-to-all-start.4 = ((f32[4,72,128]{2,1,0:T(8,128)}), f32[4,72,128]{2,1,0:T(8,128)S(1)}, u32[]{:S(2)}, u32[]{:S(2)}) async-start(f32[4,72,128]{2,1,0:T(8,128)} %shard_map.108), calls=%async_computation.4 | async-start | bytes 294912 | tf_op jit(solution)/shard_map/all_to_all | solution.py:306
  97.3 1.2 copy-done.5
  99.6 4.6 %shard_map.106 = (bf16[512,512]{1,0:T(8,128)(2,1)}, bf16[512,512]{1,0:T(8,128)(2,1)}, f32[512,512]{1,0:T(8,128)S(1)}, f32[8,128]{1,0:T(8,128)S(1)}) custom-call(f32[4]{0:T(128)S(1)} %copy-done.8, f32[16,8,128]{2,1,0:T(8,128)S(1)} %all_to_all.30.refs_1_, f32[512,512]{1,0:T(8,128)S(1)} %copy-done.5, f32[1,512]{1,0:T(1,128)S(1)} %bitcast.7, ...), custom_call_target="tpu_custom_call" | custom-call | flops 1073741824 | bytes 6291456 | tf_op jit(solution)/shard_map/pallas_call | solution.py:382
  105.2 5.0 %all-to-all-done.4.refs_2_ = f32[4,72,128]{2,1,0:T(8,128)S(1)} async-done(((f32[4,72,128]{2,1,0:T(8,128)}), f32[4,72,128]{2,1,0:T(8,128)S(1)}, u32[]{:S(2)}, u32[]{:S(2)}) %all-to-all-start.4) | async-done | bytes 147488 | tf_op jit(solution)/shard_map/all_to_all | solution.py:306
  110.8 16.2 %all_to_all.31.back = f32[8,72,128]{2,1,0:T(8,128)S(1)} all-to-all(f32[8,72,128]{2,1,0:T(8,128)S(1)} %shard_map.109), channel_id=1, replica_groups={{0,16,32,48,64,80,96,112},{128,144,160,176,192,208,224,240},{256,272,28..., dimensions={0} | all-to-all | bytes 589824 | tf_op jit(solution)/shard_map/all_to_all | solution.py:308
  127.0 2.6 %shard_map.110 = (bf16[512,512]{1,0:T(8,128)(2,1)}, bf16[512,512]{1,0:T(8,128)(2,1)}, f32[1,512]{1,0:T(1,128)}) custom-call(f32[4]{0:T(128)S(1)} %copy-done.8, f32[8,72,128]{2,1,0:T(8,128)S(1)} %all_to_all.31.back, bf16[512,512]{1,0:T(8,128)(2,1)S(1)} %copy-done, bf16[512,512]{1,0:T(8,128)(2,1)S(1)} %copy-done.1, f32[512,512]{1,0:T(8,128)S(1)} %copy-done.7, ...), custom_call_target="tpu_custom_call" | custom-call | tf_op jit(solution)/shard_map/pallas_call | solution.py:270
  (30 shorter events, 5.7 us)
Async XLA Ops:
  4.0 42.4 %copy-start.2 = (bf16[512,512]{1,0:T(8,128)(2,1)S(1)}, bf16[512,512]{1,0:T(8,128)(2,1)}, u32[]{:S(2)}) copy-start(bf16[512,512]{1,0:T(8,128)(2,1)} %queries.5) | copy-start | bytes 1572868
  4.1 19.1 %all-to-all-start = ((f32[8,64,128]{2,1,0:T(8,128)}), f32[8,64,128]{2,1,0:T(8,128)S(1)}, u32[]{:S(2)}, u32[]{:S(2)}) async-start(f32[8,64,128]{2,1,0:T(8,128)} %shard_map.101), calls=%async_computation | async-start | bytes 524288 | tf_op jit(solution)/shard_map/all_to_all | solution.py:284
  14.4 0.7 copy-start.8
  23.1 23.3 %copy-start = (bf16[512,512]{1,0:T(8,128)(2,1)S(1)}, bf16[512,512]{1,0:T(8,128)(2,1)}, u32[]{:S(2)}) copy-start(bf16[512,512]{1,0:T(8,128)(2,1)} %keys.7) | copy-start | bytes 1572868
  23.2 23.3 %copy-start.1 = (bf16[512,512]{1,0:T(8,128)(2,1)S(1)}, bf16[512,512]{1,0:T(8,128)(2,1)}, u32[]{:S(2)}) copy-start(bf16[512,512]{1,0:T(8,128)(2,1)} %values.5) | copy-start | bytes 1572868
  23.2 15.5 %collective-permute-start.2 = (f32[64,128]{1,0:T(8,128)S(1)}, f32[64,128]{1,0:T(8,128)S(1)}, u32[]{:S(2)}, u32[]{:S(2)}) collective-permute-start(f32[64,128]{1,0:T(8,128)S(1)} %fusion), channel_id=1, source_target_pairs={{0,384},{16,400},{32,416},{48,432},{64,448},{80,464},{96,480},{112... | collective-permute-start | bytes 98312 | tf_op jit(solution)/shard_map/ppermute | solution.py:291
  30.4 8.3 %collective-permute-start.1 = (f32[64,128]{1,0:T(8,128)S(1)}, f32[64,128]{1,0:T(8,128)S(1)}, u32[]{:S(2)}, u32[]{:S(2)}) collective-permute-start(f32[64,128]{1,0:T(8,128)S(1)} %fusion), channel_id=1, source_target_pairs={{0,256},{16,272},{32,288},{48,304},{64,320},{80,336},{96,352},{112... | collective-permute-start | bytes 98312 | tf_op jit(solution)/shard_map/ppermute | solution.py:291
  34.0 5.7 %collective-permute-start = (f32[64,128]{1,0:T(8,128)S(1)}, f32[64,128]{1,0:T(8,128)S(1)}, u32[]{:S(2)}, u32[]{:S(2)}) collective-permute-start(f32[64,128]{1,0:T(8,128)S(1)} %fusion), channel_id=1, source_target_pairs={{0,128},{16,144},{32,160},{48,176},{64,192},{80,208},{96,224},{112... | collective-permute-start | bytes 98312 | tf_op jit(solution)/shard_map/ppermute | solution.py:291
  41.0 14.2 %all-to-all-start.1 = ((f32[8,64,128]{2,1,0:T(8,128)}), f32[8,64,128]{2,1,0:T(8,128)S(1)}, u32[]{:S(2)}, u32[]{:S(2)}) async-start(f32[8,64,128]{2,1,0:T(8,128)} %shard_map.102), calls=%async_computation.1 | async-start | bytes 524288 | tf_op jit(solution)/shard_map/all_to_all | solution.py:294
  46.5 8.7 %copy-start.3 = (bf16[512,512]{1,0:T(8,128)(2,1)S(1)}, bf16[512,512]{1,0:T(8,128)(2,1)}, u32[]{:S(2)}) copy-start(bf16[512,512]{1,0:T(8,128)(2,1)} %refs_4_.2) | copy-start | bytes 1572868
  46.5 8.7 %copy-start.9 = (f32[512]{0:T(512)S(1)}, f32[512]{0:T(512)}, u32[]{:S(2)}) copy-start(f32[512]{0:T(512)} %param.10) | copy-start | bytes 6148
  56.4 15.2 %copy-start.4 = (f32[512,512]{1,0:T(8,128)}, f32[512,512]{1,0:T(8,128)S(1)}, u32[]{:S(2)}) copy-start(f32[512,512]{1,0:T(8,128)S(1)} %get-tuple-element.19.refs_2_) | copy-start | bytes 3145732
  71.6 0.8 copy-start.10
  72.4 15.2 %all-to-all-start.3 = ((f32[8,72,128]{2,1,0:T(8,128)}), f32[8,72,128]{2,1,0:T(8,128)S(1)}, u32[]{:S(2)}, u32[]{:S(2)}) async-start(f32[8,72,128]{2,1,0:T(8,128)} %get-tuple-element.23), calls=%async_computation.3 | async-start | bytes 589824 | tf_op jit(solution)/shard_map/all_to_all | solution.py:301
  78.2 1.0 copy-start.11
  88.8 21.3 %all-to-all-start.4 = ((f32[4,72,128]{2,1,0:T(8,128)}), f32[4,72,128]{2,1,0:T(8,128)S(1)}, u32[]{:S(2)}, u32[]{:S(2)}) async-start(f32[4,72,128]{2,1,0:T(8,128)} %shard_map.108), calls=%async_computation.4 | async-start | bytes 294912 | tf_op jit(solution)/shard_map/all_to_all | solution.py:306
  97.3 1.2 copy-start.5
  98.5 1.0 copy-start.12
  104.1 1.0 copy-start.6
  110.1 16.8 %copy-start.7 = (f32[512,512]{1,0:T(8,128)S(1)}, f32[512,512]{1,0:T(8,128)}, u32[]{:S(2)}) copy-start(f32[512,512]{1,0:T(8,128)} %copy-done.6) | copy-start | bytes 3145732

commit v4 on v3

--- a/solution.py
+++ b/solution.py
@@ -59,28 +59,34 @@
     return pl.ds(h * size, size)
 
 
-def block_sum_kernel(rates, keys, values, out, key_rows, value_rows, arrived):
+def half_start(mine, heads):
+    core = lax.axis_index("seq") % 2
+    return (core if mine else 1 - core) * (heads // 2)
+
+
+def block_sum_kernel(mine, rates, keys, values, out, key_rows, value_rows, arrived):
     length = keys.shape[0]
     heads = rates.shape[0]
     size = keys.shape[1] // heads
+    start = half_start(mine, heads)
     copies = []
-    for h in range(heads):
-        cols = column(h, size)
+    for h in range(heads // 2):
+        cols = pl.ds(pl.multiple_of((start + h) * size, size), size)
         copies.append(
             [
-                pltpu.make_async_copy(source.at[:, cols], rows.at[:, cols], arrived.at[2 * h + i])
+                pltpu.make_async_copy(source.at[:, cols], rows.at[:, column(h, size)], arrived.at[2 * h + i])
                 for i, (source, rows) in enumerate(((values, value_rows), (keys, key_rows)))
             ]
         )
         for copy in copies[-1]:
             copy.start()
-    for h in range(heads):
+    for h in range(heads // 2):
         cols = column(h, size)
-        tail = tail_out_of(rates[h], length)
+        tail = tail_out_of(rates[start + h], length)
         for copy in copies[h]:
             copy.wait()
         scaled = value_rows[:, cols].astype(F32) * tail
-        out[pl.ds(2 * h, 2)] = dot_split(key_rows[:, cols], scaled, 0, 0).reshape(2, size // 2, size)
+        out[h] = dot_split(key_rows[:, cols], scaled, 0, 0)
 
 
 def intra_kernel(rates, queries, keys, values, out):
@@ -98,13 +104,16 @@
     )
 
 
-def mixed_kernel(rates, queries, state, intra, gain, cotangent, mixed, stats, square, inner):
+def mixed_kernel(rates, queries, mine, other, intra, gain, cotangent, mixed, stats, state, square, inner):
     length = queries.shape[0]
     heads = rates.shape[0]
     size = queries.shape[1] // heads
+    start = half_start(True, heads)
     for h in range(heads):
         cols = column(h, size)
-        state_in = state[pl.ds(2 * h, 2)].reshape(size, size)
+        slot = h % (heads // 2)
+        state_in = jnp.where(start == h - slot, mine[slot], other[slot])
+        state[pl.ds(2 * h, 2)] = state_in.reshape(2, size // 2, size)
         value = intra[:, cols] + head_in_of(rates[h], length) * dot_split(queries[:, cols], state_in, 1, 0)
         mixed[:, cols] = value
         new_square, new_inner = value * value, cotangent[:, cols].astype(F32) * gain[:, cols] * value
@@ -236,15 +245,39 @@
         out[g, rows:] = extra
 
 
-def fold_forward_kernel(length, rates, parts, *refs):
-    factor, group_factor = fold_factors(rates, length)
-    *arrived, out = refs
-    carry = arrived[-1][...]
-    for ref in arrived[-2::-1]:
-        carry = group_factor * carry + ref[...]
-    for k in range(GROUP):
+def is_first(reverse):
+    return (lax.axis_index("seq") % 2) == (1 if reverse else 0)
+
+
+def chip_sum_kernel(length, reverse, rates, keep, received, out):
+    start = half_start(True, rates.shape[0])
+    first = is_first(reverse)
+    for h in range(keep.shape[0]):
+        factor = exp_scalar(-rates[start + h] * length)
+        own, other = keep[h], received[h]
+        out[h] = jnp.where(first, factor * own + other, factor * other + own)
+
+
+def fold_chips_kernel(length, reverse, rates, parts, out):
+    chips = parts.shape[0]
+    heads = rates.shape[0]
+    chip = lax.axis_index("seq") // 2
+    factor = exp_scalar(-rates[half_start(True, heads) + chip * (heads // 2) // chips] * (2 * length))
+    carry = jnp.zeros(parts.shape[1:], F32)
+    for k in range(chips - 1, -1, -1) if reverse else range(chips):
         out[k] = carry
         carry = factor * carry + parts[k]
+
+
+def states_kernel(length, reverse, rates, state, keep, received, mine, give):
+    start = half_start(True, rates.shape[0])
+    first = is_first(reverse)
+    for h in range(keep.shape[0]):
+        factor = exp_scalar(-rates[start + h] * length)
+        before = state[h]
+        after = factor * before + jnp.where(first, keep[h], received[h])
+        mine[h] = jnp.where(first, before, after)
+        give[h] = jnp.where(first, after, before)
 
 
 def fold_back_kernel(length, rates, parts, arrived, token, out):
@@ -277,21 +310,24 @@
     )(*operands)
 
 
-def scan_forward(x, rates, length):
-    count = lax.axis_size("seq")
-    groups = count // GROUP
-    members = [[g * GROUP + j for j in range(GROUP)] for g in range(groups)]
-    parts = lax.all_to_all(x, "seq", 0, 0, axis_index_groups=members)
-    rate = lax.dynamic_index_in_dim(rates, lax.axis_index("seq") % GROUP * rates.shape[0] // GROUP, 0, False)
-    factor = jnp.exp(-rate * length)
-    total = parts[0]
-    for k in range(1, GROUP):
-        total = factor * total + parts[k]
-    arrived = [
-        lax.ppermute(total, "seq", [(i, i + by * GROUP) for i in range(count - by * GROUP)]) for by in range(1, groups)
-    ]
-    out = whole_call(lambda *refs: fold_forward_kernel(length, *refs), like(x), [rates, parts, *arrived])
-    return lax.all_to_all(out, "seq", 0, 0, axis_index_groups=members)
+def swap(x):
+    return lax.ppermute(x, "seq", [(i, i ^ 1) for i in range(lax.axis_size("seq"))])
+
+
+def scan_chips(keep, received, rates, length, reverse):
+    chips = lax.axis_size("seq") // 2
+    members = [[2 * z + core for z in range(chips)] for core in range(2)]
+    flat = (chips, keep.shape[0] * keep.shape[1] // chips, keep.shape[2])
+    sums = whole_call(
+        lambda *refs: chip_sum_kernel(length, reverse, *refs), like(keep), [rates, keep, received]
+    )
+    parts = lax.all_to_all(sums.reshape(flat), "seq", 0, 0, axis_index_groups=members)
+    folded = whole_call(lambda *refs: fold_chips_kernel(length, reverse, *refs), like(parts), [rates, parts])
+    state = lax.all_to_all(folded, "seq", 0, 0, axis_index_groups=members).reshape(keep.shape)
+    mine, give = whole_call(
+        lambda *refs: states_kernel(length, reverse, *refs), [like(keep), like(keep)], [rates, state, keep, received]
+    )
+    return mine, swap(give)
 
 
 def scan_back(x, rates, length, first_token, second_token):
@@ -354,17 +390,24 @@
     in_vmem = pl.BlockSpec(memory_space=pltpu.VMEM)
     rows_scratch = pltpu.VMEM((length, channels), BF16)
     copies = pltpu.SemaphoreType.DMA((2 * heads,))
-    sums = whole_call(
-        block_sum_kernel, array(F32, 2 * heads, size // 2, size), [hbm(rates), hbm(keys), hbm(values)],
-        in_specs=[smem, anywhere, anywhere], scratch_shapes=[rows_scratch, rows_scratch, copies],
-    )
+    half_scratch = pltpu.VMEM((length, channels // 2), BF16)
+
+    def block_sums(mine):
+        return whole_call(
+            lambda *refs: block_sum_kernel(mine, *refs), array(F32, heads // 2, size, size),
+            [hbm(rates), hbm(keys), hbm(values)], in_specs=[smem, anywhere, anywhere],
+            scratch_shapes=[half_scratch, half_scratch, pltpu.SemaphoreType.DMA((heads,))],
+        )
+
+    other_sums = swap(block_sums(False))
+    own_sums = block_sums(True)
     intra = call(intra_kernel, [smem, tokens, tokens, tokens], tokens, wide, 2 * square, 4 << 20)(
         rates, queries, keys, values
     )
-    state_in = scan_forward(sums, rates, length)
-    mixed, stats = whole_call(
-        mixed_kernel, [wide, array(F32, *stats_shape)],
-        [rates, queries, state_in, intra, gain_row, cotangent], scratch_shapes=[scratch, scratch],
+    mine, other = scan_chips(own_sums, other_sums, rates, length, False)
+    mixed, stats, state_in = whole_call(
+        mixed_kernel, [wide, array(F32, *stats_shape), array(F32, 2 * heads, size // 2, size)],
+        [rates, queries, mine, other, intra, gain_row, cotangent], scratch_shapes=[scratch, scratch],
     )
     received = lax.all_to_all(stats, "head", 0, 0)
     grad, back_sums = whole_call(

time: 130 us -> 135 us (1.038)
  blocking collectives: 29.3 us -> 69.2 us
  starting transfers between devices: 45.6 us -> 23.8 us
  waiting for transfers between devices: 22.8 us -> 9.49 us
  Pallas kernels: 24 us -> 25.5 us
    all_to_all x0 -> x2, blocking collectives: none -> 39.9 us  [the longest x1 21.9 us: scan_chips(): lax.all_to_all(sums.reshape(flat), 'seq', 0, 0, axis_index_groups=members)]
    all_to_all x2 -> x0, starting transfers between devices: 15.8 us -> none  [the longest x1 10.3 us: scan_forward(): parts = lax.all_to_all(x, 'seq', 0, 0, axis_index_groups=members)]
    all_to_all x2 -> x0, waiting for transfers between devices: 12.4 us -> none  [the longest x1 6.8 us: scan_forward(): parts = lax.all_to_all(x, 'seq', 0, 0, axis_index_groups=members)]
    all_to_all x1, starting transfers between devices: 8.45 us -> 4.5 us  [scan_back(): arrived = lax.all_to_all(totals, 'seq', 0, 0, axis_index_groups=across)]
    pallas_call x7 -> x10, Pallas kernels: 12.5 us -> 13.9 us  [whole_call(): pl.pallas_call(kernel, in_specs=in_specs, out_specs=out_specs, out_shape=...]
    ppermute x3 -> x2, starting transfers between devices: 15.5 us -> 14.5 us  [swap(): lax.ppermute(x, 'seq', [(i, i ^ 1) for i in range(lax.axis_size('seq'))])]
  transfers between devices with their start and end apart: 7 -> 4, of which waited for: 5 -> 2; matrix products, arithmetic and copies ran while one was open for 0% -> 0% of each run, Pallas kernels for 9% -> 10%
where the time goes in v4:
time: 135 us
  blocking collectives  69.2 us (51%)
  Pallas kernels  25.5 us (19%)
  starting transfers between devices  23.8 us (18%)
  waiting for transfers between devices  9.49 us (7%)
  local copies, waits for them, and re-layouts  5.78 us (4%)
    all_to_all x1, blocking collectives, scan_chips(): lax.all_to_all(sums.reshape(flat), 'seq', 0, 0, axis_index_groups=members)  21.9 us
    all_to_all x1, blocking collectives, scan_chips(): lax.all_to_all(folded, 'seq', 0, 0, axis_index_groups=members)  18 us
    all_to_all x1, blocking collectives, scan_back(): return lax.all_to_all(out, 'seq', 0, 0, axis_index_groups=members)  16.2 us
    ppermute x2, starting transfers between devices, swap(): lax.ppermute(x, 'seq', [(i, i ^ 1) for i in range(lax.axis_size('seq'))])  14.5 us
    pallas_call x10, Pallas kernels, whole_call(): pl.pallas_call(kernel, in_specs=in_specs, out_specs=out_specs, out_shape=...  13.9 us
    all_to_all x1, blocking collectives, body(): received = lax.all_to_all(stats, 'head', 0, 0)  13.1 us
    unnamed x26, local copies, waits for them, and re-layouts  5.78 us
    all_to_all x1, waiting for transfers between devices, scan_back(): arrived = lax.all_to_all(totals, 'seq', 0, 0, axis_index_groups=across)  5.02 us
  transfers between devices with their start and end apart: 4, of which 2 were waited for; matrix products, arithmetic and copies ran while one was open for 0% of the time, Pallas kernels for 10%

profile of v4, /device:TPU:1, one launch (start us, length us, event | category | flops | bytes accessed | tf_op | source)
XLA Modules:
  0.0 134.5 jit_solution(6832808606468163290)
XLA Ops:
  0.6 2.2 %shard_map.102 = f32[2,128,128]{2,1,0:T(8,128)S(1)} custom-call(f32[4]{0:T(128)} %rates.7, bf16[512,512]{1,0:T(8,128)(2,1)} %keys.5, bf16[512,512]{1,0:T(8,128)(2,1)} %values.3), custom_call_target="tpu_custom_call" | custom-call | tf_op jit(solution)/shard_map/pallas_call | solution.py:303
  2.8 8.8 %collective-permute-start = (f32[2,128,128]{2,1,0:T(8,128)S(1)}, f32[2,128,128]{2,1,0:T(8,128)S(1)}, u32[]{:S(2)}, u32[]{:S(2)}) collective-permute-start(f32[2,128,128]{2,1,0:T(8,128)S(1)} %shard_map.102), channel_id=1, source_target_pairs={{0,16},{16,0},{32,48},{48,32},{64,80},{80,64},{96,112},{112,96},{1... | collective-permute-start | bytes 393224 | tf_op jit(solution)/shard_map/ppermute | solution.py:314
  11.6 2.2 %shard_map.101.refs_1_.refs_2_ = f32[2,128,128]{2,1,0:T(8,128)S(1)} custom-call(f32[4]{0:T(128)} %rates.7, bf16[512,512]{1,0:T(8,128)(2,1)} %keys.5, bf16[512,512]{1,0:T(8,128)(2,1)} %values.3), custom_call_target="tpu_custom_call" | custom-call | tf_op jit(solution)/shard_map/pallas_call | solution.py:303
  14.4 21.9 %all_to_all.30.refs_1_ = f32[16,16,128]{2,1,0:T(8,128)S(1)} all-to-all(f32[16,16,128]{2,1,0:T(8,128)S(1)} %bitcast.5), channel_id=1, replica_groups={{0,32,64,96,128,160,192,224,256,288,320,352,384,416,448,480},{16,48,80,..., dimensions={0} | all-to-all | bytes 262144 | tf_op jit(solution)/shard_map/all_to_all | solution.py:324
  37.0 18.0 %all_to_all.31 = f32[16,16,128]{2,1,0:T(8,128)S(1)} all-to-all(f32[16,16,128]{2,1,0:T(8,128)S(1)} %shard_map.104), channel_id=1, replica_groups={{0,32,64,96,128,160,192,224,256,288,320,352,384,416,448,480},{16,48,80,..., dimensions={0} | all-to-all | bytes 262144 | tf_op jit(solution)/shard_map/all_to_all | solution.py:326
  55.5 5.7 %collective-permute-start.1 = (f32[2,128,128]{2,1,0:T(8,128)S(1)}, f32[2,128,128]{2,1,0:T(8,128)S(1)}, u32[]{:S(2)}, u32[]{:S(2)}) collective-permute-start(f32[2,128,128]{2,1,0:T(8,128)S(1)} %get-tuple-element.22), channel_id=1, source_target_pairs={{0,16},{16,0},{32,48},{48,32},{64,80},{80,64},{96,112},{112,96},{1... | collective-permute-start | bytes 393224 | tf_op jit(solution)/shard_map/ppermute | solution.py:314
  61.3 3.1 %shard_map.106.intra = f32[512,512]{1,0:T(8,128)S(1)} custom-call(f32[4]{0:T(128)S(1)} %copy-done.8, bf16[512,512]{1,0:T(8,128)(2,1)S(1)} %copy-done.2, bf16[512,512]{1,0:T(8,128)(2,1)S(1)} %copy-done, bf16[512,512]{1,0:T(8,128)(2,1)S(1)} %copy-done.1), custom_call_target="tpu_custom_call" | custom-call | flops 536870912 | bytes 4194304 | tf_op jit(solution)/shard_map/pallas_call | solution.py:404
  65.1 1.2 shard_map.107
  66.3 13.1 %all_to_all.32.refs_1_ = f32[16,8,128]{2,1,0:T(8,128)S(1)} all-to-all(f32[16,8,128]{2,1,0:T(8,128)S(1)} %get-tuple-element.23), channel_id=1, replica_groups=mesh['seq'=32,'head'=16] {'head'}, dimensions={0} | all-to-all | bytes 131072 | tf_op jit(solution)/shard_map/all_to_all | solution.py:412
  79.4 2.1 %shard_map.108 = (bf16[512,512]{1,0:T(8,128)(2,1)S(1)}, f32[8,72,128]{2,1,0:T(8,128)}) custom-call(f32[4]{0:T(128)S(1)} %copy-done.8, f32[16,8,128]{2,1,0:T(8,128)S(1)} %all_to_all.32.refs_1_, f32[512,512]{1,0:T(8,128)S(1)} %get-tuple-element.24.refs_2_, f32[1,512]{1,0:T(1,128)S(1)} %bitcast.7, bf16[512,512]{1,0:T(8,128)(2,1)S(1)} %copy-done.3, ...), custom_call_target="tpu_custom_call" | custom-call | tf_op jit(solution)/shard_map/pallas_call | solution.py:303
  81.5 0.8 copy-done.10
  82.3 4.8 %all-to-all-start.3 = ((f32[8,72,128]{2,1,0:T(8,128)}), f32[8,72,128]{2,1,0:T(8,128)S(1)}, u32[]{:S(2)}, u32[]{:S(2)}) async-start(f32[8,72,128]{2,1,0:T(8,128)} %get-tuple-element.29), calls=%async_computation.3 | async-start | bytes 589824 | tf_op jit(solution)/shard_map/all_to_all | solution.py:337
  87.1 1.0 copy-done.11
  88.1 3.9 %shard_map.110 = (f32[512,512]{1,0:T(8,128)S(1)}, f32[8,128]{1,0:T(8,128)S(1)}) custom-call(f32[4]{0:T(128)S(1)} %copy-done.8, bf16[512,512]{1,0:T(8,128)(2,1)S(1)} %copy-done.2, bf16[512,512]{1,0:T(8,128)(2,1)S(1)} %copy-done, bf16[512,512]{1,0:T(8,128)(2,1)S(1)} %copy-done.11), custom_call_target="tpu_custom_call" | custom-call | flops 536870912 | bytes 4194304 | tf_op jit(solution)/shard_map/pallas_call | solution.py:421
  92.0 4.5 %all-to-all-done.3.refs_1_ = f32[8,72,128]{2,1,0:T(8,128)S(1)} async-done(((f32[8,72,128]{2,1,0:T(8,128)}), f32[8,72,128]{2,1,0:T(8,128)S(1)}, u32[]{:S(2)}, u32[]{:S(2)}) %all-to-all-start.3) | async-done | bytes 294944 | tf_op jit(solution)/shard_map/all_to_all | solution.py:337
  96.5 1.3 shard_map.111
  97.7 4.5 %all-to-all-start.4 = ((f32[4,72,128]{2,1,0:T(8,128)}), f32[4,72,128]{2,1,0:T(8,128)S(1)}, u32[]{:S(2)}, u32[]{:S(2)}) async-start(f32[4,72,128]{2,1,0:T(8,128)} %shard_map.111), calls=%async_computation.4 | async-start | bytes 294912 | tf_op jit(solution)/shard_map/all_to_all | solution.py:342
  102.2 1.2 copy-done.5
  103.4 1.0 copy-done.12
  104.5 4.6 %shard_map.109 = (bf16[512,512]{1,0:T(8,128)(2,1)}, bf16[512,512]{1,0:T(8,128)(2,1)}, f32[512,512]{1,0:T(8,128)S(1)}, f32[8,128]{1,0:T(8,128)S(1)}) custom-call(f32[4]{0:T(128)S(1)} %copy-done.8, f32[16,8,128]{2,1,0:T(8,128)S(1)} %all_to_all.32.refs_1_, f32[512,512]{1,0:T(8,128)S(1)} %copy-done.5, f32[1,512]{1,0:T(1,128)S(1)} %bitcast.8, ...), custom_call_target="tpu_custom_call" | custom-call | flops 1073741824 | bytes 6291456 | tf_op jit(solution)/shard_map/pallas_call | solution.py:425
  109.1 1.0 copy-done.6
  110.1 5.0 %all-to-all-done.4.refs_2_ = f32[4,72,128]{2,1,0:T(8,128)S(1)} async-done(((f32[4,72,128]{2,1,0:T(8,128)}), f32[4,72,128]{2,1,0:T(8,128)S(1)}, u32[]{:S(2)}, u32[]{:S(2)}) %all-to-all-start.4) | async-done | bytes 147488 | tf_op jit(solution)/shard_map/all_to_all | solution.py:342
  115.7 16.2 %all_to_all.33.back = f32[8,72,128]{2,1,0:T(8,128)S(1)} all-to-all(f32[8,72,128]{2,1,0:T(8,128)S(1)} %shard_map.112), channel_id=1, replica_groups={{0,16,32,48,64,80,96,112},{128,144,160,176,192,208,224,240},{256,272,28..., dimensions={0} | all-to-all | bytes 589824 | tf_op jit(solution)/shard_map/all_to_all | solution.py:344
  131.9 2.6 %shard_map.113 = (bf16[512,512]{1,0:T(8,128)(2,1)}, bf16[512,512]{1,0:T(8,128)(2,1)}, f32[1,512]{1,0:T(1,128)}) custom-call(f32[4]{0:T(128)S(1)} %copy-done.8, f32[8,72,128]{2,1,0:T(8,128)S(1)} %all_to_all.33.back, bf16[512,512]{1,0:T(8,128)(2,1)S(1)} %copy-done, bf16[512,512]{1,0:T(8,128)(2,1)S(1)} %copy-done.1, f32[512,512]{1,0:T(8,128)S(1)} %copy-done.7, ...), custom_call_target="tpu_custom_call" | custom-call | tf_op jit(solution)/shard_map/pallas_call | solution.py:303
  (27 shorter events, 3.1 us)
Async XLA Ops:
  2.8 11.0 %copy-start.8 = (f32[4]{0:T(128)S(1)}, f32[4]{0:T(128)}, u32[]{:S(2)}) copy-start(f32[4]{0:T(128)} %rates.7) | copy-start | bytes 52
  2.8 11.0 %collective-permute-start = (f32[2,128,128]{2,1,0:T(8,128)S(1)}, f32[2,128,128]{2,1,0:T(8,128)S(1)}, u32[]{:S(2)}, u32[]{:S(2)}) collective-permute-start(f32[2,128,128]{2,1,0:T(8,128)S(1)} %shard_map.102), channel_id=1, source_target_pairs={{0,16},{16,0},{32,48},{48,32},{64,80},{80,64},{96,112},{112,96},{1... | collective-permute-start | bytes 393224 | tf_op jit(solution)/shard_map/ppermute | solution.py:314
  13.8 47.5 %copy-start.2 = (bf16[512,512]{1,0:T(8,128)(2,1)S(1)}, bf16[512,512]{1,0:T(8,128)(2,1)}, u32[]{:S(2)}) copy-start(bf16[512,512]{1,0:T(8,128)(2,1)} %queries.5) | copy-start | bytes 1572868
  14.4 46.9 %copy-start.1 = (bf16[512,512]{1,0:T(8,128)(2,1)S(1)}, bf16[512,512]{1,0:T(8,128)(2,1)}, u32[]{:S(2)}) copy-start(bf16[512,512]{1,0:T(8,128)(2,1)} %values.3) | copy-start | bytes 1572868
  36.4 24.9 %copy-start = (bf16[512,512]{1,0:T(8,128)(2,1)S(1)}, bf16[512,512]{1,0:T(8,128)(2,1)}, u32[]{:S(2)}) copy-start(bf16[512,512]{1,0:T(8,128)(2,1)} %keys.5) | copy-start | bytes 1572868
  55.5 8.9 %copy-start.3 = (bf16[512,512]{1,0:T(8,128)(2,1)S(1)}, bf16[512,512]{1,0:T(8,128)(2,1)}, u32[]{:S(2)}) copy-start(bf16[512,512]{1,0:T(8,128)(2,1)} %refs_4_.2) | copy-start | bytes 1572868
  55.5 8.8 %collective-permute-start.1 = (f32[2,128,128]{2,1,0:T(8,128)S(1)}, f32[2,128,128]{2,1,0:T(8,128)S(1)}, u32[]{:S(2)}, u32[]{:S(2)}) collective-permute-start(f32[2,128,128]{2,1,0:T(8,128)S(1)} %get-tuple-element.22), channel_id=1, source_target_pairs={{0,16},{16,0},{32,48},{48,32},{64,80},{80,64},{96,112},{112,96},{1... | collective-permute-start | bytes 393224 | tf_op jit(solution)/shard_map/ppermute | solution.py:314
  64.4 0.7 copy-start.9
  66.3 15.2 %copy-start.4 = (f32[512,512]{1,0:T(8,128)}, f32[512,512]{1,0:T(8,128)S(1)}, u32[]{:S(2)}) copy-start(f32[512,512]{1,0:T(8,128)S(1)} %get-tuple-element.24.refs_2_) | copy-start | bytes 3145732
  81.5 0.8 copy-start.10
  82.3 14.2 %all-to-all-start.3 = ((f32[8,72,128]{2,1,0:T(8,128)}), f32[8,72,128]{2,1,0:T(8,128)S(1)}, u32[]{:S(2)}, u32[]{:S(2)}) async-start(f32[8,72,128]{2,1,0:T(8,128)} %get-tuple-element.29), calls=%async_computation.3 | async-start | bytes 589824 | tf_op jit(solution)/shard_map/all_to_all | solution.py:337
  87.1 1.0 copy-start.11
  97.7 17.4 %all-to-all-start.4 = ((f32[4,72,128]{2,1,0:T(8,128)}), f32[4,72,128]{2,1,0:T(8,128)S(1)}, u32[]{:S(2)}, u32[]{:S(2)}) async-start(f32[4,72,128]{2,1,0:T(8,128)} %shard_map.111), calls=%async_computation.4 | async-start | bytes 294912 | tf_op jit(solution)/shard_map/all_to_all | solution.py:342
  102.2 1.2 copy-start.5
  103.4 1.0 copy-start.12
  109.1 1.0 copy-start.6
  115.1 16.8 %copy-start.7 = (f32[512,512]{1,0:T(8,128)S(1)}, f32[512,512]{1,0:T(8,128)}, u32[]{:S(2)}) copy-start(f32[512,512]{1,0:T(8,128)} %copy-done.6) | copy-start | bytes 3145732

commit v5 on v3

--- a/solution.py
+++ b/solution.py
@@ -59,7 +59,7 @@
     return pl.ds(h * size, size)
 
 
-def block_sum_kernel(rates, keys, values, out, key_rows, value_rows, arrived):
+def block_sum_kernel(rates_in, keys, values, out, rates, key_rows, value_rows, sums, arrived, sent):
     length = keys.shape[0]
     heads = rates.shape[0]
     size = keys.shape[1] // heads
@@ -74,16 +74,26 @@
         )
         for copy in copies[-1]:
             copy.start()
+        if h == 0:
+            fetch = pltpu.make_async_copy(rates_in, rates, arrived.at[2 * heads])
+            fetch.start()
+    fetch.wait()
+    stores = []
     for h in range(heads):
         cols = column(h, size)
         tail = tail_out_of(rates[h], length)
         for copy in copies[h]:
             copy.wait()
         scaled = value_rows[:, cols].astype(F32) * tail
-        out[pl.ds(2 * h, 2)] = dot_split(key_rows[:, cols], scaled, 0, 0).reshape(2, size // 2, size)
-
-
-def intra_kernel(rates, queries, keys, values, out):
+        shards = pl.ds(2 * h, 2)
+        sums[shards] = dot_split(key_rows[:, cols], scaled, 0, 0).reshape(2, size // 2, size)
+        stores.append(pltpu.make_async_copy(sums.at[shards], out.at[shards], sent.at[h]))
+        stores[-1].start()
+    for store in stores:
+        store.wait()
+
+
+def intra_kernel(rates, queries, keys, values, out, token):
     rate = rates[pl.program_id(0)]
     half = queries.shape[0] // 2
     same, across = tile_weights(rate, half)
@@ -96,6 +106,7 @@
     out[second, :] = dot(probs(second, first, across), values[first, :], 1, 0) + dot(
         probs(second, second, same), values[second, :], 1, 0
     )
+    token[...] = jnp.zeros_like(token)
 
 
 def mixed_kernel(rates, queries, state, intra, gain, cotangent, mixed, stats, square, inner):
@@ -132,43 +143,40 @@
             coef_out[rows, :] = jnp.broadcast_to(coef[chunk : chunk + 1], (128, 128)).T
 
 
-def back_sum_kernel(channels, rates, received, mixed, gain, cotangent, queries, grad, sums, inv, coef):
+def back_sum_kernel(
+    channels, rates, received, mixed, gain, cotangent, queries, grad_out, sums_out, inv, coef, grad, sums, sent
+):
     length = queries.shape[0]
     heads = rates.shape[0]
     size = queries.shape[1] // heads
     token_scales(received, channels, inv, coef)
+    stores = []
     for h in range(heads):
         cols = column(h, size)
+        shards = pl.ds(2 * h, 2)
         upstream = cotangent[:, cols].astype(F32)
         value = mixed[:, cols]
         mixed_grad = (inv[...] * (upstream * gain[:, cols]) - value * coef[...]).astype(BF16)
         grad[:, cols] = mixed_grad
         scaled = mixed_grad.astype(F32) * head_in_of(rates[h], length)
-        shards = pl.ds(2 * h, 2)
         sums[shards, pl.ds(0, size // 2), :] = dot_split(queries[:, cols], scaled, 0, 0).reshape(2, size // 2, size)
         gain_grad = jnp.sum(upstream * (value * inv[...]), axis=0, keepdims=True)
         sums[shards, pl.ds(size // 2, EXTRA), :] = jnp.broadcast_to(gain_grad[None], (2, EXTRA, size))
+        stores.append(pltpu.make_async_copy(grad.at[:, cols], grad_out.at[:, cols], sent.at[2 * h]))
+        stores.append(pltpu.make_async_copy(sums.at[shards], sums_out.at[shards], sent.at[2 * h + 1]))
+        stores[-1].start()
+        stores[-2].start()
+    for store in stores:
+        store.wait()
 
 
 def weighted(a, b, t, s, weight):
     return (dot(a[t, :], b[s, :], 1, 1) * weight).astype(BF16)
 
 
-def value_part_kernel(rates, queries, keys, grad, value_part, token):
-    half = queries.shape[0] // 2
-    same, across = tile_weights(rates[pl.program_id(0)], half)
-    first, second = pl.ds(0, half), pl.ds(half, half)
-    lower = weighted(queries, keys, second, first, across)
-    value_part[first, :] = dot(weighted(queries, keys, first, first, same), grad[first, :], 0, 0) + dot(
-        lower, grad[second, :], 0, 0
-    )
-    value_part[second, :] = dot(weighted(queries, keys, second, second, same), grad[second, :], 0, 0)
-    token[...] = jnp.zeros_like(token)
-
-
 def grads_kernel(
     channels, rates, received, mixed, gain, queries, keys, values, grad, state,
-    attended, query_grad, key_part, token, inv,
+    attended, query_grad, key_part, value_part, token, inv,
 ):
     head = pl.program_id(0)
     rate = rates[head]
@@ -192,6 +200,11 @@
     ).astype(BF16)
     key_part[first, :] = dot(upper, queries[first, :], 0, 0) + dot(lower, queries[second, :], 0, 0)
     key_part[second, :] = dot(final, queries[second, :], 0, 0)
+    upper = weighted(queries, keys, first, first, same)
+    lower = weighted(queries, keys, second, first, across)
+    final = weighted(queries, keys, second, second, same)
+    value_part[first, :] = dot(upper, grad[first, :], 0, 0) + dot(lower, grad[second, :], 0, 0)
+    value_part[second, :] = dot(final, grad[second, :], 0, 0)
     token[...] = jnp.zeros_like(token)
 
 
@@ -247,7 +260,7 @@
         carry = factor * carry + parts[k]
 
 
-def fold_back_kernel(length, rates, parts, arrived, token, out):
+def fold_back_kernel(length, rates, parts, arrived, out):
     factor, group_factor = fold_factors(rates, length)
     rows = parts.shape[1] - EXTRA
     group = lax.axis_index("seq") // GROUP
@@ -277,14 +290,14 @@
     )(*operands)
 
 
-def scan_forward(x, rates, length):
+def scan_forward(x, rates, length, token):
     count = lax.axis_size("seq")
     groups = count // GROUP
     members = [[g * GROUP + j for j in range(GROUP)] for g in range(groups)]
     parts = lax.all_to_all(x, "seq", 0, 0, axis_index_groups=members)
     rate = lax.dynamic_index_in_dim(rates, lax.axis_index("seq") % GROUP * rates.shape[0] // GROUP, 0, False)
     factor = jnp.exp(-rate * length)
-    total = parts[0]
+    total = parts[0] + token[:1]
     for k in range(1, GROUP):
         total = factor * total + parts[k]
     arrived = [
@@ -294,17 +307,17 @@
     return lax.all_to_all(out, "seq", 0, 0, axis_index_groups=members)
 
 
-def scan_back(x, rates, length, first_token, second_token):
+def scan_back(x, rates, length, token):
     groups = lax.axis_size("seq") // GROUP
     members = [[g * GROUP + j for j in range(GROUP)] for g in range(groups)]
     across = [[g * GROUP + j for g in range(groups)] for j in range(GROUP)]
     parts = lax.all_to_all(x, "seq", 0, 0, axis_index_groups=members)
     totals = whole_call(
         lambda *refs: totals_kernel(length, *refs), jax.ShapeDtypeStruct((groups,) + x.shape[1:], F32),
-        [rates, parts, first_token],
+        [rates, parts, token],
     )
     arrived = lax.all_to_all(totals, "seq", 0, 0, axis_index_groups=across)
-    out = whole_call(lambda *refs: fold_back_kernel(length, *refs), like(x), [rates, parts, arrived, second_token])
+    out = whole_call(lambda *refs: fold_back_kernel(length, *refs), like(x), [rates, parts, arrived])
     return lax.all_to_all(out, "seq", 0, 0, axis_index_groups=members)
 
 
@@ -354,37 +367,41 @@
     in_vmem = pl.BlockSpec(memory_space=pltpu.VMEM)
     rows_scratch = pltpu.VMEM((length, channels), BF16)
     copies = pltpu.SemaphoreType.DMA((2 * heads,))
+    sums_shape = (2 * heads, size // 2, size)
     sums = whole_call(
-        block_sum_kernel, array(F32, 2 * heads, size // 2, size), [hbm(rates), hbm(keys), hbm(values)],
-        in_specs=[smem, anywhere, anywhere], scratch_shapes=[rows_scratch, rows_scratch, copies],
-    )
-    intra = call(intra_kernel, [smem, tokens, tokens, tokens], tokens, wide, 2 * square, 4 << 20)(
-        rates, queries, keys, values
-    )
-    state_in = scan_forward(sums, rates, length)
+        block_sum_kernel, pltpu.HBM(sums_shape, F32), [hbm(rates), hbm(keys), hbm(values)],
+        in_specs=[anywhere] * 3, out_specs=anywhere,
+        scratch_shapes=[
+            pltpu.SMEM((heads,), F32), rows_scratch, rows_scratch, pltpu.VMEM(sums_shape, F32),
+            pltpu.SemaphoreType.DMA((2 * heads + 1,)), pltpu.SemaphoreType.DMA((heads,)),
+        ],
+    )
+    token = array(F32, 8, 128)
+    token_spec = pl.BlockSpec((8, 128), lambda h: (0, 0))
+    intra, first_token = call(
+        intra_kernel, [smem, tokens, tokens, tokens], [tokens, token_spec], [wide, token], 2 * square, 4 << 20
+    )(rates, queries, keys, values)
+    state_in = scan_forward(sums, rates, length, first_token)
     mixed, stats = whole_call(
         mixed_kernel, [wide, array(F32, *stats_shape)],
         [rates, queries, state_in, intra, gain_row, cotangent], scratch_shapes=[scratch, scratch],
     )
     received = lax.all_to_all(stats, "head", 0, 0)
+    sums_shape = (2 * heads, size // 2 + EXTRA, size)
     grad, back_sums = whole_call(
         lambda *refs: back_sum_kernel(total_channels, *refs),
-        [narrow, array(F32, 2 * heads, size // 2 + EXTRA, size)],
-        [rates, received, mixed, gain_row, cotangent, queries], scratch_shapes=[scratch, scratch],
-    )
-    token = array(F32, 8, 128)
-    token_spec = pl.BlockSpec((8, 128), lambda h: (0, 0))
+        [pltpu.HBM((length, channels), BF16), pltpu.HBM(sums_shape, F32)],
+        [rates, received, mixed, gain_row, cotangent, queries], out_specs=[anywhere, anywhere],
+        scratch_shapes=[scratch, scratch, rows_scratch, pltpu.VMEM(sums_shape, F32), copies],
+    )
     part = pltpu.VMEM((length, channels), F32)
-    value_part, first_token = call(
-        value_part_kernel, [smem, tokens, tokens, tokens], [tokens, token_spec],
-        [part, token], 2 * square, 4 << 20,
-    )(rates, queries, keys, grad)
-    attended, query_grad, key_part, second_token = call(
+    attended, query_grad, key_part, value_part, second_token = call(
         lambda *refs: grads_kernel(total_channels, *refs),
         [smem, stats_spec, tokens, row, tokens, tokens, tokens, tokens, shards],
-        [tokens, tokens, tokens, token_spec], [narrow, narrow, part, token], 4 * square, 6 << 20, [scratch],
-    )(rates, received, mixed, gain_row, queries, keys, values, grad, state_in)
-    back_in = scan_back(back_sums, rates, length, first_token, second_token)
+        [tokens, tokens, tokens, tokens, token_spec], [narrow, narrow, part, part, token],
+        6 * square, 6 << 20, [scratch],
+    )(rates, received, hbm(mixed), gain_row, queries, keys, values, hbm(grad), state_in)
+    back_in = scan_back(back_sums, rates, length, second_token)
     key_grad, value_grad, gain_grad = whole_call(
         finish_kernel, [narrow, narrow, array(F32, 1, channels)],
         [rates, back_in, keys, values, vmem(key_part), vmem(value_part)],

time: 130 us -> 128 us (0.985)
  blocking collectives: 29.3 us -> 64.8 us
  waiting for transfers between devices: 22.8 us -> 6.74 us
  starting transfers between devices: 45.6 us -> 31.6 us
  Pallas kernels: 24 us -> 20 us
  local copies, waits for them, and re-layouts: 6.39 us -> 2.94 us
    all_to_all x0 -> x2, blocking collectives: none -> 35.3 us  [the longest x1 22 us: scan_back(): arrived = lax.all_to_all(totals, 'seq', 0, 0, axis_index_groups=across)]
    all_to_all x2 -> x0, starting transfers between devices: 13.9 us -> none  [the longest x1 8.45 us: scan_back(): arrived = lax.all_to_all(totals, 'seq', 0, 0, axis_index_groups=across)]
    all_to_all x2 -> x0, waiting for transfers between devices: 10.6 us -> none  [the longest x1 5.62 us: scan_forward(): return lax.all_to_all(out, 'seq', 0, 0, axis_index_groups=members)]
    pallas_call x2 -> x1, Pallas kernels: 6.94 us -> 3.06 us  [body(): call(intra_kernel, [smem, tokens, tokens, tokens], [tokens, token_spec],...]
    unnamed x26 -> x18, local copies, waits for them, and re-layouts: 5.8 us -> 2.35 us
    all_to_all x1, waiting for transfers between devices: 6.8 us -> 3.69 us  [scan_forward(): parts = lax.all_to_all(x, 'seq', 0, 0, axis_index_groups=members)]
    all_to_all x1, waiting for transfers between devices: 4.45 us -> 2.07 us  [scan_back(): parts = lax.all_to_all(x, 'seq', 0, 0, axis_index_groups=members)]
    pallas_call x7, Pallas kernels: 12.5 us -> 10.6 us  [whole_call(): pl.pallas_call(kernel, in_specs=in_specs, out_specs=out_specs, out_shape=...]
  transfers between devices with their start and end apart: 7 -> 5, of which waited for: 5 -> 3; matrix products, arithmetic and copies ran while one was open for 0% -> 0% of each run, Pallas kernels for 9% -> 7%
where the time goes in v5:
time: 128 us
  blocking collectives  64.8 us (51%)
  starting transfers between devices  31.6 us (25%)
  Pallas kernels  20 us (16%)
  waiting for transfers between devices  6.74 us (5%)
  local copies, waits for them, and re-layouts  2.94 us (2%)
  between operations  1.51 us (1%)
    all_to_all x1, blocking collectives, scan_back(): arrived = lax.all_to_all(totals, 'seq', 0, 0, axis_index_groups=across)  22 us
    all_to_all x1, blocking collectives, scan_back(): return lax.all_to_all(out, 'seq', 0, 0, axis_index_groups=members)  16.5 us
    ppermute x3, starting transfers between devices, scan_forward(): lax.ppermute(total, 'seq', [(i, i + by * GROUP) for i in range(count - by...  15.5 us
    all_to_all x1, blocking collectives, scan_forward(): return lax.all_to_all(out, 'seq', 0, 0, axis_index_groups=members)  13.3 us
    all_to_all x1, blocking collectives, body(): received = lax.all_to_all(stats, 'head', 0, 0)  13.1 us
    pallas_call x7, Pallas kernels, whole_call(): pl.pallas_call(kernel, in_specs=in_specs, out_specs=out_specs, out_shape=...  10.6 us
    all_to_all x1, starting transfers between devices, scan_forward(): parts = lax.all_to_all(x, 'seq', 0, 0, axis_index_groups=members)  10.3 us
    pallas_call x1, Pallas kernels, body(): call(lambda *refs: grads_kernel(total_channels, *refs), [smem, stats_spec...  6.32 us
  transfers between devices with their start and end apart: 5, of which 3 were waited for; matrix products, arithmetic and copies ran while one was open for 0% of the time, Pallas kernels for 7%

profile of v5, /device:TPU:1, one launch (start us, length us, event | category | flops | bytes accessed | tf_op | source)
XLA Modules:
  0.0 127.6 jit_solution(13876912909633148451)
XLA Ops:
  0.7 2.8 %shard_map.101 = f32[8,64,128]{2,1,0:T(8,128)} custom-call(f32[4]{0:T(128)} %rates.5, bf16[512,512]{1,0:T(8,128)(2,1)} %keys.5, bf16[512,512]{1,0:T(8,128)(2,1)} %values.5), custom_call_target="tpu_custom_call" | custom-call | tf_op jit(solution)/shard_map/pallas_call | solution.py:283
  3.5 10.3 %all-to-all-start = ((f32[8,64,128]{2,1,0:T(8,128)}), f32[8,64,128]{2,1,0:T(8,128)S(1)}, u32[]{:S(2)}, u32[]{:S(2)}) async-start(f32[8,64,128]{2,1,0:T(8,128)} %shard_map.101), calls=%async_computation | async-start | bytes 524288 | tf_op jit(solution)/shard_map/all_to_all | solution.py:297
  13.8 0.7 copy-done.7
  15.8 3.1 %shard_map.102 = (f32[512,512]{1,0:T(8,128)S(1)}, f32[8,128]{1,0:T(8,128)S(1)}) custom-call(f32[4]{0:T(128)S(1)} %copy-done.7, bf16[512,512]{1,0:T(8,128)(2,1)S(1)} %copy-done.3, bf16[512,512]{1,0:T(8,128)(2,1)S(1)} %copy-done, bf16[512,512]{1,0:T(8,128)(2,1)S(1)} %copy-done.1), custom_call_target="tpu_custom_call" | custom-call | flops 536870912 | bytes 4194304 | tf_op jit(solution)/shard_map/pallas_call | solution.py:381
  18.8 3.7 %all-to-all-done.refs_1_ = f32[8,64,128]{2,1,0:T(8,128)S(1)} async-done(((f32[8,64,128]{2,1,0:T(8,128)}), f32[8,64,128]{2,1,0:T(8,128)S(1)}, u32[]{:S(2)}, u32[]{:S(2)}) %all-to-all-start) | async-done | bytes 262176 | tf_op jit(solution)/shard_map/all_to_all | solution.py:297
  22.6 7.2 %collective-permute-start.2 = (f32[64,128]{1,0:T(8,128)S(1)}, f32[64,128]{1,0:T(8,128)S(1)}, u32[]{:S(2)}, u32[]{:S(2)}) collective-permute-start(f32[64,128]{1,0:T(8,128)S(1)} %fusion), channel_id=1, source_target_pairs={{0,384},{16,400},{32,416},{48,432},{64,448},{80,464},{96,480},{112... | collective-permute-start | bytes 98312 | tf_op jit(solution)/shard_map/ppermute | solution.py:304
  29.8 3.7 %collective-permute-start.1 = (f32[64,128]{1,0:T(8,128)S(1)}, f32[64,128]{1,0:T(8,128)S(1)}, u32[]{:S(2)}, u32[]{:S(2)}) collective-permute-start(f32[64,128]{1,0:T(8,128)S(1)} %fusion), channel_id=1, source_target_pairs={{0,256},{16,272},{32,288},{48,304},{64,320},{80,336},{96,352},{112... | collective-permute-start | bytes 98312 | tf_op jit(solution)/shard_map/ppermute | solution.py:304
  33.4 4.6 %collective-permute-start = (f32[64,128]{1,0:T(8,128)S(1)}, f32[64,128]{1,0:T(8,128)S(1)}, u32[]{:S(2)}, u32[]{:S(2)}) collective-permute-start(f32[64,128]{1,0:T(8,128)S(1)} %fusion), channel_id=1, source_target_pairs={{0,128},{16,144},{32,160},{48,176},{64,192},{80,208},{96,224},{112... | collective-permute-start | bytes 98312 | tf_op jit(solution)/shard_map/ppermute | solution.py:304
  38.1 1.0 collective-permute-done.refs_2_
  39.1 0.6 shard_map.103
  39.7 13.3 %all_to_all.30.state.refs_8_ = f32[8,64,128]{2,1,0:T(8,128)S(1)} all-to-all(f32[8,64,128]{2,1,0:T(8,128)S(1)} %shard_map.103), channel_id=1, replica_groups={{0,16,32,48,64,80,96,112},{128,144,160,176,192,208,224,240},{256,272,28..., dimensions={0} | all-to-all | bytes 524288 | tf_op jit(solution)/shard_map/all_to_all | solution.py:307
  53.0 0.7 copy-done.8
  53.7 1.2 shard_map.104
  54.9 13.1 %all_to_all.31.refs_1_ = f32[16,8,128]{2,1,0:T(8,128)S(1)} all-to-all(f32[16,8,128]{2,1,0:T(8,128)S(1)} %get-tuple-element.21), channel_id=1, replica_groups=mesh['seq'=32,'head'=16] {'head'}, dimensions={0} | all-to-all | bytes 131072 | tf_op jit(solution)/shard_map/all_to_all | solution.py:389
  67.9 2.2 %shard_map.105 = (bf16[512,512]{1,0:T(8,128)(2,1)}, f32[8,72,128]{2,1,0:T(8,128)}) custom-call(f32[4]{0:T(128)S(1)} %copy-done.7, f32[16,8,128]{2,1,0:T(8,128)S(1)} %all_to_all.31.refs_1_, f32[512,512]{1,0:T(8,128)S(1)} %get-tuple-element.22.refs_2_, f32[1,512]{1,0:T(1,128)S(1)} %bitcast.66, bf16[512,512]{1,0:T(8,128)(2,1)S(1)} %copy-done.2, ...), custom_call_target="tpu_custom_call" | custom-call | tf_op jit(solution)/shard_map/pallas_call | solution.py:283
  70.2 5.8 %all-to-all-start.3 = ((f32[8,72,128]{2,1,0:T(8,128)}), f32[8,72,128]{2,1,0:T(8,128)S(1)}, u32[]{:S(2)}, u32[]{:S(2)}) async-start(f32[8,72,128]{2,1,0:T(8,128)} %get-tuple-element.26), calls=%async_computation.3 | async-start | bytes 589824 | tf_op jit(solution)/shard_map/all_to_all | solution.py:314
  76.0 6.3 %shard_map.106 = (bf16[512,512]{1,0:T(8,128)(2,1)}, bf16[512,512]{1,0:T(8,128)(2,1)}, f32[512,512]{1,0:T(8,128)S(1)}, f32[512,512]{1,0:T(8,128)S(1)}, f32[8,128]{1,0:T(8,128)S(1)}) custom-call(f32[4]{0:T(128)S(1)} %copy-done.7, f32[16,8,128]{2,1,0:T(8,128)S(1)} %all_to_all.31.refs_1_, f32[512,512]{1,0:T(8,128)} %copy-done.6, f32[1,512]{1,0:T(1,128)S(1)} %bitcast.67, ...), custom_call_target="tpu_custom_call" | custom-call | flops 1610612736 | bytes 6291456 | tf_op jit(solution)/shard_map/pallas_call | solution.py:398
  82.3 1.0 copy-done.4
  83.3 2.1 %all-to-all-done.3.refs_1_ = f32[8,72,128]{2,1,0:T(8,128)S(1)} async-done(((f32[8,72,128]{2,1,0:T(8,128)}), f32[8,72,128]{2,1,0:T(8,128)S(1)}, u32[]{:S(2)}, u32[]{:S(2)}) %all-to-all-start.3) | async-done | bytes 294944 | tf_op jit(solution)/shard_map/all_to_all | solution.py:314
  85.4 0.6 shard_map.107
  86.0 22.0 %all_to_all.32.refs_2_ = f32[4,72,128]{2,1,0:T(8,128)S(1)} all-to-all(f32[4,72,128]{2,1,0:T(8,128)S(1)} %shard_map.107), channel_id=1, replica_groups={{0,128,256,384},{16,144,272,400},{32,160,288,416},{48,176,304,432},{64,..., dimensions={0} | all-to-all | bytes 294912 | tf_op jit(solution)/shard_map/all_to_all | solution.py:319
  108.0 0.6 shard_map.108
  108.6 16.5 %all_to_all.33.back = f32[8,72,128]{2,1,0:T(8,128)S(1)} all-to-all(f32[8,72,128]{2,1,0:T(8,128)S(1)} %shard_map.108), channel_id=1, replica_groups={{0,16,32,48,64,80,96,112},{128,144,160,176,192,208,224,240},{256,272,28..., dimensions={0} | all-to-all | bytes 589824 | tf_op jit(solution)/shard_map/all_to_all | solution.py:321
  125.1 2.6 %shard_map.109 = (bf16[512,512]{1,0:T(8,128)(2,1)}, bf16[512,512]{1,0:T(8,128)(2,1)}, f32[1,512]{1,0:T(1,128)}) custom-call(f32[4]{0:T(128)S(1)} %copy-done.7, f32[8,72,128]{2,1,0:T(8,128)S(1)} %all_to_all.33.back, bf16[512,512]{1,0:T(8,128)(2,1)S(1)} %copy-done, bf16[512,512]{1,0:T(8,128)(2,1)S(1)} %copy-done.1, f32[512,512]{1,0:T(8,128)S(1)} %get-tuple-element.28.key_part, ...), custom_call_target="tpu_custom_call" | custom-call | tf_op jit(solution)/shard_map/pallas_call | solution.py:283
  (20 shorter events, 0.6 us)
Async XLA Ops:
  0.6 15.1 %copy-start.1 = (bf16[512,512]{1,0:T(8,128)(2,1)S(1)}, bf16[512,512]{1,0:T(8,128)(2,1)}, u32[]{:S(2)}) copy-start(bf16[512,512]{1,0:T(8,128)(2,1)} %values.5) | copy-start | bytes 1572868
  0.6 15.1 %copy-start.3 = (bf16[512,512]{1,0:T(8,128)(2,1)S(1)}, bf16[512,512]{1,0:T(8,128)(2,1)}, u32[]{:S(2)}) copy-start(bf16[512,512]{1,0:T(8,128)(2,1)} %refs_4_.3) | copy-start | bytes 1572868
  3.5 12.3 %copy-start = (bf16[512,512]{1,0:T(8,128)(2,1)S(1)}, bf16[512,512]{1,0:T(8,128)(2,1)}, u32[]{:S(2)}) copy-start(bf16[512,512]{1,0:T(8,128)(2,1)} %keys.5) | copy-start | bytes 1572868
  3.5 19.1 %all-to-all-start = ((f32[8,64,128]{2,1,0:T(8,128)}), f32[8,64,128]{2,1,0:T(8,128)S(1)}, u32[]{:S(2)}, u32[]{:S(2)}) async-start(f32[8,64,128]{2,1,0:T(8,128)} %shard_map.101), calls=%async_computation | async-start | bytes 524288 | tf_op jit(solution)/shard_map/all_to_all | solution.py:297
  13.8 0.7 copy-start.7
  22.6 30.4 %copy-start.2 = (bf16[512,512]{1,0:T(8,128)(2,1)S(1)}, bf16[512,512]{1,0:T(8,128)(2,1)}, u32[]{:S(2)}) copy-start(bf16[512,512]{1,0:T(8,128)(2,1)} %refs_4_.2) | copy-start | bytes 1572868
  22.6 15.5 %collective-permute-start.2 = (f32[64,128]{1,0:T(8,128)S(1)}, f32[64,128]{1,0:T(8,128)S(1)}, u32[]{:S(2)}, u32[]{:S(2)}) collective-permute-start(f32[64,128]{1,0:T(8,128)S(1)} %fusion), channel_id=1, source_target_pairs={{0,384},{16,400},{32,416},{48,432},{64,448},{80,464},{96,480},{112... | collective-permute-start | bytes 98312 | tf_op jit(solution)/shard_map/ppermute | solution.py:304
  29.8 8.3 %collective-permute-start.1 = (f32[64,128]{1,0:T(8,128)S(1)}, f32[64,128]{1,0:T(8,128)S(1)}, u32[]{:S(2)}, u32[]{:S(2)}) collective-permute-start(f32[64,128]{1,0:T(8,128)S(1)} %fusion), channel_id=1, source_target_pairs={{0,256},{16,272},{32,288},{48,304},{64,320},{80,336},{96,352},{112... | collective-permute-start | bytes 98312 | tf_op jit(solution)/shard_map/ppermute | solution.py:304
  33.4 5.6 %collective-permute-start = (f32[64,128]{1,0:T(8,128)S(1)}, f32[64,128]{1,0:T(8,128)S(1)}, u32[]{:S(2)}, u32[]{:S(2)}) collective-permute-start(f32[64,128]{1,0:T(8,128)S(1)} %fusion), channel_id=1, source_target_pairs={{0,128},{16,144},{32,160},{48,176},{64,192},{80,208},{96,224},{112... | collective-permute-start | bytes 98312 | tf_op jit(solution)/shard_map/ppermute | solution.py:304
  53.0 0.7 copy-start.8
  54.9 15.3 %copy-start.6 = (f32[512,512]{1,0:T(8,128)}, f32[512,512]{1,0:T(8,128)S(1)}, u32[]{:S(2)}) copy-start(f32[512,512]{1,0:T(8,128)S(1)} %get-tuple-element.22.refs_2_) | copy-start | bytes 3145732
  70.2 15.2 %all-to-all-start.3 = ((f32[8,72,128]{2,1,0:T(8,128)}), f32[8,72,128]{2,1,0:T(8,128)S(1)}, u32[]{:S(2)}, u32[]{:S(2)}) async-start(f32[8,72,128]{2,1,0:T(8,128)} %get-tuple-element.26), calls=%async_computation.3 | async-start | bytes 589824 | tf_op jit(solution)/shard_map/all_to_all | solution.py:314
  82.3 1.0 copy-start.4
  85.4 39.7 %copy-start.5 = (f32[512,512]{1,0:T(8,128)S(1)}, f32[512,512]{1,0:T(8,128)}, u32[]{:S(2)}) copy-start(f32[512,512]{1,0:T(8,128)} %copy-done.4) | copy-start | bytes 3145732

commit v6 on v5

--- a/solution.py
+++ b/solution.py
@@ -31,28 +31,25 @@
     return lax.broadcasted_iota(jnp.int32, (length, width), 0).astype(F32)
 
 
-def exp_scalar(x):
-    return jnp.exp(jnp.full((8, 128), x, F32))[:1]
-
-
 def head_in_of(rate, length):
     base = jnp.exp(-rate * (rows_of(128) + 1.0))
-    return jnp.concatenate([base * exp_scalar(-rate * start) for start in range(0, length, 128)], axis=0)
+    return jnp.concatenate([base * jnp.exp(-rate * start) for start in range(0, length, 128)], axis=0)
 
 
 def tail_out_of(rate, length):
     base = jnp.exp(-rate * (127.0 - rows_of(128)))
-    return jnp.concatenate([base * exp_scalar(-rate * (length - 128 - start)) for start in range(0, length, 128)], axis=0)
+    return jnp.concatenate([base * jnp.exp(-rate * (length - 128 - start)) for start in range(0, length, 128)], axis=0)
 
 
 def tile_weights(rate, half):
+    rate = jnp.concatenate([rate] * (half // 128), axis=1)
     distance = (
         lax.broadcasted_iota(jnp.int32, (half, half), 0) - lax.broadcasted_iota(jnp.int32, (half, half), 1)
     ).astype(F32)
     same = jnp.where(distance >= 0, jnp.exp(-rate * jnp.maximum(distance, 0.0)), 0.0)
-    column = jnp.exp(-rate * (rows_of(half) + 1.0))
-    row = jnp.exp(-rate * (half - 1.0 - lax.broadcasted_iota(jnp.int32, (8, half), 1).astype(F32)))[:1]
-    return same, jnp.concatenate([column] * (half // 128), axis=1) * row
+    column = jnp.exp(-rate * (rows_of(half, half) + 1.0))
+    row = jnp.exp(-rate * (half - 1.0 - lax.broadcasted_iota(jnp.int32, (1, half), 1).astype(F32)))
+    return same, column * row
 
 
 def column(h, size):
@@ -81,7 +78,7 @@
     stores = []
     for h in range(heads):
         cols = column(h, size)
-        tail = tail_out_of(rates[h], length)
+        tail = tail_out_of(jnp.full((1, size), rates[h], F32), length)
         for copy in copies[h]:
             copy.wait()
         scaled = value_rows[:, cols].astype(F32) * tail
@@ -93,8 +90,12 @@
         store.wait()
 
 
-def intra_kernel(rates, queries, keys, values, out, token):
-    rate = rates[pl.program_id(0)]
+GAIN, RATE, ZERO = 0, 1, 2
+
+
+def intra_kernel(rates, gain, queries, keys, values, out, consts):
+    rate = jnp.full(gain.shape, rates[pl.program_id(0)], F32)
+    consts[...] = jnp.concatenate([gain[...], rate, jnp.zeros((6, rate.shape[1]), F32)], axis=0)
     half = queries.shape[0] // 2
     same, across = tile_weights(rate, half)
     first, second = pl.ds(0, half), pl.ds(half, half)
@@ -106,19 +107,18 @@
     out[second, :] = dot(probs(second, first, across), values[first, :], 1, 0) + dot(
         probs(second, second, same), values[second, :], 1, 0
     )
-    token[...] = jnp.zeros_like(token)
-
-
-def mixed_kernel(rates, queries, state, intra, gain, cotangent, mixed, stats, square, inner):
+
+
+def mixed_kernel(consts, queries, state, intra, cotangent, mixed, stats, square, inner):
     length = queries.shape[0]
-    heads = rates.shape[0]
-    size = queries.shape[1] // heads
+    size = 128
+    heads = queries.shape[1] // size
     for h in range(heads):
         cols = column(h, size)
         state_in = state[pl.ds(2 * h, 2)].reshape(size, size)
-        value = intra[:, cols] + head_in_of(rates[h], length) * dot_split(queries[:, cols], state_in, 1, 0)
+        value = intra[:, cols] + head_in_of(consts[pl.ds(RATE, 1), cols], length) * dot_split(queries[:, cols], state_in, 1, 0)
         mixed[:, cols] = value
-        new_square, new_inner = value * value, cotangent[:, cols].astype(F32) * gain[:, cols] * value
+        new_square, new_inner = value * value, cotangent[:, cols].astype(F32) * consts[pl.ds(GAIN, 1), cols] * value
         if h > 0:
             new_square, new_inner = new_square + square[...], new_inner + inner[...]
         square[...] = new_square
@@ -144,11 +144,11 @@
 
 
 def back_sum_kernel(
-    channels, rates, received, mixed, gain, cotangent, queries, grad_out, sums_out, inv, coef, grad, sums, sent
+    channels, consts, received, mixed, cotangent, queries, grad_out, sums_out, inv, coef, grad, sums, sent
 ):
     length = queries.shape[0]
-    heads = rates.shape[0]
-    size = queries.shape[1] // heads
+    size = 128
+    heads = queries.shape[1] // size
     token_scales(received, channels, inv, coef)
     stores = []
     for h in range(heads):
@@ -156,9 +156,9 @@
         shards = pl.ds(2 * h, 2)
         upstream = cotangent[:, cols].astype(F32)
         value = mixed[:, cols]
-        mixed_grad = (inv[...] * (upstream * gain[:, cols]) - value * coef[...]).astype(BF16)
+        mixed_grad = (inv[...] * (upstream * consts[pl.ds(GAIN, 1), cols]) - value * coef[...]).astype(BF16)
         grad[:, cols] = mixed_grad
-        scaled = mixed_grad.astype(F32) * head_in_of(rates[h], length)
+        scaled = mixed_grad.astype(F32) * head_in_of(consts[pl.ds(RATE, 1), cols], length)
         sums[shards, pl.ds(0, size // 2), :] = dot_split(queries[:, cols], scaled, 0, 0).reshape(2, size // 2, size)
         gain_grad = jnp.sum(upstream * (value * inv[...]), axis=0, keepdims=True)
         sums[shards, pl.ds(size // 2, EXTRA), :] = jnp.broadcast_to(gain_grad[None], (2, EXTRA, size))
@@ -175,19 +175,18 @@
 
 
 def grads_kernel(
-    channels, rates, received, mixed, gain, queries, keys, values, grad, state,
+    channels, consts, received, mixed, queries, keys, values, grad, state,
     attended, query_grad, key_part, value_part, token, inv,
 ):
-    head = pl.program_id(0)
-    rate = rates[head]
+    rate = consts[pl.ds(RATE, 1), :]
     length, size = queries.shape
     half = length // 2
 
-    @pl.when(head == 0)
+    @pl.when(pl.program_id(0) == 0)
     def _():
         token_scales(received, channels, inv, None)
 
-    attended[...] = (mixed[...] * inv[...] * gain[...]).astype(BF16)
+    attended[...] = (mixed[...] * inv[...] * consts[pl.ds(GAIN, 1), :]).astype(BF16)
     same, across = tile_weights(rate, half)
     first, second = pl.ds(0, half), pl.ds(half, half)
     state_part = head_in_of(rate, length) * dot_split(grad[...], state[...].reshape(size, size), 1, 1)
@@ -209,18 +208,18 @@
 
 
 def finish_kernel(
-    rates, back, keys, values, key_part, value_part, key_grad, value_grad, gain_grad, key_rows, value_rows, sent
+    consts, back, keys, values, key_part, value_part, key_grad, value_grad, gain_grad, key_rows, value_rows, sent
 ):
     length = keys.shape[0]
-    heads = rates.shape[0]
-    size = keys.shape[1] // heads
+    size = 128
+    heads = keys.shape[1] // size
     half = size // 2
     copies = []
     for h in range(heads):
         cols = column(h, size)
         back_in = back[pl.ds(2 * h, 2), pl.ds(0, half), :].reshape(size, size)
         gain_grad[:, cols] = back[2 * h, pl.ds(half, 1), :]
-        tail = tail_out_of(rates[h], length)
+        tail = tail_out_of(consts[pl.ds(RATE, 1), cols], length)
         key_rows[:, cols] = (key_part[:, cols] + tail * dot_split(values[:, cols], back_in, 1, 1)).astype(BF16)
         value_rows[:, cols] = (value_part[:, cols] + tail * dot_split(keys[:, cols], back_in, 1, 0)).astype(BF16)
         for i, (rows, target) in enumerate(((key_rows, key_grad), (value_rows, value_grad))):
@@ -231,26 +230,25 @@
         copy.wait()
 
 
-def fold_factors(rates, length):
+def fold_factors(consts, length):
     member = lax.axis_index("seq") % GROUP
-    rate = rates[member * rates.shape[0] // GROUP]
-    return exp_scalar(-rate * length), exp_scalar(-rate * (length * GROUP))
-
-
-def totals_kernel(length, rates, parts, token, out):
-    factor, _ = fold_factors(rates, length)
+    head = member * (consts.shape[1] // 128) // GROUP
+    rate = consts[pl.ds(RATE, 1), pl.ds(pl.multiple_of(head * 128, 128), 128)]
+    return jnp.exp(-rate * length), jnp.exp(-rate * (length * GROUP))
+
+
+def totals_kernel(length, consts, parts, token, out):
+    factor, _ = fold_factors(consts, length)
     rows = parts.shape[1] - EXTRA
     total = parts[GROUP - 1, :rows]
     for k in range(GROUP - 2, -1, -1):
         total = factor * total + parts[k, :rows]
-    extra = sum(parts[k, rows:] for k in range(GROUP))
-    for g in range(out.shape[0]):
-        out[g, :rows] = total
-        out[g, rows:] = extra
-
-
-def fold_forward_kernel(length, rates, parts, *refs):
-    factor, group_factor = fold_factors(rates, length)
+    out[:rows] = total
+    out[rows:] = sum(parts[k, rows:] for k in range(GROUP))
+
+
+def fold_forward_kernel(length, consts, parts, *refs):
+    factor, group_factor = fold_factors(consts, length)
     *arrived, out = refs
     carry = arrived[-1][...]
     for ref in arrived[-2::-1]:
@@ -260,8 +258,8 @@
         carry = factor * carry + parts[k]
 
 
-def fold_back_kernel(length, rates, parts, arrived, out):
-    factor, group_factor = fold_factors(rates, length)
+def fold_back_kernel(length, consts, parts, arrived, out):
+    factor, group_factor = fold_factors(consts, length)
     rows = parts.shape[1] - EXTRA
     group = lax.axis_index("seq") // GROUP
     carry = jnp.zeros((rows, parts.shape[2]), F32)
@@ -277,7 +275,7 @@
 def whole_call(kernel, out_shape, operands, in_specs=None, out_specs=None, **rest):
     vmem = pl.BlockSpec(memory_space=pltpu.VMEM)
     if in_specs is None:
-        in_specs = [pl.BlockSpec(memory_space=pltpu.SMEM)] + [vmem] * (len(operands) - 1)
+        in_specs = [vmem] * len(operands)
     if out_specs is None:
         out_specs = jax.tree.map(lambda _: vmem, out_shape)
     return pl.pallas_call(
@@ -290,34 +288,34 @@
     )(*operands)
 
 
-def scan_forward(x, rates, length, token):
+def scan_forward(x, rates, consts, length):
     count = lax.axis_size("seq")
     groups = count // GROUP
     members = [[g * GROUP + j for j in range(GROUP)] for g in range(groups)]
     parts = lax.all_to_all(x, "seq", 0, 0, axis_index_groups=members)
     rate = lax.dynamic_index_in_dim(rates, lax.axis_index("seq") % GROUP * rates.shape[0] // GROUP, 0, False)
     factor = jnp.exp(-rate * length)
-    total = parts[0] + token[:1]
+    total = parts[0] + consts[ZERO : ZERO + 1, :128]
     for k in range(1, GROUP):
         total = factor * total + parts[k]
     arrived = [
         lax.ppermute(total, "seq", [(i, i + by * GROUP) for i in range(count - by * GROUP)]) for by in range(1, groups)
     ]
-    out = whole_call(lambda *refs: fold_forward_kernel(length, *refs), like(x), [rates, parts, *arrived])
+    out = whole_call(lambda *refs: fold_forward_kernel(length, *refs), like(x), [consts, parts, *arrived])
     return lax.all_to_all(out, "seq", 0, 0, axis_index_groups=members)
 
 
-def scan_back(x, rates, length, token):
+def scan_back(x, consts, length, token):
     groups = lax.axis_size("seq") // GROUP
     members = [[g * GROUP + j for j in range(GROUP)] for g in range(groups)]
     across = [[g * GROUP + j for g in range(groups)] for j in range(GROUP)]
     parts = lax.all_to_all(x, "seq", 0, 0, axis_index_groups=members)
     totals = whole_call(
-        lambda *refs: totals_kernel(length, *refs), jax.ShapeDtypeStruct((groups,) + x.shape[1:], F32),
-        [rates, parts, token],
-    )
-    arrived = lax.all_to_all(totals, "seq", 0, 0, axis_index_groups=across)
-    out = whole_call(lambda *refs: fold_back_kernel(length, *refs), like(x), [rates, parts, arrived])
+        lambda *refs: totals_kernel(length, *refs), jax.ShapeDtypeStruct(x.shape[1:], F32),
+        [consts, parts, token],
+    )
+    arrived = lax.all_gather(totals, "seq", axis_index_groups=across)
+    out = whole_call(lambda *refs: fold_back_kernel(length, *refs), like(x), [consts, parts, arrived])
     return lax.all_to_all(out, "seq", 0, 0, axis_index_groups=members)
 
 
@@ -331,7 +329,6 @@
     size = channels // heads
     head_devices = lax.axis_size("head")
     total_channels = channels * head_devices
-    gain_row = gain.reshape(1, channels)
 
     smem = pl.BlockSpec(memory_space=pltpu.SMEM)
     tokens = pl.BlockSpec((length, size), lambda h: (0, h))
@@ -376,35 +373,36 @@
             pltpu.SemaphoreType.DMA((2 * heads + 1,)), pltpu.SemaphoreType.DMA((heads,)),
         ],
     )
-    token = array(F32, 8, 128)
-    token_spec = pl.BlockSpec((8, 128), lambda h: (0, 0))
-    intra, first_token = call(
-        intra_kernel, [smem, tokens, tokens, tokens], [tokens, token_spec], [wide, token], 2 * square, 4 << 20
-    )(rates, queries, keys, values)
-    state_in = scan_forward(sums, rates, length, first_token)
+    consts_spec = pl.BlockSpec((8, size), lambda h: (0, h))
+    intra, consts = call(
+        intra_kernel, [smem, row, tokens, tokens, tokens], [tokens, consts_spec],
+        [wide, array(F32, 8, channels)], 2 * square, 4 << 20,
+    )(rates, gain.reshape(1, channels), queries, keys, values)
+    state_in = scan_forward(sums, rates, consts, length)
     mixed, stats = whole_call(
         mixed_kernel, [wide, array(F32, *stats_shape)],
-        [rates, queries, state_in, intra, gain_row, cotangent], scratch_shapes=[scratch, scratch],
+        [consts, queries, state_in, intra, cotangent], scratch_shapes=[scratch, scratch],
     )
     received = lax.all_to_all(stats, "head", 0, 0)
     sums_shape = (2 * heads, size // 2 + EXTRA, size)
     grad, back_sums = whole_call(
         lambda *refs: back_sum_kernel(total_channels, *refs),
         [pltpu.HBM((length, channels), BF16), pltpu.HBM(sums_shape, F32)],
-        [rates, received, mixed, gain_row, cotangent, queries], out_specs=[anywhere, anywhere],
+        [consts, received, mixed, cotangent, queries], out_specs=[anywhere, anywhere],
         scratch_shapes=[scratch, scratch, rows_scratch, pltpu.VMEM(sums_shape, F32), copies],
     )
     part = pltpu.VMEM((length, channels), F32)
-    attended, query_grad, key_part, value_part, second_token = call(
+    attended, query_grad, key_part, value_part, token = call(
         lambda *refs: grads_kernel(total_channels, *refs),
-        [smem, stats_spec, tokens, row, tokens, tokens, tokens, tokens, shards],
-        [tokens, tokens, tokens, tokens, token_spec], [narrow, narrow, part, part, token],
+        [consts_spec, stats_spec, tokens, tokens, tokens, tokens, tokens, shards],
+        [tokens, tokens, tokens, tokens, pl.BlockSpec((8, 128), lambda h: (0, 0))],
+        [narrow, narrow, part, part, array(F32, 8, 128)],
         6 * square, 6 << 20, [scratch],
-    )(rates, received, hbm(mixed), gain_row, queries, keys, values, hbm(grad), state_in)
-    back_in = scan_back(back_sums, rates, length, second_token)
+    )(consts, received, hbm(mixed), queries, keys, values, hbm(grad), state_in)
+    back_in = scan_back(back_sums, consts, length, token)
     key_grad, value_grad, gain_grad = whole_call(
         finish_kernel, [narrow, narrow, array(F32, 1, channels)],
-        [rates, back_in, keys, values, vmem(key_part), vmem(value_part)],
+        [consts, back_in, keys, values, vmem(key_part), vmem(value_part)],
         out_specs=[anywhere, anywhere, in_vmem], scratch_shapes=[rows_scratch, rows_scratch, copies],
     )
     return attended, query_grad, key_grad, value_grad, gain_grad.reshape(channels)

time: 128 us -> 120 us (0.938)
  blocking collectives: 64.8 us -> 60.4 us
  Pallas kernels: 20 us -> 16.6 us
    all_to_all x1 -> x0, blocking collectives: 22 us -> none  [scan_back(): arrived = lax.all_to_all(totals, 'seq', 0, 0, axis_index_groups=across)]
    all_gather x0 -> x1, blocking collectives: none -> 17.9 us  [scan_back(): arrived = lax.all_gather(totals, 'seq', axis_index_groups=across)]
    pallas_call x7, Pallas kernels: 10.6 us -> 7.25 us  [whole_call(): pl.pallas_call(kernel, in_specs=in_specs, out_specs=out_specs, out_shape=...]
  transfers between devices with their start and end apart: 5 -> 5, of which waited for: 3 -> 3; matrix products, arithmetic and copies ran while one was open for 0% -> 0% of each run, Pallas kernels for 7% -> 8%
where the time goes in v6:
time: 120 us; the launch traced here: 119 us
  blocking collectives  60.4 us (50%)
  starting transfers between devices  31.6 us (26%)
  Pallas kernels  16.6 us (14%)
  waiting for transfers between devices  6.2 us (5%)
  local copies, waits for them, and re-layouts  2.87 us (2%)
  between operations  1.51 us (1%)
    all_gather x1, blocking collectives, scan_back(): arrived = lax.all_gather(totals, 'seq', axis_index_groups=across)  17.9 us
    all_to_all x1, blocking collectives, scan_back(): return lax.all_to_all(out, 'seq', 0, 0, axis_index_groups=members)  16.2 us
    ppermute x3, starting transfers between devices, scan_forward(): lax.ppermute(total, 'seq', [(i, i + by * GROUP) for i in range(count - by...  15.5 us
    all_to_all x1, blocking collectives, scan_forward(): return lax.all_to_all(out, 'seq', 0, 0, axis_index_groups=members)  13.3 us
    all_to_all x1, blocking collectives, body(): received = lax.all_to_all(stats, 'head', 0, 0)  13.1 us
    all_to_all x1, starting transfers between devices, scan_forward(): parts = lax.all_to_all(x, 'seq', 0, 0, axis_index_groups=members)  10.3 us
    pallas_call x7, Pallas kernels, whole_call(): pl.pallas_call(kernel, in_specs=in_specs, out_specs=out_specs, out_shape=...  7.25 us
    pallas_call x1, Pallas kernels, body(): call(lambda *refs: grads_kernel(total_channels, *refs), [consts_spec, sta...  6.27 us
  transfers between devices with their start and end apart: 5, of which 3 were waited for; matrix products, arithmetic and copies ran while one was open for 0% of the time, Pallas kernels for 8%

profile of v6, /device:TPU:1, one launch (start us, length us, event | category | flops | bytes accessed | tf_op | source)
XLA Modules:
  0.0 119.2 jit_solution(533726991121623666)
XLA Ops:
  0.7 2.8 %shard_map.102 = f32[8,64,128]{2,1,0:T(8,128)} custom-call(f32[4]{0:T(128)} %rates_in.1, bf16[512,512]{1,0:T(8,128)(2,1)} %keys.5, bf16[512,512]{1,0:T(8,128)(2,1)} %values.5), custom_call_target="tpu_custom_call" | custom-call | tf_op jit(solution)/shard_map/pallas_call | solution.py:281
  3.5 0.0 copy-start
  3.5 10.3 %all-to-all-start = ((f32[8,64,128]{2,1,0:T(8,128)}), f32[8,64,128]{2,1,0:T(8,128)S(1)}, u32[]{:S(2)}, u32[]{:S(2)}) async-start(f32[8,64,128]{2,1,0:T(8,128)} %shard_map.102), calls=%async_computation | async-start | bytes 524288 | tf_op jit(solution)/shard_map/all_to_all | solution.py:295
  13.8 0.7 copy-done.7
  14.5 0.6 dynamic_slice.4
  15.7 0.0 copy-start.8
  15.8 0.6 copy-done.8
  16.4 3.0 %shard_map.101 = (f32[512,512]{1,0:T(8,128)S(1)}, f32[8,512]{1,0:T(8,128)S(1)}) custom-call(f32[4]{0:T(128)S(1)} %copy-done.7, f32[1,512]{1,0:T(1,128)S(1)} %bitcast.67, bf16[512,512]{1,0:T(8,128)(2,1)S(1)} %copy-done.3, bf16[512,512]{1,0:T(8,128)(2,1)S(1)} %copy-done, bf16[512,512]{1,0:T(8,128)(2,1)S(1)} %copy-done.1), custom_call_target="tpu_custom_call" | custom-call | flops 536870912 | bytes 4194304 | tf_op jit(solution)/shard_map/pallas_call | solution.py:377
  19.4 3.1 %all-to-all-done.refs_1_ = f32[8,64,128]{2,1,0:T(8,128)S(1)} async-done(((f32[8,64,128]{2,1,0:T(8,128)}), f32[8,64,128]{2,1,0:T(8,128)S(1)}, u32[]{:S(2)}, u32[]{:S(2)}) %all-to-all-start) | async-done | bytes 262176 | tf_op jit(solution)/shard_map/all_to_all | solution.py:295
  22.6 7.2 %collective-permute-start.2 = (f32[64,128]{1,0:T(8,128)S(1)}, f32[64,128]{1,0:T(8,128)S(1)}, u32[]{:S(2)}, u32[]{:S(2)}) collective-permute-start(f32[64,128]{1,0:T(8,128)S(1)} %fusion), channel_id=1, source_target_pairs={{0,384},{16,400},{32,416},{48,432},{64,448},{80,464},{96,480},{112... | collective-permute-start | bytes 98312 | tf_op jit(solution)/shard_map/ppermute | solution.py:302
  29.8 3.7 %collective-permute-start.1 = (f32[64,128]{1,0:T(8,128)S(1)}, f32[64,128]{1,0:T(8,128)S(1)}, u32[]{:S(2)}, u32[]{:S(2)}) collective-permute-start(f32[64,128]{1,0:T(8,128)S(1)} %fusion), channel_id=1, source_target_pairs={{0,256},{16,272},{32,288},{48,304},{64,320},{80,336},{96,352},{112... | collective-permute-start | bytes 98312 | tf_op jit(solution)/shard_map/ppermute | solution.py:302
  33.4 4.6 %collective-permute-start = (f32[64,128]{1,0:T(8,128)S(1)}, f32[64,128]{1,0:T(8,128)S(1)}, u32[]{:S(2)}, u32[]{:S(2)}) collective-permute-start(f32[64,128]{1,0:T(8,128)S(1)} %fusion), channel_id=1, source_target_pairs={{0,128},{16,144},{32,160},{48,176},{64,192},{80,208},{96,224},{112... | collective-permute-start | bytes 98312 | tf_op jit(solution)/shard_map/ppermute | solution.py:302
  38.1 1.0 collective-permute-done.refs_2_
  39.1 13.3 %all_to_all.25.state.refs_7_ = f32[8,64,128]{2,1,0:T(8,128)S(1)} all-to-all(f32[8,64,128]{2,1,0:T(8,128)S(1)} %shard_map.103), channel_id=1, replica_groups={{0,16,32,48,64,80,96,112},{128,144,160,176,192,208,224,240},{256,272,28..., dimensions={0} | all-to-all | bytes 524288 | tf_op jit(solution)/shard_map/all_to_all | solution.py:305
  52.4 0.6 shard_map.104
  53.0 13.1 %all_to_all.26.refs_1_ = f32[16,8,128]{2,1,0:T(8,128)S(1)} all-to-all(f32[16,8,128]{2,1,0:T(8,128)S(1)} %get-tuple-element.21), channel_id=1, replica_groups=mesh['seq'=32,'head'=16] {'head'}, dimensions={0} | all-to-all | bytes 131072 | tf_op jit(solution)/shard_map/all_to_all | solution.py:386
  66.1 1.7 %shard_map.105 = (bf16[512,512]{1,0:T(8,128)(2,1)}, f32[8,72,128]{2,1,0:T(8,128)}) custom-call(f32[8,512]{1,0:T(8,128)S(1)} %get-tuple-element.19.refs_0_.consts, f32[16,8,128]{2,1,0:T(8,128)S(1)} %all_to_all.26.refs_1_, f32[512,512]{1,0:T(8,128)S(1)} %get-tuple-element.22.refs_2_, bf16[512,512]{1,0:T(8,128)(2,1)S(1)} %copy-done.2, ...), custom_call_target="tpu_custom_call" | custom-call | tf_op jit(solution)/shard_map/pallas_call | solution.py:281
  67.8 5.8 %all-to-all-start.3 = ((f32[8,72,128]{2,1,0:T(8,128)}), f32[8,72,128]{2,1,0:T(8,128)S(1)}, u32[]{:S(2)}, u32[]{:S(2)}) async-start(f32[8,72,128]{2,1,0:T(8,128)} %get-tuple-element.26), calls=%async_computation.3 | async-start | bytes 589824 | tf_op jit(solution)/shard_map/all_to_all | solution.py:312
  73.6 6.3 %shard_map.106 = (bf16[512,512]{1,0:T(8,128)(2,1)}, bf16[512,512]{1,0:T(8,128)(2,1)}, f32[512,512]{1,0:T(8,128)S(1)}, f32[512,512]{1,0:T(8,128)S(1)}, f32[8,128]{1,0:T(8,128)S(1)}) custom-call(f32[8,512]{1,0:T(8,128)S(1)} %get-tuple-element.19.refs_0_.consts, f32[16,8,128]{2,1,0:T(8,128)S(1)} %all_to_all.26.refs_1_, f32[512,512]{1,0:T(8,128)} %copy-done.6, ...), custom_call_target="tpu_custom_call" | custom-call | flops 1610612736 | bytes 6291456 | tf_op jit(solution)/shard_map/pallas_call | solution.py:395
  79.9 1.0 copy-done.4
  80.9 2.1 %all-to-all-done.3.refs_1_ = f32[8,72,128]{2,1,0:T(8,128)S(1)} async-done(((f32[8,72,128]{2,1,0:T(8,128)}), f32[8,72,128]{2,1,0:T(8,128)S(1)}, u32[]{:S(2)}, u32[]{:S(2)}) %all-to-all-start.3) | async-done | bytes 294944 | tf_op jit(solution)/shard_map/all_to_all | solution.py:312
  83.1 17.9 %all-gather = f32[288,128]{1,0:T(8,128)S(1)} all-gather(f32[72,128]{1,0:T(8,128)S(1)} %shard_map.107), channel_id=2, replica_groups={{0,128,256,384},{16,144,272,400},{32,160,288,416},{48,176,304,432},{64,..., dimensions={0}, use_global_device_ids=true | all-gather | bytes 184320 | tf_op jit(solution)/shard_map/all_gather | solution.py:317
  101.0 16.2 %all_to_all.27.back = f32[8,72,128]{2,1,0:T(8,128)S(1)} all-to-all(f32[8,72,128]{2,1,0:T(8,128)S(1)} %shard_map.108), channel_id=1, replica_groups={{0,16,32,48,64,80,96,112},{128,144,160,176,192,208,224,240},{256,272,28..., dimensions={0} | all-to-all | bytes 589824 | tf_op jit(solution)/shard_map/all_to_all | solution.py:319
  117.2 2.0 %shard_map.109 = (bf16[512,512]{1,0:T(8,128)(2,1)}, bf16[512,512]{1,0:T(8,128)(2,1)}, f32[1,512]{1,0:T(1,128)}) custom-call(f32[8,512]{1,0:T(8,128)S(1)} %get-tuple-element.19.refs_0_.consts, f32[8,72,128]{2,1,0:T(8,128)S(1)} %all_to_all.27.back, bf16[512,512]{1,0:T(8,128)(2,1)S(1)} %copy-done, bf16[512,512]{1,0:T(8,128)(2,1)S(1)} %copy-done.1, ...), custom_call_target="tpu_custom_call" | custom-call | tf_op jit(solution)/shard_map/pallas_call | solution.py:281
  (20 shorter events, 0.2 us)
Async XLA Ops:
  0.6 15.1 %copy-start.1 = (bf16[512,512]{1,0:T(8,128)(2,1)S(1)}, bf16[512,512]{1,0:T(8,128)(2,1)}, u32[]{:S(2)}) copy-start(bf16[512,512]{1,0:T(8,128)(2,1)} %values.5) | copy-start | bytes 1572868
  0.6 15.1 %copy-start.3 = (bf16[512,512]{1,0:T(8,128)(2,1)S(1)}, bf16[512,512]{1,0:T(8,128)(2,1)}, u32[]{:S(2)}) copy-start(bf16[512,512]{1,0:T(8,128)(2,1)} %refs_3_.3) | copy-start | bytes 1572868
  3.5 12.3 %copy-start = (bf16[512,512]{1,0:T(8,128)(2,1)S(1)}, bf16[512,512]{1,0:T(8,128)(2,1)}, u32[]{:S(2)}) copy-start(bf16[512,512]{1,0:T(8,128)(2,1)} %keys.5) | copy-start | bytes 1572868
  3.5 19.1 %all-to-all-start = ((f32[8,64,128]{2,1,0:T(8,128)}), f32[8,64,128]{2,1,0:T(8,128)S(1)}, u32[]{:S(2)}, u32[]{:S(2)}) async-start(f32[8,64,128]{2,1,0:T(8,128)} %shard_map.102), calls=%async_computation | async-start | bytes 524288 | tf_op jit(solution)/shard_map/all_to_all | solution.py:295
  13.8 0.7 copy-start.7
  15.7 0.7 copy-start.8
  22.6 29.9 %copy-start.2 = (bf16[512,512]{1,0:T(8,128)(2,1)S(1)}, bf16[512,512]{1,0:T(8,128)(2,1)}, u32[]{:S(2)}) copy-start(bf16[512,512]{1,0:T(8,128)(2,1)} %refs_3_.2) | copy-start | bytes 1572868
  22.6 15.5 %collective-permute-start.2 = (f32[64,128]{1,0:T(8,128)S(1)}, f32[64,128]{1,0:T(8,128)S(1)}, u32[]{:S(2)}, u32[]{:S(2)}) collective-permute-start(f32[64,128]{1,0:T(8,128)S(1)} %fusion), channel_id=1, source_target_pairs={{0,384},{16,400},{32,416},{48,432},{64,448},{80,464},{96,480},{112... | collective-permute-start | bytes 98312 | tf_op jit(solution)/shard_map/ppermute | solution.py:302
  29.8 8.3 %collective-permute-start.1 = (f32[64,128]{1,0:T(8,128)S(1)}, f32[64,128]{1,0:T(8,128)S(1)}, u32[]{:S(2)}, u32[]{:S(2)}) collective-permute-start(f32[64,128]{1,0:T(8,128)S(1)} %fusion), channel_id=1, source_target_pairs={{0,256},{16,272},{32,288},{48,304},{64,320},{80,336},{96,352},{112... | collective-permute-start | bytes 98312 | tf_op jit(solution)/shard_map/ppermute | solution.py:302
  33.4 5.6 %collective-permute-start = (f32[64,128]{1,0:T(8,128)S(1)}, f32[64,128]{1,0:T(8,128)S(1)}, u32[]{:S(2)}, u32[]{:S(2)}) collective-permute-start(f32[64,128]{1,0:T(8,128)S(1)} %fusion), channel_id=1, source_target_pairs={{0,128},{16,144},{32,160},{48,176},{64,192},{80,208},{96,224},{112... | collective-permute-start | bytes 98312 | tf_op jit(solution)/shard_map/ppermute | solution.py:302
  53.0 14.8 %copy-start.6 = (f32[512,512]{1,0:T(8,128)}, f32[512,512]{1,0:T(8,128)S(1)}, u32[]{:S(2)}) copy-start(f32[512,512]{1,0:T(8,128)S(1)} %get-tuple-element.22.refs_2_) | copy-start | bytes 3145732
  67.8 15.2 %all-to-all-start.3 = ((f32[8,72,128]{2,1,0:T(8,128)}), f32[8,72,128]{2,1,0:T(8,128)S(1)}, u32[]{:S(2)}, u32[]{:S(2)}) async-start(f32[8,72,128]{2,1,0:T(8,128)} %get-tuple-element.26), calls=%async_computation.3 | async-start | bytes 589824 | tf_op jit(solution)/shard_map/all_to_all | solution.py:312
  79.9 1.0 copy-start.4
  83.0 34.2 %copy-start.5 = (f32[512,512]{1,0:T(8,128)S(1)}, f32[512,512]{1,0:T(8,128)}, u32[]{:S(2)}) copy-start(f32[512,512]{1,0:T(8,128)} %copy-done.4) | copy-start | bytes 3145732

commit v7 on v6

--- a/solution.py
+++ b/solution.py
@@ -90,23 +90,28 @@
         store.wait()
 
 
-GAIN, RATE, ZERO = 0, 1, 2
+GAIN, RATE = 0, 1
+
+
+def weighted(a, b, t, s, weight):
+    return (dot(a[t, :], b[s, :], 1, 1) * weight).astype(BF16)
 
 
 def intra_kernel(rates, gain, queries, keys, values, out, consts):
-    rate = jnp.full(gain.shape, rates[pl.program_id(0)], F32)
-    consts[...] = jnp.concatenate([gain[...], rate, jnp.zeros((6, rate.shape[1]), F32)], axis=0)
-    half = queries.shape[0] // 2
-    same, across = tile_weights(rate, half)
+    length = queries.shape[0]
+    size = 128
+    half = length // 2
     first, second = pl.ds(0, half), pl.ds(half, half)
-
-    def probs(t, s, weight):
-        return (dot(queries[t, :], keys[s, :], 1, 1) * weight).astype(BF16)
-
-    out[first, :] = dot(probs(first, first, same), values[first, :], 1, 0)
-    out[second, :] = dot(probs(second, first, across), values[first, :], 1, 0) + dot(
-        probs(second, second, same), values[second, :], 1, 0
-    )
+    for h in range(queries.shape[1] // size):
+        cols = column(h, size)
+        rate = jnp.full((1, size), rates[h], F32)
+        consts[:, cols] = jnp.concatenate([gain[:, cols], rate, jnp.zeros((6, size), F32)], axis=0)
+        same, across = tile_weights(rate, half)
+        q, k, v = (ref.at[:, cols] for ref in (queries, keys, values))
+        out[first, cols] = dot(weighted(q, k, first, first, same), v[first, :], 1, 0)
+        out[second, cols] = dot(weighted(q, k, second, first, across), v[first, :], 1, 0) + dot(
+            weighted(q, k, second, second, same), v[second, :], 1, 0
+        )
 
 
 def mixed_kernel(consts, queries, state, intra, cotangent, mixed, stats, square, inner):
@@ -170,41 +175,58 @@
         store.wait()
 
 
-def weighted(a, b, t, s, weight):
-    return (dot(a[t, :], b[s, :], 1, 1) * weight).astype(BF16)
-
-
 def grads_kernel(
-    channels, consts, received, mixed, queries, keys, values, grad, state,
-    attended, query_grad, key_part, value_part, token, inv,
+    channels, consts, received, mixed_in, queries, keys, values, grad_in, state,
+    attended_out, query_out, key_part, value_part, token,
+    inv, mixed, grad, attended, query_grad, arrived, sent,
 ):
-    rate = consts[pl.ds(RATE, 1), :]
-    length, size = queries.shape
+    length = queries.shape[0]
+    size = 128
+    heads = queries.shape[1] // size
     half = length // 2
-
-    @pl.when(pl.program_id(0) == 0)
-    def _():
-        token_scales(received, channels, inv, None)
-
-    attended[...] = (mixed[...] * inv[...] * consts[pl.ds(GAIN, 1), :]).astype(BF16)
-    same, across = tile_weights(rate, half)
     first, second = pl.ds(0, half), pl.ds(half, half)
-    state_part = head_in_of(rate, length) * dot_split(grad[...], state[...].reshape(size, size), 1, 1)
-    upper = weighted(grad, values, first, first, same)
-    lower = weighted(grad, values, second, first, across)
-    final = weighted(grad, values, second, second, same)
-    query_grad[first, :] = (dot(upper, keys[first, :], 1, 0) + state_part[:half]).astype(BF16)
-    query_grad[second, :] = (
-        dot(lower, keys[first, :], 1, 0) + dot(final, keys[second, :], 1, 0) + state_part[half:]
-    ).astype(BF16)
-    key_part[first, :] = dot(upper, queries[first, :], 0, 0) + dot(lower, queries[second, :], 0, 0)
-    key_part[second, :] = dot(final, queries[second, :], 0, 0)
-    upper = weighted(queries, keys, first, first, same)
-    lower = weighted(queries, keys, second, first, across)
-    final = weighted(queries, keys, second, second, same)
-    value_part[first, :] = dot(upper, grad[first, :], 0, 0) + dot(lower, grad[second, :], 0, 0)
-    value_part[second, :] = dot(final, grad[second, :], 0, 0)
+    copies, stores = [], []
+    for h in range(heads):
+        cols = column(h, size)
+        copies.append(
+            [
+                pltpu.make_async_copy(source.at[:, cols], rows.at[:, cols], arrived.at[2 * h + i])
+                for i, (source, rows) in enumerate(((grad_in, grad), (mixed_in, mixed)))
+            ]
+        )
+        for copy in copies[-1]:
+            copy.start()
     token[...] = jnp.zeros_like(token)
+    token_scales(received, channels, inv, None)
+    for h in range(heads):
+        cols = column(h, size)
+        rate = consts[pl.ds(RATE, 1), cols]
+        same, across = tile_weights(rate, half)
+        q, k, v, g = (ref.at[:, cols] for ref in (queries, keys, values, grad))
+        for copy in copies[h]:
+            copy.wait()
+        attended[:, cols] = (mixed[:, cols] * inv[...] * consts[pl.ds(GAIN, 1), cols]).astype(BF16)
+        state_in = state[pl.ds(2 * h, 2)].reshape(size, size)
+        state_part = head_in_of(rate, length) * dot_split(g[...], state_in, 1, 1)
+        upper = weighted(g, v, first, first, same)
+        lower = weighted(g, v, second, first, across)
+        final = weighted(g, v, second, second, same)
+        query_grad[first, cols] = (dot(upper, k[first, :], 1, 0) + state_part[:half]).astype(BF16)
+        query_grad[second, cols] = (
+            dot(lower, k[first, :], 1, 0) + dot(final, k[second, :], 1, 0) + state_part[half:]
+        ).astype(BF16)
+        for i, (rows, target) in enumerate(((attended, attended_out), (query_grad, query_out))):
+            stores.append(pltpu.make_async_copy(rows.at[:, cols], target.at[:, cols], sent.at[2 * h + i]))
+            stores[-1].start()
+        key_part[first, cols] = dot(upper, q[first, :], 0, 0) + dot(lower, q[second, :], 0, 0)
+        key_part[second, cols] = dot(final, q[second, :], 0, 0)
+        upper = weighted(q, k, first, first, same)
+        lower = weighted(q, k, second, first, across)
+        final = weighted(q, k, second, second, same)
+        value_part[first, cols] = dot(upper, g[first, :], 0, 0) + dot(lower, g[second, :], 0, 0)
+        value_part[second, cols] = dot(final, g[second, :], 0, 0)
+    for store in stores:
+        store.wait()
 
 
 def finish_kernel(
@@ -247,12 +269,22 @@
     out[rows:] = sum(parts[k, rows:] for k in range(GROUP))
 
 
-def fold_forward_kernel(length, consts, parts, *refs):
+def forward_totals_kernel(length, consts, parts, out):
+    factor, _ = fold_factors(consts, length)
+    total = parts[0]
+    for k in range(1, GROUP):
+        total = factor * total + parts[k]
+    out[...] = total
+
+
+def join_kernel(length, consts, total, before, out):
+    _, group_factor = fold_factors(consts, length)
+    out[...] = total[...] + group_factor * before[...]
+
+
+def fold_forward_kernel(length, consts, parts, nearest, near, far, out):
     factor, group_factor = fold_factors(consts, length)
-    *arrived, out = refs
-    carry = arrived[-1][...]
-    for ref in arrived[-2::-1]:
-        carry = group_factor * carry + ref[...]
+    carry = nearest[...] + near[...] + group_factor * far[...]
     for k in range(GROUP):
         out[k] = carry
         carry = factor * carry + parts[k]
@@ -288,20 +320,21 @@
     )(*operands)
 
 
-def scan_forward(x, rates, consts, length):
-    count = lax.axis_size("seq")
-    groups = count // GROUP
+def send(x, pairs):
+    return lax.ppermute(x, "seq", [(a * GROUP + j, b * GROUP + j) for a, b in pairs for j in range(GROUP)])
+
+
+def scan_forward(x, consts, length):
+    groups = lax.axis_size("seq") // GROUP
     members = [[g * GROUP + j for j in range(GROUP)] for g in range(groups)]
     parts = lax.all_to_all(x, "seq", 0, 0, axis_index_groups=members)
-    rate = lax.dynamic_index_in_dim(rates, lax.axis_index("seq") % GROUP * rates.shape[0] // GROUP, 0, False)
-    factor = jnp.exp(-rate * length)
-    total = parts[0] + consts[ZERO : ZERO + 1, :128]
-    for k in range(1, GROUP):
-        total = factor * total + parts[k]
-    arrived = [
-        lax.ppermute(total, "seq", [(i, i + by * GROUP) for i in range(count - by * GROUP)]) for by in range(1, groups)
-    ]
-    out = whole_call(lambda *refs: fold_forward_kernel(length, *refs), like(x), [consts, parts, *arrived])
+    one = jax.ShapeDtypeStruct(x.shape[1:], F32)
+    total = whole_call(lambda *refs: forward_totals_kernel(length, *refs), one, [consts, parts])
+    nearest = send(total, [(0, 1)])
+    total = whole_call(lambda *refs: join_kernel(length, *refs), one, [consts, total, nearest])
+    far = send(total, [(1, 3)])
+    near = send(total, [(1, 2), (2, 3)])
+    out = whole_call(lambda *refs: fold_forward_kernel(length, *refs), like(x), [consts, parts, nearest, near, far])
     return lax.all_to_all(out, "seq", 0, 0, axis_index_groups=members)
 
 
@@ -331,28 +364,11 @@
     total_channels = channels * head_devices
 
     smem = pl.BlockSpec(memory_space=pltpu.SMEM)
-    tokens = pl.BlockSpec((length, size), lambda h: (0, h))
-    row = pl.BlockSpec((1, size), lambda h: (0, h))
-    shards = pl.BlockSpec((2, size // 2, size), lambda h: (h, 0, 0))
-    shards_extra = pl.BlockSpec((2, size // 2 + EXTRA, size), lambda h: (h, 0, 0))
     stats_shape = (head_devices, 2 * length // 128, 128)
-    stats_spec = pl.BlockSpec(stats_shape, lambda h: (0, 0, 0))
     scratch = pltpu.VMEM((length, size), F32)
 
     def array(kind, *shape):
         return jax.ShapeDtypeStruct(shape, kind)
-
-    def call(kernel, in_specs, out_specs, out_shape, flops, nbytes, scratches=()):
-        return pl.pallas_call(
-            kernel,
-            grid=(heads,),
-            in_specs=in_specs,
-            out_specs=out_specs,
-            out_shape=out_shape,
-            scratch_shapes=list(scratches),
-            compiler_params=pltpu.CompilerParams(vmem_limit_bytes=VMEM_LIMIT),
-            cost_estimate=pl.CostEstimate(flops=flops, bytes_accessed=nbytes, transcendentals=0),
-        )
 
     square = 2 * heads * length * length * size
     wide = array(F32, length, channels)
@@ -373,12 +389,14 @@
             pltpu.SemaphoreType.DMA((2 * heads + 1,)), pltpu.SemaphoreType.DMA((heads,)),
         ],
     )
-    consts_spec = pl.BlockSpec((8, size), lambda h: (0, h))
-    intra, consts = call(
-        intra_kernel, [smem, row, tokens, tokens, tokens], [tokens, consts_spec],
-        [wide, array(F32, 8, channels)], 2 * square, 4 << 20,
-    )(rates, gain.reshape(1, channels), queries, keys, values)
-    state_in = scan_forward(sums, rates, consts, length)
+    def cost(flops):
+        return pl.CostEstimate(flops=flops, bytes_accessed=6 << 20, transcendentals=0)
+
+    intra, consts = whole_call(
+        intra_kernel, [wide, array(F32, 8, channels)], [rates, gain.reshape(1, channels), queries, keys, values],
+        in_specs=[smem] + [in_vmem] * 4, cost_estimate=cost(2 * square),
+    )
+    state_in = scan_forward(sums, consts, length)
     mixed, stats = whole_call(
         mixed_kernel, [wide, array(F32, *stats_shape)],
         [consts, queries, state_in, intra, cotangent], scratch_shapes=[scratch, scratch],
@@ -392,13 +410,14 @@
         scratch_shapes=[scratch, scratch, rows_scratch, pltpu.VMEM(sums_shape, F32), copies],
     )
     part = pltpu.VMEM((length, channels), F32)
-    attended, query_grad, key_part, value_part, token = call(
-        lambda *refs: grads_kernel(total_channels, *refs),
-        [consts_spec, stats_spec, tokens, tokens, tokens, tokens, tokens, shards],
-        [tokens, tokens, tokens, tokens, pl.BlockSpec((8, 128), lambda h: (0, 0))],
-        [narrow, narrow, part, part, array(F32, 8, 128)],
-        6 * square, 6 << 20, [scratch],
-    )(consts, received, hbm(mixed), queries, keys, values, hbm(grad), state_in)
+    attended, query_grad, key_part, value_part, token = whole_call(
+        lambda *refs: grads_kernel(total_channels, *refs), [narrow, narrow, part, part, array(F32, 8, 128)],
+        [consts, received, hbm(mixed), queries, keys, values, hbm(grad), state_in],
+        in_specs=[in_vmem, in_vmem, anywhere, in_vmem, in_vmem, in_vmem, anywhere, in_vmem],
+        out_specs=[anywhere, anywhere, in_vmem, in_vmem, in_vmem],
+        scratch_shapes=[scratch, pltpu.VMEM((length, channels), F32), rows_scratch, rows_scratch, rows_scratch, copies, copies],
+        cost_estimate=cost(6 * square),
+    )
     back_in = scan_back(back_sums, consts, length, token)
     key_grad, value_grad, gain_grad = whole_call(
         finish_kernel, [narrow, narrow, array(F32, 1, channels)],

time: 120 us -> 119 us (level)
  starting transfers between devices: 31.6 us -> 23.6 us
  blocking collectives: 60.4 us -> 67.7 us
  waiting for transfers between devices: 6.2 us -> 9.2 us
  local copies, waits for them, and re-layouts: 2.87 us -> 1.64 us
    pallas_call x2 -> x0, Pallas kernels: 9.31 us -> none  [the longest x1 6.27 us: body(): call(lambda *refs: grads_kernel(total_channels, *refs), [consts_spec, sta...]
    pallas_call x7 -> x11, Pallas kernels: 7.25 us -> 15.6 us  [whole_call(): pl.pallas_call(kernel, in_specs=in_specs, out_specs=out_specs, out_shape=...]
    ppermute x3, starting transfers between devices: 15.5 us -> 7.46 us  [send(): lax.ppermute(x, 'seq', [(a * GROUP + j, b * GROUP + j) for a, b in pairs...]
    all_gather x1, blocking collectives: 17.9 us -> 24.2 us  [scan_back(): arrived = lax.all_gather(totals, 'seq', axis_index_groups=across)]
    all_to_all x1, waiting for transfers between devices: 3.09 us -> 5.85 us  [scan_forward(): parts = lax.all_to_all(x, 'seq', 0, 0, axis_index_groups=members)]
  transfers between devices with their start and end apart: 5 -> 5, of which waited for: 3 -> 3; matrix products, arithmetic and copies ran while one was open for 0% -> 0% of each run, Pallas kernels for 8% -> 7%
where the time goes in v7:
time: 119 us
  blocking collectives  67.7 us (57%)
  starting transfers between devices  23.6 us (20%)
  Pallas kernels  15.6 us (13%)
  waiting for transfers between devices  9.2 us (8%)
  local copies, waits for them, and re-layouts  1.64 us (1%)
    all_gather x1, blocking collectives, scan_back(): arrived = lax.all_gather(totals, 'seq', axis_index_groups=across)  24.2 us
    all_to_all x1, blocking collectives, scan_back(): return lax.all_to_all(out, 'seq', 0, 0, axis_index_groups=members)  16.3 us
    pallas_call x11, Pallas kernels, whole_call(): pl.pallas_call(kernel, in_specs=in_specs, out_specs=out_specs, out_shape=...  15.6 us
    all_to_all x1, blocking collectives, scan_forward(): return lax.all_to_all(out, 'seq', 0, 0, axis_index_groups=members)  14.1 us
    all_to_all x1, blocking collectives, body(): received = lax.all_to_all(stats, 'head', 0, 0)  13.1 us
    all_to_all x1, starting transfers between devices, scan_forward(): parts = lax.all_to_all(x, 'seq', 0, 0, axis_index_groups=members)  10.3 us
    ppermute x3, starting transfers between devices, send(): lax.ppermute(x, 'seq', [(a * GROUP + j, b * GROUP + j) for a, b in pairs...  7.46 us
    all_to_all x1, waiting for transfers between devices, scan_forward(): parts = lax.all_to_all(x, 'seq', 0, 0, axis_index_groups=members)  5.85 us
  transfers between devices with their start and end apart: 5, of which 3 were waited for; matrix products, arithmetic and copies ran while one was open for 0% of the time, Pallas kernels for 7%

profile of v7, /device:TPU:1, one launch (start us, length us, event | category | flops | bytes accessed | tf_op | source)
XLA Modules:
  0.0 118.5 jit_solution(12208212221858405987)
XLA Ops:
  0.7 2.8 %shard_map.102 = f32[8,64,128]{2,1,0:T(8,128)} custom-call(f32[4]{0:T(128)} %rates_in.1, bf16[512,512]{1,0:T(8,128)(2,1)} %keys.5, bf16[512,512]{1,0:T(8,128)(2,1)} %values.5), custom_call_target="tpu_custom_call" | custom-call | tf_op jit(solution)/shard_map/pallas_call | solution.py:313
  3.5 0.0 copy-start
  3.5 10.3 %all-to-all-start = ((f32[8,64,128]{2,1,0:T(8,128)}), f32[8,64,128]{2,1,0:T(8,128)S(1)}, u32[]{:S(2)}, u32[]{:S(2)}) async-start(f32[8,64,128]{2,1,0:T(8,128)} %shard_map.102), calls=%async_computation | async-start | bytes 524288 | tf_op jit(solution)/shard_map/all_to_all | solution.py:330
  13.8 0.6 copy-done.7
  14.5 2.2 %shard_map.101 = (f32[512,512]{1,0:T(8,128)S(1)}, f32[8,512]{1,0:T(8,128)S(1)}) custom-call(f32[4]{0:T(128)S(1)} %copy-done.7, f32[1,512]{1,0:T(1,128)S(1)} %bitcast.4, bf16[512,512]{1,0:T(8,128)(2,1)S(1)} %copy-done.3, bf16[512,512]{1,0:T(8,128)(2,1)S(1)} %copy-done, bf16[512,512]{1,0:T(8,128)(2,1)S(1)} %copy-done.1), custom_call_target="tpu_custom_call" | custom-call | flops 536870912 | bytes 6291456 | tf_op jit(solution)/shard_map/pallas_call | solution.py:313
  16.7 5.8 %all-to-all-done.refs_1_ = f32[8,64,128]{2,1,0:T(8,128)S(1)} async-done(((f32[8,64,128]{2,1,0:T(8,128)}), f32[8,64,128]{2,1,0:T(8,128)S(1)}, u32[]{:S(2)}, u32[]{:S(2)}) %all-to-all-start) | async-done | bytes 262176 | tf_op jit(solution)/shard_map/all_to_all | solution.py:330
  22.6 6.0 %collective-permute-start = (f32[64,128]{1,0:T(8,128)S(1)}, f32[64,128]{1,0:T(8,128)S(1)}, u32[]{:S(2)}, u32[]{:S(2)}) collective-permute-start(f32[64,128]{1,0:T(8,128)S(1)} %shard_map.103.refs_1_), channel_id=1, source_target_pairs={{0,128},{16,144},{32,160},{48,176},{64,192},{80,208},{96,224},{112... | collective-permute-start | bytes 98312 | tf_op jit(solution)/shard_map/ppermute | solution.py:324
  28.6 1.0 collective-permute-done.refs_2_
  29.6 0.0 copy-start.2
  29.6 0.8 collective-permute-start.2
  30.4 0.7 collective-permute-start.1
  31.1 0.0 collective-permute-done.2.refs_4_
  31.1 0.1 shard_map.105
  31.2 14.1 %all_to_all.25.state.refs_7_ = f32[8,64,128]{2,1,0:T(8,128)S(1)} all-to-all(f32[8,64,128]{2,1,0:T(8,128)S(1)} %shard_map.105), channel_id=1, replica_groups={{0,16,32,48,64,80,96,112},{128,144,160,176,192,208,224,240},{256,272,28..., dimensions={0} | all-to-all | bytes 524288 | tf_op jit(solution)/shard_map/all_to_all | solution.py:338
  45.2 0.6 shard_map.106
  45.8 13.1 %all_to_all.26.refs_1_ = f32[16,8,128]{2,1,0:T(8,128)S(1)} all-to-all(f32[16,8,128]{2,1,0:T(8,128)S(1)} %get-tuple-element.21), channel_id=1, replica_groups=mesh['seq'=32,'head'=16] {'head'}, dimensions={0} | all-to-all | bytes 131072 | tf_op jit(solution)/shard_map/all_to_all | solution.py:404
  58.9 1.7 %shard_map.107 = (bf16[512,512]{1,0:T(8,128)(2,1)}, f32[8,72,128]{2,1,0:T(8,128)}) custom-call(f32[8,512]{1,0:T(8,128)S(1)} %get-tuple-element.19.refs_0_.consts, f32[16,8,128]{2,1,0:T(8,128)S(1)} %all_to_all.26.refs_1_, f32[512,512]{1,0:T(8,128)S(1)} %get-tuple-element.22.refs_2_, bf16[512,512]{1,0:T(8,128)(2,1)S(1)} %copy-done.2, ...), custom_call_target="tpu_custom_call" | custom-call | tf_op jit(solution)/shard_map/pallas_call | solution.py:313
  60.6 5.8 %all-to-all-start.3 = ((f32[8,72,128]{2,1,0:T(8,128)}), f32[8,72,128]{2,1,0:T(8,128)S(1)}, u32[]{:S(2)}, u32[]{:S(2)}) async-start(f32[8,72,128]{2,1,0:T(8,128)} %get-tuple-element.26), calls=%async_computation.3 | async-start | bytes 589824 | tf_op jit(solution)/shard_map/all_to_all | solution.py:345
  66.4 6.0 %shard_map.108 = (bf16[512,512]{1,0:T(8,128)(2,1)}, bf16[512,512]{1,0:T(8,128)(2,1)}, f32[512,512]{1,0:T(8,128)S(1)}, f32[512,512]{1,0:T(8,128)S(1)}, f32[8,128]{1,0:T(8,128)S(1)}) custom-call(f32[8,512]{1,0:T(8,128)S(1)} %get-tuple-element.19.refs_0_.consts, f32[16,8,128]{2,1,0:T(8,128)S(1)} %all_to_all.26.refs_1_, f32[512,512]{1,0:T(8,128)} %copy-done.6, ...), custom_call_target="tpu_custom_call" | custom-call | flops 1610612736 | bytes 6291456 | tf_op jit(solution)/shard_map/pallas_call | solution.py:313
  72.5 1.0 copy-done.4
  73.5 2.3 %all-to-all-done.3.refs_1_ = f32[8,72,128]{2,1,0:T(8,128)S(1)} async-done(((f32[8,72,128]{2,1,0:T(8,128)}), f32[8,72,128]{2,1,0:T(8,128)S(1)}, u32[]{:S(2)}, u32[]{:S(2)}) %all-to-all-start.3) | async-done | bytes 294944 | tf_op jit(solution)/shard_map/all_to_all | solution.py:345
  75.9 24.2 %all-gather = f32[288,128]{1,0:T(8,128)S(1)} all-gather(f32[72,128]{1,0:T(8,128)S(1)} %shard_map.109), channel_id=2, replica_groups={{0,128,256,384},{16,144,272,400},{32,160,288,416},{48,176,304,432},{64,..., dimensions={0}, use_global_device_ids=true | all-gather | bytes 184320 | tf_op jit(solution)/shard_map/all_gather | solution.py:350
  100.1 16.3 %all_to_all.27.back = f32[8,72,128]{2,1,0:T(8,128)S(1)} all-to-all(f32[8,72,128]{2,1,0:T(8,128)S(1)} %shard_map.110), channel_id=1, replica_groups={{0,16,32,48,64,80,96,112},{128,144,160,176,192,208,224,240},{256,272,28..., dimensions={0} | all-to-all | bytes 589824 | tf_op jit(solution)/shard_map/all_to_all | solution.py:352
  116.5 2.0 %shard_map.111 = (bf16[512,512]{1,0:T(8,128)(2,1)}, bf16[512,512]{1,0:T(8,128)(2,1)}, f32[1,512]{1,0:T(1,128)}) custom-call(f32[8,512]{1,0:T(8,128)S(1)} %get-tuple-element.19.refs_0_.consts, f32[8,72,128]{2,1,0:T(8,128)S(1)} %all_to_all.27.back, bf16[512,512]{1,0:T(8,128)(2,1)S(1)} %copy-done, bf16[512,512]{1,0:T(8,128)(2,1)S(1)} %copy-done.1, ...), custom_call_target="tpu_custom_call" | custom-call | tf_op jit(solution)/shard_map/pallas_call | solution.py:313
  (19 shorter events, 0.2 us)
Async XLA Ops:
  0.6 13.2 %copy-start.1 = (bf16[512,512]{1,0:T(8,128)(2,1)S(1)}, bf16[512,512]{1,0:T(8,128)(2,1)}, u32[]{:S(2)}) copy-start(bf16[512,512]{1,0:T(8,128)(2,1)} %values.5) | copy-start | bytes 1572868
  0.6 13.2 %copy-start.3 = (bf16[512,512]{1,0:T(8,128)(2,1)S(1)}, bf16[512,512]{1,0:T(8,128)(2,1)}, u32[]{:S(2)}) copy-start(bf16[512,512]{1,0:T(8,128)(2,1)} %refs_3_.3) | copy-start | bytes 1572868
  0.7 13.2 %copy-start.8 = (f32[512]{0:T(512)S(1)}, f32[512]{0:T(512)}, u32[]{:S(2)}) copy-start(f32[512]{0:T(512)} %param.10) | copy-start | bytes 6148
  3.5 10.4 %copy-start = (bf16[512,512]{1,0:T(8,128)(2,1)S(1)}, bf16[512,512]{1,0:T(8,128)(2,1)}, u32[]{:S(2)}) copy-start(bf16[512,512]{1,0:T(8,128)(2,1)} %keys.5) | copy-start | bytes 1572868
  3.5 19.1 %all-to-all-start = ((f32[8,64,128]{2,1,0:T(8,128)}), f32[8,64,128]{2,1,0:T(8,128)S(1)}, u32[]{:S(2)}, u32[]{:S(2)}) async-start(f32[8,64,128]{2,1,0:T(8,128)} %shard_map.102), calls=%async_computation | async-start | bytes 524288 | tf_op jit(solution)/shard_map/all_to_all | solution.py:330
  13.8 0.7 copy-start.7
  22.6 7.0 %collective-permute-start = (f32[64,128]{1,0:T(8,128)S(1)}, f32[64,128]{1,0:T(8,128)S(1)}, u32[]{:S(2)}, u32[]{:S(2)}) collective-permute-start(f32[64,128]{1,0:T(8,128)S(1)} %shard_map.103.refs_1_), channel_id=1, source_target_pairs={{0,128},{16,144},{32,160},{48,176},{64,192},{80,208},{96,224},{112... | collective-permute-start | bytes 98312 | tf_op jit(solution)/shard_map/ppermute | solution.py:324
  29.6 15.6 %copy-start.2 = (bf16[512,512]{1,0:T(8,128)(2,1)S(1)}, bf16[512,512]{1,0:T(8,128)(2,1)}, u32[]{:S(2)}) copy-start(bf16[512,512]{1,0:T(8,128)(2,1)} %refs_3_.2) | copy-start | bytes 1572868
  29.6 1.5 %collective-permute-start.2 = (f32[64,128]{1,0:T(8,128)S(1)}, f32[64,128]{1,0:T(8,128)S(1)}, u32[]{:S(2)}, u32[]{:S(2)}) collective-permute-start(f32[64,128]{1,0:T(8,128)S(1)} %shard_map.104), channel_id=1, source_target_pairs={{128,384},{144,400},{160,416},{176,432},{192,448},{208,464},{224,4... | collective-permute-start | bytes 98312 | tf_op jit(solution)/shard_map/ppermute | solution.py:324
  30.4 0.7 collective-permute-start.1
  45.8 14.8 %copy-start.6 = (f32[512,512]{1,0:T(8,128)}, f32[512,512]{1,0:T(8,128)S(1)}, u32[]{:S(2)}) copy-start(f32[512,512]{1,0:T(8,128)S(1)} %get-tuple-element.22.refs_2_) | copy-start | bytes 3145732
  60.6 15.2 %all-to-all-start.3 = ((f32[8,72,128]{2,1,0:T(8,128)}), f32[8,72,128]{2,1,0:T(8,128)S(1)}, u32[]{:S(2)}, u32[]{:S(2)}) async-start(f32[8,72,128]{2,1,0:T(8,128)} %get-tuple-element.26), calls=%async_computation.3 | async-start | bytes 589824 | tf_op jit(solution)/shard_map/all_to_all | solution.py:345
  72.5 1.0 copy-start.4
  75.8 40.7 %copy-start.5 = (f32[512,512]{1,0:T(8,128)S(1)}, f32[512,512]{1,0:T(8,128)}, u32[]{:S(2)}) copy-start(f32[512,512]{1,0:T(8,128)} %copy-done.4) | copy-start | bytes 3145732

commit v8 on v0

v8 whole, which is shorter than its diff:
```python
import jax
import jax.numpy as jnp
from jax import lax
from jax.experimental import pallas as pl
from jax.experimental.pallas import tpu as pltpu
from jax.sharding import PartitionSpec as P

epsilon = 1e-06
F32, BF16 = jnp.float32, jnp.bfloat16
SIZE = 128
CHIPS = 4
EXTRA = 8
GAIN, RATE = 0, 1
VMEM_LIMIT = 16 * 1024 * 1024


def dot(a, b, over_a, over_b):
    return lax.dot_general(a, b, (((over_a,), (over_b,)), ((), ())), preferred_element_type=F32)


def dot_split(a, x, over_a, over_x):
    high = x.astype(BF16)
    low = (x - high.astype(F32)).astype(BF16)
    both = dot(a, jnp.concatenate([high, low], axis=1 - over_x), over_a, over_x)
    return both[:, : both.shape[1] // 2] + both[:, both.shape[1] // 2 :]


def rows_of(length):
    return lax.broadcasted_iota(jnp.int32, (length, SIZE), 0).astype(F32)


def lanes_of():
    return lax.broadcasted_iota(jnp.int32, (1, SIZE), 1).astype(F32)


def head_in_of(rate, length):
    base = jnp.exp(-rate * (rows_of(SIZE) + 1.0))
    return jnp.concatenate([base * jnp.exp(-rate * start) for start in range(0, length, SIZE)], axis=0)


def tail_out_of(rate, length):
    base = jnp.exp(-rate * (SIZE - 1.0 - rows_of(SIZE)))
    return jnp.concatenate([base * jnp.exp(-rate * (length - SIZE - start)) for start in range(0, length, SIZE)], axis=0)


def tile_weights(rate, turned):
    rows, lanes = rows_of(SIZE), lanes_of()
    distance = lanes - rows if turned else rows - lanes
    near = jnp.where(distance >= 0, jnp.exp(-rate * jnp.maximum(distance, 0.0)), 0.0)
    if turned:
        far = jnp.exp(-rate * (SIZE - 1.0 - rows)) * jnp.exp(-rate * (lanes + 1.0))
    else:
        far = jnp.exp(-rate * (rows + 1.0)) * jnp.exp(-rate * (SIZE - 1.0 - lanes))
    step = jnp.exp(-rate * SIZE)
    farther = far * step
    farthest = farther * step
    none = jnp.zeros_like(near)

    def square(a, b, c, d):
        return jnp.concatenate([jnp.concatenate([a, b], axis=1), jnp.concatenate([c, d], axis=1)], axis=0)

    if turned:
        return square(near, far, none, near), square(farther, farthest, far, farther)
    return square(near, none, far, near), square(farther, far, farthest, farther)


def weighted(a, b, rows_a, rows_b, weight):
    return (dot(a[rows_a, :], b[rows_b, :], 1, 1) * weight).astype(BF16)


def column(h):
    return pl.ds(h * SIZE, SIZE)


def heads_of(mine, heads):
    core = lax.axis_index("seq") % 2
    start = (core if mine else 1 - core) * (heads // 2)
    return [pl.ds(pl.multiple_of((start + slot) * SIZE, SIZE), SIZE) for slot in range(heads // 2)]


def first_sums_kernel(
    rates_in, gain_in, keys, values, out, consts, rates, gain, key_rows, value_rows, arrived
):
    length = keys.shape[0]
    heads = rates.shape[0]
    copies = []
    for slot, cols in enumerate(heads_of(False, heads)):
        copies.append(
            [
                pltpu.make_async_copy(source.at[:, cols], rows.at[:, column(slot)], arrived.at[2 * slot + i])
                for i, (source, rows) in enumerate(((values, value_rows), (keys, key_rows)))
            ]
        )
        for copy in copies[-1]:
            copy.start()
    small = [
        pltpu.make_async_copy(rates_in, rates, arrived.at[heads]),
        pltpu.make_async_copy(gain_in, gain, arrived.at[heads + 1]),
    ]
    for copy in small:
        copy.start()
    for copy in small:
        copy.wait()
    for h in range(heads):
        rate = jnp.full((1, SIZE), rates[h], F32)
        consts[:, column(h)] = jnp.concatenate([gain[:, column(h)], rate, jnp.zeros((6, SIZE), F32)], axis=0)
    for slot, cols in enumerate(heads_of(False, heads)):
        tail = tail_out_of(consts[pl.ds(RATE, 1), cols], length)
        for copy in copies[slot]:
            copy.wait()
        scaled = value_rows[:, column(slot)].astype(F32) * tail
        out[slot] = dot_split(key_rows[:, column(slot)], scaled, 0, 0)


def own_sums_kernel(consts, keys, values, out):
    length = keys.shape[0]
    for slot, cols in enumerate(heads_of(True, keys.shape[1] // SIZE)):
        scaled = values[:, cols].astype(F32) * tail_out_of(consts[pl.ds(RATE, 1), cols], length)
        out[slot] = dot_split(keys[:, cols], scaled, 0, 0)


def intra_kernel(consts, queries, keys, values, token_in, out, token):
    half = queries.shape[0] // 2
    first, second = pl.ds(0, half), pl.ds(half, half)
    for h in range(queries.shape[1] // SIZE):
        cols = column(h)
        same, across = tile_weights(consts[pl.ds(RATE, 1), cols], False)
        q, k, v = (ref.at[:, cols] for ref in (queries, keys, values))
        out[first, cols] = dot(weighted(q, k, first, first, same), v[first, :], 1, 0)
        out[second, cols] = dot(weighted(q, k, second, first, across), v[first, :], 1, 0) + dot(
            weighted(q, k, second, second, same), v[second, :], 1, 0
        )
    token[...] = jnp.zeros_like(token)


def mixed_kernel(consts, queries, mine, other, intra, cotangent, mixed, stats, square, inner):
    length = queries.shape[0]
    heads = queries.shape[1] // SIZE
    core = lax.axis_index("seq") % 2
    for h in range(heads):
        cols = column(h)
        slot = h % (heads // 2)
        state_in = jnp.where(core == h // (heads // 2), mine[slot], other[slot])
        head_in = head_in_of(consts[pl.ds(RATE, 1), cols], length)
        value = intra[:, cols] + head_in * dot_split(queries[:, cols], state_in, 1, 0)
        mixed[:, cols] = value
        new_square = value * value
        new_inner = cotangent[:, cols].astype(F32) * consts[pl.ds(GAIN, 1), cols] * value
        if h > 0:
            new_square, new_inner = new_square + square[...], new_inner + inner[...]
        square[...] = new_square
        inner[...] = new_inner
    pieces = []
    for ref in (square, inner):
        for start in range(0, length, SIZE):
            pieces.append(jnp.sum(ref[pl.ds(start, SIZE), :].T, axis=0, keepdims=True))
    stats[...] = jnp.broadcast_to(jnp.concatenate(pieces, axis=0)[None], stats.shape)


def token_scales(received, channels, inv_out, coef_out):
    total = jnp.sum(received[...], axis=0)
    chunks = total.shape[0] // 2
    inv = lax.rsqrt(total[:chunks] / channels + epsilon)
    coef = inv * inv * inv * total[chunks:] / channels
    for chunk in range(chunks):
        rows = pl.ds(chunk * SIZE, SIZE)
        inv_out[rows, :] = jnp.broadcast_to(inv[chunk : chunk + 1], (SIZE, SIZE)).T
        coef_out[rows, :] = jnp.broadcast_to(coef[chunk : chunk + 1], (SIZE, SIZE)).T


def mixed_grad_of(consts, cols, upstream, value, inv, coef):
    return (inv * (upstream * consts[pl.ds(GAIN, 1), cols]) - value * coef).astype(BF16)


def back_sum_kernel(mine, channels, consts, received, mixed, cotangent, queries, sums, inv, coef):
    length = queries.shape[0]
    token_scales(received, channels, inv, coef)
    for slot, cols in enumerate(heads_of(mine, queries.shape[1] // SIZE)):
        upstream = cotangent[:, cols].astype(F32)
        value = mixed[:, cols]
        mixed_grad = mixed_grad_of(consts, cols, upstream, value, inv[...], coef[...])
        scaled = mixed_grad.astype(F32) * head_in_of(consts[pl.ds(RATE, 1), cols], length)
        sums[slot, pl.ds(0, SIZE), :] = dot_split(queries[:, cols], scaled, 0, 0)
        gain_grad = jnp.sum(upstream * (value * inv[...]), axis=0, keepdims=True)
        sums[slot, pl.ds(SIZE, EXTRA), :] = jnp.broadcast_to(gain_grad, (EXTRA, SIZE))


def grads_kernel(
    channels, consts, received, mixed_in, cotangent, queries, keys, values, mine, other,
    attended_out, query_out, key_out, value_out, token,
    inv, coef, mixed, grad, attended, query_grad, key_part, value_part, arrived, sent,
):
    length = queries.shape[0]
    heads = queries.shape[1] // SIZE
    half = length // 2
    first, second = pl.ds(0, half), pl.ds(half, half)
    copies, stores = [], []
    for h in range(heads):
        copies.append(pltpu.make_async_copy(mixed_in.at[:, column(h)], mixed.at[:, column(h)], arrived.at[h]))
        copies[-1].start()
    token[...] = jnp.zeros_like(token)
    token_scales(received, channels, inv, coef)
    core = lax.axis_index("seq") % 2
    for h in range(heads):
        cols = column(h)
        slot = h % (heads // 2)
        rate = consts[pl.ds(RATE, 1), cols]
        state_in = jnp.where(core == h // (heads // 2), mine[slot], other[slot])
        same, across = tile_weights(rate, False)
        same_turned, across_turned = tile_weights(rate, True)
        copies[h].wait()
        value = mixed[:, cols]
        attended[:, cols] = (value * inv[...] * consts[pl.ds(GAIN, 1), cols]).astype(BF16)
        grad[:, cols] = mixed_grad_of(consts, cols, cotangent[:, cols].astype(F32), value, inv[...], coef[...])
        q, k, v, g = (ref.at[:, cols] for ref in (queries, keys, values, grad))
        state_part = head_in_of(rate, length) * dot_split(g[...], state_in, 1, 1)
        query_grad[first, cols] = (
            dot(weighted(g, v, first, first, same), k[first, :], 1, 0) + state_part[:half]
        ).astype(BF16)
        query_grad[second, cols] = (
            dot(weighted(g, v, second, first, across), k[first, :], 1, 0)
            + dot(weighted(g, v, second, second, same), k[second, :], 1, 0)
            + state_part[half:]
        ).astype(BF16)
        key_part[first, cols] = dot(weighted(v, g, first, first, same_turned), q[first, :], 1, 0) + dot(
            weighted(v, g, first, second, across_turned), q[second, :], 1, 0
        )
        key_part[second, cols] = dot(weighted(v, g, second, second, same_turned), q[second, :], 1, 0)
        value_part[first, cols] = dot(weighted(k, q, first, first, same_turned), g[first, :], 1, 0) + dot(
            weighted(k, q, first, second, across_turned), g[second, :], 1, 0
        )
        value_part[second, cols] = dot(weighted(k, q, second, second, same_turned), g[second, :], 1, 0)
        targets = ((attended, attended_out), (query_grad, query_out), (key_part, key_out), (value_part, value_out))
        for i, (rows, target) in enumerate(targets):
            stores.append(pltpu.make_async_copy(rows.at[:, cols], target.at[:, cols], sent.at[4 * h + i]))
            stores[-1].start()
    for store in stores:
        store.wait()


def finish_kernel(
    mine, consts, back, keys, values, key_part, value_part, *refs
):
    key_grad, value_grad, key_rows, value_rows, sent = refs[-5:]
    length = keys.shape[0]
    copies = []
    for slot, cols in enumerate(heads_of(mine, keys.shape[1] // SIZE)):
        back_in = back[slot, pl.ds(0, SIZE), :]
        tail = tail_out_of(consts[pl.ds(RATE, 1), cols], length)
        to = column(slot)
        key_rows[:, to] = (key_part[:, cols] + tail * dot_split(values[:, cols], back_in, 1, 1)).astype(BF16)
        value_rows[:, to] = (value_part[:, cols] + tail * dot_split(keys[:, cols], back_in, 1, 0)).astype(BF16)
        for i, (rows, target) in enumerate(((key_rows, key_grad), (value_rows, value_grad))):
            copies.append(pltpu.make_async_copy(rows.at[:, to], target.at[:, cols], sent.at[2 * slot + i]))
            copies[-1].start()
    for copy in copies:
        copy.wait()


def gain_kernel(mine, other, out):
    heads = out.shape[1] // SIZE
    core = lax.axis_index("seq") % 2
    for h in range(heads):
        slot = h % (heads // 2)
        rows = pl.ds(SIZE, 1)
        out[:, column(h)] = jnp.where(core == h // (heads // 2), mine[slot, rows, :], other[slot, rows, :])


def is_first(reverse):
    return (lax.axis_index("seq") % 2) == (1 if reverse else 0)


def chip_sum_kernel(length, reverse, consts, keep, received, out):
    first = is_first(reverse)
    half = SIZE // 2
    extra = keep.shape[1] - SIZE
    for slot, cols in enumerate(heads_of(True, consts.shape[1] // SIZE)):
        factor = jnp.exp(-consts[pl.ds(RATE, 1), cols] * length)
        own, other = keep[slot, pl.ds(0, SIZE), :], received[slot, pl.ds(0, SIZE), :]
        total = jnp.where(first, factor * own + other, factor * other + own)
        for i in range(2):
            out[2 * slot + i, pl.ds(0, half), :] = total[i * half : (i + 1) * half]
            if extra:
                out[2 * slot + i, pl.ds(half, extra), :] = keep[slot, pl.ds(SIZE, extra), :] + received[slot, pl.ds(SIZE, extra), :]


def shard_factors(consts, length):
    position = lax.axis_index("seq")
    heads = consts.shape[1] // SIZE
    head = position % 2 * (heads // 2) + position // 2 % CHIPS * (heads // 2) // CHIPS
    rate = consts[pl.ds(RATE, 1), pl.ds(pl.multiple_of(head * SIZE, SIZE), SIZE)]
    return jnp.exp(-rate * (2 * length)), jnp.exp(-rate * (2 * length * CHIPS))


def chip_order(reverse):
    return range(CHIPS - 1, -1, -1) if reverse else range(CHIPS)


def totals_kernel(length, reverse, consts, parts, token, out):
    factor, _ = shard_factors(consts, length)
    rows = SIZE // 2
    total = jnp.zeros((rows, SIZE), F32)
    for k in chip_order(reverse):
        total = factor * total + parts[k, :rows]
    out[:rows] = total
    if parts.shape[1] > rows:
        out[rows:] = sum(parts[k, rows:] for k in range(CHIPS))


def fold_forward_kernel(length, consts, parts, nearest, near, far, token, out):
    factor, group_factor = shard_factors(consts, length)
    carry = nearest[...] + group_factor * (near[...] + group_factor * far[...])
    for k in chip_order(False):
        out[k] = carry
        carry = factor * carry + parts[k]


def fold_back_kernel(length, consts, parts, arrived, out):
    factor, group_factor = shard_factors(consts, length)
    rows = SIZE // 2
    group = lax.axis_index("seq") // (2 * CHIPS)
    carry = jnp.zeros((rows, SIZE), F32)
    for g in range(arrived.shape[0] - 1, 0, -1):
        carry = jnp.where(group < g, group_factor * carry + arrived[g, :rows], carry)
    extra = sum(arrived[g, rows:] for g in range(arrived.shape[0]))
    for k in chip_order(True):
        out[k, :rows] = carry
        out[k, rows:] = extra
        carry = factor * carry + parts[k, :rows]


def states_kernel(length, reverse, consts, shards, keep, received, mine, give):
    first = is_first(reverse)
    half = SIZE // 2
    extra = keep.shape[1] - SIZE
    rows = pl.ds(0, SIZE)
    for slot, cols in enumerate(heads_of(True, consts.shape[1] // SIZE)):
        factor = jnp.exp(-consts[pl.ds(RATE, 1), cols] * length)
        before = shards[pl.ds(2 * slot, 2), pl.ds(0, half), :].reshape(SIZE, SIZE)
        after = factor * before + jnp.where(first, keep[slot, rows, :], received[slot, rows, :])
        mine[slot, rows, :] = jnp.where(first, before, after)
        give[slot, rows, :] = jnp.where(first, after, before)
        if extra:
            total = shards[2 * slot, pl.ds(half, extra), :]
            mine[slot, pl.ds(SIZE, extra), :] = total
            give[slot, pl.ds(SIZE, extra), :] = total


def like(x):
    return jax.ShapeDtypeStruct(x.shape, x.dtype)


def array(kind, *shape):
    return jax.ShapeDtypeStruct(shape, kind)


def whole_call(kernel, out_shape, operands, in_specs=None, out_specs=None, **rest):
    vmem = pl.BlockSpec(memory_space=pltpu.VMEM)
    return pl.pallas_call(
        kernel,
        in_specs=in_specs or [vmem] * len(operands),
        out_specs=out_specs or jax.tree.map(lambda _: vmem, out_shape),
        out_shape=out_shape,
        compiler_params=pltpu.CompilerParams(vmem_limit_bytes=VMEM_LIMIT),
        **rest,
    )(*operands)


def swap(x):
    return lax.ppermute(x, "seq", [(i, i ^ 1) for i in range(lax.axis_size("seq"))])


def exchange(x):
    groups = lax.axis_size("seq") // (2 * CHIPS)
    members = [[2 * (g * CHIPS + c) + core for c in range(CHIPS)] for g in range(groups) for core in range(2)]
    return lax.all_to_all(x, "seq", 0, 0, axis_index_groups=members)


def onward(x, by):
    count, step = lax.axis_size("seq"), by * 2 * CHIPS
    return lax.ppermute(x, "seq", [(i, i + step) for i in range(count - step)])


def among_groups(x):
    groups = lax.axis_size("seq") // (2 * CHIPS)
    return lax.all_gather(
        x, "seq", axis_index_groups=[[g * 2 * CHIPS + j for g in range(groups)] for j in range(2 * CHIPS)]
    )


def body(queries, keys, values, rates, gain, cotangent):
    length, channels = queries.shape
    heads = rates.shape[0]
    head_devices = lax.axis_size("head")
    total_channels = channels * head_devices

    anywhere = pl.BlockSpec(memory_space=pl.ANY)
    in_vmem = pl.BlockSpec(memory_space=pltpu.VMEM)
    hbm = lambda x: pltpu.with_memory_space_constraint(x, pltpu.HBM)
    vmem = lambda x: pltpu.with_memory_space_constraint(x, pltpu.VMEM)
    wide = array(F32, length, channels)
    narrow = array(BF16, length, channels)
    scratch = pltpu.VMEM((length, SIZE), F32)
    half_rows = pltpu.VMEM((length, channels // 2), BF16)
    rows = pltpu.VMEM((length, channels), BF16)
    wide_rows = pltpu.VMEM((length, channels), F32)
    dma = pltpu.SemaphoreType.DMA
    token_shape = array(F32, 8, SIZE)
    states_shape = array(F32, heads // 2, SIZE, SIZE)
    shards = (CHIPS, SIZE // 2, SIZE)
    square = 2 * heads * length * length * SIZE

    def cost(flops):
        return pl.CostEstimate(flops=flops, bytes_accessed=6 << 20, transcendentals=0)

    other_sums, consts = whole_call(
        first_sums_kernel, [states_shape, array(F32, 8, channels)],
        [hbm(rates), hbm(gain.reshape(1, channels)), hbm(keys), hbm(values)], in_specs=[anywhere] * 4,
        scratch_shapes=[pltpu.SMEM((heads,), F32), pltpu.VMEM((1, channels), F32), half_rows, half_rows, dma((heads + 2,))],
    )
    received = swap(other_sums)
    keep = whole_call(own_sums_kernel, states_shape, [consts, keys, values])
    sums = whole_call(
        lambda *refs: chip_sum_kernel(length, False, *refs), array(F32, *shards), [consts, keep, received]
    )
    parts = exchange(sums)
    total = whole_call(
        lambda *refs: totals_kernel(length, False, *refs), array(F32, *shards[1:]), [consts, parts, consts]
    )
    intra, token = whole_call(
        intra_kernel, [wide, token_shape], [consts, queries, keys, values, total], cost_estimate=cost(2 * square)
    )
    near = onward(total, 2)
    nearest, far = onward(total, 1), onward(total, 3)
    folded = whole_call(
        lambda *refs: fold_forward_kernel(length, *refs), array(F32, *shards),
        [consts, parts, nearest, near, far, token],
    )
    mine, give = whole_call(
        lambda *refs: states_kernel(length, False, *refs), [states_shape, states_shape],
        [consts, exchange(folded), keep, received],
    )
    other = swap(give)
    stats_shape = (head_devices, 2 * length // SIZE, SIZE)
    mixed, stats = whole_call(
        mixed_kernel, [wide, array(F32, *stats_shape)],
        [consts, queries, mine, other, intra, cotangent], scratch_shapes=[scratch, scratch],
    )
    stats = lax.all_to_all(stats, "head", 0, 0)

    sums_shape = array(F32, heads // 2, SIZE + EXTRA, SIZE)
    shards = (CHIPS, SIZE // 2 + EXTRA, SIZE)

    def back_sums(mine):
        return whole_call(
            lambda *refs: back_sum_kernel(mine, total_channels, *refs), sums_shape,
            [consts, stats, mixed, cotangent, queries], scratch_shapes=[scratch, scratch],
        )

    received = swap(back_sums(False))
    keep = back_sums(True)
    sums = whole_call(
        lambda *refs: chip_sum_kernel(length, True, *refs), array(F32, *shards), [consts, keep, received]
    )
    parts = exchange(sums)
    part = pltpu.HBM((length, channels), F32)
    attended, query_grad, key_part, value_part, token = whole_call(
        lambda *refs: grads_kernel(total_channels, *refs), [narrow, narrow, part, part, token_shape],
        [consts, stats, hbm(mixed), cotangent, queries, keys, values, mine, other],
        in_specs=[in_vmem, in_vmem, anywhere] + [in_vmem] * 6, out_specs=[anywhere] * 4 + [in_vmem],
        scratch_shapes=[scratch, scratch, wide_rows, rows, rows, rows, wide_rows, wide_rows, dma((heads,)), dma((4 * heads,))],
        cost_estimate=cost(6 * square),
    )
    total = whole_call(
        lambda *refs: totals_kernel(length, True, *refs), array(F32, *shards[1:]), [consts, parts, token]
    )
    folded = whole_call(
        lambda *refs: fold_back_kernel(length, *refs), array(F32, *shards), [consts, parts, among_groups(total)]
    )
    mine, give = whole_call(
        lambda *refs: states_kernel(length, True, *refs), [sums_shape, sums_shape],
        [consts, exchange(folded), keep, received],
    )
    other = swap(give)

    def finish(is_mine, back, *begun):
        return whole_call(
            lambda *refs: finish_kernel(is_mine, *refs), [narrow, narrow],
            [consts, back, keys, values, vmem(key_part), vmem(value_part), *begun],
            in_specs=[in_vmem] * 6 + [anywhere] * len(begun), out_specs=[anywhere] * 2,
            scratch_shapes=[half_rows, half_rows, dma((heads,))],
            input_output_aliases={6: 0, 7: 1} if begun else {},
        )

    key_grad, value_grad = finish(False, other, *finish(True, mine))
    gain_grad = whole_call(gain_kernel, array(F32, 1, channels), [mine, other])
    return attended, query_grad, key_grad, value_grad, gain_grad.reshape(channels)


def solution(mesh):
    placed = (
        P("seq", "head"),
        P("seq", "head"),
        P("seq", "head"),
        P("head"),
        P("head"),
        P("seq", "head"),
    )
    return jax.shard_map(
        body,
        mesh=mesh,
        in_specs=placed,
        out_specs=(
            P("seq", "head"),
            P("seq", "head"),
            P("seq", "head"),
            P("seq", "head"),
            P("head"),
        ),
        check_vma=False,
    )
```

time: 337 us -> 121 us (0.36)
  blocking collectives: 178 us -> 56.6 us
  other arithmetic: 70.3 us -> 0 us
  starting transfers between devices: 0.08 us -> 43.3 us
  waiting for transfers between devices: 31.5 us -> 1.98 us
  matrix products: 21.3 us -> 0 us
  Pallas kernels: 0 us -> 16.4 us
  between operations: 15 us -> 0.97 us
  local copies, waits for them, and re-layouts: 15.3 us -> 1.28 us
    psum x3 -> x0, blocking collectives: 124 us -> none  [the longest x1 62.2 us: body(): lax.psum(jnp.sum(upstream * normed, axis=0).reshape(channels), 'seq')]
    select_n x64 -> x0, other arithmetic: 67.6 us -> none  [lap(): return jax.tree.map(lambda a, b: jnp.where(reached, a, b), new, before)]
    unnamed x1 -> x0, blocking collectives: 54.7 us -> none
    ppermute x0 -> x7, starting transfers between devices: none -> 39.9 us  [the longest x4 24.3 us: swap(): lax.ppermute(x, 'seq', [(i, i ^ 1) for i in range(lax.axis_size('seq'))])]
    all_to_all x0 -> x4, blocking collectives: none -> 38.5 us  [the longest x3 25.4 us: exchange(): return lax.all_to_all(x, 'seq', 0, 0, axis_index_groups=members)]
    all_gather x2 -> x0, waiting for transfers between devices: 31.5 us -> none  [carried_in(): everything = jax.tree.map(lambda part: lax.all_gather(part, axis), x)]
    dot_general x12 -> x0, matrix products: 21.3 us -> none  [the longest x1 2.83 us: body(): jnp.einsum('the,she->hts', mixed_grad, value_rows, preferred_element_type...]
    all_gather x0 -> x1, blocking collectives: none -> 18.2 us  [among_groups(): lax.all_gather(x, 'seq', axis_index_groups=[[g * 2 * CHIPS + j for g in r...]
  transfers between devices with their start and end apart: 2 -> 8, of which waited for: 2 -> 3; matrix products, arithmetic and copies ran while one was open for 6% -> 0% of each run, Pallas kernels for 0% -> 9%
where the time goes in v8:
time: 121 us
  blocking collectives  56.6 us (47%)
  starting transfers between devices  43.3 us (36%)
  Pallas kernels  16.4 us (14%)
  waiting for transfers between devices  1.98 us (2%)
  local copies, waits for them, and re-layouts  1.28 us (1%)
    all_to_all x3, blocking collectives, exchange(): return lax.all_to_all(x, 'seq', 0, 0, axis_index_groups=members)  25.4 us
    ppermute x4, starting transfers between devices, swap(): lax.ppermute(x, 'seq', [(i, i ^ 1) for i in range(lax.axis_size('seq'))])  24.3 us
    all_gather x1, blocking collectives, among_groups(): lax.all_gather(x, 'seq', axis_index_groups=[[g * 2 * CHIPS + j for g in r...  18.2 us
    pallas_call x18, Pallas kernels, whole_call(): pl.pallas_call(kernel, in_specs=in_specs or [vmem] * len(operands), out_s...  16.4 us
    ppermute x3, starting transfers between devices, onward(): return lax.ppermute(x, 'seq', [(i, i + step) for i in range(count - step)])  15.6 us
    all_to_all x1, blocking collectives, body(): stats = lax.all_to_all(stats, 'head', 0, 0)  13.1 us
    all_to_all x1, starting transfers between devices, exchange(): return lax.all_to_all(x, 'seq', 0, 0, axis_index_groups=members)  3.47 us
  transfers between devices with their start and end apart: 8, of which 3 were waited for; matrix products, arithmetic and copies ran while one was open for 0% of the time, Pallas kernels for 9%

profile of v8, /device:TPU:1, one launch (start us, length us, event | category | flops | bytes accessed | tf_op | source)
XLA Modules:
  0.0 120.6 jit_solution(2195554965397261840)
XLA Ops:
  0.7 1.6 %shard_map.101 = (f32[2,128,128]{2,1,0:T(8,128)S(1)}, f32[8,512]{1,0:T(8,128)S(1)}) custom-call(f32[4]{0:T(128)} %rates_in.1, f32[1,512]{1,0:T(1,128)} %bitcast.4, bf16[512,512]{1,0:T(8,128)(2,1)} %refs_2_.3, bf16[512,512]{1,0:T(8,128)(2,1)} %refs_3_.9), custom_call_target="tpu_custom_call" | custom-call | tf_op jit(solution)/shard_map/pallas_call | solution.py:359
  2.3 8.8 %collective-permute-start = (f32[2,128,128]{2,1,0:T(8,128)S(1)}, f32[2,128,128]{2,1,0:T(8,128)S(1)}, u32[]{:S(2)}, u32[]{:S(2)}) collective-permute-start(f32[2,128,128]{2,1,0:T(8,128)S(1)} %get-tuple-element.25), channel_id=1, source_target_pairs={{0,16},{16,0},{32,48},{48,32},{64,80},{80,64},{96,112},{112,96},{1... | collective-permute-start | bytes 393224 | tf_op jit(solution)/shard_map/ppermute | solution.py:370
  11.5 0.6 collective-permute-done.refs_2_.refs_3_
  12.1 7.3 %all_to_all.25.refs_1_ = f32[4,64,128]{2,1,0:T(8,128)S(1)} all-to-all(f32[4,64,128]{2,1,0:T(8,128)S(1)} %shard_map.103), channel_id=1, replica_groups={{0,32,64,96},{16,48,80,112},{128,160,192,224},{144,176,208,240},{256,28..., dimensions={0} | all-to-all | bytes 262144 | tf_op jit(solution)/shard_map/all_to_all | solution.py:376
  19.4 7.3 %collective-permute-start.3 = (f32[64,128]{1,0:T(8,128)S(1)}, f32[64,128]{1,0:T(8,128)S(1)}, u32[]{:S(2)}, u32[]{:S(2)}) collective-permute-start(f32[64,128]{1,0:T(8,128)S(1)} %shard_map.104.token_in), channel_id=1, source_target_pairs={{0,384},{16,400},{32,416},{48,432},{64,448},{80,464},{96,480},{112... | collective-permute-start | bytes 98312 | tf_op jit(solution)/shard_map/ppermute | solution.py:381
  26.7 3.7 %collective-permute-start.2 = (f32[64,128]{1,0:T(8,128)S(1)}, f32[64,128]{1,0:T(8,128)S(1)}, u32[]{:S(2)}, u32[]{:S(2)}) collective-permute-start(f32[64,128]{1,0:T(8,128)S(1)} %shard_map.104.token_in), channel_id=1, source_target_pairs={{0,256},{16,272},{32,288},{48,304},{64,320},{80,336},{96,352},{112... | collective-permute-start | bytes 98312 | tf_op jit(solution)/shard_map/ppermute | solution.py:381
  30.4 4.6 %collective-permute-start.1 = (f32[64,128]{1,0:T(8,128)S(1)}, f32[64,128]{1,0:T(8,128)S(1)}, u32[]{:S(2)}, u32[]{:S(2)}) collective-permute-start(f32[64,128]{1,0:T(8,128)S(1)} %shard_map.104.token_in), channel_id=1, source_target_pairs={{0,128},{16,144},{32,160},{48,176},{64,192},{80,208},{96,224},{112... | collective-permute-start | bytes 98312 | tf_op jit(solution)/shard_map/ppermute | solution.py:381
  35.0 1.7 %shard_map.105 = (f32[512,512]{1,0:T(8,128)S(1)}, f32[8,128]{1,0:T(8,128)S(1)}) custom-call(f32[8,512]{1,0:T(8,128)S(1)} %get-tuple-element.24.consts.refs_0_.refs_2_, bf16[512,512]{1,0:T(8,128)(2,1)S(1)} %copy-done.2, bf16[512,512]{1,0:T(8,128)(2,1)S(1)} %copy-done, bf16[512,512]{1,0:T(8,128)(2,1)S(1)} %copy-done.1, f32[64,128]{1,0:T(8,128)S(1)} %shard_map.104.token_in), custom_call_target="tpu_custom_call" | custom-call | flops 536870912 | bytes 6291456 | tf_op jit(solution)/shard_map/pallas_call | solution.py:359
  36.8 8.3 %all_to_all.26.refs_1_ = f32[4,64,128]{2,1,0:T(8,128)S(1)} all-to-all(f32[4,64,128]{2,1,0:T(8,128)S(1)} %shard_map.106), channel_id=1, replica_groups={{0,32,64,96},{16,48,80,112},{128,160,192,224},{144,176,208,240},{256,28..., dimensions={0} | all-to-all | bytes 262144 | tf_op jit(solution)/shard_map/all_to_all | solution.py:376
  45.2 5.0 %collective-permute-start.4 = (f32[2,128,128]{2,1,0:T(8,128)S(1)}, f32[2,128,128]{2,1,0:T(8,128)S(1)}, u32[]{:S(2)}, u32[]{:S(2)}) collective-permute-start(f32[2,128,128]{2,1,0:T(8,128)S(1)} %get-tuple-element.28), channel_id=1, source_target_pairs={{0,16},{16,0},{32,48},{48,32},{64,80},{80,64},{96,112},{112,96},{1... | collective-permute-start | bytes 393224 | tf_op jit(solution)/shard_map/ppermute | solution.py:370
  50.2 1.0 collective-permute-done.4.other.refs_8_
  51.1 0.6 shard_map.108
  51.8 13.1 %all_to_all.27.refs_1_ = f32[16,8,128]{2,1,0:T(8,128)S(1)} all-to-all(f32[16,8,128]{2,1,0:T(8,128)S(1)} %get-tuple-element.30), channel_id=1, replica_groups=mesh['seq'=32,'head'=16] {'head'}, dimensions={0} | all-to-all | bytes 131072 | tf_op jit(solution)/shard_map/all_to_all | solution.py:449
  65.4 3.7 %collective-permute-start.5 = (f32[2,136,128]{2,1,0:T(8,128)S(1)}, f32[2,136,128]{2,1,0:T(8,128)S(1)}, u32[]{:S(2)}, u32[]{:S(2)}) collective-permute-start(f32[2,136,128]{2,1,0:T(8,128)S(1)} %shard_map.111), channel_id=1, source_target_pairs={{0,16},{16,0},{32,48},{48,32},{64,80},{80,64},{96,112},{112,96},{1... | collective-permute-start | bytes 417800 | tf_op jit(solution)/shard_map/ppermute | solution.py:370
  70.1 0.7 shard_map.112
  70.8 3.5 %all-to-all-start.3 = ((f32[4,72,128]{2,1,0:T(8,128)}), f32[4,72,128]{2,1,0:T(8,128)S(1)}, u32[]{:S(2)}, u32[]{:S(2)}) async-start(f32[4,72,128]{2,1,0:T(8,128)} %shard_map.112), calls=%async_computation.3 | async-start | bytes 294912 | tf_op jit(solution)/shard_map/all_to_all | solution.py:376
  74.3 7.2 %shard_map.109 = (bf16[512,512]{1,0:T(8,128)(2,1)}, bf16[512,512]{1,0:T(8,128)(2,1)}, f32[512,512]{1,0:T(8,128)}, f32[512,512]{1,0:T(8,128)}, f32[8,128]{1,0:T(8,128)S(1)}) custom-call(f32[8,512]{1,0:T(8,128)S(1)} %get-tuple-element.24.consts.refs_0_.refs_2_, f32[16,8,128]{2,1,0:T(8,128)S(1)} %all_to_all.27.refs_1_, f32[512,512]{1,0:T(8,128)} %copy-done.7, ...), custom_call_target="tpu_custom_call" | custom-call | flops 1610612736 | bytes 6291456 | tf_op jit(solution)/shard_map/pallas_call | solution.py:359
  81.6 18.2 %all-gather = f32[288,128]{1,0:T(8,128)S(1)} all-gather(f32[72,128]{1,0:T(8,128)S(1)} %shard_map.113), channel_id=2, replica_groups={{0,128,256,384},{16,144,272,400},{32,160,288,416},{48,176,304,432},{64,..., dimensions={0}, use_global_device_ids=true | all-gather | bytes 184320 | tf_op jit(solution)/shard_map/all_gather | solution.py:386
  99.8 9.8 %all_to_all.28.refs_1_ = f32[4,72,128]{2,1,0:T(8,128)S(1)} all-to-all(f32[4,72,128]{2,1,0:T(8,128)S(1)} %shard_map.114), channel_id=1, replica_groups={{0,32,64,96},{16,48,80,112},{128,160,192,224},{144,176,208,240},{256,28..., dimensions={0} | all-to-all | bytes 294912 | tf_op jit(solution)/shard_map/all_to_all | solution.py:376
  109.7 6.8 %collective-permute-start.6 = (f32[2,136,128]{2,1,0:T(8,128)S(1)}, f32[2,136,128]{2,1,0:T(8,128)S(1)}, u32[]{:S(2)}, u32[]{:S(2)}) collective-permute-start(f32[2,136,128]{2,1,0:T(8,128)S(1)} %get-tuple-element.35), channel_id=1, source_target_pairs={{0,16},{16,0},{32,48},{48,32},{64,80},{80,64},{96,112},{112,96},{1... | collective-permute-start | bytes 417800 | tf_op jit(solution)/shard_map/ppermute | solution.py:370
  116.5 1.2 %copy-done.5 = f32[512,512]{1,0:T(8,128)S(1)} copy-done((f32[512,512]{1,0:T(8,128)S(1)}, f32[512,512]{1,0:T(8,128)}, u32[]{:S(2)}) %copy-start.5) | copy-done | bytes 1048600
  117.7 1.2 shard_map.116
  118.9 0.6 shard_map.118
  119.5 1.2 shard_map.117
  (39 shorter events, 2.2 us)
Async XLA Ops:
  0.6 10.5 %copy-start = (bf16[512,512]{1,0:T(8,128)(2,1)S(1)}, bf16[512,512]{1,0:T(8,128)(2,1)}, u32[]{:S(2)}) copy-start(bf16[512,512]{1,0:T(8,128)(2,1)} %refs_2_.3) | copy-start | bytes 1572868
  0.6 10.5 %copy-start.1 = (bf16[512,512]{1,0:T(8,128)(2,1)S(1)}, bf16[512,512]{1,0:T(8,128)(2,1)}, u32[]{:S(2)}) copy-start(bf16[512,512]{1,0:T(8,128)(2,1)} %refs_3_.9) | copy-start | bytes 1572868
  2.3 9.8 %collective-permute-start = (f32[2,128,128]{2,1,0:T(8,128)S(1)}, f32[2,128,128]{2,1,0:T(8,128)S(1)}, u32[]{:S(2)}, u32[]{:S(2)}) collective-permute-start(f32[2,128,128]{2,1,0:T(8,128)S(1)} %get-tuple-element.25), channel_id=1, source_target_pairs={{0,16},{16,0},{32,48},{48,32},{64,80},{80,64},{96,112},{112,96},{1... | collective-permute-start | bytes 393224 | tf_op jit(solution)/shard_map/ppermute | solution.py:370
  11.4 23.6 %copy-start.2 = (bf16[512,512]{1,0:T(8,128)(2,1)S(1)}, bf16[512,512]{1,0:T(8,128)(2,1)}, u32[]{:S(2)}) copy-start(bf16[512,512]{1,0:T(8,128)(2,1)} %refs_4_.5) | copy-start | bytes 1572868
  19.4 17.3 %collective-permute-start.3 = (f32[64,128]{1,0:T(8,128)S(1)}, f32[64,128]{1,0:T(8,128)S(1)}, u32[]{:S(2)}, u32[]{:S(2)}) collective-permute-start(f32[64,128]{1,0:T(8,128)S(1)} %shard_map.104.token_in), channel_id=1, source_target_pairs={{0,384},{16,400},{32,416},{48,432},{64,448},{80,464},{96,480},{112... | collective-permute-start | bytes 98312 | tf_op jit(solution)/shard_map/ppermute | solution.py:381
  26.7 10.0 %collective-permute-start.2 = (f32[64,128]{1,0:T(8,128)S(1)}, f32[64,128]{1,0:T(8,128)S(1)}, u32[]{:S(2)}, u32[]{:S(2)}) collective-permute-start(f32[64,128]{1,0:T(8,128)S(1)} %shard_map.104.token_in), channel_id=1, source_target_pairs={{0,256},{16,272},{32,288},{48,304},{64,320},{80,336},{96,352},{112... | collective-permute-start | bytes 98312 | tf_op jit(solution)/shard_map/ppermute | solution.py:381
  30.4 6.4 %collective-permute-start.1 = (f32[64,128]{1,0:T(8,128)S(1)}, f32[64,128]{1,0:T(8,128)S(1)}, u32[]{:S(2)}, u32[]{:S(2)}) collective-permute-start(f32[64,128]{1,0:T(8,128)S(1)} %shard_map.104.token_in), channel_id=1, source_target_pairs={{0,128},{16,144},{32,160},{48,176},{64,192},{80,208},{96,224},{112... | collective-permute-start | bytes 98312 | tf_op jit(solution)/shard_map/ppermute | solution.py:381
  36.7 14.4 %copy-start.3 = (bf16[512,512]{1,0:T(8,128)(2,1)S(1)}, bf16[512,512]{1,0:T(8,128)(2,1)}, u32[]{:S(2)}) copy-start(bf16[512,512]{1,0:T(8,128)(2,1)} %refs_3_.7) | copy-start | bytes 1572868
  45.2 6.6 %copy-start.8 = (f32[2,128,128]{2,1,0:T(8,128)}, f32[2,128,128]{2,1,0:T(8,128)S(1)}, u32[]{:S(2)}) copy-start(f32[2,128,128]{2,1,0:T(8,128)S(1)} %get-tuple-element.27.mine.refs_7_) | copy-start | bytes 393220
  45.2 6.0 %collective-permute-start.4 = (f32[2,128,128]{2,1,0:T(8,128)S(1)}, f32[2,128,128]{2,1,0:T(8,128)S(1)}, u32[]{:S(2)}, u32[]{:S(2)}) collective-permute-start(f32[2,128,128]{2,1,0:T(8,128)S(1)} %get-tuple-element.28), channel_id=1, source_target_pairs={{0,16},{16,0},{32,48},{48,32},{64,80},{80,64},{96,112},{112,96},{1... | collective-permute-start | bytes 393224 | tf_op jit(solution)/shard_map/ppermute | solution.py:370
  51.1 0.7 copy-start.10
  51.8 17.3 %copy-start.7 = (f32[512,512]{1,0:T(8,128)}, f32[512,512]{1,0:T(8,128)S(1)}, u32[]{:S(2)}) copy-start(f32[512,512]{1,0:T(8,128)S(1)} %get-tuple-element.31.refs_2_) | copy-start | bytes 3145732
  65.4 4.7 %collective-permute-start.5 = (f32[2,136,128]{2,1,0:T(8,128)S(1)}, f32[2,136,128]{2,1,0:T(8,128)S(1)}, u32[]{:S(2)}, u32[]{:S(2)}) collective-permute-start(f32[2,136,128]{2,1,0:T(8,128)S(1)} %shard_map.111), channel_id=1, source_target_pairs={{0,16},{16,0},{32,48},{48,32},{64,80},{80,64},{96,112},{112,96},{1... | collective-permute-start | bytes 417800 | tf_op jit(solution)/shard_map/ppermute | solution.py:370
  70.8 3.5 %copy-start.9 = (f32[2,128,128]{2,1,0:T(8,128)S(1)}, f32[2,128,128]{2,1,0:T(8,128)}, u32[]{:S(2)}) copy-start(f32[2,128,128]{2,1,0:T(8,128)} %copy-done.8) | copy-start | bytes 393220
  70.8 3.5 %copy-start.11 = (f32[2,128,128]{2,1,0:T(8,128)S(1)}, f32[2,128,128]{2,1,0:T(8,128)}, u32[]{:S(2)}) copy-start(f32[2,128,128]{2,1,0:T(8,128)} %copy-done.10) | copy-start | bytes 393220
  70.8 10.7 %all-to-all-start.3 = ((f32[4,72,128]{2,1,0:T(8,128)}), f32[4,72,128]{2,1,0:T(8,128)S(1)}, u32[]{:S(2)}, u32[]{:S(2)}) async-start(f32[4,72,128]{2,1,0:T(8,128)} %shard_map.112), calls=%async_computation.3 | async-start | bytes 294912 | tf_op jit(solution)/shard_map/all_to_all | solution.py:376
  81.5 35.0 %copy-start.4 = (f32[512,512]{1,0:T(8,128)S(1)}, f32[512,512]{1,0:T(8,128)}, u32[]{:S(2)}) copy-start(f32[512,512]{1,0:T(8,128)} %get-tuple-element.36.refs_4_) | copy-start | bytes 3145732
  109.7 9.2 %collective-permute-start.6 = (f32[2,136,128]{2,1,0:T(8,128)S(1)}, f32[2,136,128]{2,1,0:T(8,128)S(1)}, u32[]{:S(2)}, u32[]{:S(2)}) collective-permute-start(f32[2,136,128]{2,1,0:T(8,128)S(1)} %get-tuple-element.35), channel_id=1, source_target_pairs={{0,16},{16,0},{32,48},{48,32},{64,80},{80,64},{96,112},{112,96},{1... | collective-permute-start | bytes 417800 | tf_op jit(solution)/shard_map/ppermute | solution.py:370
  116.5 1.2 %copy-start.5 = (f32[512,512]{1,0:T(8,128)S(1)}, f32[512,512]{1,0:T(8,128)}, u32[]{:S(2)}) copy-start(f32[512,512]{1,0:T(8,128)} %get-tuple-element.37.refs_5_) | copy-start | bytes 3145732
  117.7 1.8 %copy-start.6 = (f32[512,512]{1,0:T(8,128)S(1)}, f32[512,512]{1,0:T(8,128)}, u32[]{:S(2)}) copy-start(f32[512,512]{1,0:T(8,128)} %get-tuple-element.37.refs_5_) | copy-start | bytes 3145732

commit v9 on v8

--- a/solution.py
+++ b/solution.py
@@ -43,25 +43,18 @@
     return jnp.concatenate([base * jnp.exp(-rate * (length - SIZE - start)) for start in range(0, length, SIZE)], axis=0)
 
 
-def tile_weights(rate, turned):
+def tile_weights(rate):
     rows, lanes = rows_of(SIZE), lanes_of()
-    distance = lanes - rows if turned else rows - lanes
+    distance = rows - lanes
     near = jnp.where(distance >= 0, jnp.exp(-rate * jnp.maximum(distance, 0.0)), 0.0)
-    if turned:
-        far = jnp.exp(-rate * (SIZE - 1.0 - rows)) * jnp.exp(-rate * (lanes + 1.0))
-    else:
-        far = jnp.exp(-rate * (rows + 1.0)) * jnp.exp(-rate * (SIZE - 1.0 - lanes))
+    far = jnp.exp(-rate * (rows + 1.0)) * jnp.exp(-rate * (SIZE - 1.0 - lanes))
     step = jnp.exp(-rate * SIZE)
     farther = far * step
-    farthest = farther * step
-    none = jnp.zeros_like(near)
 
     def square(a, b, c, d):
         return jnp.concatenate([jnp.concatenate([a, b], axis=1), jnp.concatenate([c, d], axis=1)], axis=0)
 
-    if turned:
-        return square(near, far, none, near), square(farther, farthest, far, farther)
-    return square(near, none, far, near), square(farther, far, farthest, farther)
+    return square(near, jnp.zeros_like(near), far, near), square(farther, far, farther * step, farther)
 
 
 def weighted(a, b, rows_a, rows_b, weight):
@@ -124,7 +117,7 @@
     first, second = pl.ds(0, half), pl.ds(half, half)
     for h in range(queries.shape[1] // SIZE):
         cols = column(h)
-        same, across = tile_weights(consts[pl.ds(RATE, 1), cols], False)
+        same, across = tile_weights(consts[pl.ds(RATE, 1), cols])
         q, k, v = (ref.at[:, cols] for ref in (queries, keys, values))
         out[first, cols] = dot(weighted(q, k, first, first, same), v[first, :], 1, 0)
         out[second, cols] = dot(weighted(q, k, second, first, across), v[first, :], 1, 0) + dot(
@@ -186,9 +179,9 @@
 
 
 def grads_kernel(
-    channels, consts, received, mixed_in, cotangent, queries, keys, values, mine, other,
-    attended_out, query_out, key_out, value_out, token,
-    inv, coef, mixed, grad, attended, query_grad, key_part, value_part, arrived, sent,
+    channels, consts, received, mixed_in, cotangent, queries, keys, values, mine, other, totals,
+    attended_out, query_out, key_part, value_part, token,
+    inv, coef, mixed, grad, attended, query_grad, arrived, sent,
 ):
     length = queries.shape[0]
     heads = queries.shape[1] // SIZE
@@ -206,42 +199,43 @@
         slot = h % (heads // 2)
         rate = consts[pl.ds(RATE, 1), cols]
         state_in = jnp.where(core == h // (heads // 2), mine[slot], other[slot])
-        same, across = tile_weights(rate, False)
-        same_turned, across_turned = tile_weights(rate, True)
+        same, across = tile_weights(rate)
         copies[h].wait()
         value = mixed[:, cols]
         attended[:, cols] = (value * inv[...] * consts[pl.ds(GAIN, 1), cols]).astype(BF16)
         grad[:, cols] = mixed_grad_of(consts, cols, cotangent[:, cols].astype(F32), value, inv[...], coef[...])
         q, k, v, g = (ref.at[:, cols] for ref in (queries, keys, values, grad))
         state_part = head_in_of(rate, length) * dot_split(g[...], state_in, 1, 1)
-        query_grad[first, cols] = (
-            dot(weighted(g, v, first, first, same), k[first, :], 1, 0) + state_part[:half]
+        upper = weighted(g, v, first, first, same)
+        lower = weighted(g, v, second, first, across)
+        final = weighted(g, v, second, second, same)
+        query_grad[first, cols] = (dot(upper, k[first, :], 1, 0) + state_part[:half]).astype(BF16)
+        query_grad[second, cols] = (
+            dot(lower, k[first, :], 1, 0) + dot(final, k[second, :], 1, 0) + state_part[half:]
         ).astype(BF16)
-        query_grad[second, cols] = (
-            dot(weighted(g, v, second, first, across), k[first, :], 1, 0)
-            + dot(weighted(g, v, second, second, same), k[second, :], 1, 0)
-            + state_part[half:]
-        ).astype(BF16)
-        key_part[first, cols] = dot(weighted(v, g, first, first, same_turned), q[first, :], 1, 0) + dot(
-            weighted(v, g, first, second, across_turned), q[second, :], 1, 0
-        )
-        key_part[second, cols] = dot(weighted(v, g, second, second, same_turned), q[second, :], 1, 0)
-        value_part[first, cols] = dot(weighted(k, q, first, first, same_turned), g[first, :], 1, 0) + dot(
-            weighted(k, q, first, second, across_turned), g[second, :], 1, 0
-        )
-        value_part[second, cols] = dot(weighted(k, q, second, second, same_turned), g[second, :], 1, 0)
-        targets = ((attended, attended_out), (query_grad, query_out), (key_part, key_out), (value_part, value_out))
-        for i, (rows, target) in enumerate(targets):
-            stores.append(pltpu.make_async_copy(rows.at[:, cols], target.at[:, cols], sent.at[4 * h + i]))
+        for i, (rows, target) in enumerate(((attended, attended_out), (query_grad, query_out))):
+            stores.append(pltpu.make_async_copy(rows.at[:, cols], target.at[:, cols], sent.at[2 * h + i]))
             stores[-1].start()
+        key_part[first, cols] = dot(upper, q[first, :], 0, 0) + dot(lower, q[second, :], 0, 0)
+        key_part[second, cols] = dot(final, q[second, :], 0, 0)
+        upper = weighted(q, k, first, first, same)
+        lower = weighted(q, k, second, first, across)
+        final = weighted(q, k, second, second, same)
+        value_part[first, cols] = dot(upper, g[first, :], 0, 0) + dot(lower, g[second, :], 0, 0)
+        value_part[second, cols] = dot(final, g[second, :], 0, 0)
     for store in stores:
         store.wait()
 
 
-def finish_kernel(
-    mine, consts, back, keys, values, key_part, value_part, *refs
-):
-    key_grad, value_grad, key_rows, value_rows, sent = refs[-5:]
+def finish_kernel(mine, consts, back, keys, values, key_part, value_part, *refs):
+    key_grad, value_grad, gain_grad, key_rows, value_rows, sent = refs[-6:]
+    half = keys.shape[1] // SIZE // 2
+    if mine:
+        gain_grad[...] = jnp.zeros_like(gain_grad)
+    else:
+        for states, heads in ((refs[0], heads_of(True, 2 * half)), (back, heads_of(False, 2 * half))):
+            for slot, cols in enumerate(heads):
+                gain_grad[:, cols] = states[slot, pl.ds(SIZE, 1), :]
     length = keys.shape[0]
     copies = []
     for slot, cols in enumerate(heads_of(mine, keys.shape[1] // SIZE)):
@@ -257,15 +251,6 @@
         copy.wait()
 
 
-def gain_kernel(mine, other, out):
-    heads = out.shape[1] // SIZE
-    core = lax.axis_index("seq") % 2
-    for h in range(heads):
-        slot = h % (heads // 2)
-        rows = pl.ds(SIZE, 1)
-        out[:, column(h)] = jnp.where(core == h // (heads // 2), mine[slot, rows, :], other[slot, rows, :])
-
-
 def is_first(reverse):
     return (lax.axis_index("seq") % 2) == (1 if reverse else 0)
 
@@ -296,15 +281,19 @@
     return range(CHIPS - 1, -1, -1) if reverse else range(CHIPS)
 
 
-def totals_kernel(length, reverse, consts, parts, token, out):
+def totals_kernel(length, reverse, consts, parts, out):
     factor, _ = shard_factors(consts, length)
     rows = SIZE // 2
     total = jnp.zeros((rows, SIZE), F32)
     for k in chip_order(reverse):
         total = factor * total + parts[k, :rows]
-    out[:rows] = total
-    if parts.shape[1] > rows:
-        out[rows:] = sum(parts[k, rows:] for k in range(CHIPS))
+    if parts.shape[1] == rows:
+        out[...] = total
+        return
+    extra = sum(parts[k, rows:] for k in range(CHIPS))
+    for g in range(out.shape[0]):
+        out[g, :rows] = total
+        out[g, rows:] = extra
 
 
 def fold_forward_kernel(length, consts, parts, nearest, near, far, token, out):
@@ -315,7 +304,7 @@
         carry = factor * carry + parts[k]
 
 
-def fold_back_kernel(length, consts, parts, arrived, out):
+def fold_back_kernel(length, consts, parts, arrived, token, out):
     factor, group_factor = shard_factors(consts, length)
     rows = SIZE // 2
     group = lax.axis_index("seq") // (2 * CHIPS)
@@ -383,9 +372,8 @@
 
 def among_groups(x):
     groups = lax.axis_size("seq") // (2 * CHIPS)
-    return lax.all_gather(
-        x, "seq", axis_index_groups=[[g * 2 * CHIPS + j for g in range(groups)] for j in range(2 * CHIPS)]
-    )
+    members = [[g * 2 * CHIPS + j for g in range(groups)] for j in range(2 * CHIPS)]
+    return lax.all_to_all(x, "seq", 0, 0, axis_index_groups=members)
 
 
 def body(queries, keys, values, rates, gain, cotangent):
@@ -425,7 +413,7 @@
     )
     parts = exchange(sums)
     total = whole_call(
-        lambda *refs: totals_kernel(length, False, *refs), array(F32, *shards[1:]), [consts, parts, consts]
+        lambda *refs: totals_kernel(length, False, *refs), array(F32, *shards[1:]), [consts, parts]
     )
     intra, token = whole_call(
         intra_kernel, [wide, token_shape], [consts, queries, keys, values, total], cost_estimate=cost(2 * square)
@@ -463,19 +451,22 @@
         lambda *refs: chip_sum_kernel(length, True, *refs), array(F32, *shards), [consts, keep, received]
     )
     parts = exchange(sums)
-    part = pltpu.HBM((length, channels), F32)
+    groups = lax.axis_size("seq") // (2 * CHIPS)
+    totals = whole_call(
+        lambda *refs: totals_kernel(length, True, *refs), array(F32, groups, *shards[1:]), [consts, parts]
+    )
+    part = pltpu.VMEM((length, channels), F32)
     attended, query_grad, key_part, value_part, token = whole_call(
         lambda *refs: grads_kernel(total_channels, *refs), [narrow, narrow, part, part, token_shape],
-        [consts, stats, hbm(mixed), cotangent, queries, keys, values, mine, other],
-        in_specs=[in_vmem, in_vmem, anywhere] + [in_vmem] * 6, out_specs=[anywhere] * 4 + [in_vmem],
-        scratch_shapes=[scratch, scratch, wide_rows, rows, rows, rows, wide_rows, wide_rows, dma((heads,)), dma((4 * heads,))],
+        [consts, stats, hbm(mixed), cotangent, queries, keys, values, mine, other, totals],
+        in_specs=[in_vmem, in_vmem, anywhere] + [in_vmem] * 6 + [anywhere],
+        out_specs=[anywhere] * 2 + [in_vmem] * 3,
+        scratch_shapes=[scratch, scratch, wide_rows, rows, rows, rows, dma((heads,)), dma((2 * heads,))],
         cost_estimate=cost(6 * square),
     )
-    total = whole_call(
-        lambda *refs: totals_kernel(length, True, *refs), array(F32, *shards[1:]), [consts, parts, token]
-    )
     folded = whole_call(
-        lambda *refs: fold_back_kernel(length, *refs), array(F32, *shards), [consts, parts, among_groups(total)]
+        lambda *refs: fold_back_kernel(length, *refs), array(F32, *shards),
+        [consts, parts, among_groups(totals), token],
     )
     mine, give = whole_call(
         lambda *refs: states_kernel(length, True, *refs), [sums_shape, sums_shape],
@@ -485,15 +476,16 @@
 
     def finish(is_mine, back, *begun):
         return whole_call(
-            lambda *refs: finish_kernel(is_mine, *refs), [narrow, narrow],
+            lambda *refs: finish_kernel(is_mine, *refs), [narrow, narrow, array(F32, 1, channels)],
             [consts, back, keys, values, vmem(key_part), vmem(value_part), *begun],
-            in_specs=[in_vmem] * 6 + [anywhere] * len(begun), out_specs=[anywhere] * 2,
+            in_specs=[in_vmem] * 6 + [in_vmem, anywhere, anywhere][: len(begun)],
+            out_specs=[anywhere] * 2 + [in_vmem],
             scratch_shapes=[half_rows, half_rows, dma((heads,))],
-            input_output_aliases={6: 0, 7: 1} if begun else {},
+            input_output_aliases={7: 0, 8: 1} if begun else {},
         )
 
-    key_grad, value_grad = finish(False, other, *finish(True, mine))
-    gain_grad = whole_call(gain_kernel, array(F32, 1, channels), [mine, other])
+    key_grad, value_grad, _ = finish(True, mine)
+    key_grad, value_grad, gain_grad = finish(False, other, mine, key_grad, value_grad)
     return attended, query_grad, key_grad, value_grad, gain_grad.reshape(channels)
 
 

time: 121 us -> 124 us (1.025)
  blocking collectives: 56.6 us -> 46.6 us
  starting transfers between devices: 43.3 us -> 49 us
  waiting for transfers between devices: 1.98 us -> 6.13 us
  local copies, waits for them, and re-layouts: 1.28 us -> 4.39 us
    all_gather x1 -> x0, blocking collectives: 18.2 us -> none  [among_groups(): lax.all_gather(x, 'seq', axis_index_groups=[[g * 2 * CHIPS + j for g in r...]
    all_to_all x3 -> x4, blocking collectives: 25.4 us -> 33.5 us  [exchange(): return lax.all_to_all(x, 'seq', 0, 0, axis_index_groups=members)]
    all_to_all x1, starting transfers between devices: 3.47 us -> 8.74 us  [among_groups(): return lax.all_to_all(x, 'seq', 0, 0, axis_index_groups=members)]
    all_to_all x1, waiting for transfers between devices: 0.01 us -> 4.16 us  [among_groups(): return lax.all_to_all(x, 'seq', 0, 0, axis_index_groups=members)]
    unnamed x24 -> x26, local copies, waits for them, and re-layouts: 1.28 us -> 4.39 us
    pallas_call x18 -> x17, Pallas kernels: 16.4 us -> 16.1 us  [whole_call(): pl.pallas_call(kernel, in_specs=in_specs or [vmem] * len(operands), out_s...]
  transfers between devices with their start and end apart: 8 -> 8, of which waited for: 3 -> 4; matrix products, arithmetic and copies ran while one was open for 0% -> 0% of each run, Pallas kernels for 9% -> 8%
where the time goes in v9:
time: 124 us; the launch traced here: 123 us
  starting transfers between devices  49 us (40%)
  blocking collectives  46.6 us (38%)
  Pallas kernels  16.1 us (13%)
  waiting for transfers between devices  6.13 us (5%)
  local copies, waits for them, and re-layouts  4.39 us (4%)
    all_to_all x4, blocking collectives, exchange(): return lax.all_to_all(x, 'seq', 0, 0, axis_index_groups=members)  33.5 us
    ppermute x4, starting transfers between devices, swap(): lax.ppermute(x, 'seq', [(i, i ^ 1) for i in range(lax.axis_size('seq'))])  24.6 us
    pallas_call x17, Pallas kernels, whole_call(): pl.pallas_call(kernel, in_specs=in_specs or [vmem] * len(operands), out_s...  16.1 us
    ppermute x3, starting transfers between devices, onward(): return lax.ppermute(x, 'seq', [(i, i + step) for i in range(count - step)])  15.6 us
    all_to_all x1, blocking collectives, body(): stats = lax.all_to_all(stats, 'head', 0, 0)  13.1 us
    all_to_all x1, starting transfers between devices, among_groups(): return lax.all_to_all(x, 'seq', 0, 0, axis_index_groups=members)  8.74 us
    unnamed x26, local copies, waits for them, and re-layouts  4.39 us
    all_to_all x1, waiting for transfers between devices, among_groups(): return lax.all_to_all(x, 'seq', 0, 0, axis_index_groups=members)  4.16 us
  transfers between devices with their start and end apart: 8, of which 4 were waited for; matrix products, arithmetic and copies ran while one was open for 0% of the time, Pallas kernels for 8%

profile of v9, /device:TPU:1, one launch (start us, length us, event | category | flops | bytes accessed | tf_op | source)
XLA Modules:
  0.0 123.1 jit_solution(13663617255231624509)
XLA Ops:
  0.7 1.6 %shard_map.101 = (f32[2,128,128]{2,1,0:T(8,128)S(1)}, f32[8,512]{1,0:T(8,128)S(1)}) custom-call(f32[4]{0:T(128)} %rates_in.1, f32[1,512]{1,0:T(1,128)} %bitcast.2, bf16[512,512]{1,0:T(8,128)(2,1)} %refs_2_.3, bf16[512,512]{1,0:T(8,128)(2,1)} %refs_3_.9), custom_call_target="tpu_custom_call" | custom-call | tf_op jit(solution)/shard_map/pallas_call | solution.py:348
  2.3 8.8 %collective-permute-start = (f32[2,128,128]{2,1,0:T(8,128)S(1)}, f32[2,128,128]{2,1,0:T(8,128)S(1)}, u32[]{:S(2)}, u32[]{:S(2)}) collective-permute-start(f32[2,128,128]{2,1,0:T(8,128)S(1)} %get-tuple-element.26), channel_id=1, source_target_pairs={{0,16},{16,0},{32,48},{48,32},{64,80},{80,64},{96,112},{112,96},{1... | collective-permute-start | bytes 393224 | tf_op jit(solution)/shard_map/ppermute | solution.py:359
  12.1 7.3 %all_to_all.30.refs_1_ = f32[4,64,128]{2,1,0:T(8,128)S(1)} all-to-all(f32[4,64,128]{2,1,0:T(8,128)S(1)} %shard_map.103), channel_id=1, replica_groups={{0,32,64,96},{16,48,80,112},{128,160,192,224},{144,176,208,240},{256,28..., dimensions={0} | all-to-all | bytes 262144 | tf_op jit(solution)/shard_map/all_to_all | solution.py:365
  19.4 7.3 %collective-permute-start.3 = (f32[64,128]{1,0:T(8,128)S(1)}, f32[64,128]{1,0:T(8,128)S(1)}, u32[]{:S(2)}, u32[]{:S(2)}) collective-permute-start(f32[64,128]{1,0:T(8,128)S(1)} %shard_map.104.token_in), channel_id=1, source_target_pairs={{0,384},{16,400},{32,416},{48,432},{64,448},{80,464},{96,480},{112... | collective-permute-start | bytes 98312 | tf_op jit(solution)/shard_map/ppermute | solution.py:370
  26.7 3.7 %collective-permute-start.2 = (f32[64,128]{1,0:T(8,128)S(1)}, f32[64,128]{1,0:T(8,128)S(1)}, u32[]{:S(2)}, u32[]{:S(2)}) collective-permute-start(f32[64,128]{1,0:T(8,128)S(1)} %shard_map.104.token_in), channel_id=1, source_target_pairs={{0,256},{16,272},{32,288},{48,304},{64,320},{80,336},{96,352},{112... | collective-permute-start | bytes 98312 | tf_op jit(solution)/shard_map/ppermute | solution.py:370
  30.4 4.6 %collective-permute-start.1 = (f32[64,128]{1,0:T(8,128)S(1)}, f32[64,128]{1,0:T(8,128)S(1)}, u32[]{:S(2)}, u32[]{:S(2)}) collective-permute-start(f32[64,128]{1,0:T(8,128)S(1)} %shard_map.104.token_in), channel_id=1, source_target_pairs={{0,128},{16,144},{32,160},{48,176},{64,192},{80,208},{96,224},{112... | collective-permute-start | bytes 98312 | tf_op jit(solution)/shard_map/ppermute | solution.py:370
  35.0 1.7 %shard_map.105 = (f32[512,512]{1,0:T(8,128)S(1)}, f32[8,128]{1,0:T(8,128)S(1)}) custom-call(f32[8,512]{1,0:T(8,128)S(1)} %get-tuple-element.25.consts.refs_0_, bf16[512,512]{1,0:T(8,128)(2,1)S(1)} %copy-done.2, bf16[512,512]{1,0:T(8,128)(2,1)S(1)} %copy-done, bf16[512,512]{1,0:T(8,128)(2,1)S(1)} %copy-done.1, f32[64,128]{1,0:T(8,128)S(1)} %shard_map.104.token_in), custom_call_target="tpu_custom_call" | custom-call | flops 536870912 | bytes 6291456 | tf_op jit(solution)/shard_map/pallas_call | solution.py:348
  36.8 8.3 %all_to_all.31.refs_1_ = f32[4,64,128]{2,1,0:T(8,128)S(1)} all-to-all(f32[4,64,128]{2,1,0:T(8,128)S(1)} %shard_map.106), channel_id=1, replica_groups={{0,32,64,96},{16,48,80,112},{128,160,192,224},{144,176,208,240},{256,28..., dimensions={0} | all-to-all | bytes 262144 | tf_op jit(solution)/shard_map/all_to_all | solution.py:365
  45.2 5.0 %collective-permute-start.4 = (f32[2,128,128]{2,1,0:T(8,128)S(1)}, f32[2,128,128]{2,1,0:T(8,128)S(1)}, u32[]{:S(2)}, u32[]{:S(2)}) collective-permute-start(f32[2,128,128]{2,1,0:T(8,128)S(1)} %get-tuple-element.29), channel_id=1, source_target_pairs={{0,16},{16,0},{32,48},{48,32},{64,80},{80,64},{96,112},{112,96},{1... | collective-permute-start | bytes 393224 | tf_op jit(solution)/shard_map/ppermute | solution.py:359
  50.2 1.0 collective-permute-done.4.other.refs_8_
  51.8 13.1 %all_to_all.32.refs_1_ = f32[16,8,128]{2,1,0:T(8,128)S(1)} all-to-all(f32[16,8,128]{2,1,0:T(8,128)S(1)} %get-tuple-element.31), channel_id=1, replica_groups=mesh['seq'=32,'head'=16] {'head'}, dimensions={0} | all-to-all | bytes 131072 | tf_op jit(solution)/shard_map/all_to_all | solution.py:437
  65.4 3.7 %collective-permute-start.5 = (f32[2,136,128]{2,1,0:T(8,128)S(1)}, f32[2,136,128]{2,1,0:T(8,128)S(1)}, u32[]{:S(2)}, u32[]{:S(2)}) collective-permute-start(f32[2,136,128]{2,1,0:T(8,128)S(1)} %shard_map.110), channel_id=1, source_target_pairs={{0,16},{16,0},{32,48},{48,32},{64,80},{80,64},{96,112},{112,96},{1... | collective-permute-start | bytes 417800 | tf_op jit(solution)/shard_map/ppermute | solution.py:359
  70.8 8.3 %all_to_all.33.refs_1_ = f32[4,72,128]{2,1,0:T(8,128)S(1)} all-to-all(f32[4,72,128]{2,1,0:T(8,128)S(1)} %shard_map.111), channel_id=1, replica_groups={{0,32,64,96},{16,48,80,112},{128,160,192,224},{144,176,208,240},{256,28..., dimensions={0} | all-to-all | bytes 294912 | tf_op jit(solution)/shard_map/all_to_all | solution.py:365
  79.8 8.7 %all-to-all-start.4 = ((f32[4,72,128]{2,1,0:T(8,128)}), f32[4,72,128]{2,1,0:T(8,128)}, u32[]{:S(2)}, u32[]{:S(2)}) async-start(f32[4,72,128]{2,1,0:T(8,128)} %shard_map.112.refs_9_), calls=%async_computation.4 | async-start | bytes 294912 | tf_op jit(solution)/shard_map/all_to_all | solution.py:376
  88.6 0.9 copy-done.10
  90.4 5.3 %shard_map.113 = (bf16[512,512]{1,0:T(8,128)(2,1)}, bf16[512,512]{1,0:T(8,128)(2,1)}, f32[512,512]{1,0:T(8,128)S(1)}, f32[512,512]{1,0:T(8,128)S(1)}, f32[8,128]{1,0:T(8,128)S(1)}) custom-call(f32[8,512]{1,0:T(8,128)S(1)} %get-tuple-element.25.consts.refs_0_, f32[16,8,128]{2,1,0:T(8,128)S(1)} %all_to_all.32.refs_1_, f32[512,512]{1,0:T(8,128)} %copy-done.6, ...), custom_call_target="tpu_custom_call" | custom-call | flops 1610612736 | bytes 6291456 | tf_op jit(solution)/shard_map/pallas_call | solution.py:348
  95.7 1.0 copy-done.4
  96.7 4.2 %all-to-all-done.4.refs_2_ = f32[4,72,128]{2,1,0:T(8,128)} async-done(((f32[4,72,128]{2,1,0:T(8,128)}), f32[4,72,128]{2,1,0:T(8,128)}, u32[]{:S(2)}, u32[]{:S(2)}) %all-to-all-start.4) | async-done | bytes 147488 | tf_op jit(solution)/shard_map/all_to_all | solution.py:376
  100.9 1.0 shard_map.114
  101.9 9.6 %all_to_all.34.refs_1_ = f32[4,72,128]{2,1,0:T(8,128)S(1)} all-to-all(f32[4,72,128]{2,1,0:T(8,128)S(1)} %shard_map.114), channel_id=1, replica_groups={{0,32,64,96},{16,48,80,112},{128,160,192,224},{144,176,208,240},{256,28..., dimensions={0} | all-to-all | bytes 294912 | tf_op jit(solution)/shard_map/all_to_all | solution.py:365
  111.5 0.9 copy-done.8
  112.5 7.1 %collective-permute-start.6 = (f32[2,136,128]{2,1,0:T(8,128)S(1)}, f32[2,136,128]{2,1,0:T(8,128)S(1)}, u32[]{:S(2)}, u32[]{:S(2)}) collective-permute-start(f32[2,136,128]{2,1,0:T(8,128)S(1)} %get-tuple-element.36), channel_id=1, source_target_pairs={{0,16},{16,0},{32,48},{48,32},{64,80},{80,64},{96,112},{112,96},{1... | collective-permute-start | bytes 417800 | tf_op jit(solution)/shard_map/ppermute | solution.py:359
  119.7 1.7 %shard_map.116 = (bf16[512,512]{1,0:T(8,128)(2,1)}, bf16[512,512]{1,0:T(8,128)(2,1)}, f32[1,512]{1,0:T(1,128)}) custom-call(f32[8,512]{1,0:T(8,128)S(1)} %get-tuple-element.25.consts.refs_0_, f32[2,136,128]{2,1,0:T(8,128)S(1)} %get-tuple-element.39.refs_1_.refs_6_, bf16[512,512]{1,0:T(8,128)(2,1)S(1)} %copy-done, bf16[512,512]{1,0:T(8,128)(2,1)S(1)} %copy-done.1, ...), custom_call_target="tpu_custom_call" | custom-call | tf_op jit(solution)/shard_map/pallas_call | solution.py:348
  121.4 1.7 %shard_map.117 = (bf16[512,512]{1,0:T(8,128)(2,1)}, bf16[512,512]{1,0:T(8,128)(2,1)}, f32[1,512]{1,0:T(1,128)}) custom-call(f32[8,512]{1,0:T(8,128)S(1)} %get-tuple-element.25.consts.refs_0_, f32[2,136,128]{2,1,0:T(8,128)S(1)} %collective-permute-done.6.refs_1_, bf16[512,512]{1,0:T(8,128)(2,1)S(1)} %copy-done, ...), custom_call_target="tpu_custom_call", output_to_operand_aliasing={{0}: (7, {}), {1}: (8, {})} | custom-call | tf_op jit(solution)/shard_map/pallas_call | solution.py:348
  (40 shorter events, 5.6 us)
Async XLA Ops:
  0.6 10.5 %copy-start = (bf16[512,512]{1,0:T(8,128)(2,1)S(1)}, bf16[512,512]{1,0:T(8,128)(2,1)}, u32[]{:S(2)}) copy-start(bf16[512,512]{1,0:T(8,128)(2,1)} %refs_2_.3) | copy-start | bytes 1572868
  0.6 10.5 %copy-start.1 = (bf16[512,512]{1,0:T(8,128)(2,1)S(1)}, bf16[512,512]{1,0:T(8,128)(2,1)}, u32[]{:S(2)}) copy-start(bf16[512,512]{1,0:T(8,128)(2,1)} %refs_3_.9) | copy-start | bytes 1572868
  2.3 9.8 %collective-permute-start = (f32[2,128,128]{2,1,0:T(8,128)S(1)}, f32[2,128,128]{2,1,0:T(8,128)S(1)}, u32[]{:S(2)}, u32[]{:S(2)}) collective-permute-start(f32[2,128,128]{2,1,0:T(8,128)S(1)} %get-tuple-element.26), channel_id=1, source_target_pairs={{0,16},{16,0},{32,48},{48,32},{64,80},{80,64},{96,112},{112,96},{1... | collective-permute-start | bytes 393224 | tf_op jit(solution)/shard_map/ppermute | solution.py:359
  11.4 23.6 %copy-start.2 = (bf16[512,512]{1,0:T(8,128)(2,1)S(1)}, bf16[512,512]{1,0:T(8,128)(2,1)}, u32[]{:S(2)}) copy-start(bf16[512,512]{1,0:T(8,128)(2,1)} %refs_4_.5) | copy-start | bytes 1572868
  19.4 17.3 %collective-permute-start.3 = (f32[64,128]{1,0:T(8,128)S(1)}, f32[64,128]{1,0:T(8,128)S(1)}, u32[]{:S(2)}, u32[]{:S(2)}) collective-permute-start(f32[64,128]{1,0:T(8,128)S(1)} %shard_map.104.token_in), channel_id=1, source_target_pairs={{0,384},{16,400},{32,416},{48,432},{64,448},{80,464},{96,480},{112... | collective-permute-start | bytes 98312 | tf_op jit(solution)/shard_map/ppermute | solution.py:370
  26.7 10.0 %collective-permute-start.2 = (f32[64,128]{1,0:T(8,128)S(1)}, f32[64,128]{1,0:T(8,128)S(1)}, u32[]{:S(2)}, u32[]{:S(2)}) collective-permute-start(f32[64,128]{1,0:T(8,128)S(1)} %shard_map.104.token_in), channel_id=1, source_target_pairs={{0,256},{16,272},{32,288},{48,304},{64,320},{80,336},{96,352},{112... | collective-permute-start | bytes 98312 | tf_op jit(solution)/shard_map/ppermute | solution.py:370
  30.4 6.4 %collective-permute-start.1 = (f32[64,128]{1,0:T(8,128)S(1)}, f32[64,128]{1,0:T(8,128)S(1)}, u32[]{:S(2)}, u32[]{:S(2)}) collective-permute-start(f32[64,128]{1,0:T(8,128)S(1)} %shard_map.104.token_in), channel_id=1, source_target_pairs={{0,128},{16,144},{32,160},{48,176},{64,192},{80,208},{96,224},{112... | collective-permute-start | bytes 98312 | tf_op jit(solution)/shard_map/ppermute | solution.py:370
  36.7 14.4 %copy-start.3 = (bf16[512,512]{1,0:T(8,128)(2,1)S(1)}, bf16[512,512]{1,0:T(8,128)(2,1)}, u32[]{:S(2)}) copy-start(bf16[512,512]{1,0:T(8,128)(2,1)} %refs_3_.7) | copy-start | bytes 1572868
  45.2 6.6 %copy-start.9 = (f32[2,128,128]{2,1,0:T(8,128)}, f32[2,128,128]{2,1,0:T(8,128)S(1)}, u32[]{:S(2)}) copy-start(f32[2,128,128]{2,1,0:T(8,128)S(1)} %get-tuple-element.28.mine.refs_7_) | copy-start | bytes 393220
  45.2 6.0 %collective-permute-start.4 = (f32[2,128,128]{2,1,0:T(8,128)S(1)}, f32[2,128,128]{2,1,0:T(8,128)S(1)}, u32[]{:S(2)}, u32[]{:S(2)}) collective-permute-start(f32[2,128,128]{2,1,0:T(8,128)S(1)} %get-tuple-element.29), channel_id=1, source_target_pairs={{0,16},{16,0},{32,48},{48,32},{64,80},{80,64},{96,112},{112,96},{1... | collective-permute-start | bytes 393224 | tf_op jit(solution)/shard_map/ppermute | solution.py:359
  51.1 0.7 copy-start.11
  51.8 17.4 %copy-start.6 = (f32[512,512]{1,0:T(8,128)}, f32[512,512]{1,0:T(8,128)S(1)}, u32[]{:S(2)}) copy-start(f32[512,512]{1,0:T(8,128)S(1)} %get-tuple-element.32.refs_2_) | copy-start | bytes 3145732
  65.4 4.7 %collective-permute-start.5 = (f32[2,136,128]{2,1,0:T(8,128)S(1)}, f32[2,136,128]{2,1,0:T(8,128)S(1)}, u32[]{:S(2)}, u32[]{:S(2)}) collective-permute-start(f32[2,136,128]{2,1,0:T(8,128)S(1)} %shard_map.110), channel_id=1, source_target_pairs={{0,16},{16,0},{32,48},{48,32},{64,80},{80,64},{96,112},{112,96},{1... | collective-permute-start | bytes 417800 | tf_op jit(solution)/shard_map/ppermute | solution.py:359
  70.2 0.7 copy-start.7
  79.8 21.0 %all-to-all-start.4 = ((f32[4,72,128]{2,1,0:T(8,128)}), f32[4,72,128]{2,1,0:T(8,128)}, u32[]{:S(2)}, u32[]{:S(2)}) async-start(f32[4,72,128]{2,1,0:T(8,128)} %shard_map.112.refs_9_), calls=%async_computation.4 | async-start | bytes 294912 | tf_op jit(solution)/shard_map/all_to_all | solution.py:376
  88.6 0.9 copy-start.10
  89.5 0.9 copy-start.12
  95.7 1.0 copy-start.4
  100.9 18.8 %copy-start.5 = (f32[512,512]{1,0:T(8,128)S(1)}, f32[512,512]{1,0:T(8,128)}, u32[]{:S(2)}) copy-start(f32[512,512]{1,0:T(8,128)} %copy-done.4) | copy-start | bytes 3145732
  111.5 0.9 copy-start.8
  112.5 8.9 %collective-permute-start.6 = (f32[2,136,128]{2,1,0:T(8,128)S(1)}, f32[2,136,128]{2,1,0:T(8,128)S(1)}, u32[]{:S(2)}, u32[]{:S(2)}) collective-permute-start(f32[2,136,128]{2,1,0:T(8,128)S(1)} %get-tuple-element.36), channel_id=1, source_target_pairs={{0,16},{16,0},{32,48},{48,32},{64,80},{80,64},{96,112},{112,96},{1... | collective-permute-start | bytes 417800 | tf_op jit(solution)/shard_map/ppermute | solution.py:359

commit v10 on v7

--- a/solution.py
+++ b/solution.py
@@ -41,25 +41,35 @@
     return jnp.concatenate([base * jnp.exp(-rate * (length - 128 - start)) for start in range(0, length, 128)], axis=0)
 
 
-def tile_weights(rate, half):
-    rate = jnp.concatenate([rate] * (half // 128), axis=1)
-    distance = (
-        lax.broadcasted_iota(jnp.int32, (half, half), 0) - lax.broadcasted_iota(jnp.int32, (half, half), 1)
-    ).astype(F32)
-    same = jnp.where(distance >= 0, jnp.exp(-rate * jnp.maximum(distance, 0.0)), 0.0)
-    column = jnp.exp(-rate * (rows_of(half, half) + 1.0))
-    row = jnp.exp(-rate * (half - 1.0 - lax.broadcasted_iota(jnp.int32, (1, half), 1).astype(F32)))
-    return same, column * row
+def tile_weights(rate):
+    rows, lanes = rows_of(128), lax.broadcasted_iota(jnp.int32, (1, 128), 1).astype(F32)
+    distance = rows - lanes
+    near = jnp.where(distance >= 0, jnp.exp(-rate * jnp.maximum(distance, 0.0)), 0.0)
+    far = jnp.exp(-rate * (rows + 1.0)) * jnp.exp(-rate * (128 - 1.0 - lanes))
+    step = jnp.exp(-rate * 128)
+    farther = far * step
+
+    def square(a, b, c, d):
+        return jnp.concatenate([jnp.concatenate([a, b], axis=1), jnp.concatenate([c, d], axis=1)], axis=0)
+
+    return square(near, jnp.zeros_like(near), far, near), square(farther, far, farther * step, farther)
 
 
 def column(h, size):
     return pl.ds(h * size, size)
 
 
-def block_sum_kernel(rates_in, keys, values, out, rates, key_rows, value_rows, sums, arrived, sent):
+GAIN, RATE = 0, 1
+
+
+def block_sum_kernel(rates_in, gain_in, keys, values, out, consts, rates, gain, key_rows, value_rows, arrived):
     length = keys.shape[0]
     heads = rates.shape[0]
     size = keys.shape[1] // heads
+    small = [
+        pltpu.make_async_copy(rates_in, rates, arrived.at[2 * heads]),
+        pltpu.make_async_copy(gain_in, gain, arrived.at[2 * heads + 1]),
+    ]
     copies = []
     for h in range(heads):
         cols = column(h, size)
@@ -72,46 +82,39 @@
         for copy in copies[-1]:
             copy.start()
         if h == 0:
-            fetch = pltpu.make_async_copy(rates_in, rates, arrived.at[2 * heads])
-            fetch.start()
-    fetch.wait()
-    stores = []
-    for h in range(heads):
-        cols = column(h, size)
-        tail = tail_out_of(jnp.full((1, size), rates[h], F32), length)
+            for copy in small:
+                copy.start()
+    for copy in small:
+        copy.wait()
+    for h in range(heads):
+        cols = column(h, size)
+        rate = jnp.full((1, size), rates[h], F32)
+        consts[:, cols] = jnp.concatenate([gain[:, cols], rate, jnp.zeros((6, size), F32)], axis=0)
+        tail = tail_out_of(rate, length)
         for copy in copies[h]:
             copy.wait()
         scaled = value_rows[:, cols].astype(F32) * tail
-        shards = pl.ds(2 * h, 2)
-        sums[shards] = dot_split(key_rows[:, cols], scaled, 0, 0).reshape(2, size // 2, size)
-        stores.append(pltpu.make_async_copy(sums.at[shards], out.at[shards], sent.at[h]))
-        stores[-1].start()
-    for store in stores:
-        store.wait()
-
-
-GAIN, RATE = 0, 1
+        out[pl.ds(2 * h, 2)] = dot_split(key_rows[:, cols], scaled, 0, 0).reshape(2, size // 2, size)
 
 
 def weighted(a, b, t, s, weight):
     return (dot(a[t, :], b[s, :], 1, 1) * weight).astype(BF16)
 
 
-def intra_kernel(rates, gain, queries, keys, values, out, consts):
+def intra_kernel(consts, queries, keys, values, total, out, token):
     length = queries.shape[0]
     size = 128
     half = length // 2
     first, second = pl.ds(0, half), pl.ds(half, half)
     for h in range(queries.shape[1] // size):
         cols = column(h, size)
-        rate = jnp.full((1, size), rates[h], F32)
-        consts[:, cols] = jnp.concatenate([gain[:, cols], rate, jnp.zeros((6, size), F32)], axis=0)
-        same, across = tile_weights(rate, half)
+        same, across = tile_weights(consts[pl.ds(RATE, 1), cols])
         q, k, v = (ref.at[:, cols] for ref in (queries, keys, values))
         out[first, cols] = dot(weighted(q, k, first, first, same), v[first, :], 1, 0)
         out[second, cols] = dot(weighted(q, k, second, first, across), v[first, :], 1, 0) + dot(
             weighted(q, k, second, second, same), v[second, :], 1, 0
         )
+    token[...] = jnp.zeros_like(token)
 
 
 def mixed_kernel(consts, queries, state, intra, cotangent, mixed, stats, square, inner):
@@ -144,13 +147,14 @@
     for chunk in range(chunks):
         rows = pl.ds(chunk * 128, 128)
         inv_out[rows, :] = jnp.broadcast_to(inv[chunk : chunk + 1], (128, 128)).T
-        if coef_out is not None:
-            coef_out[rows, :] = jnp.broadcast_to(coef[chunk : chunk + 1], (128, 128)).T
-
-
-def back_sum_kernel(
-    channels, consts, received, mixed, cotangent, queries, grad_out, sums_out, inv, coef, grad, sums, sent
-):
+        coef_out[rows, :] = jnp.broadcast_to(coef[chunk : chunk + 1], (128, 128)).T
+
+
+def mixed_grad_of(consts, cols, upstream, value, inv, coef):
+    return (inv * (upstream * consts[pl.ds(GAIN, 1), cols]) - value * coef).astype(BF16)
+
+
+def back_sum_kernel(channels, consts, received, mixed, cotangent, queries, sums_out, inv, coef, sums, sent):
     length = queries.shape[0]
     size = 128
     heads = queries.shape[1] // size
@@ -161,24 +165,21 @@
         shards = pl.ds(2 * h, 2)
         upstream = cotangent[:, cols].astype(F32)
         value = mixed[:, cols]
-        mixed_grad = (inv[...] * (upstream * consts[pl.ds(GAIN, 1), cols]) - value * coef[...]).astype(BF16)
-        grad[:, cols] = mixed_grad
+        mixed_grad = mixed_grad_of(consts, cols, upstream, value, inv[...], coef[...])
         scaled = mixed_grad.astype(F32) * head_in_of(consts[pl.ds(RATE, 1), cols], length)
         sums[shards, pl.ds(0, size // 2), :] = dot_split(queries[:, cols], scaled, 0, 0).reshape(2, size // 2, size)
         gain_grad = jnp.sum(upstream * (value * inv[...]), axis=0, keepdims=True)
         sums[shards, pl.ds(size // 2, EXTRA), :] = jnp.broadcast_to(gain_grad[None], (2, EXTRA, size))
-        stores.append(pltpu.make_async_copy(grad.at[:, cols], grad_out.at[:, cols], sent.at[2 * h]))
-        stores.append(pltpu.make_async_copy(sums.at[shards], sums_out.at[shards], sent.at[2 * h + 1]))
+        stores.append(pltpu.make_async_copy(sums.at[shards], sums_out.at[shards], sent.at[h]))
         stores[-1].start()
-        stores[-2].start()
     for store in stores:
         store.wait()
 
 
 def grads_kernel(
-    channels, consts, received, mixed_in, queries, keys, values, grad_in, state,
+    channels, consts, received, mixed_in, cotangent, queries, keys, values, state,
     attended_out, query_out, key_part, value_part, token,
-    inv, mixed, grad, attended, query_grad, arrived, sent,
+    inv, coef, mixed, grad, attended, query_grad, arrived, sent,
 ):
     length = queries.shape[0]
     size = 128
@@ -187,26 +188,20 @@
     first, second = pl.ds(0, half), pl.ds(half, half)
     copies, stores = [], []
     for h in range(heads):
-        cols = column(h, size)
-        copies.append(
-            [
-                pltpu.make_async_copy(source.at[:, cols], rows.at[:, cols], arrived.at[2 * h + i])
-                for i, (source, rows) in enumerate(((grad_in, grad), (mixed_in, mixed)))
-            ]
-        )
-        for copy in copies[-1]:
-            copy.start()
+        copies.append(pltpu.make_async_copy(mixed_in.at[:, column(h, size)], mixed.at[:, column(h, size)], arrived.at[h]))
+        copies[-1].start()
     token[...] = jnp.zeros_like(token)
-    token_scales(received, channels, inv, None)
+    token_scales(received, channels, inv, coef)
     for h in range(heads):
         cols = column(h, size)
         rate = consts[pl.ds(RATE, 1), cols]
-        same, across = tile_weights(rate, half)
+        state_in = state[pl.ds(2 * h, 2)].reshape(size, size)
+        same, across = tile_weights(rate)
+        copies[h].wait()
+        value = mixed[:, cols]
+        attended[:, cols] = (value * inv[...] * consts[pl.ds(GAIN, 1), cols]).astype(BF16)
+        grad[:, cols] = mixed_grad_of(consts, cols, cotangent[:, cols].astype(F32), value, inv[...], coef[...])
         q, k, v, g = (ref.at[:, cols] for ref in (queries, keys, values, grad))
-        for copy in copies[h]:
-            copy.wait()
-        attended[:, cols] = (mixed[:, cols] * inv[...] * consts[pl.ds(GAIN, 1), cols]).astype(BF16)
-        state_in = state[pl.ds(2 * h, 2)].reshape(size, size)
         state_part = head_in_of(rate, length) * dot_split(g[...], state_in, 1, 1)
         upper = weighted(g, v, first, first, same)
         lower = weighted(g, v, second, first, across)
@@ -282,7 +277,7 @@
     out[...] = total[...] + group_factor * before[...]
 
 
-def fold_forward_kernel(length, consts, parts, nearest, near, far, out):
+def fold_forward_kernel(length, consts, parts, nearest, near, far, token, out):
     factor, group_factor = fold_factors(consts, length)
     carry = nearest[...] + near[...] + group_factor * far[...]
     for k in range(GROUP):
@@ -324,18 +319,19 @@
     return lax.ppermute(x, "seq", [(a * GROUP + j, b * GROUP + j) for a, b in pairs for j in range(GROUP)])
 
 
-def scan_forward(x, consts, length):
+def scan_forward(x, consts, length, beside):
     groups = lax.axis_size("seq") // GROUP
     members = [[g * GROUP + j for j in range(GROUP)] for g in range(groups)]
     parts = lax.all_to_all(x, "seq", 0, 0, axis_index_groups=members)
     one = jax.ShapeDtypeStruct(x.shape[1:], F32)
     total = whole_call(lambda *refs: forward_totals_kernel(length, *refs), one, [consts, parts])
+    result, token = beside(total)
     nearest = send(total, [(0, 1)])
     total = whole_call(lambda *refs: join_kernel(length, *refs), one, [consts, total, nearest])
+    near = send(total, [(1, 2), (2, 3)])
     far = send(total, [(1, 3)])
-    near = send(total, [(1, 2), (2, 3)])
-    out = whole_call(lambda *refs: fold_forward_kernel(length, *refs), like(x), [consts, parts, nearest, near, far])
-    return lax.all_to_all(out, "seq", 0, 0, axis_index_groups=members)
+    out = whole_call(lambda *refs: fold_forward_kernel(length, *refs), like(x), [consts, parts, nearest, near, far, token])
+    return lax.all_to_all(out, "seq", 0, 0, axis_index_groups=members), result
 
 
 def scan_back(x, consts, length, token):
@@ -381,41 +377,44 @@
     rows_scratch = pltpu.VMEM((length, channels), BF16)
     copies = pltpu.SemaphoreType.DMA((2 * heads,))
     sums_shape = (2 * heads, size // 2, size)
-    sums = whole_call(
-        block_sum_kernel, pltpu.HBM(sums_shape, F32), [hbm(rates), hbm(keys), hbm(values)],
-        in_specs=[anywhere] * 3, out_specs=anywhere,
+    sums, consts = whole_call(
+        block_sum_kernel, [array(F32, 2 * heads, size // 2, size), array(F32, 8, channels)],
+        [hbm(rates), hbm(gain.reshape(1, channels)), hbm(keys), hbm(values)], in_specs=[anywhere] * 4,
         scratch_shapes=[
-            pltpu.SMEM((heads,), F32), rows_scratch, rows_scratch, pltpu.VMEM(sums_shape, F32),
-            pltpu.SemaphoreType.DMA((2 * heads + 1,)), pltpu.SemaphoreType.DMA((heads,)),
+            pltpu.SMEM((heads,), F32), pltpu.VMEM((1, channels), F32), rows_scratch, rows_scratch,
+            pltpu.SemaphoreType.DMA((2 * heads + 2,)),
         ],
     )
+
     def cost(flops):
         return pl.CostEstimate(flops=flops, bytes_accessed=6 << 20, transcendentals=0)
 
-    intra, consts = whole_call(
-        intra_kernel, [wide, array(F32, 8, channels)], [rates, gain.reshape(1, channels), queries, keys, values],
-        in_specs=[smem] + [in_vmem] * 4, cost_estimate=cost(2 * square),
-    )
-    state_in = scan_forward(sums, consts, length)
+    def beside(total):
+        return whole_call(
+            intra_kernel, [wide, array(F32, 8, 128)], [consts, queries, keys, values, total], cost_estimate=cost(2 * square)
+        )
+
+    state_in, intra = scan_forward(sums, consts, length, beside)
     mixed, stats = whole_call(
         mixed_kernel, [wide, array(F32, *stats_shape)],
         [consts, queries, state_in, intra, cotangent], scratch_shapes=[scratch, scratch],
     )
     received = lax.all_to_all(stats, "head", 0, 0)
     sums_shape = (2 * heads, size // 2 + EXTRA, size)
-    grad, back_sums = whole_call(
-        lambda *refs: back_sum_kernel(total_channels, *refs),
-        [pltpu.HBM((length, channels), BF16), pltpu.HBM(sums_shape, F32)],
-        [consts, received, mixed, cotangent, queries], out_specs=[anywhere, anywhere],
-        scratch_shapes=[scratch, scratch, rows_scratch, pltpu.VMEM(sums_shape, F32), copies],
+    back_sums = whole_call(
+        lambda *refs: back_sum_kernel(total_channels, *refs), pltpu.HBM(sums_shape, F32),
+        [consts, received, mixed, cotangent, queries], out_specs=anywhere,
+        scratch_shapes=[scratch, scratch, pltpu.VMEM(sums_shape, F32), pltpu.SemaphoreType.DMA((heads,))],
     )
     part = pltpu.VMEM((length, channels), F32)
     attended, query_grad, key_part, value_part, token = whole_call(
         lambda *refs: grads_kernel(total_channels, *refs), [narrow, narrow, part, part, array(F32, 8, 128)],
-        [consts, received, hbm(mixed), queries, keys, values, hbm(grad), state_in],
-        in_specs=[in_vmem, in_vmem, anywhere, in_vmem, in_vmem, in_vmem, anywhere, in_vmem],
+        [consts, received, hbm(mixed), cotangent, queries, keys, values, state_in],
+        in_specs=[in_vmem, in_vmem, anywhere] + [in_vmem] * 5,
         out_specs=[anywhere, anywhere, in_vmem, in_vmem, in_vmem],
-        scratch_shapes=[scratch, pltpu.VMEM((length, channels), F32), rows_scratch, rows_scratch, rows_scratch, copies, copies],
+        scratch_shapes=[
+            scratch, scratch, pltpu.VMEM((length, channels), F32), rows_scratch, rows_scratch, rows_scratch, copies, copies,
+        ],
         cost_estimate=cost(6 * square),
     )
     back_in = scan_back(back_sums, consts, length, token)

time: 119 us -> 117 us (0.983)
  blocking collectives: 67.7 us -> 83.2 us
  starting transfers between devices: 23.6 us -> 13.5 us
  waiting for transfers between devices: 9.2 us -> 3.12 us
  Pallas kernels: 15.6 us -> 13.5 us
    all_to_all x1 -> x2, blocking collectives: 14.1 us -> 32.6 us  [the longest x1 18.1 us: scan_forward(): parts = lax.all_to_all(x, 'seq', 0, 0, axis_index_groups=members)]
    all_to_all x1 -> x0, starting transfers between devices: 10.3 us -> none  [scan_forward(): parts = lax.all_to_all(x, 'seq', 0, 0, axis_index_groups=members)]
    all_to_all x1 -> x0, waiting for transfers between devices: 5.85 us -> none  [scan_forward(): parts = lax.all_to_all(x, 'seq', 0, 0, axis_index_groups=members)]
    pallas_call x11, Pallas kernels: 15.6 us -> 13.5 us  [whole_call(): pl.pallas_call(kernel, in_specs=in_specs, out_specs=out_specs, out_shape=...]
    all_gather x1, blocking collectives: 24.2 us -> 22.2 us  [scan_back(): arrived = lax.all_gather(totals, 'seq', axis_index_groups=across)]
  transfers between devices with their start and end apart: 5 -> 4, of which waited for: 3 -> 2; matrix products, arithmetic and copies ran while one was open for 0% -> 0% of each run, Pallas kernels for 7% -> 6%
where the time goes in v10:
time: 117 us; the launch traced here: 116 us
  blocking collectives  83.2 us (71%)
  Pallas kernels  13.5 us (12%)
  starting transfers between devices  13.5 us (12%)
  waiting for transfers between devices  3.12 us (3%)
  local copies, waits for them, and re-layouts  2.04 us (2%)
    all_gather x1, blocking collectives, scan_back(): arrived = lax.all_gather(totals, 'seq', axis_index_groups=across)  22.2 us
    all_to_all x1, blocking collectives, scan_forward(): parts = lax.all_to_all(x, 'seq', 0, 0, axis_index_groups=members)  18.1 us
    all_to_all x1, blocking collectives, scan_back(): return lax.all_to_all(out, 'seq', 0, 0, axis_index_groups=members)  15.3 us
    all_to_all x1, blocking collectives, scan_forward(): return (lax.all_to_all(out, 'seq', 0, 0, axis_index_groups=members), result)  14.5 us
    pallas_call x11, Pallas kernels, whole_call(): pl.pallas_call(kernel, in_specs=in_specs, out_specs=out_specs, out_shape=...  13.5 us
    all_to_all x1, blocking collectives, body(): received = lax.all_to_all(stats, 'head', 0, 0)  13.1 us
    ppermute x3, starting transfers between devices, send(): lax.ppermute(x, 'seq', [(a * GROUP + j, b * GROUP + j) for a, b in pairs...  8.06 us
    all_to_all x1, starting transfers between devices, scan_back(): parts = lax.all_to_all(x, 'seq', 0, 0, axis_index_groups=members)  5.44 us
  transfers between devices with their start and end apart: 4, of which 2 were waited for; matrix products, arithmetic and copies ran while one was open for 0% of the time, Pallas kernels for 6%

profile of v10, /device:TPU:1, one launch (start us, length us, event | category | flops | bytes accessed | tf_op | source)
XLA Modules:
  0.0 116.2 jit_solution(1383459590813073188)
XLA Ops:
  0.7 2.1 %shard_map.101 = (f32[8,64,128]{2,1,0:T(8,128)S(1)}, f32[8,512]{1,0:T(8,128)S(1)}) custom-call(f32[4]{0:T(128)} %rates_in.1, f32[1,512]{1,0:T(1,128)} %bitcast.4, bf16[512,512]{1,0:T(8,128)(2,1)} %keys.5, bf16[512,512]{1,0:T(8,128)(2,1)} %values.5), custom_call_target="tpu_custom_call" | custom-call | tf_op jit(solution)/shard_map/pallas_call | solution.py:308
  2.8 0.0 copy-start
  2.8 18.1 %all_to_all.25.refs_1_ = f32[8,64,128]{2,1,0:T(8,128)S(1)} all-to-all(f32[8,64,128]{2,1,0:T(8,128)S(1)} %get-tuple-element.20), channel_id=1, replica_groups={{0,16,32,48,64,80,96,112},{128,144,160,176,192,208,224,240},{256,272,28..., dimensions={0} | all-to-all | bytes 524288 | tf_op jit(solution)/shard_map/all_to_all | solution.py:325
  21.0 6.7 %collective-permute-start = (f32[64,128]{1,0:T(8,128)S(1)}, f32[64,128]{1,0:T(8,128)S(1)}, u32[]{:S(2)}, u32[]{:S(2)}) collective-permute-start(f32[64,128]{1,0:T(8,128)S(1)} %shard_map.102.refs_1_.total), channel_id=1, source_target_pairs={{0,128},{16,144},{32,160},{48,176},{64,192},{80,208},{96,224},{112... | collective-permute-start | bytes 98312 | tf_op jit(solution)/shard_map/ppermute | solution.py:319
  27.7 1.0 collective-permute-done.refs_2_
  28.7 0.7 collective-permute-start.1
  29.4 0.7 collective-permute-start.2
  30.1 1.7 %shard_map.104 = (f32[512,512]{1,0:T(8,128)S(1)}, f32[8,128]{1,0:T(8,128)S(1)}) custom-call(f32[8,512]{1,0:T(8,128)S(1)} %get-tuple-element.19.refs_0_.consts, bf16[512,512]{1,0:T(8,128)(2,1)S(1)} %copy-done, bf16[512,512]{1,0:T(8,128)(2,1)S(1)} %copy-done.2, bf16[512,512]{1,0:T(8,128)(2,1)S(1)} %copy-done.3, f32[64,128]{1,0:T(8,128)S(1)} %shard_map.102.refs_1_.total), custom_call_target="tpu_custom_call" | custom-call | flops 536870912 | bytes 6291456 | tf_op jit(solution)/shard_map/pallas_call | solution.py:308
  31.8 0.0 collective-permute-done.1.refs_3_
  31.8 0.0 copy-start.1
  31.8 0.1 shard_map.105
  31.9 14.5 %all_to_all.26.state.refs_7_ = f32[8,64,128]{2,1,0:T(8,128)S(1)} all-to-all(f32[8,64,128]{2,1,0:T(8,128)S(1)} %shard_map.105), channel_id=1, replica_groups={{0,16,32,48,64,80,96,112},{128,144,160,176,192,208,224,240},{256,272,28..., dimensions={0} | all-to-all | bytes 524288 | tf_op jit(solution)/shard_map/all_to_all | solution.py:334
  46.4 0.6 shard_map.106
  47.0 0.1 copy-done.5
  47.1 13.1 %all_to_all.27.refs_1_ = f32[16,8,128]{2,1,0:T(8,128)S(1)} all-to-all(f32[16,8,128]{2,1,0:T(8,128)S(1)} %get-tuple-element.23), channel_id=1, replica_groups=mesh['seq'=32,'head'=16] {'head'}, dimensions={0} | all-to-all | bytes 131072 | tf_op jit(solution)/shard_map/all_to_all | solution.py:402
  60.2 1.5 %shard_map.108 = f32[8,72,128]{2,1,0:T(8,128)} custom-call(f32[8,512]{1,0:T(8,128)S(1)} %get-tuple-element.19.refs_0_.consts, f32[16,8,128]{2,1,0:T(8,128)S(1)} %all_to_all.27.refs_1_, f32[512,512]{1,0:T(8,128)S(1)} %get-tuple-element.24.refs_2_, bf16[512,512]{1,0:T(8,128)(2,1)S(1)} %copy-done.1, bf16[512,512]{1,0:T(8,128)(2,1)S(1)} %copy-done), custom_call_target="tpu_custom_call" | custom-call | tf_op jit(solution)/shard_map/pallas_call | solution.py:308
  61.7 5.4 %all-to-all-start.3 = ((f32[8,72,128]{2,1,0:T(8,128)}), f32[8,72,128]{2,1,0:T(8,128)S(1)}, u32[]{:S(2)}, u32[]{:S(2)}) async-start(f32[8,72,128]{2,1,0:T(8,128)} %shard_map.108), calls=%async_computation.3 | async-start | bytes 589824 | tf_op jit(solution)/shard_map/all_to_all | solution.py:341
  67.2 0.9 copy-done.6
  68.1 5.3 %shard_map.107 = (bf16[512,512]{1,0:T(8,128)(2,1)}, bf16[512,512]{1,0:T(8,128)(2,1)}, f32[512,512]{1,0:T(8,128)S(1)}, f32[512,512]{1,0:T(8,128)S(1)}, f32[8,128]{1,0:T(8,128)S(1)}) custom-call(f32[8,512]{1,0:T(8,128)S(1)} %get-tuple-element.19.refs_0_.consts, f32[16,8,128]{2,1,0:T(8,128)S(1)} %all_to_all.27.refs_1_, f32[512,512]{1,0:T(8,128)} %copy-done.4, ...), custom_call_target="tpu_custom_call" | custom-call | flops 1610612736 | bytes 6291456 | tf_op jit(solution)/shard_map/pallas_call | solution.py:308
  73.5 1.0 copy-done.7
  74.4 2.1 %all-to-all-done.3.refs_1_ = f32[8,72,128]{2,1,0:T(8,128)S(1)} async-done(((f32[8,72,128]{2,1,0:T(8,128)}), f32[8,72,128]{2,1,0:T(8,128)S(1)}, u32[]{:S(2)}, u32[]{:S(2)}) %all-to-all-start.3) | async-done | bytes 294944 | tf_op jit(solution)/shard_map/all_to_all | solution.py:341
  76.6 22.2 %all-gather = f32[288,128]{1,0:T(8,128)S(1)} all-gather(f32[72,128]{1,0:T(8,128)S(1)} %shard_map.109), channel_id=2, replica_groups={{0,128,256,384},{16,144,272,400},{32,160,288,416},{48,176,304,432},{64,..., dimensions={0}, use_global_device_ids=true | all-gather | bytes 184320 | tf_op jit(solution)/shard_map/all_gather | solution.py:346
  98.8 15.3 %all_to_all.28.back = f32[8,72,128]{2,1,0:T(8,128)S(1)} all-to-all(f32[8,72,128]{2,1,0:T(8,128)S(1)} %shard_map.110), channel_id=1, replica_groups={{0,16,32,48,64,80,96,112},{128,144,160,176,192,208,224,240},{256,272,28..., dimensions={0} | all-to-all | bytes 589824 | tf_op jit(solution)/shard_map/all_to_all | solution.py:348
  114.1 2.0 %shard_map.111 = (bf16[512,512]{1,0:T(8,128)(2,1)}, bf16[512,512]{1,0:T(8,128)(2,1)}, f32[1,512]{1,0:T(1,128)}) custom-call(f32[8,512]{1,0:T(8,128)S(1)} %get-tuple-element.19.refs_0_.consts, f32[8,72,128]{2,1,0:T(8,128)S(1)} %all_to_all.28.back, bf16[512,512]{1,0:T(8,128)(2,1)S(1)} %copy-done.2, bf16[512,512]{1,0:T(8,128)(2,1)S(1)} %copy-done.3, ...), custom_call_target="tpu_custom_call" | custom-call | tf_op jit(solution)/shard_map/pallas_call | solution.py:308
  (18 shorter events, 0.2 us)
Async XLA Ops:
  0.6 29.4 %copy-start.2 = (bf16[512,512]{1,0:T(8,128)(2,1)S(1)}, bf16[512,512]{1,0:T(8,128)(2,1)}, u32[]{:S(2)}) copy-start(bf16[512,512]{1,0:T(8,128)(2,1)} %keys.5) | copy-start | bytes 1572868
  0.6 29.4 %copy-start.3 = (bf16[512,512]{1,0:T(8,128)(2,1)S(1)}, bf16[512,512]{1,0:T(8,128)(2,1)}, u32[]{:S(2)}) copy-start(bf16[512,512]{1,0:T(8,128)(2,1)} %values.5) | copy-start | bytes 1572868
  2.8 27.3 %copy-start = (bf16[512,512]{1,0:T(8,128)(2,1)S(1)}, bf16[512,512]{1,0:T(8,128)(2,1)}, u32[]{:S(2)}) copy-start(bf16[512,512]{1,0:T(8,128)(2,1)} %refs_4_.3) | copy-start | bytes 1572868
  21.0 7.7 %collective-permute-start = (f32[64,128]{1,0:T(8,128)S(1)}, f32[64,128]{1,0:T(8,128)S(1)}, u32[]{:S(2)}, u32[]{:S(2)}) collective-permute-start(f32[64,128]{1,0:T(8,128)S(1)} %shard_map.102.refs_1_.total), channel_id=1, source_target_pairs={{0,128},{16,144},{32,160},{48,176},{64,192},{80,208},{96,224},{112... | collective-permute-start | bytes 98312 | tf_op jit(solution)/shard_map/ppermute | solution.py:319
  28.7 3.1 %collective-permute-start.1 = (f32[64,128]{1,0:T(8,128)S(1)}, f32[64,128]{1,0:T(8,128)S(1)}, u32[]{:S(2)}, u32[]{:S(2)}) collective-permute-start(f32[64,128]{1,0:T(8,128)S(1)} %shard_map.103), channel_id=1, source_target_pairs={{128,256},{144,272},{160,288},{176,304},{192,320},{208,336},{224,3... | collective-permute-start | bytes 98312 | tf_op jit(solution)/shard_map/ppermute | solution.py:319
  29.4 2.4 %collective-permute-start.2 = (f32[64,128]{1,0:T(8,128)S(1)}, f32[64,128]{1,0:T(8,128)S(1)}, u32[]{:S(2)}, u32[]{:S(2)}) collective-permute-start(f32[64,128]{1,0:T(8,128)S(1)} %shard_map.103), channel_id=1, source_target_pairs={{128,384},{144,400},{160,416},{176,432},{192,448},{208,464},{224,4... | collective-permute-start | bytes 98312 | tf_op jit(solution)/shard_map/ppermute | solution.py:319
  31.8 14.6 %copy-start.1 = (bf16[512,512]{1,0:T(8,128)(2,1)S(1)}, bf16[512,512]{1,0:T(8,128)(2,1)}, u32[]{:S(2)}) copy-start(bf16[512,512]{1,0:T(8,128)(2,1)} %refs_3_.3) | copy-start | bytes 1572868
  46.4 0.7 copy-start.5
  47.1 14.6 %copy-start.4 = (f32[512,512]{1,0:T(8,128)}, f32[512,512]{1,0:T(8,128)S(1)}, u32[]{:S(2)}) copy-start(f32[512,512]{1,0:T(8,128)S(1)} %get-tuple-element.24.refs_2_) | copy-start | bytes 3145732
  61.7 14.8 %all-to-all-start.3 = ((f32[8,72,128]{2,1,0:T(8,128)}), f32[8,72,128]{2,1,0:T(8,128)S(1)}, u32[]{:S(2)}, u32[]{:S(2)}) async-start(f32[8,72,128]{2,1,0:T(8,128)} %shard_map.108), calls=%async_computation.3 | async-start | bytes 589824 | tf_op jit(solution)/shard_map/all_to_all | solution.py:341
  67.2 0.9 copy-start.6
  73.5 1.0 copy-start.7
  76.5 37.6 %copy-start.8 = (f32[512,512]{1,0:T(8,128)S(1)}, f32[512,512]{1,0:T(8,128)}, u32[]{:S(2)}) copy-start(f32[512,512]{1,0:T(8,128)} %copy-done.7) | copy-start | bytes 3145732

commit v11 on v10

--- a/solution.py
+++ b/solution.py
@@ -154,12 +154,13 @@
     return (inv * (upstream * consts[pl.ds(GAIN, 1), cols]) - value * coef).astype(BF16)
 
 
-def back_sum_kernel(channels, consts, received, mixed, cotangent, queries, sums_out, inv, coef, sums, sent):
+def back_sum_kernel(channels, consts, received, mixed, cotangent, queries, sums_out, gains, inv, coef, sums, sent):
     length = queries.shape[0]
     size = 128
     heads = queries.shape[1] // size
     token_scales(received, channels, inv, coef)
     stores = []
+    gains[...] = jnp.zeros_like(gains)
     for h in range(heads):
         cols = column(h, size)
         shards = pl.ds(2 * h, 2)
@@ -167,9 +168,8 @@
         value = mixed[:, cols]
         mixed_grad = mixed_grad_of(consts, cols, upstream, value, inv[...], coef[...])
         scaled = mixed_grad.astype(F32) * head_in_of(consts[pl.ds(RATE, 1), cols], length)
-        sums[shards, pl.ds(0, size // 2), :] = dot_split(queries[:, cols], scaled, 0, 0).reshape(2, size // 2, size)
-        gain_grad = jnp.sum(upstream * (value * inv[...]), axis=0, keepdims=True)
-        sums[shards, pl.ds(size // 2, EXTRA), :] = jnp.broadcast_to(gain_grad[None], (2, EXTRA, size))
+        sums[shards] = dot_split(queries[:, cols], scaled, 0, 0).reshape(2, size // 2, size)
+        gains[pl.ds(h, 1), :] = jnp.sum(upstream * (value * inv[...]), axis=0, keepdims=True)
         stores.append(pltpu.make_async_copy(sums.at[shards], sums_out.at[shards], sent.at[h]))
         stores[-1].start()
     for store in stores:
@@ -177,9 +177,9 @@
 
 
 def grads_kernel(
-    channels, consts, received, mixed_in, cotangent, queries, keys, values, state,
+    channels, consts, received, mixed_in, cotangent_in, queries, keys, values, state,
     attended_out, query_out, key_part, value_part, token,
-    inv, coef, mixed, grad, attended, query_grad, arrived, sent,
+    inv, coef, mixed, cotangent, grad, attended, query_grad, arrived, sent,
 ):
     length = queries.shape[0]
     size = 128
@@ -188,8 +188,15 @@
     first, second = pl.ds(0, half), pl.ds(half, half)
     copies, stores = [], []
     for h in range(heads):
-        copies.append(pltpu.make_async_copy(mixed_in.at[:, column(h, size)], mixed.at[:, column(h, size)], arrived.at[h]))
-        copies[-1].start()
+        cols = column(h, size)
+        copies.append(
+            [
+                pltpu.make_async_copy(source.at[:, cols], rows.at[:, cols], arrived.at[2 * h + i])
+                for i, (source, rows) in enumerate(((mixed_in, mixed), (cotangent_in, cotangent)))
+            ]
+        )
+        for copy in copies[-1]:
+            copy.start()
     token[...] = jnp.zeros_like(token)
     token_scales(received, channels, inv, coef)
     for h in range(heads):
@@ -197,7 +204,8 @@
         rate = consts[pl.ds(RATE, 1), cols]
         state_in = state[pl.ds(2 * h, 2)].reshape(size, size)
         same, across = tile_weights(rate)
-        copies[h].wait()
+        for copy in copies[h]:
+            copy.wait()
         value = mixed[:, cols]
         attended[:, cols] = (value * inv[...] * consts[pl.ds(GAIN, 1), cols]).astype(BF16)
         grad[:, cols] = mixed_grad_of(consts, cols, cotangent[:, cols].astype(F32), value, inv[...], coef[...])
@@ -235,7 +243,7 @@
     for h in range(heads):
         cols = column(h, size)
         back_in = back[pl.ds(2 * h, 2), pl.ds(0, half), :].reshape(size, size)
-        gain_grad[:, cols] = back[2 * h, pl.ds(half, 1), :]
+        gain_grad[:, cols] = sum(back[k, pl.ds(half + h, 1), :] for k in range(GROUP))
         tail = tail_out_of(consts[pl.ds(RATE, 1), cols], length)
         key_rows[:, cols] = (key_part[:, cols] + tail * dot_split(values[:, cols], back_in, 1, 1)).astype(BF16)
         value_rows[:, cols] = (value_part[:, cols] + tail * dot_split(keys[:, cols], back_in, 1, 0)).astype(BF16)
@@ -254,14 +262,14 @@
     return jnp.exp(-rate * length), jnp.exp(-rate * (length * GROUP))
 
 
-def totals_kernel(length, consts, parts, token, out):
+def totals_kernel(length, consts, parts, gains, token, out):
     factor, _ = fold_factors(consts, length)
-    rows = parts.shape[1] - EXTRA
-    total = parts[GROUP - 1, :rows]
+    rows = parts.shape[1]
+    total = parts[GROUP - 1]
     for k in range(GROUP - 2, -1, -1):
-        total = factor * total + parts[k, :rows]
+        total = factor * total + parts[k]
     out[:rows] = total
-    out[rows:] = sum(parts[k, rows:] for k in range(GROUP))
+    out[rows:] = gains[...]
 
 
 def forward_totals_kernel(length, consts, parts, out):
@@ -287,16 +295,16 @@
 
 def fold_back_kernel(length, consts, parts, arrived, out):
     factor, group_factor = fold_factors(consts, length)
-    rows = parts.shape[1] - EXTRA
+    rows = parts.shape[1]
     group = lax.axis_index("seq") // GROUP
-    carry = jnp.zeros((rows, parts.shape[2]), F32)
+    carry = jnp.zeros(parts.shape[1:], F32)
     for g in range(arrived.shape[0] - 1, 0, -1):
         carry = jnp.where(group < g, group_factor * carry + arrived[g, :rows], carry)
     extra = sum(arrived[g, rows:] for g in range(arrived.shape[0]))
     for k in range(GROUP - 1, -1, -1):
         out[k, :rows] = carry
         out[k, rows:] = extra
-        carry = factor * carry + parts[k, :rows]
+        carry = factor * carry + parts[k]
 
 
 def whole_call(kernel, out_shape, operands, in_specs=None, out_specs=None, **rest):
@@ -334,17 +342,21 @@
     return lax.all_to_all(out, "seq", 0, 0, axis_index_groups=members), result
 
 
-def scan_back(x, consts, length, token):
+def scan_back(x, gains, consts, length, token):
     groups = lax.axis_size("seq") // GROUP
     members = [[g * GROUP + j for j in range(GROUP)] for g in range(groups)]
     across = [[g * GROUP + j for g in range(groups)] for j in range(GROUP)]
     parts = lax.all_to_all(x, "seq", 0, 0, axis_index_groups=members)
     totals = whole_call(
-        lambda *refs: totals_kernel(length, *refs), jax.ShapeDtypeStruct(x.shape[1:], F32),
-        [consts, parts, token],
+        lambda *refs: totals_kernel(length, *refs), jax.ShapeDtypeStruct((x.shape[1] + EXTRA, x.shape[2]), F32),
+        [consts, parts, gains, token],
     )
     arrived = lax.all_gather(totals, "seq", axis_index_groups=across)
-    out = whole_call(lambda *refs: fold_back_kernel(length, *refs), like(x), [consts, parts, arrived])
+    out = whole_call(
+        lambda *refs: fold_back_kernel(length, *refs),
+        jax.ShapeDtypeStruct((GROUP,) + arrived.shape[1:], F32),
+        [consts, parts, arrived],
+    )
     return lax.all_to_all(out, "seq", 0, 0, axis_index_groups=members)
 
 
@@ -400,24 +412,25 @@
         [consts, queries, state_in, intra, cotangent], scratch_shapes=[scratch, scratch],
     )
     received = lax.all_to_all(stats, "head", 0, 0)
-    sums_shape = (2 * heads, size // 2 + EXTRA, size)
-    back_sums = whole_call(
-        lambda *refs: back_sum_kernel(total_channels, *refs), pltpu.HBM(sums_shape, F32),
-        [consts, received, mixed, cotangent, queries], out_specs=anywhere,
+    sums_shape = (2 * heads, size // 2, size)
+    back_sums, gains = whole_call(
+        lambda *refs: back_sum_kernel(total_channels, *refs), [pltpu.HBM(sums_shape, F32), array(F32, EXTRA, size)],
+        [consts, received, mixed, cotangent, queries], out_specs=[anywhere, in_vmem],
         scratch_shapes=[scratch, scratch, pltpu.VMEM(sums_shape, F32), pltpu.SemaphoreType.DMA((heads,))],
     )
     part = pltpu.VMEM((length, channels), F32)
     attended, query_grad, key_part, value_part, token = whole_call(
         lambda *refs: grads_kernel(total_channels, *refs), [narrow, narrow, part, part, array(F32, 8, 128)],
-        [consts, received, hbm(mixed), cotangent, queries, keys, values, state_in],
-        in_specs=[in_vmem, in_vmem, anywhere] + [in_vmem] * 5,
+        [consts, received, hbm(mixed), hbm(cotangent), queries, keys, values, state_in],
+        in_specs=[in_vmem, in_vmem, anywhere, anywhere] + [in_vmem] * 4,
         out_specs=[anywhere, anywhere, in_vmem, in_vmem, in_vmem],
         scratch_shapes=[
-            scratch, scratch, pltpu.VMEM((length, channels), F32), rows_scratch, rows_scratch, rows_scratch, copies, copies,
+            scratch, scratch, pltpu.VMEM((length, channels), F32), rows_scratch, rows_scratch, rows_scratch,
+            rows_scratch, copies, copies,
         ],
         cost_estimate=cost(6 * square),
     )
-    back_in = scan_back(back_sums, consts, length, token)
+    back_in = scan_back(back_sums, gains, consts, length, token)
     key_grad, value_grad, gain_grad = whole_call(
         finish_kernel, [narrow, narrow, array(F32, 1, channels)],
         [consts, back_in, keys, values, vmem(key_part), vmem(value_part)],

time: 117 us -> 118 us (level)
  no operation moved by 1% of the time
where the time goes in v11:
time: 118 us; the launch traced here: 117 us
  blocking collectives  83.9 us (71%)
  Pallas kernels  13.5 us (11%)
  starting transfers between devices  13.5 us (11%)
  local copies, waits for them, and re-layouts  3.21 us (3%)
  waiting for transfers between devices  2.42 us (2%)
    all_gather x1, blocking collectives, scan_back(): arrived = lax.all_gather(totals, 'seq', axis_index_groups=across)  22.5 us
    all_to_all x1, blocking collectives, scan_forward(): parts = lax.all_to_all(x, 'seq', 0, 0, axis_index_groups=members)  18.1 us
    all_to_all x1, blocking collectives, scan_back(): return lax.all_to_all(out, 'seq', 0, 0, axis_index_groups=members)  15.6 us
    all_to_all x1, blocking collectives, scan_forward(): return (lax.all_to_all(out, 'seq', 0, 0, axis_index_groups=members), result)  14.5 us
    pallas_call x11, Pallas kernels, whole_call(): pl.pallas_call(kernel, in_specs=in_specs, out_specs=out_specs, out_shape=...  13.5 us
    all_to_all x1, blocking collectives, body(): received = lax.all_to_all(stats, 'head', 0, 0)  13.1 us
    ppermute x3, starting transfers between devices, send(): lax.ppermute(x, 'seq', [(a * GROUP + j, b * GROUP + j) for a, b in pairs...  8.06 us
    all_to_all x1, starting transfers between devices, scan_back(): parts = lax.all_to_all(x, 'seq', 0, 0, axis_index_groups=members)  5.43 us
  transfers between devices with their start and end apart: 4, of which 2 were waited for; matrix products, arithmetic and copies ran while one was open for 0% of the time, Pallas kernels for 6%

profile of v11, /device:TPU:1, one launch (start us, length us, event | category | flops | bytes accessed | tf_op | source)
XLA Modules:
  0.0 117.4 jit_solution(3269144503113860369)
XLA Ops:
  0.7 2.1 %shard_map.101 = (f32[8,64,128]{2,1,0:T(8,128)S(1)}, f32[8,512]{1,0:T(8,128)S(1)}) custom-call(f32[4]{0:T(128)} %rates_in.1, f32[1,512]{1,0:T(1,128)} %bitcast.4, bf16[512,512]{1,0:T(8,128)(2,1)} %keys.5, bf16[512,512]{1,0:T(8,128)(2,1)} %values.5), custom_call_target="tpu_custom_call" | custom-call | tf_op jit(solution)/shard_map/pallas_call | solution.py:316
  2.8 0.0 copy-start
  2.8 18.1 %all_to_all.25.refs_1_ = f32[8,64,128]{2,1,0:T(8,128)S(1)} all-to-all(f32[8,64,128]{2,1,0:T(8,128)S(1)} %get-tuple-element.22), channel_id=1, replica_groups={{0,16,32,48,64,80,96,112},{128,144,160,176,192,208,224,240},{256,272,28..., dimensions={0} | all-to-all | bytes 524288 | tf_op jit(solution)/shard_map/all_to_all | solution.py:333
  21.0 6.7 %collective-permute-start = (f32[64,128]{1,0:T(8,128)S(1)}, f32[64,128]{1,0:T(8,128)S(1)}, u32[]{:S(2)}, u32[]{:S(2)}) collective-permute-start(f32[64,128]{1,0:T(8,128)S(1)} %shard_map.102.refs_1_.total), channel_id=1, source_target_pairs={{0,128},{16,144},{32,160},{48,176},{64,192},{80,208},{96,224},{112... | collective-permute-start | bytes 98312 | tf_op jit(solution)/shard_map/ppermute | solution.py:327
  27.7 1.0 collective-permute-done.refs_2_
  28.7 0.7 collective-permute-start.1
  29.4 0.7 collective-permute-start.2
  30.1 1.7 %shard_map.104 = (f32[512,512]{1,0:T(8,128)S(1)}, f32[8,128]{1,0:T(8,128)S(1)}) custom-call(f32[8,512]{1,0:T(8,128)S(1)} %get-tuple-element.21.refs_0_.consts, bf16[512,512]{1,0:T(8,128)(2,1)S(1)} %copy-done, bf16[512,512]{1,0:T(8,128)(2,1)S(1)} %copy-done.2, bf16[512,512]{1,0:T(8,128)(2,1)S(1)} %copy-done.3, f32[64,128]{1,0:T(8,128)S(1)} %shard_map.102.refs_1_.total), custom_call_target="tpu_custom_call" | custom-call | flops 536870912 | bytes 6291456 | tf_op jit(solution)/shard_map/pallas_call | solution.py:316
  31.8 0.0 collective-permute-done.1.refs_3_
  31.8 0.0 copy-start.1
  31.8 0.1 shard_map.105
  31.9 14.5 %all_to_all.26.state.refs_7_ = f32[8,64,128]{2,1,0:T(8,128)S(1)} all-to-all(f32[8,64,128]{2,1,0:T(8,128)S(1)} %shard_map.105), channel_id=1, replica_groups={{0,16,32,48,64,80,96,112},{128,144,160,176,192,208,224,240},{256,272,28..., dimensions={0} | all-to-all | bytes 524288 | tf_op jit(solution)/shard_map/all_to_all | solution.py:342
  46.4 0.6 shard_map.106
  47.0 13.1 %all_to_all.27.refs_1_ = f32[16,8,128]{2,1,0:T(8,128)S(1)} all-to-all(f32[16,8,128]{2,1,0:T(8,128)S(1)} %get-tuple-element.25), channel_id=1, replica_groups=mesh['seq'=32,'head'=16] {'head'}, dimensions={0} | all-to-all | bytes 131072 | tf_op jit(solution)/shard_map/all_to_all | solution.py:414
  60.1 1.5 %shard_map.108 = (f32[8,64,128]{2,1,0:T(8,128)}, f32[8,128]{1,0:T(8,128)S(1)}) custom-call(f32[8,512]{1,0:T(8,128)S(1)} %get-tuple-element.21.refs_0_.consts, f32[16,8,128]{2,1,0:T(8,128)S(1)} %all_to_all.27.refs_1_, f32[512,512]{1,0:T(8,128)S(1)} %get-tuple-element.26.refs_2_, bf16[512,512]{1,0:T(8,128)(2,1)S(1)} %copy-done.1, bf16[512,512]{1,0:T(8,128)(2,1)S(1)} %copy-done), custom_call_target="tpu_custom_call" | custom-call | tf_op jit(solution)/shard_map/pallas_call | solution.py:316
  61.6 5.4 %all-to-all-start.3 = ((f32[8,64,128]{2,1,0:T(8,128)}), f32[8,64,128]{2,1,0:T(8,128)S(1)}, u32[]{:S(2)}, u32[]{:S(2)}) async-start(f32[8,64,128]{2,1,0:T(8,128)} %get-tuple-element.29), calls=%async_computation.3 | async-start | bytes 524288 | tf_op jit(solution)/shard_map/all_to_all | solution.py:349
  67.1 5.3 %shard_map.107 = (bf16[512,512]{1,0:T(8,128)(2,1)}, bf16[512,512]{1,0:T(8,128)(2,1)}, f32[512,512]{1,0:T(8,128)S(1)}, f32[512,512]{1,0:T(8,128)S(1)}, f32[8,128]{1,0:T(8,128)S(1)}) custom-call(f32[8,512]{1,0:T(8,128)S(1)} %get-tuple-element.21.refs_0_.consts, f32[16,8,128]{2,1,0:T(8,128)S(1)} %all_to_all.27.refs_1_, f32[512,512]{1,0:T(8,128)} %copy-done.8, ...), custom_call_target="tpu_custom_call" | custom-call | flops 1610612736 | bytes 6291456 | tf_op jit(solution)/shard_map/pallas_call | solution.py:316
  72.4 1.0 copy-done.4
  73.4 1.0 copy-done.6
  74.4 1.4 %all-to-all-done.3.refs_1_ = f32[8,64,128]{2,1,0:T(8,128)S(1)} async-done(((f32[8,64,128]{2,1,0:T(8,128)}), f32[8,64,128]{2,1,0:T(8,128)S(1)}, u32[]{:S(2)}, u32[]{:S(2)}) %all-to-all-start.3) | async-done | bytes 262176 | tf_op jit(solution)/shard_map/all_to_all | solution.py:349
  75.8 22.5 %all-gather = f32[288,128]{1,0:T(8,128)S(1)} all-gather(f32[72,128]{1,0:T(8,128)S(1)} %shard_map.109), channel_id=2, replica_groups={{0,128,256,384},{16,144,272,400},{32,160,288,416},{48,176,304,432},{64,..., dimensions={0}, use_global_device_ids=true | all-gather | bytes 184320 | tf_op jit(solution)/shard_map/all_gather | solution.py:354
  98.4 15.6 %all_to_all.28.back = f32[8,72,128]{2,1,0:T(8,128)S(1)} all-to-all(f32[8,72,128]{2,1,0:T(8,128)S(1)} %shard_map.110), channel_id=1, replica_groups={{0,16,32,48,64,80,96,112},{128,144,160,176,192,208,224,240},{256,272,28..., dimensions={0} | all-to-all | bytes 589824 | tf_op jit(solution)/shard_map/all_to_all | solution.py:360
  114.1 1.2 %copy-done.7 = f32[512,512]{1,0:T(8,128)S(1)} copy-done((f32[512,512]{1,0:T(8,128)S(1)}, f32[512,512]{1,0:T(8,128)}, u32[]{:S(2)}) %copy-start.7) | copy-done | bytes 1048600
  115.3 2.0 %shard_map.111 = (bf16[512,512]{1,0:T(8,128)(2,1)}, bf16[512,512]{1,0:T(8,128)(2,1)}, f32[1,512]{1,0:T(1,128)}) custom-call(f32[8,512]{1,0:T(8,128)S(1)} %get-tuple-element.21.refs_0_.consts, f32[8,72,128]{2,1,0:T(8,128)S(1)} %all_to_all.28.back, bf16[512,512]{1,0:T(8,128)(2,1)S(1)} %copy-done.2, bf16[512,512]{1,0:T(8,128)(2,1)S(1)} %copy-done.3, ...), custom_call_target="tpu_custom_call" | custom-call | tf_op jit(solution)/shard_map/pallas_call | solution.py:316
  (18 shorter events, 0.2 us)
Async XLA Ops:
  0.6 29.4 %copy-start.2 = (bf16[512,512]{1,0:T(8,128)(2,1)S(1)}, bf16[512,512]{1,0:T(8,128)(2,1)}, u32[]{:S(2)}) copy-start(bf16[512,512]{1,0:T(8,128)(2,1)} %keys.5) | copy-start | bytes 1572868
  0.6 29.4 %copy-start.3 = (bf16[512,512]{1,0:T(8,128)(2,1)S(1)}, bf16[512,512]{1,0:T(8,128)(2,1)}, u32[]{:S(2)}) copy-start(bf16[512,512]{1,0:T(8,128)(2,1)} %values.5) | copy-start | bytes 1572868
  2.8 27.3 %copy-start = (bf16[512,512]{1,0:T(8,128)(2,1)S(1)}, bf16[512,512]{1,0:T(8,128)(2,1)}, u32[]{:S(2)}) copy-start(bf16[512,512]{1,0:T(8,128)(2,1)} %refs_4_.3) | copy-start | bytes 1572868
  21.0 7.7 %collective-permute-start = (f32[64,128]{1,0:T(8,128)S(1)}, f32[64,128]{1,0:T(8,128)S(1)}, u32[]{:S(2)}, u32[]{:S(2)}) collective-permute-start(f32[64,128]{1,0:T(8,128)S(1)} %shard_map.102.refs_1_.total), channel_id=1, source_target_pairs={{0,128},{16,144},{32,160},{48,176},{64,192},{80,208},{96,224},{112... | collective-permute-start | bytes 98312 | tf_op jit(solution)/shard_map/ppermute | solution.py:327
  28.7 3.1 %collective-permute-start.1 = (f32[64,128]{1,0:T(8,128)S(1)}, f32[64,128]{1,0:T(8,128)S(1)}, u32[]{:S(2)}, u32[]{:S(2)}) collective-permute-start(f32[64,128]{1,0:T(8,128)S(1)} %shard_map.103), channel_id=1, source_target_pairs={{128,256},{144,272},{160,288},{176,304},{192,320},{208,336},{224,3... | collective-permute-start | bytes 98312 | tf_op jit(solution)/shard_map/ppermute | solution.py:327
  29.4 2.4 %collective-permute-start.2 = (f32[64,128]{1,0:T(8,128)S(1)}, f32[64,128]{1,0:T(8,128)S(1)}, u32[]{:S(2)}, u32[]{:S(2)}) collective-permute-start(f32[64,128]{1,0:T(8,128)S(1)} %shard_map.103), channel_id=1, source_target_pairs={{128,384},{144,400},{160,416},{176,432},{192,448},{208,464},{224,4... | collective-permute-start | bytes 98312 | tf_op jit(solution)/shard_map/ppermute | solution.py:327
  31.8 14.6 %copy-start.1 = (bf16[512,512]{1,0:T(8,128)(2,1)S(1)}, bf16[512,512]{1,0:T(8,128)(2,1)}, u32[]{:S(2)}) copy-start(bf16[512,512]{1,0:T(8,128)(2,1)} %refs_3_.3) | copy-start | bytes 1572868
  47.0 14.6 %copy-start.8 = (f32[512,512]{1,0:T(8,128)}, f32[512,512]{1,0:T(8,128)S(1)}, u32[]{:S(2)}) copy-start(f32[512,512]{1,0:T(8,128)S(1)} %get-tuple-element.26.refs_2_) | copy-start | bytes 3145732
  61.6 14.2 %all-to-all-start.3 = ((f32[8,64,128]{2,1,0:T(8,128)}), f32[8,64,128]{2,1,0:T(8,128)S(1)}, u32[]{:S(2)}, u32[]{:S(2)}) async-start(f32[8,64,128]{2,1,0:T(8,128)} %get-tuple-element.29), calls=%async_computation.3 | async-start | bytes 524288 | tf_op jit(solution)/shard_map/all_to_all | solution.py:349
  72.4 1.0 copy-start.4
  73.4 1.0 copy-start.6
  75.8 38.3 %copy-start.5 = (f32[512,512]{1,0:T(8,128)S(1)}, f32[512,512]{1,0:T(8,128)}, u32[]{:S(2)}) copy-start(f32[512,512]{1,0:T(8,128)} %copy-done.4) | copy-start | bytes 3145732
  114.1 1.2 %copy-start.7 = (f32[512,512]{1,0:T(8,128)S(1)}, f32[512,512]{1,0:T(8,128)}, u32[]{:S(2)}) copy-start(f32[512,512]{1,0:T(8,128)} %copy-done.6) | copy-start | bytes 3145732

commit v12 on v11

--- a/solution.py
+++ b/solution.py
@@ -178,7 +178,7 @@
 
 def grads_kernel(
     channels, consts, received, mixed_in, cotangent_in, queries, keys, values, state,
-    attended_out, query_out, key_part, value_part, token,
+    attended_out, query_out, key_part, value_part,
     inv, coef, mixed, cotangent, grad, attended, query_grad, arrived, sent,
 ):
     length = queries.shape[0]
@@ -197,7 +197,6 @@
         )
         for copy in copies[-1]:
             copy.start()
-    token[...] = jnp.zeros_like(token)
     token_scales(received, channels, inv, coef)
     for h in range(heads):
         cols = column(h, size)
@@ -262,7 +261,8 @@
     return jnp.exp(-rate * length), jnp.exp(-rate * (length * GROUP))
 
 
-def totals_kernel(length, consts, parts, gains, token, out):
+def totals_kernel(length, consts, parts, gains, *refs):
+    out = refs[len(refs) // 2]
     factor, _ = fold_factors(consts, length)
     rows = parts.shape[1]
     total = parts[GROUP - 1]
@@ -293,7 +293,8 @@
         carry = factor * carry + parts[k]
 
 
-def fold_back_kernel(length, consts, parts, arrived, out):
+def fold_back_kernel(length, consts, parts, arrived, *refs):
+    out = refs[len(refs) // 2]
     factor, group_factor = fold_factors(consts, length)
     rows = parts.shape[1]
     group = lax.axis_index("seq") // GROUP
@@ -342,22 +343,34 @@
     return lax.all_to_all(out, "seq", 0, 0, axis_index_groups=members), result
 
 
-def scan_back(x, gains, consts, length, token):
+def scan_back(x, gains, consts, length, kept):
     groups = lax.axis_size("seq") // GROUP
     members = [[g * GROUP + j for j in range(GROUP)] for g in range(groups)]
     across = [[g * GROUP + j for g in range(groups)] for j in range(GROUP)]
     parts = lax.all_to_all(x, "seq", 0, 0, axis_index_groups=members)
-    totals = whole_call(
-        lambda *refs: totals_kernel(length, *refs), jax.ShapeDtypeStruct((x.shape[1] + EXTRA, x.shape[2]), F32),
-        [consts, parts, gains, token],
+    totals, *kept = passing(
+        lambda *refs: totals_kernel(length, *refs), array(F32, x.shape[1] + EXTRA, x.shape[2]), [consts, parts, gains], kept
     )
     arrived = lax.all_gather(totals, "seq", axis_index_groups=across)
-    out = whole_call(
-        lambda *refs: fold_back_kernel(length, *refs),
-        jax.ShapeDtypeStruct((GROUP,) + arrived.shape[1:], F32),
-        [consts, parts, arrived],
-    )
-    return lax.all_to_all(out, "seq", 0, 0, axis_index_groups=members)
+    out, *kept = passing(
+        lambda *refs: fold_back_kernel(length, *refs), array(F32, GROUP, *arrived.shape[1:]), [consts, parts, arrived], kept
+    )
+    return lax.all_to_all(out, "seq", 0, 0, axis_index_groups=members), kept
+
+
+def passing(kernel, out_shape, operands, kept):
+    return whole_call(
+        kernel, [out_shape] + [pltpu.VMEM(x.shape, x.dtype) for x in kept], operands + [in_vmem_space(x) for x in kept],
+        input_output_aliases={len(operands) + i: 1 + i for i in range(len(kept))},
+    )
+
+
+def in_vmem_space(x):
+    return pltpu.with_memory_space_constraint(x, pltpu.VMEM)
+
+
+def array(kind, *shape):
+    return jax.ShapeDtypeStruct(shape, kind)
 
 
 def like(x):
@@ -375,15 +388,11 @@
     stats_shape = (head_devices, 2 * length // 128, 128)
     scratch = pltpu.VMEM((length, size), F32)
 
-    def array(kind, *shape):
-        return jax.ShapeDtypeStruct(shape, kind)
-
     square = 2 * heads * length * length * size
     wide = array(F32, length, channels)
     narrow = array(BF16, length, channels)
 
     hbm = lambda x: pltpu.with_memory_space_constraint(x, pltpu.HBM)
-    vmem = lambda x: pltpu.with_memory_space_constraint(x, pltpu.VMEM)
     anywhere = pl.BlockSpec(memory_space=pl.ANY)
     in_vmem = pl.BlockSpec(memory_space=pltpu.VMEM)
     rows_scratch = pltpu.VMEM((length, channels), BF16)
@@ -419,21 +428,21 @@
         scratch_shapes=[scratch, scratch, pltpu.VMEM(sums_shape, F32), pltpu.SemaphoreType.DMA((heads,))],
     )
     part = pltpu.VMEM((length, channels), F32)
-    attended, query_grad, key_part, value_part, token = whole_call(
-        lambda *refs: grads_kernel(total_channels, *refs), [narrow, narrow, part, part, array(F32, 8, 128)],
+    attended, query_grad, key_part, value_part = whole_call(
+        lambda *refs: grads_kernel(total_channels, *refs), [narrow, narrow, part, part],
         [consts, received, hbm(mixed), hbm(cotangent), queries, keys, values, state_in],
         in_specs=[in_vmem, in_vmem, anywhere, anywhere] + [in_vmem] * 4,
-        out_specs=[anywhere, anywhere, in_vmem, in_vmem, in_vmem],
+        out_specs=[anywhere, anywhere, in_vmem, in_vmem],
         scratch_shapes=[
             scratch, scratch, pltpu.VMEM((length, channels), F32), rows_scratch, rows_scratch, rows_scratch,
             rows_scratch, copies, copies,
         ],
         cost_estimate=cost(6 * square),
     )
-    back_in = scan_back(back_sums, gains, consts, length, token)
+    back_in, (key_part, value_part) = scan_back(back_sums, gains, consts, length, [key_part, value_part])
     key_grad, value_grad, gain_grad = whole_call(
         finish_kernel, [narrow, narrow, array(F32, 1, channels)],
-        [consts, back_in, keys, values, vmem(key_part), vmem(value_part)],
+        [consts, back_in, keys, values, in_vmem_space(key_part), in_vmem_space(value_part)],
         out_specs=[anywhere, anywhere, in_vmem], scratch_shapes=[rows_scratch, rows_scratch, copies],
     )
     return attended, query_grad, key_grad, value_grad, gain_grad.reshape(channels)

time: 118 us -> 118 us (level)
  blocking collectives: 83.9 us -> 85.3 us
    all_to_all x1, blocking collectives: 15.6 us -> 17.2 us  [scan_back(): return (lax.all_to_all(out, 'seq', 0, 0, axis_index_groups=members), kept)]
    unnamed x18 -> x20, local copies, waits for them, and re-layouts: 3.21 us -> 2.13 us
where the time goes in v12:
time: 118 us
  blocking collectives  85.3 us (72%)
  Pallas kernels  13.5 us (11%)
  starting transfers between devices  13.5 us (11%)
  waiting for transfers between devices  2.35 us (2%)
  local copies, waits for them, and re-layouts  2.13 us (2%)
    all_gather x1, blocking collectives, scan_back(): arrived = lax.all_gather(totals, 'seq', axis_index_groups=across)  23 us
    all_to_all x1, blocking collectives, scan_forward(): parts = lax.all_to_all(x, 'seq', 0, 0, axis_index_groups=members)  18.1 us
    all_to_all x1, blocking collectives, scan_back(): return (lax.all_to_all(out, 'seq', 0, 0, axis_index_groups=members), kept)  17.2 us
    all_to_all x1, blocking collectives, scan_forward(): return (lax.all_to_all(out, 'seq', 0, 0, axis_index_groups=members), result)  13.9 us
    pallas_call x11, Pallas kernels, whole_call(): pl.pallas_call(kernel, in_specs=in_specs, out_specs=out_specs, out_shape=...  13.5 us
    all_to_all x1, blocking collectives, body(): received = lax.all_to_all(stats, 'head', 0, 0)  13.1 us
    ppermute x3, starting transfers between devices, send(): lax.ppermute(x, 'seq', [(a * GROUP + j, b * GROUP + j) for a, b in pairs...  8.06 us
    all_to_all x1, starting transfers between devices, scan_back(): parts = lax.all_to_all(x, 'seq', 0, 0, axis_index_groups=members)  5.48 us
  transfers between devices with their start and end apart: 4, of which 2 were waited for; matrix products, arithmetic and copies ran while one was open for 0% of the time, Pallas kernels for 6%

profile of v12, /device:TPU:1, one launch (start us, length us, event | category | flops | bytes accessed | tf_op | source)
XLA Modules:
  0.0 117.6 jit_solution(11894395999836576539)
XLA Ops:
  0.6 0.0 copy-start.2
  0.7 2.1 %shard_map.101 = (f32[8,64,128]{2,1,0:T(8,128)S(1)}, f32[8,512]{1,0:T(8,128)S(1)}) custom-call(f32[4]{0:T(128)} %rates_in.1, f32[1,512]{1,0:T(1,128)} %bitcast.4, bf16[512,512]{1,0:T(8,128)(2,1)} %keys.5, bf16[512,512]{1,0:T(8,128)(2,1)} %values.5), custom_call_target="tpu_custom_call" | custom-call | tf_op jit(solution)/shard_map/pallas_call | solution.py:317
  2.8 0.0 copy-start
  2.8 18.1 %all_to_all.25.refs_1_ = f32[8,64,128]{2,1,0:T(8,128)S(1)} all-to-all(f32[8,64,128]{2,1,0:T(8,128)S(1)} %get-tuple-element.27), channel_id=1, replica_groups={{0,16,32,48,64,80,96,112},{128,144,160,176,192,208,224,240},{256,272,28..., dimensions={0} | all-to-all | bytes 524288 | tf_op jit(solution)/shard_map/all_to_all | solution.py:334
  21.0 6.7 %collective-permute-start = (f32[64,128]{1,0:T(8,128)S(1)}, f32[64,128]{1,0:T(8,128)S(1)}, u32[]{:S(2)}, u32[]{:S(2)}) collective-permute-start(f32[64,128]{1,0:T(8,128)S(1)} %shard_map.102.refs_1_.total), channel_id=1, source_target_pairs={{0,128},{16,144},{32,160},{48,176},{64,192},{80,208},{96,224},{112... | collective-permute-start | bytes 98312 | tf_op jit(solution)/shard_map/ppermute | solution.py:328
  27.7 1.0 collective-permute-done.refs_2_
  28.7 0.7 collective-permute-start.2
  29.4 0.7 collective-permute-start.1
  30.1 1.7 %shard_map.104 = (f32[512,512]{1,0:T(8,128)S(1)}, f32[8,128]{1,0:T(8,128)S(1)}) custom-call(f32[8,512]{1,0:T(8,128)S(1)} %get-tuple-element.26.refs_0_.consts, bf16[512,512]{1,0:T(8,128)(2,1)S(1)} %copy-done, bf16[512,512]{1,0:T(8,128)(2,1)S(1)} %copy-done.2, bf16[512,512]{1,0:T(8,128)(2,1)S(1)} %copy-done.4, f32[64,128]{1,0:T(8,128)S(1)} %shard_map.102.refs_1_.total), custom_call_target="tpu_custom_call" | custom-call | flops 536870912 | bytes 6291456 | tf_op jit(solution)/shard_map/pallas_call | solution.py:317
  31.8 0.1 shard_map.105
  31.9 13.9 %all_to_all.26.state.refs_7_ = f32[8,64,128]{2,1,0:T(8,128)S(1)} all-to-all(f32[8,64,128]{2,1,0:T(8,128)S(1)} %shard_map.105), channel_id=1, replica_groups={{0,16,32,48,64,80,96,112},{128,144,160,176,192,208,224,240},{256,272,28..., dimensions={0} | all-to-all | bytes 524288 | tf_op jit(solution)/shard_map/all_to_all | solution.py:343
  45.8 0.6 shard_map.106
  46.4 0.1 copy-done.7
  46.5 13.1 %all_to_all.27.refs_1_ = f32[16,8,128]{2,1,0:T(8,128)S(1)} all-to-all(f32[16,8,128]{2,1,0:T(8,128)S(1)} %get-tuple-element.30), channel_id=1, replica_groups=mesh['seq'=32,'head'=16] {'head'}, dimensions={0} | all-to-all | bytes 131072 | tf_op jit(solution)/shard_map/all_to_all | solution.py:423
  59.6 1.5 %shard_map.108 = (f32[8,64,128]{2,1,0:T(8,128)}, f32[8,128]{1,0:T(8,128)S(1)}) custom-call(f32[8,512]{1,0:T(8,128)S(1)} %get-tuple-element.26.refs_0_.consts, f32[16,8,128]{2,1,0:T(8,128)S(1)} %all_to_all.27.refs_1_, f32[512,512]{1,0:T(8,128)S(1)} %get-tuple-element.31.refs_2_, bf16[512,512]{1,0:T(8,128)(2,1)S(1)} %copy-done.1, bf16[512,512]{1,0:T(8,128)(2,1)S(1)} %copy-done), custom_call_target="tpu_custom_call" | custom-call | tf_op jit(solution)/shard_map/pallas_call | solution.py:317
  61.1 0.0 copy-start.3
  61.1 5.5 %all-to-all-start.3 = ((f32[8,64,128]{2,1,0:T(8,128)}), f32[8,64,128]{2,1,0:T(8,128)S(1)}, u32[]{:S(2)}, u32[]{:S(2)}) async-start(f32[8,64,128]{2,1,0:T(8,128)} %get-tuple-element.34), calls=%async_computation.3 | async-start | bytes 524288 | tf_op jit(solution)/shard_map/all_to_all | solution.py:350
  66.6 1.0 copy-done.5
  67.6 0.9 copy-done.8
  68.6 5.4 %shard_map.107 = (bf16[512,512]{1,0:T(8,128)(2,1)}, bf16[512,512]{1,0:T(8,128)(2,1)}, f32[512,512]{1,0:T(8,128)S(1)}, f32[512,512]{1,0:T(8,128)S(1)}) custom-call(f32[8,512]{1,0:T(8,128)S(1)} %get-tuple-element.26.refs_0_.consts, f32[16,8,128]{2,1,0:T(8,128)S(1)} %all_to_all.27.refs_1_, f32[512,512]{1,0:T(8,128)} %copy-done.9, bf16[512,512]{1,0:T(8,128)(2,1)} %refs_3_.3, ...), custom_call_target="tpu_custom_call" | custom-call | flops 1610612736 | bytes 6291456 | tf_op jit(solution)/shard_map/pallas_call | solution.py:317
  74.0 1.3 %all-to-all-done.3.refs_1_ = f32[8,64,128]{2,1,0:T(8,128)S(1)} async-done(((f32[8,64,128]{2,1,0:T(8,128)}), f32[8,64,128]{2,1,0:T(8,128)S(1)}, u32[]{:S(2)}, u32[]{:S(2)}) %all-to-all-start.3) | async-done | bytes 262176 | tf_op jit(solution)/shard_map/all_to_all | solution.py:350
  75.3 23.0 %all-gather = f32[288,128]{1,0:T(8,128)S(1)} all-gather(f32[72,128]{1,0:T(8,128)S(1)} %get-tuple-element.38), channel_id=2, replica_groups={{0,128,256,384},{16,144,272,400},{32,160,288,416},{48,176,304,432},{64,..., dimensions={0}, use_global_device_ids=true | all-gather | bytes 184320 | tf_op jit(solution)/shard_map/all_gather | solution.py:354
  98.4 17.2 %all_to_all.28.back = f32[8,72,128]{2,1,0:T(8,128)S(1)} all-to-all(f32[8,72,128]{2,1,0:T(8,128)S(1)} %get-tuple-element.41), channel_id=1, replica_groups={{0,16,32,48,64,80,96,112},{128,144,160,176,192,208,224,240},{256,272,28..., dimensions={0} | all-to-all | bytes 589824 | tf_op jit(solution)/shard_map/all_to_all | solution.py:358
  115.6 2.0 %shard_map.111 = (bf16[512,512]{1,0:T(8,128)(2,1)}, bf16[512,512]{1,0:T(8,128)(2,1)}, f32[1,512]{1,0:T(1,128)}) custom-call(f32[8,512]{1,0:T(8,128)S(1)} %get-tuple-element.26.refs_0_.consts, f32[8,72,128]{2,1,0:T(8,128)S(1)} %all_to_all.28.back, bf16[512,512]{1,0:T(8,128)(2,1)S(1)} %copy-done.3, bf16[512,512]{1,0:T(8,128)(2,1)S(1)} %copy-done.6, ...), custom_call_target="tpu_custom_call" | custom-call | tf_op jit(solution)/shard_map/pallas_call | solution.py:317
  (20 shorter events, 0.1 us)
Async XLA Ops:
  0.6 29.4 %copy-start.2 = (bf16[512,512]{1,0:T(8,128)(2,1)S(1)}, bf16[512,512]{1,0:T(8,128)(2,1)}, u32[]{:S(2)}) copy-start(bf16[512,512]{1,0:T(8,128)(2,1)} %keys.5) | copy-start | bytes 1572868
  0.6 29.4 %copy-start.4 = (bf16[512,512]{1,0:T(8,128)(2,1)S(1)}, bf16[512,512]{1,0:T(8,128)(2,1)}, u32[]{:S(2)}) copy-start(bf16[512,512]{1,0:T(8,128)(2,1)} %values.5) | copy-start | bytes 1572868
  2.8 27.3 %copy-start = (bf16[512,512]{1,0:T(8,128)(2,1)S(1)}, bf16[512,512]{1,0:T(8,128)(2,1)}, u32[]{:S(2)}) copy-start(bf16[512,512]{1,0:T(8,128)(2,1)} %refs_4_.3) | copy-start | bytes 1572868
  21.0 7.7 %collective-permute-start = (f32[64,128]{1,0:T(8,128)S(1)}, f32[64,128]{1,0:T(8,128)S(1)}, u32[]{:S(2)}, u32[]{:S(2)}) collective-permute-start(f32[64,128]{1,0:T(8,128)S(1)} %shard_map.102.refs_1_.total), channel_id=1, source_target_pairs={{0,128},{16,144},{32,160},{48,176},{64,192},{80,208},{96,224},{112... | collective-permute-start | bytes 98312 | tf_op jit(solution)/shard_map/ppermute | solution.py:328
  28.7 3.1 %collective-permute-start.2 = (f32[64,128]{1,0:T(8,128)S(1)}, f32[64,128]{1,0:T(8,128)S(1)}, u32[]{:S(2)}, u32[]{:S(2)}) collective-permute-start(f32[64,128]{1,0:T(8,128)S(1)} %shard_map.103), channel_id=1, source_target_pairs={{128,384},{144,400},{160,416},{176,432},{192,448},{208,464},{224,4... | collective-permute-start | bytes 98312 | tf_op jit(solution)/shard_map/ppermute | solution.py:328
  29.4 2.4 %collective-permute-start.1 = (f32[64,128]{1,0:T(8,128)S(1)}, f32[64,128]{1,0:T(8,128)S(1)}, u32[]{:S(2)}, u32[]{:S(2)}) collective-permute-start(f32[64,128]{1,0:T(8,128)S(1)} %shard_map.103), channel_id=1, source_target_pairs={{128,256},{144,272},{160,288},{176,304},{192,320},{208,336},{224,3... | collective-permute-start | bytes 98312 | tf_op jit(solution)/shard_map/ppermute | solution.py:328
  31.8 14.0 %copy-start.1 = (bf16[512,512]{1,0:T(8,128)(2,1)S(1)}, bf16[512,512]{1,0:T(8,128)(2,1)}, u32[]{:S(2)}) copy-start(bf16[512,512]{1,0:T(8,128)(2,1)} %refs_3_.3) | copy-start | bytes 1572868
  45.8 0.7 copy-start.7
  46.5 14.6 %copy-start.9 = (f32[512,512]{1,0:T(8,128)}, f32[512,512]{1,0:T(8,128)S(1)}, u32[]{:S(2)}) copy-start(f32[512,512]{1,0:T(8,128)S(1)} %get-tuple-element.31.refs_2_) | copy-start | bytes 3145732
  61.1 5.5 %copy-start.3 = (bf16[512,512]{1,0:T(8,128)(2,1)S(1)}, bf16[512,512]{1,0:T(8,128)(2,1)}, u32[]{:S(2)}) copy-start(bf16[512,512]{1,0:T(8,128)(2,1)} %keys.5) | copy-start | bytes 1572868
  61.1 14.2 %all-to-all-start.3 = ((f32[8,64,128]{2,1,0:T(8,128)}), f32[8,64,128]{2,1,0:T(8,128)S(1)}, u32[]{:S(2)}, u32[]{:S(2)}) async-start(f32[8,64,128]{2,1,0:T(8,128)} %get-tuple-element.34), calls=%async_computation.3 | async-start | bytes 524288 | tf_op jit(solution)/shard_map/all_to_all | solution.py:350
  66.6 1.0 copy-start.5
  67.6 0.9 copy-start.8
  98.4 17.2 %copy-start.6 = (bf16[512,512]{1,0:T(8,128)(2,1)S(1)}, bf16[512,512]{1,0:T(8,128)(2,1)}, u32[]{:S(2)}) copy-start(bf16[512,512]{1,0:T(8,128)(2,1)} %values.5) | copy-start | bytes 1572868

commit v13 on v12

--- a/solution.py
+++ b/solution.py
@@ -101,7 +101,7 @@
     return (dot(a[t, :], b[s, :], 1, 1) * weight).astype(BF16)
 
 
-def intra_kernel(consts, queries, keys, values, total, out, token):
+def intra_kernel(consts, queries, keys, values, total, out, total_out):
     length = queries.shape[0]
     size = 128
     half = length // 2
@@ -114,7 +114,7 @@
         out[second, cols] = dot(weighted(q, k, second, first, across), v[first, :], 1, 0) + dot(
             weighted(q, k, second, second, same), v[second, :], 1, 0
         )
-    token[...] = jnp.zeros_like(token)
+    total_out[...] = total[...]
 
 
 def mixed_kernel(consts, queries, state, intra, cotangent, mixed, stats, square, inner):
@@ -177,9 +177,9 @@
 
 
 def grads_kernel(
-    channels, consts, received, mixed_in, cotangent_in, queries, keys, values, state,
+    channels, consts, received, mixed_in, cotangent_in, queries_in, keys_in, values_in, state,
     attended_out, query_out, key_part, value_part,
-    inv, coef, mixed, cotangent, grad, attended, query_grad, arrived, sent,
+    inv, coef, mixed, cotangent, queries, keys, values, grad, attended, query_grad, arrived, sent,
 ):
     length = queries.shape[0]
     size = 128
@@ -191,8 +191,16 @@
         cols = column(h, size)
         copies.append(
             [
-                pltpu.make_async_copy(source.at[:, cols], rows.at[:, cols], arrived.at[2 * h + i])
-                for i, (source, rows) in enumerate(((mixed_in, mixed), (cotangent_in, cotangent)))
+                pltpu.make_async_copy(source.at[:, cols], rows.at[:, cols], arrived.at[5 * h + i])
+                for i, (source, rows) in enumerate(
+                    (
+                        (mixed_in, mixed),
+                        (cotangent_in, cotangent),
+                        (values_in, values),
+                        (keys_in, keys),
+                        (queries_in, queries),
+                    )
+                )
             ]
         )
         for copy in copies[-1]:
@@ -285,7 +293,7 @@
     out[...] = total[...] + group_factor * before[...]
 
 
-def fold_forward_kernel(length, consts, parts, nearest, near, far, token, out):
+def fold_forward_kernel(length, consts, parts, nearest, near, far, out):
     factor, group_factor = fold_factors(consts, length)
     carry = nearest[...] + near[...] + group_factor * far[...]
     for k in range(GROUP):
@@ -334,12 +342,12 @@
     parts = lax.all_to_all(x, "seq", 0, 0, axis_index_groups=members)
     one = jax.ShapeDtypeStruct(x.shape[1:], F32)
     total = whole_call(lambda *refs: forward_totals_kernel(length, *refs), one, [consts, parts])
-    result, token = beside(total)
     nearest = send(total, [(0, 1)])
     total = whole_call(lambda *refs: join_kernel(length, *refs), one, [consts, total, nearest])
     near = send(total, [(1, 2), (2, 3)])
+    result, total = beside(total)
     far = send(total, [(1, 3)])
-    out = whole_call(lambda *refs: fold_forward_kernel(length, *refs), like(x), [consts, parts, nearest, near, far, token])
+    out = whole_call(lambda *refs: fold_forward_kernel(length, *refs), like(x), [consts, parts, nearest, near, far])
     return lax.all_to_all(out, "seq", 0, 0, axis_index_groups=members), result
 
 
@@ -412,7 +420,7 @@
 
     def beside(total):
         return whole_call(
-            intra_kernel, [wide, array(F32, 8, 128)], [consts, queries, keys, values, total], cost_estimate=cost(2 * square)
+            intra_kernel, [wide, array(F32, *total.shape)], [consts, queries, keys, values, total], cost_estimate=cost(2 * square)
         )
 
     state_in, intra = scan_forward(sums, consts, length, beside)
@@ -430,12 +438,12 @@
     part = pltpu.VMEM((length, channels), F32)
     attended, query_grad, key_part, value_part = whole_call(
         lambda *refs: grads_kernel(total_channels, *refs), [narrow, narrow, part, part],
-        [consts, received, hbm(mixed), hbm(cotangent), queries, keys, values, state_in],
-        in_specs=[in_vmem, in_vmem, anywhere, anywhere] + [in_vmem] * 4,
+        [consts, received, hbm(mixed), hbm(cotangent), hbm(queries), hbm(keys), hbm(values), state_in],
+        in_specs=[in_vmem] * 2 + [anywhere] * 5 + [in_vmem],
         out_specs=[anywhere, anywhere, in_vmem, in_vmem],
         scratch_shapes=[
             scratch, scratch, pltpu.VMEM((length, channels), F32), rows_scratch, rows_scratch, rows_scratch,
-            rows_scratch, copies, copies,
+            rows_scratch, rows_scratch, rows_scratch, rows_scratch, pltpu.SemaphoreType.DMA((5 * heads,)), copies,
         ],
         cost_estimate=cost(6 * square),
     )

time: 118 us -> 118 us (level)
  local copies, waits for them, and re-layouts: 2.13 us -> 0.14 us
  waiting for transfers between devices: 2.35 us -> 4.08 us
    unnamed x20 -> x18, local copies, waits for them, and re-layouts: 2.13 us -> 0.14 us
    all_to_all x1, blocking collectives: 17.2 us -> 15.2 us  [scan_back(): return (lax.all_to_all(out, 'seq', 0, 0, axis_index_groups=members), kept)]
    all_to_all x1, waiting for transfers between devices: 1.34 us -> 3.07 us  [scan_back(): parts = lax.all_to_all(x, 'seq', 0, 0, axis_index_groups=members)]
where the time goes in v13:
time: 118 us; the launch traced here: 117 us
  blocking collectives  84.3 us (71%)
  starting transfers between devices  14.1 us (12%)
  Pallas kernels  13.8 us (12%)
  waiting for transfers between devices  4.08 us (3%)
    all_gather x1, blocking collectives, scan_back(): arrived = lax.all_gather(totals, 'seq', axis_index_groups=across)  23.8 us
    all_to_all x1, blocking collectives, scan_forward(): parts = lax.all_to_all(x, 'seq', 0, 0, axis_index_groups=members)  18.1 us
    all_to_all x1, blocking collectives, scan_back(): return (lax.all_to_all(out, 'seq', 0, 0, axis_index_groups=members), kept)  15.2 us
    all_to_all x1, blocking collectives, scan_forward(): return (lax.all_to_all(out, 'seq', 0, 0, axis_index_groups=members), result)  14.2 us
    pallas_call x11, Pallas kernels, whole_call(): pl.pallas_call(kernel, in_specs=in_specs, out_specs=out_specs, out_shape=...  13.8 us
    all_to_all x1, blocking collectives, body(): received = lax.all_to_all(stats, 'head', 0, 0)  13.1 us
    ppermute x3, starting transfers between devices, send(): lax.ppermute(x, 'seq', [(a * GROUP + j, b * GROUP + j) for a, b in pairs...  8.19 us
    all_to_all x1, starting transfers between devices, scan_back(): parts = lax.all_to_all(x, 'seq', 0, 0, axis_index_groups=members)  5.93 us
  transfers between devices with their start and end apart: 4, of which 2 were waited for; matrix products, arithmetic and copies ran while one was open for 0% of the time, Pallas kernels for 6%

profile of v13, /device:TPU:1, one launch (start us, length us, event | category | flops | bytes accessed | tf_op | source)
XLA Modules:
  0.0 117.3 jit_solution(5808307993784011754)
XLA Ops:
  0.6 0.0 copy-start.2
  0.6 0.0 copy-start.4
  0.7 2.1 %shard_map.101 = (f32[8,64,128]{2,1,0:T(8,128)S(1)}, f32[8,512]{1,0:T(8,128)S(1)}) custom-call(f32[4]{0:T(128)} %rates_in.1, f32[1,512]{1,0:T(1,128)} %bitcast.4, bf16[512,512]{1,0:T(8,128)(2,1)} %keys.5, bf16[512,512]{1,0:T(8,128)(2,1)} %values.5), custom_call_target="tpu_custom_call" | custom-call | tf_op jit(solution)/shard_map/pallas_call | solution.py:325
  2.8 0.0 copy-start
  2.8 18.1 %all_to_all.25.refs_1_ = f32[8,64,128]{2,1,0:T(8,128)S(1)} all-to-all(f32[8,64,128]{2,1,0:T(8,128)S(1)} %get-tuple-element.27), channel_id=1, replica_groups={{0,16,32,48,64,80,96,112},{128,144,160,176,192,208,224,240},{256,272,28..., dimensions={0} | all-to-all | bytes 524288 | tf_op jit(solution)/shard_map/all_to_all | solution.py:342
  21.0 6.7 %collective-permute-start = (f32[64,128]{1,0:T(8,128)S(1)}, f32[64,128]{1,0:T(8,128)S(1)}, u32[]{:S(2)}, u32[]{:S(2)}) collective-permute-start(f32[64,128]{1,0:T(8,128)S(1)} %shard_map.102.refs_1_), channel_id=1, source_target_pairs={{0,128},{16,144},{32,160},{48,176},{64,192},{80,208},{96,224},{112... | collective-permute-start | bytes 98312 | tf_op jit(solution)/shard_map/ppermute | solution.py:336
  27.7 1.0 collective-permute-done.refs_2_
  28.7 0.7 collective-permute-start.1
  29.4 1.7 %shard_map.104 = (f32[512,512]{1,0:T(8,128)S(1)}, f32[64,128]{1,0:T(8,128)S(1)}) custom-call(f32[8,512]{1,0:T(8,128)S(1)} %get-tuple-element.26.refs_0_.consts, bf16[512,512]{1,0:T(8,128)(2,1)S(1)} %copy-done, bf16[512,512]{1,0:T(8,128)(2,1)S(1)} %copy-done.2, bf16[512,512]{1,0:T(8,128)(2,1)S(1)} %copy-done.4, f32[64,128]{1,0:T(8,128)S(1)} %shard_map.103.total), custom_call_target="tpu_custom_call" | custom-call | flops 536870912 | bytes 6291456 | tf_op jit(solution)/shard_map/pallas_call | solution.py:325
  31.1 0.8 collective-permute-start.2
  32.0 0.1 shard_map.105
  32.0 14.2 %all_to_all.26.state.refs_7_ = f32[8,64,128]{2,1,0:T(8,128)S(1)} all-to-all(f32[8,64,128]{2,1,0:T(8,128)S(1)} %shard_map.105), channel_id=1, replica_groups={{0,16,32,48,64,80,96,112},{128,144,160,176,192,208,224,240},{256,272,28..., dimensions={0} | all-to-all | bytes 524288 | tf_op jit(solution)/shard_map/all_to_all | solution.py:351
  46.2 0.6 shard_map.106
  46.8 0.1 copy-done.6
  46.9 13.1 %all_to_all.27.refs_1_ = f32[16,8,128]{2,1,0:T(8,128)S(1)} all-to-all(f32[16,8,128]{2,1,0:T(8,128)S(1)} %get-tuple-element.30), channel_id=1, replica_groups=mesh['seq'=32,'head'=16] {'head'}, dimensions={0} | all-to-all | bytes 131072 | tf_op jit(solution)/shard_map/all_to_all | solution.py:431
  59.9 1.5 %shard_map.108 = (f32[8,64,128]{2,1,0:T(8,128)}, f32[8,128]{1,0:T(8,128)S(1)}) custom-call(f32[8,512]{1,0:T(8,128)S(1)} %get-tuple-element.26.refs_0_.consts, f32[16,8,128]{2,1,0:T(8,128)S(1)} %all_to_all.27.refs_1_, f32[512,512]{1,0:T(8,128)S(1)} %get-tuple-element.31.refs_2_, bf16[512,512]{1,0:T(8,128)(2,1)S(1)} %copy-done.1, bf16[512,512]{1,0:T(8,128)(2,1)S(1)} %copy-done), custom_call_target="tpu_custom_call" | custom-call | tf_op jit(solution)/shard_map/pallas_call | solution.py:325
  61.5 5.9 %all-to-all-start.3 = ((f32[8,64,128]{2,1,0:T(8,128)}), f32[8,64,128]{2,1,0:T(8,128)S(1)}, u32[]{:S(2)}, u32[]{:S(2)}) async-start(f32[8,64,128]{2,1,0:T(8,128)} %get-tuple-element.34), calls=%async_computation.3 | async-start | bytes 524288 | tf_op jit(solution)/shard_map/all_to_all | solution.py:358
  67.4 5.6 %shard_map.107 = (bf16[512,512]{1,0:T(8,128)(2,1)}, bf16[512,512]{1,0:T(8,128)(2,1)}, f32[512,512]{1,0:T(8,128)S(1)}, f32[512,512]{1,0:T(8,128)S(1)}) custom-call(f32[8,512]{1,0:T(8,128)S(1)} %get-tuple-element.26.refs_0_.consts, f32[16,8,128]{2,1,0:T(8,128)S(1)} %all_to_all.27.refs_1_, f32[512,512]{1,0:T(8,128)} %copy-done.8, bf16[512,512]{1,0:T(8,128)(2,1)} %refs_3_.3, ...), custom_call_target="tpu_custom_call" | custom-call | flops 1610612736 | bytes 6291456 | tf_op jit(solution)/shard_map/pallas_call | solution.py:325
  73.0 3.1 %all-to-all-done.3.refs_1_ = f32[8,64,128]{2,1,0:T(8,128)S(1)} async-done(((f32[8,64,128]{2,1,0:T(8,128)}), f32[8,64,128]{2,1,0:T(8,128)S(1)}, u32[]{:S(2)}, u32[]{:S(2)}) %all-to-all-start.3) | async-done | bytes 262176 | tf_op jit(solution)/shard_map/all_to_all | solution.py:358
  76.1 23.8 %all-gather = f32[288,128]{1,0:T(8,128)S(1)} all-gather(f32[72,128]{1,0:T(8,128)S(1)} %get-tuple-element.38), channel_id=2, replica_groups={{0,128,256,384},{16,144,272,400},{32,160,288,416},{48,176,304,432},{64,..., dimensions={0}, use_global_device_ids=true | all-gather | bytes 184320 | tf_op jit(solution)/shard_map/all_gather | solution.py:362
  99.9 0.1 shard_map.110
  100.0 0.0 copy-start.3
  100.0 15.2 %all_to_all.28.back = f32[8,72,128]{2,1,0:T(8,128)S(1)} all-to-all(f32[8,72,128]{2,1,0:T(8,128)S(1)} %get-tuple-element.41), channel_id=1, replica_groups={{0,16,32,48,64,80,96,112},{128,144,160,176,192,208,224,240},{256,272,28..., dimensions={0} | all-to-all | bytes 589824 | tf_op jit(solution)/shard_map/all_to_all | solution.py:366
  115.2 2.0 %shard_map.111 = (bf16[512,512]{1,0:T(8,128)(2,1)}, bf16[512,512]{1,0:T(8,128)(2,1)}, f32[1,512]{1,0:T(1,128)}) custom-call(f32[8,512]{1,0:T(8,128)S(1)} %get-tuple-element.26.refs_0_.consts, f32[8,72,128]{2,1,0:T(8,128)S(1)} %all_to_all.28.back, bf16[512,512]{1,0:T(8,128)(2,1)S(1)} %copy-done.3, bf16[512,512]{1,0:T(8,128)(2,1)S(1)} %copy-done.5, ...), custom_call_target="tpu_custom_call" | custom-call | tf_op jit(solution)/shard_map/pallas_call | solution.py:325
  (18 shorter events, 0.1 us)
Async XLA Ops:
  0.6 28.8 %copy-start.2 = (bf16[512,512]{1,0:T(8,128)(2,1)S(1)}, bf16[512,512]{1,0:T(8,128)(2,1)}, u32[]{:S(2)}) copy-start(bf16[512,512]{1,0:T(8,128)(2,1)} %keys.5) | copy-start | bytes 1572868
  0.6 28.8 %copy-start.4 = (bf16[512,512]{1,0:T(8,128)(2,1)S(1)}, bf16[512,512]{1,0:T(8,128)(2,1)}, u32[]{:S(2)}) copy-start(bf16[512,512]{1,0:T(8,128)(2,1)} %values.5) | copy-start | bytes 1572868
  2.8 26.6 %copy-start = (bf16[512,512]{1,0:T(8,128)(2,1)S(1)}, bf16[512,512]{1,0:T(8,128)(2,1)}, u32[]{:S(2)}) copy-start(bf16[512,512]{1,0:T(8,128)(2,1)} %refs_4_.3) | copy-start | bytes 1572868
  21.0 7.7 %collective-permute-start = (f32[64,128]{1,0:T(8,128)S(1)}, f32[64,128]{1,0:T(8,128)S(1)}, u32[]{:S(2)}, u32[]{:S(2)}) collective-permute-start(f32[64,128]{1,0:T(8,128)S(1)} %shard_map.102.refs_1_), channel_id=1, source_target_pairs={{0,128},{16,144},{32,160},{48,176},{64,192},{80,208},{96,224},{112... | collective-permute-start | bytes 98312 | tf_op jit(solution)/shard_map/ppermute | solution.py:336
  28.7 3.2 %collective-permute-start.1 = (f32[64,128]{1,0:T(8,128)S(1)}, f32[64,128]{1,0:T(8,128)S(1)}, u32[]{:S(2)}, u32[]{:S(2)}) collective-permute-start(f32[64,128]{1,0:T(8,128)S(1)} %shard_map.103.total), channel_id=1, source_target_pairs={{128,256},{144,272},{160,288},{176,304},{192,320},{208,336},{224,3... | collective-permute-start | bytes 98312 | tf_op jit(solution)/shard_map/ppermute | solution.py:336
  31.1 15.1 %copy-start.1 = (bf16[512,512]{1,0:T(8,128)(2,1)S(1)}, bf16[512,512]{1,0:T(8,128)(2,1)}, u32[]{:S(2)}) copy-start(bf16[512,512]{1,0:T(8,128)(2,1)} %refs_3_.3) | copy-start | bytes 1572868
  31.1 0.8 collective-permute-start.2
  46.2 0.7 copy-start.6
  46.9 14.6 %copy-start.8 = (f32[512,512]{1,0:T(8,128)}, f32[512,512]{1,0:T(8,128)S(1)}, u32[]{:S(2)}) copy-start(f32[512,512]{1,0:T(8,128)S(1)} %get-tuple-element.31.refs_2_) | copy-start | bytes 3145732
  61.4 5.9 %copy-start.7 = (f32[8,64,128]{2,1,0:T(8,128)S(1)}, f32[8,64,128]{2,1,0:T(8,128)}, u32[]{:S(2)}) copy-start(f32[8,64,128]{2,1,0:T(8,128)} %copy-done.6) | copy-start | bytes 786436
  61.5 14.7 %all-to-all-start.3 = ((f32[8,64,128]{2,1,0:T(8,128)}), f32[8,64,128]{2,1,0:T(8,128)S(1)}, u32[]{:S(2)}, u32[]{:S(2)}) async-start(f32[8,64,128]{2,1,0:T(8,128)} %get-tuple-element.34), calls=%async_computation.3 | async-start | bytes 524288 | tf_op jit(solution)/shard_map/all_to_all | solution.py:358
  99.9 15.3 %copy-start.5 = (bf16[512,512]{1,0:T(8,128)(2,1)S(1)}, bf16[512,512]{1,0:T(8,128)(2,1)}, u32[]{:S(2)}) copy-start(bf16[512,512]{1,0:T(8,128)(2,1)} %values.5) | copy-start | bytes 1572868
  100.0 15.3 %copy-start.3 = (bf16[512,512]{1,0:T(8,128)(2,1)S(1)}, bf16[512,512]{1,0:T(8,128)(2,1)}, u32[]{:S(2)}) copy-start(bf16[512,512]{1,0:T(8,128)(2,1)} %keys.5) | copy-start | bytes 1572868

commit v14 on v13

--- a/solution.py
+++ b/solution.py
@@ -101,7 +101,7 @@
     return (dot(a[t, :], b[s, :], 1, 1) * weight).astype(BF16)
 
 
-def intra_kernel(consts, queries, keys, values, total, out, total_out):
+def intra_kernel(consts, queries, keys, values, total, out, token):
     length = queries.shape[0]
     size = 128
     half = length // 2
@@ -114,7 +114,7 @@
         out[second, cols] = dot(weighted(q, k, second, first, across), v[first, :], 1, 0) + dot(
             weighted(q, k, second, second, same), v[second, :], 1, 0
         )
-    total_out[...] = total[...]
+    token[...] = jnp.zeros_like(token)
 
 
 def mixed_kernel(consts, queries, state, intra, cotangent, mixed, stats, square, inner):
@@ -293,7 +293,11 @@
     out[...] = total[...] + group_factor * before[...]
 
 
-def fold_forward_kernel(length, consts, parts, nearest, near, far, out):
+def copy_kernel(x, out):
+    out[...] = x[...]
+
+
+def fold_forward_kernel(length, consts, parts, nearest, near, far, token, out):
     factor, group_factor = fold_factors(consts, length)
     carry = nearest[...] + near[...] + group_factor * far[...]
     for k in range(GROUP):
@@ -345,9 +349,10 @@
     nearest = send(total, [(0, 1)])
     total = whole_call(lambda *refs: join_kernel(length, *refs), one, [consts, total, nearest])
     near = send(total, [(1, 2), (2, 3)])
-    result, total = beside(total)
+    total = whole_call(copy_kernel, one, [total])
     far = send(total, [(1, 3)])
-    out = whole_call(lambda *refs: fold_forward_kernel(length, *refs), like(x), [consts, parts, nearest, near, far])
+    result, token = beside(total)
+    out = whole_call(lambda *refs: fold_forward_kernel(length, *refs), like(x), [consts, parts, nearest, near, far, token])
     return lax.all_to_all(out, "seq", 0, 0, axis_index_groups=members), result
 
 
@@ -420,7 +425,7 @@
 
     def beside(total):
         return whole_call(
-            intra_kernel, [wide, array(F32, *total.shape)], [consts, queries, keys, values, total], cost_estimate=cost(2 * square)
+            intra_kernel, [wide, array(F32, 8, 128)], [consts, queries, keys, values, total], cost_estimate=cost(2 * square)
         )
 
     state_in, intra = scan_forward(sums, consts, length, beside)

time: 118 us -> 116 us (0.983)
    all_gather x1, blocking collectives: 23.8 us -> 21.9 us  [scan_back(): arrived = lax.all_gather(totals, 'seq', axis_index_groups=across)]
    pallas_call x11 -> x12, Pallas kernels: 13.8 us -> 13.8 us  [whole_call(): pl.pallas_call(kernel, in_specs=in_specs, out_specs=out_specs, out_shape=...]
where the time goes in v14:
time: 116 us
  blocking collectives  83.2 us (72%)
  Pallas kernels  13.8 us (12%)
  starting transfers between devices  13.6 us (12%)
  waiting for transfers between devices  4.07 us (4%)
    all_gather x1, blocking collectives, scan_back(): arrived = lax.all_gather(totals, 'seq', axis_index_groups=across)  21.9 us
    all_to_all x1, blocking collectives, scan_forward(): parts = lax.all_to_all(x, 'seq', 0, 0, axis_index_groups=members)  18.1 us
    all_to_all x1, blocking collectives, scan_back(): return (lax.all_to_all(out, 'seq', 0, 0, axis_index_groups=members), kept)  15.5 us
    all_to_all x1, blocking collectives, scan_forward(): return (lax.all_to_all(out, 'seq', 0, 0, axis_index_groups=members), result)  14.5 us
    pallas_call x12, Pallas kernels, whole_call(): pl.pallas_call(kernel, in_specs=in_specs, out_specs=out_specs, out_shape=...  13.8 us
    all_to_all x1, blocking collectives, body(): received = lax.all_to_all(stats, 'head', 0, 0)  13.1 us
    ppermute x3, starting transfers between devices, send(): lax.ppermute(x, 'seq', [(a * GROUP + j, b * GROUP + j) for a, b in pairs...  8.06 us
    all_to_all x1, starting transfers between devices, scan_back(): parts = lax.all_to_all(x, 'seq', 0, 0, axis_index_groups=members)  5.56 us
  transfers between devices with their start and end apart: 4, of which 2 were waited for; matrix products, arithmetic and copies ran while one was open for 0% of the time, Pallas kernels for 6%

profile of v14, /device:TPU:1, one launch (start us, length us, event | category | flops | bytes accessed | tf_op | source)
XLA Modules:
  0.0 115.6 jit_solution(10907806179160597759)
XLA Ops:
  0.6 0.0 copy-start.2
  0.6 0.0 copy-start.4
  0.7 2.1 %shard_map.101 = (f32[8,64,128]{2,1,0:T(8,128)S(1)}, f32[8,512]{1,0:T(8,128)S(1)}) custom-call(f32[4]{0:T(128)} %rates_in.1, f32[1,512]{1,0:T(1,128)} %bitcast.4, bf16[512,512]{1,0:T(8,128)(2,1)} %keys.5, bf16[512,512]{1,0:T(8,128)(2,1)} %values.5), custom_call_target="tpu_custom_call" | custom-call | tf_op jit(solution)/shard_map/pallas_call | solution.py:329
  2.8 0.0 copy-start
  2.8 18.1 %all_to_all.25.refs_1_ = f32[8,64,128]{2,1,0:T(8,128)S(1)} all-to-all(f32[8,64,128]{2,1,0:T(8,128)S(1)} %get-tuple-element.27), channel_id=1, replica_groups={{0,16,32,48,64,80,96,112},{128,144,160,176,192,208,224,240},{256,272,28..., dimensions={0} | all-to-all | bytes 524288 | tf_op jit(solution)/shard_map/all_to_all | solution.py:346
  21.0 6.7 %collective-permute-start = (f32[64,128]{1,0:T(8,128)S(1)}, f32[64,128]{1,0:T(8,128)S(1)}, u32[]{:S(2)}, u32[]{:S(2)}) collective-permute-start(f32[64,128]{1,0:T(8,128)S(1)} %shard_map.102.refs_1_), channel_id=1, source_target_pairs={{0,128},{16,144},{32,160},{48,176},{64,192},{80,208},{96,224},{112... | collective-permute-start | bytes 98312 | tf_op jit(solution)/shard_map/ppermute | solution.py:340
  27.7 1.0 collective-permute-done.refs_2_
  28.7 0.7 collective-permute-start.1
  29.4 0.7 collective-permute-start.2
  30.1 1.7 %shard_map.105 = (f32[512,512]{1,0:T(8,128)S(1)}, f32[8,128]{1,0:T(8,128)S(1)}) custom-call(f32[8,512]{1,0:T(8,128)S(1)} %get-tuple-element.26.refs_0_.consts, bf16[512,512]{1,0:T(8,128)(2,1)S(1)} %copy-done, bf16[512,512]{1,0:T(8,128)(2,1)S(1)} %copy-done.2, bf16[512,512]{1,0:T(8,128)(2,1)S(1)} %copy-done.4, f32[64,128]{1,0:T(8,128)S(1)} %shard_map.104.total), custom_call_target="tpu_custom_call" | custom-call | flops 536870912 | bytes 6291456 | tf_op jit(solution)/shard_map/pallas_call | solution.py:329
  31.8 0.0 copy-start.1
  31.8 0.1 shard_map.106
  31.9 14.5 %all_to_all.26.state.refs_7_ = f32[8,64,128]{2,1,0:T(8,128)S(1)} all-to-all(f32[8,64,128]{2,1,0:T(8,128)S(1)} %shard_map.106), channel_id=1, replica_groups={{0,16,32,48,64,80,96,112},{128,144,160,176,192,208,224,240},{256,272,28..., dimensions={0} | all-to-all | bytes 524288 | tf_op jit(solution)/shard_map/all_to_all | solution.py:356
  46.4 0.6 shard_map.107
  47.0 0.1 copy-done.6
  47.1 13.1 %all_to_all.27.refs_1_ = f32[16,8,128]{2,1,0:T(8,128)S(1)} all-to-all(f32[16,8,128]{2,1,0:T(8,128)S(1)} %get-tuple-element.30), channel_id=1, replica_groups=mesh['seq'=32,'head'=16] {'head'}, dimensions={0} | all-to-all | bytes 131072 | tf_op jit(solution)/shard_map/all_to_all | solution.py:436
  60.2 1.5 %shard_map.109 = (f32[8,64,128]{2,1,0:T(8,128)}, f32[8,128]{1,0:T(8,128)S(1)}) custom-call(f32[8,512]{1,0:T(8,128)S(1)} %get-tuple-element.26.refs_0_.consts, f32[16,8,128]{2,1,0:T(8,128)S(1)} %all_to_all.27.refs_1_, f32[512,512]{1,0:T(8,128)S(1)} %get-tuple-element.31.refs_2_, bf16[512,512]{1,0:T(8,128)(2,1)S(1)} %copy-done.1, bf16[512,512]{1,0:T(8,128)(2,1)S(1)} %copy-done), custom_call_target="tpu_custom_call" | custom-call | tf_op jit(solution)/shard_map/pallas_call | solution.py:329
  61.7 5.6 %all-to-all-start.3 = ((f32[8,64,128]{2,1,0:T(8,128)}), f32[8,64,128]{2,1,0:T(8,128)S(1)}, u32[]{:S(2)}, u32[]{:S(2)}) async-start(f32[8,64,128]{2,1,0:T(8,128)} %get-tuple-element.34), calls=%async_computation.3 | async-start | bytes 524288 | tf_op jit(solution)/shard_map/all_to_all | solution.py:363
  67.3 5.7 %shard_map.108 = (bf16[512,512]{1,0:T(8,128)(2,1)}, bf16[512,512]{1,0:T(8,128)(2,1)}, f32[512,512]{1,0:T(8,128)S(1)}, f32[512,512]{1,0:T(8,128)S(1)}) custom-call(f32[8,512]{1,0:T(8,128)S(1)} %get-tuple-element.26.refs_0_.consts, f32[16,8,128]{2,1,0:T(8,128)S(1)} %all_to_all.27.refs_1_, f32[512,512]{1,0:T(8,128)} %copy-done.8, bf16[512,512]{1,0:T(8,128)(2,1)} %refs_3_.3, ...), custom_call_target="tpu_custom_call" | custom-call | flops 1610612736 | bytes 6291456 | tf_op jit(solution)/shard_map/pallas_call | solution.py:329
  73.0 3.1 %all-to-all-done.3.refs_1_ = f32[8,64,128]{2,1,0:T(8,128)S(1)} async-done(((f32[8,64,128]{2,1,0:T(8,128)}), f32[8,64,128]{2,1,0:T(8,128)S(1)}, u32[]{:S(2)}, u32[]{:S(2)}) %all-to-all-start.3) | async-done | bytes 262176 | tf_op jit(solution)/shard_map/all_to_all | solution.py:363
  76.1 21.9 %all-gather = f32[288,128]{1,0:T(8,128)S(1)} all-gather(f32[72,128]{1,0:T(8,128)S(1)} %get-tuple-element.38), channel_id=2, replica_groups={{0,128,256,384},{16,144,272,400},{32,160,288,416},{48,176,304,432},{64,..., dimensions={0}, use_global_device_ids=true | all-gather | bytes 184320 | tf_op jit(solution)/shard_map/all_gather | solution.py:367
  98.0 0.1 shard_map.111
  98.1 15.5 %all_to_all.28.back = f32[8,72,128]{2,1,0:T(8,128)S(1)} all-to-all(f32[8,72,128]{2,1,0:T(8,128)S(1)} %get-tuple-element.41), channel_id=1, replica_groups={{0,16,32,48,64,80,96,112},{128,144,160,176,192,208,224,240},{256,272,28..., dimensions={0} | all-to-all | bytes 589824 | tf_op jit(solution)/shard_map/all_to_all | solution.py:371
  113.6 2.0 %shard_map.112 = (bf16[512,512]{1,0:T(8,128)(2,1)}, bf16[512,512]{1,0:T(8,128)(2,1)}, f32[1,512]{1,0:T(1,128)}) custom-call(f32[8,512]{1,0:T(8,128)S(1)} %get-tuple-element.26.refs_0_.consts, f32[8,72,128]{2,1,0:T(8,128)S(1)} %all_to_all.28.back, bf16[512,512]{1,0:T(8,128)(2,1)S(1)} %copy-done.3, bf16[512,512]{1,0:T(8,128)(2,1)S(1)} %copy-done.5, ...), custom_call_target="tpu_custom_call" | custom-call | tf_op jit(solution)/shard_map/pallas_call | solution.py:329
  (19 shorter events, 0.1 us)
Async XLA Ops:
  0.6 29.5 %copy-start.2 = (bf16[512,512]{1,0:T(8,128)(2,1)S(1)}, bf16[512,512]{1,0:T(8,128)(2,1)}, u32[]{:S(2)}) copy-start(bf16[512,512]{1,0:T(8,128)(2,1)} %keys.5) | copy-start | bytes 1572868
  0.6 29.5 %copy-start.4 = (bf16[512,512]{1,0:T(8,128)(2,1)S(1)}, bf16[512,512]{1,0:T(8,128)(2,1)}, u32[]{:S(2)}) copy-start(bf16[512,512]{1,0:T(8,128)(2,1)} %values.5) | copy-start | bytes 1572868
  2.8 27.3 %copy-start = (bf16[512,512]{1,0:T(8,128)(2,1)S(1)}, bf16[512,512]{1,0:T(8,128)(2,1)}, u32[]{:S(2)}) copy-start(bf16[512,512]{1,0:T(8,128)(2,1)} %refs_4_.3) | copy-start | bytes 1572868
  21.0 7.7 %collective-permute-start = (f32[64,128]{1,0:T(8,128)S(1)}, f32[64,128]{1,0:T(8,128)S(1)}, u32[]{:S(2)}, u32[]{:S(2)}) collective-permute-start(f32[64,128]{1,0:T(8,128)S(1)} %shard_map.102.refs_1_), channel_id=1, source_target_pairs={{0,128},{16,144},{32,160},{48,176},{64,192},{80,208},{96,224},{112... | collective-permute-start | bytes 98312 | tf_op jit(solution)/shard_map/ppermute | solution.py:340
  28.7 3.1 %collective-permute-start.1 = (f32[64,128]{1,0:T(8,128)S(1)}, f32[64,128]{1,0:T(8,128)S(1)}, u32[]{:S(2)}, u32[]{:S(2)}) collective-permute-start(f32[64,128]{1,0:T(8,128)S(1)} %shard_map.103.x), channel_id=1, source_target_pairs={{128,256},{144,272},{160,288},{176,304},{192,320},{208,336},{224,3... | collective-permute-start | bytes 98312 | tf_op jit(solution)/shard_map/ppermute | solution.py:340
  29.4 2.4 %collective-permute-start.2 = (f32[64,128]{1,0:T(8,128)S(1)}, f32[64,128]{1,0:T(8,128)S(1)}, u32[]{:S(2)}, u32[]{:S(2)}) collective-permute-start(f32[64,128]{1,0:T(8,128)S(1)} %shard_map.104.total), channel_id=1, source_target_pairs={{128,384},{144,400},{160,416},{176,432},{192,448},{208,464},{224,4... | collective-permute-start | bytes 98312 | tf_op jit(solution)/shard_map/ppermute | solution.py:340
  31.8 14.6 %copy-start.1 = (bf16[512,512]{1,0:T(8,128)(2,1)S(1)}, bf16[512,512]{1,0:T(8,128)(2,1)}, u32[]{:S(2)}) copy-start(bf16[512,512]{1,0:T(8,128)(2,1)} %refs_3_.3) | copy-start | bytes 1572868
  46.4 0.7 copy-start.6
  47.1 14.6 %copy-start.8 = (f32[512,512]{1,0:T(8,128)}, f32[512,512]{1,0:T(8,128)S(1)}, u32[]{:S(2)}) copy-start(f32[512,512]{1,0:T(8,128)S(1)} %get-tuple-element.31.refs_2_) | copy-start | bytes 3145732
  61.7 5.6 %copy-start.7 = (f32[8,64,128]{2,1,0:T(8,128)S(1)}, f32[8,64,128]{2,1,0:T(8,128)}, u32[]{:S(2)}) copy-start(f32[8,64,128]{2,1,0:T(8,128)} %copy-done.6) | copy-start | bytes 786436
  61.7 14.3 %all-to-all-start.3 = ((f32[8,64,128]{2,1,0:T(8,128)}), f32[8,64,128]{2,1,0:T(8,128)S(1)}, u32[]{:S(2)}, u32[]{:S(2)}) async-start(f32[8,64,128]{2,1,0:T(8,128)} %get-tuple-element.34), calls=%async_computation.3 | async-start | bytes 524288 | tf_op jit(solution)/shard_map/all_to_all | solution.py:363
  98.0 15.6 %copy-start.5 = (bf16[512,512]{1,0:T(8,128)(2,1)S(1)}, bf16[512,512]{1,0:T(8,128)(2,1)}, u32[]{:S(2)}) copy-start(bf16[512,512]{1,0:T(8,128)(2,1)} %values.5) | copy-start | bytes 1572868
  98.1 15.5 %copy-start.3 = (bf16[512,512]{1,0:T(8,128)(2,1)S(1)}, bf16[512,512]{1,0:T(8,128)(2,1)}, u32[]{:S(2)}) copy-start(bf16[512,512]{1,0:T(8,128)(2,1)} %keys.5) | copy-start | bytes 1572868

commit v15 on v14

--- a/solution.py
+++ b/solution.py
@@ -169,9 +169,12 @@
         mixed_grad = mixed_grad_of(consts, cols, upstream, value, inv[...], coef[...])
         scaled = mixed_grad.astype(F32) * head_in_of(consts[pl.ds(RATE, 1), cols], length)
         sums[shards] = dot_split(queries[:, cols], scaled, 0, 0).reshape(2, size // 2, size)
-        gains[pl.ds(h, 1), :] = jnp.sum(upstream * (value * inv[...]), axis=0, keepdims=True)
         stores.append(pltpu.make_async_copy(sums.at[shards], sums_out.at[shards], sent.at[h]))
         stores[-1].start()
+    for h in range(heads):
+        cols = column(h, size)
+        products = cotangent[:, cols].astype(F32) * (mixed[:, cols] * inv[...])
+        gains[pl.ds(h, 1), :] = jnp.sum(products, axis=0, keepdims=True)
     for store in stores:
         store.wait()
 
@@ -250,7 +253,6 @@
     for h in range(heads):
         cols = column(h, size)
         back_in = back[pl.ds(2 * h, 2), pl.ds(0, half), :].reshape(size, size)
-        gain_grad[:, cols] = sum(back[k, pl.ds(half + h, 1), :] for k in range(GROUP))
         tail = tail_out_of(consts[pl.ds(RATE, 1), cols], length)
         key_rows[:, cols] = (key_part[:, cols] + tail * dot_split(values[:, cols], back_in, 1, 1)).astype(BF16)
         value_rows[:, cols] = (value_part[:, cols] + tail * dot_split(keys[:, cols], back_in, 1, 0)).astype(BF16)
@@ -258,6 +260,8 @@
             copy = pltpu.make_async_copy(rows.at[:, cols], target.at[:, cols], sent.at[2 * h + i])
             copy.start()
             copies.append(copy)
+    for h in range(heads):
+        gain_grad[:, column(h, size)] = sum(back[k, pl.ds(half + h, 1), :] for k in range(GROUP))
     for copy in copies:
         copy.wait()
 

time: 116 us -> 116 us (level)
  no operation moved by 1% of the time
where the time goes in v15:
time: 116 us
  blocking collectives  83.2 us (72%)
  Pallas kernels  13.8 us (12%)
  starting transfers between devices  13.6 us (12%)
  waiting for transfers between devices  4.07 us (4%)
    all_gather x1, blocking collectives, scan_back(): arrived = lax.all_gather(totals, 'seq', axis_index_groups=across)  22 us
    all_to_all x1, blocking collectives, scan_forward(): parts = lax.all_to_all(x, 'seq', 0, 0, axis_index_groups=members)  18.1 us
    all_to_all x1, blocking collectives, scan_back(): return (lax.all_to_all(out, 'seq', 0, 0, axis_index_groups=members), kept)  15.5 us
    all_to_all x1, blocking collectives, scan_forward(): return (lax.all_to_all(out, 'seq', 0, 0, axis_index_groups=members), result)  14.5 us
    pallas_call x12, Pallas kernels, whole_call(): pl.pallas_call(kernel, in_specs=in_specs, out_specs=out_specs, out_shape=...  13.8 us
    all_to_all x1, blocking collectives, body(): received = lax.all_to_all(stats, 'head', 0, 0)  13.1 us
    ppermute x3, starting transfers between devices, send(): lax.ppermute(x, 'seq', [(a * GROUP + j, b * GROUP + j) for a, b in pairs...  8.06 us
    all_to_all x1, starting transfers between devices, scan_back(): parts = lax.all_to_all(x, 'seq', 0, 0, axis_index_groups=members)  5.56 us
  transfers between devices with their start and end apart: 4, of which 2 were waited for; matrix products, arithmetic and copies ran while one was open for 0% of the time, Pallas kernels for 6%

profile of v15, /device:TPU:1, one launch (start us, length us, event | category | flops | bytes accessed | tf_op | source)
XLA Modules:
  0.0 115.7 jit_solution(12127683704119137287)
XLA Ops:
  0.6 0.0 copy-start.2
  0.7 2.1 %shard_map.101 = (f32[8,64,128]{2,1,0:T(8,128)S(1)}, f32[8,512]{1,0:T(8,128)S(1)}) custom-call(f32[4]{0:T(128)} %rates_in.1, f32[1,512]{1,0:T(1,128)} %bitcast.4, bf16[512,512]{1,0:T(8,128)(2,1)} %keys.5, bf16[512,512]{1,0:T(8,128)(2,1)} %values.5), custom_call_target="tpu_custom_call" | custom-call | tf_op jit(solution)/shard_map/pallas_call | solution.py:333
  2.8 0.0 copy-start
  2.8 18.1 %all_to_all.25.refs_1_ = f32[8,64,128]{2,1,0:T(8,128)S(1)} all-to-all(f32[8,64,128]{2,1,0:T(8,128)S(1)} %get-tuple-element.27), channel_id=1, replica_groups={{0,16,32,48,64,80,96,112},{128,144,160,176,192,208,224,240},{256,272,28..., dimensions={0} | all-to-all | bytes 524288 | tf_op jit(solution)/shard_map/all_to_all | solution.py:350
  21.0 6.7 %collective-permute-start = (f32[64,128]{1,0:T(8,128)S(1)}, f32[64,128]{1,0:T(8,128)S(1)}, u32[]{:S(2)}, u32[]{:S(2)}) collective-permute-start(f32[64,128]{1,0:T(8,128)S(1)} %shard_map.102.refs_1_), channel_id=1, source_target_pairs={{0,128},{16,144},{32,160},{48,176},{64,192},{80,208},{96,224},{112... | collective-permute-start | bytes 98312 | tf_op jit(solution)/shard_map/ppermute | solution.py:344
  27.7 1.0 collective-permute-done.refs_2_
  28.7 0.7 collective-permute-start.1
  29.4 0.7 collective-permute-start.2
  30.1 1.7 %shard_map.105 = (f32[512,512]{1,0:T(8,128)S(1)}, f32[8,128]{1,0:T(8,128)S(1)}) custom-call(f32[8,512]{1,0:T(8,128)S(1)} %get-tuple-element.26.refs_0_.consts, bf16[512,512]{1,0:T(8,128)(2,1)S(1)} %copy-done, bf16[512,512]{1,0:T(8,128)(2,1)S(1)} %copy-done.2, bf16[512,512]{1,0:T(8,128)(2,1)S(1)} %copy-done.4, f32[64,128]{1,0:T(8,128)S(1)} %shard_map.104.total), custom_call_target="tpu_custom_call" | custom-call | flops 536870912 | bytes 6291456 | tf_op jit(solution)/shard_map/pallas_call | solution.py:333
  31.8 0.0 copy-start.1
  31.8 0.1 shard_map.106
  31.9 14.5 %all_to_all.26.state.refs_7_ = f32[8,64,128]{2,1,0:T(8,128)S(1)} all-to-all(f32[8,64,128]{2,1,0:T(8,128)S(1)} %shard_map.106), channel_id=1, replica_groups={{0,16,32,48,64,80,96,112},{128,144,160,176,192,208,224,240},{256,272,28..., dimensions={0} | all-to-all | bytes 524288 | tf_op jit(solution)/shard_map/all_to_all | solution.py:360
  46.4 0.6 shard_map.107
  47.0 0.1 copy-done.6
  47.1 13.1 %all_to_all.27.refs_1_ = f32[16,8,128]{2,1,0:T(8,128)S(1)} all-to-all(f32[16,8,128]{2,1,0:T(8,128)S(1)} %get-tuple-element.30), channel_id=1, replica_groups=mesh['seq'=32,'head'=16] {'head'}, dimensions={0} | all-to-all | bytes 131072 | tf_op jit(solution)/shard_map/all_to_all | solution.py:440
  60.2 1.5 %shard_map.109 = (f32[8,64,128]{2,1,0:T(8,128)}, f32[8,128]{1,0:T(8,128)S(1)}) custom-call(f32[8,512]{1,0:T(8,128)S(1)} %get-tuple-element.26.refs_0_.consts, f32[16,8,128]{2,1,0:T(8,128)S(1)} %all_to_all.27.refs_1_, f32[512,512]{1,0:T(8,128)S(1)} %get-tuple-element.31.refs_2_, bf16[512,512]{1,0:T(8,128)(2,1)S(1)} %copy-done.1, bf16[512,512]{1,0:T(8,128)(2,1)S(1)} %copy-done), custom_call_target="tpu_custom_call" | custom-call | tf_op jit(solution)/shard_map/pallas_call | solution.py:333
  61.8 0.0 copy-start.7
  61.8 5.6 %all-to-all-start.3 = ((f32[8,64,128]{2,1,0:T(8,128)}), f32[8,64,128]{2,1,0:T(8,128)S(1)}, u32[]{:S(2)}, u32[]{:S(2)}) async-start(f32[8,64,128]{2,1,0:T(8,128)} %get-tuple-element.34), calls=%async_computation.3 | async-start | bytes 524288 | tf_op jit(solution)/shard_map/all_to_all | solution.py:367
  67.3 5.7 %shard_map.108 = (bf16[512,512]{1,0:T(8,128)(2,1)}, bf16[512,512]{1,0:T(8,128)(2,1)}, f32[512,512]{1,0:T(8,128)S(1)}, f32[512,512]{1,0:T(8,128)S(1)}) custom-call(f32[8,512]{1,0:T(8,128)S(1)} %get-tuple-element.26.refs_0_.consts, f32[16,8,128]{2,1,0:T(8,128)S(1)} %all_to_all.27.refs_1_, f32[512,512]{1,0:T(8,128)} %copy-done.8, bf16[512,512]{1,0:T(8,128)(2,1)} %refs_3_.3, ...), custom_call_target="tpu_custom_call" | custom-call | flops 1610612736 | bytes 6291456 | tf_op jit(solution)/shard_map/pallas_call | solution.py:333
  73.0 3.1 %all-to-all-done.3.refs_1_ = f32[8,64,128]{2,1,0:T(8,128)S(1)} async-done(((f32[8,64,128]{2,1,0:T(8,128)}), f32[8,64,128]{2,1,0:T(8,128)S(1)}, u32[]{:S(2)}, u32[]{:S(2)}) %all-to-all-start.3) | async-done | bytes 262176 | tf_op jit(solution)/shard_map/all_to_all | solution.py:367
  76.1 22.0 %all-gather = f32[288,128]{1,0:T(8,128)S(1)} all-gather(f32[72,128]{1,0:T(8,128)S(1)} %get-tuple-element.38), channel_id=2, replica_groups={{0,128,256,384},{16,144,272,400},{32,160,288,416},{48,176,304,432},{64,..., dimensions={0}, use_global_device_ids=true | all-gather | bytes 184320 | tf_op jit(solution)/shard_map/all_gather | solution.py:371
  98.1 0.1 shard_map.111
  98.1 15.5 %all_to_all.28.back = f32[8,72,128]{2,1,0:T(8,128)S(1)} all-to-all(f32[8,72,128]{2,1,0:T(8,128)S(1)} %get-tuple-element.41), channel_id=1, replica_groups={{0,16,32,48,64,80,96,112},{128,144,160,176,192,208,224,240},{256,272,28..., dimensions={0} | all-to-all | bytes 589824 | tf_op jit(solution)/shard_map/all_to_all | solution.py:375
  113.6 2.0 %shard_map.112 = (bf16[512,512]{1,0:T(8,128)(2,1)}, bf16[512,512]{1,0:T(8,128)(2,1)}, f32[1,512]{1,0:T(1,128)}) custom-call(f32[8,512]{1,0:T(8,128)S(1)} %get-tuple-element.26.refs_0_.consts, f32[8,72,128]{2,1,0:T(8,128)S(1)} %all_to_all.28.back, bf16[512,512]{1,0:T(8,128)(2,1)S(1)} %copy-done.3, bf16[512,512]{1,0:T(8,128)(2,1)S(1)} %copy-done.5, ...), custom_call_target="tpu_custom_call" | custom-call | tf_op jit(solution)/shard_map/pallas_call | solution.py:333
  (19 shorter events, 0.1 us)
Async XLA Ops:
  0.6 29.5 %copy-start.2 = (bf16[512,512]{1,0:T(8,128)(2,1)S(1)}, bf16[512,512]{1,0:T(8,128)(2,1)}, u32[]{:S(2)}) copy-start(bf16[512,512]{1,0:T(8,128)(2,1)} %keys.5) | copy-start | bytes 1572868
  0.6 29.5 %copy-start.4 = (bf16[512,512]{1,0:T(8,128)(2,1)S(1)}, bf16[512,512]{1,0:T(8,128)(2,1)}, u32[]{:S(2)}) copy-start(bf16[512,512]{1,0:T(8,128)(2,1)} %values.5) | copy-start | bytes 1572868
  2.8 27.3 %copy-start = (bf16[512,512]{1,0:T(8,128)(2,1)S(1)}, bf16[512,512]{1,0:T(8,128)(2,1)}, u32[]{:S(2)}) copy-start(bf16[512,512]{1,0:T(8,128)(2,1)} %refs_4_.3) | copy-start | bytes 1572868
  21.0 7.7 %collective-permute-start = (f32[64,128]{1,0:T(8,128)S(1)}, f32[64,128]{1,0:T(8,128)S(1)}, u32[]{:S(2)}, u32[]{:S(2)}) collective-permute-start(f32[64,128]{1,0:T(8,128)S(1)} %shard_map.102.refs_1_), channel_id=1, source_target_pairs={{0,128},{16,144},{32,160},{48,176},{64,192},{80,208},{96,224},{112... | collective-permute-start | bytes 98312 | tf_op jit(solution)/shard_map/ppermute | solution.py:344
  28.7 3.1 %collective-permute-start.1 = (f32[64,128]{1,0:T(8,128)S(1)}, f32[64,128]{1,0:T(8,128)S(1)}, u32[]{:S(2)}, u32[]{:S(2)}) collective-permute-start(f32[64,128]{1,0:T(8,128)S(1)} %shard_map.103.x), channel_id=1, source_target_pairs={{128,256},{144,272},{160,288},{176,304},{192,320},{208,336},{224,3... | collective-permute-start | bytes 98312 | tf_op jit(solution)/shard_map/ppermute | solution.py:344
  29.4 2.4 %collective-permute-start.2 = (f32[64,128]{1,0:T(8,128)S(1)}, f32[64,128]{1,0:T(8,128)S(1)}, u32[]{:S(2)}, u32[]{:S(2)}) collective-permute-start(f32[64,128]{1,0:T(8,128)S(1)} %shard_map.104.total), channel_id=1, source_target_pairs={{128,384},{144,400},{160,416},{176,432},{192,448},{208,464},{224,4... | collective-permute-start | bytes 98312 | tf_op jit(solution)/shard_map/ppermute | solution.py:344
  31.8 14.6 %copy-start.1 = (bf16[512,512]{1,0:T(8,128)(2,1)S(1)}, bf16[512,512]{1,0:T(8,128)(2,1)}, u32[]{:S(2)}) copy-start(bf16[512,512]{1,0:T(8,128)(2,1)} %refs_3_.3) | copy-start | bytes 1572868
  46.4 0.7 copy-start.6
  47.1 14.6 %copy-start.8 = (f32[512,512]{1,0:T(8,128)}, f32[512,512]{1,0:T(8,128)S(1)}, u32[]{:S(2)}) copy-start(f32[512,512]{1,0:T(8,128)S(1)} %get-tuple-element.31.refs_2_) | copy-start | bytes 3145732
  61.8 5.6 %copy-start.7 = (f32[8,64,128]{2,1,0:T(8,128)S(1)}, f32[8,64,128]{2,1,0:T(8,128)}, u32[]{:S(2)}) copy-start(f32[8,64,128]{2,1,0:T(8,128)} %copy-done.6) | copy-start | bytes 786436
  61.8 14.3 %all-to-all-start.3 = ((f32[8,64,128]{2,1,0:T(8,128)}), f32[8,64,128]{2,1,0:T(8,128)S(1)}, u32[]{:S(2)}, u32[]{:S(2)}) async-start(f32[8,64,128]{2,1,0:T(8,128)} %get-tuple-element.34), calls=%async_computation.3 | async-start | bytes 524288 | tf_op jit(solution)/shard_map/all_to_all | solution.py:367
  98.0 15.6 %copy-start.5 = (bf16[512,512]{1,0:T(8,128)(2,1)S(1)}, bf16[512,512]{1,0:T(8,128)(2,1)}, u32[]{:S(2)}) copy-start(bf16[512,512]{1,0:T(8,128)(2,1)} %values.5) | copy-start | bytes 1572868
  98.1 15.5 %copy-start.3 = (bf16[512,512]{1,0:T(8,128)(2,1)S(1)}, bf16[512,512]{1,0:T(8,128)(2,1)}, u32[]{:S(2)}) copy-start(bf16[512,512]{1,0:T(8,128)(2,1)} %keys.5) | copy-start | bytes 1572868

commit v16 on v15

--- a/solution.py
+++ b/solution.py
@@ -70,6 +70,7 @@
         pltpu.make_async_copy(rates_in, rates, arrived.at[2 * heads]),
         pltpu.make_async_copy(gain_in, gain, arrived.at[2 * heads + 1]),
     ]
+    small[0].start()
     copies = []
     for h in range(heads):
         cols = column(h, size)
@@ -81,20 +82,20 @@
         )
         for copy in copies[-1]:
             copy.start()
-        if h == 0:
-            for copy in small:
-                copy.start()
-    for copy in small:
-        copy.wait()
-    for h in range(heads):
-        cols = column(h, size)
-        rate = jnp.full((1, size), rates[h], F32)
-        consts[:, cols] = jnp.concatenate([gain[:, cols], rate, jnp.zeros((6, size), F32)], axis=0)
-        tail = tail_out_of(rate, length)
+    small[1].start()
+    small[0].wait()
+    for h in range(heads):
+        cols = column(h, size)
+        tail = tail_out_of(jnp.full((1, size), rates[h], F32), length)
         for copy in copies[h]:
             copy.wait()
         scaled = value_rows[:, cols].astype(F32) * tail
         out[pl.ds(2 * h, 2)] = dot_split(key_rows[:, cols], scaled, 0, 0).reshape(2, size // 2, size)
+    small[1].wait()
+    for h in range(heads):
+        cols = column(h, size)
+        rate = jnp.full((1, size), rates[h], F32)
+        consts[:, cols] = jnp.concatenate([gain[:, cols], rate, jnp.zeros((6, size), F32)], axis=0)
 
 
 def weighted(a, b, t, s, weight):

time: 116 us -> 116 us (level)
  no operation moved by 1% of the time
where the time goes in v16:
time: 116 us
  blocking collectives  83.2 us (72%)
  Pallas kernels  13.8 us (12%)
  starting transfers between devices  13.6 us (12%)
  waiting for transfers between devices  4.07 us (4%)
    all_gather x1, blocking collectives, scan_back(): arrived = lax.all_gather(totals, 'seq', axis_index_groups=across)  22 us
    all_to_all x1, blocking collectives, scan_forward(): parts = lax.all_to_all(x, 'seq', 0, 0, axis_index_groups=members)  18.1 us
    all_to_all x1, blocking collectives, scan_back(): return (lax.all_to_all(out, 'seq', 0, 0, axis_index_groups=members), kept)  15.5 us
    all_to_all x1, blocking collectives, scan_forward(): return (lax.all_to_all(out, 'seq', 0, 0, axis_index_groups=members), result)  14.5 us
    pallas_call x12, Pallas kernels, whole_call(): pl.pallas_call(kernel, in_specs=in_specs, out_specs=out_specs, out_shape=...  13.8 us
    all_to_all x1, blocking collectives, body(): received = lax.all_to_all(stats, 'head', 0, 0)  13.1 us
    ppermute x3, starting transfers between devices, send(): lax.ppermute(x, 'seq', [(a * GROUP + j, b * GROUP + j) for a, b in pairs...  8.06 us
    all_to_all x1, starting transfers between devices, scan_back(): parts = lax.all_to_all(x, 'seq', 0, 0, axis_index_groups=members)  5.56 us
  transfers between devices with their start and end apart: 4, of which 2 were waited for; matrix products, arithmetic and copies ran while one was open for 0% of the time, Pallas kernels for 6%

profile of v16, /device:TPU:1, one launch (start us, length us, event | category | flops | bytes accessed | tf_op | source)
XLA Modules:
  0.0 115.7 jit_solution(16764927895340628372)
XLA Ops:
  0.6 0.0 copy-start.2
  0.6 0.0 copy-start.4
  0.7 2.1 %shard_map.101 = (f32[8,64,128]{2,1,0:T(8,128)S(1)}, f32[8,512]{1,0:T(8,128)S(1)}) custom-call(f32[4]{0:T(128)} %rates_in.1, f32[1,512]{1,0:T(1,128)} %bitcast.4, bf16[512,512]{1,0:T(8,128)(2,1)} %keys.5, bf16[512,512]{1,0:T(8,128)(2,1)} %values.5), custom_call_target="tpu_custom_call" | custom-call | tf_op jit(solution)/shard_map/pallas_call | solution.py:334
  2.8 0.0 copy-start
  2.8 18.1 %all_to_all.25.refs_1_ = f32[8,64,128]{2,1,0:T(8,128)S(1)} all-to-all(f32[8,64,128]{2,1,0:T(8,128)S(1)} %get-tuple-element.27), channel_id=1, replica_groups={{0,16,32,48,64,80,96,112},{128,144,160,176,192,208,224,240},{256,272,28..., dimensions={0} | all-to-all | bytes 524288 | tf_op jit(solution)/shard_map/all_to_all | solution.py:351
  21.0 6.7 %collective-permute-start = (f32[64,128]{1,0:T(8,128)S(1)}, f32[64,128]{1,0:T(8,128)S(1)}, u32[]{:S(2)}, u32[]{:S(2)}) collective-permute-start(f32[64,128]{1,0:T(8,128)S(1)} %shard_map.102.refs_1_), channel_id=1, source_target_pairs={{0,128},{16,144},{32,160},{48,176},{64,192},{80,208},{96,224},{112... | collective-permute-start | bytes 98312 | tf_op jit(solution)/shard_map/ppermute | solution.py:345
  27.7 1.0 collective-permute-done.refs_2_
  28.7 0.7 collective-permute-start.1
  29.4 0.7 collective-permute-start.2
  30.1 1.7 %shard_map.105 = (f32[512,512]{1,0:T(8,128)S(1)}, f32[8,128]{1,0:T(8,128)S(1)}) custom-call(f32[8,512]{1,0:T(8,128)S(1)} %get-tuple-element.26.refs_0_.consts, bf16[512,512]{1,0:T(8,128)(2,1)S(1)} %copy-done, bf16[512,512]{1,0:T(8,128)(2,1)S(1)} %copy-done.2, bf16[512,512]{1,0:T(8,128)(2,1)S(1)} %copy-done.4, f32[64,128]{1,0:T(8,128)S(1)} %shard_map.104.total), custom_call_target="tpu_custom_call" | custom-call | flops 536870912 | bytes 6291456 | tf_op jit(solution)/shard_map/pallas_call | solution.py:334
  31.8 0.0 copy-start.1
  31.8 0.1 shard_map.106
  31.9 14.5 %all_to_all.26.state.refs_7_ = f32[8,64,128]{2,1,0:T(8,128)S(1)} all-to-all(f32[8,64,128]{2,1,0:T(8,128)S(1)} %shard_map.106), channel_id=1, replica_groups={{0,16,32,48,64,80,96,112},{128,144,160,176,192,208,224,240},{256,272,28..., dimensions={0} | all-to-all | bytes 524288 | tf_op jit(solution)/shard_map/all_to_all | solution.py:361
  46.4 0.6 shard_map.107
  47.0 0.1 copy-done.6
  47.1 13.1 %all_to_all.27.refs_1_ = f32[16,8,128]{2,1,0:T(8,128)S(1)} all-to-all(f32[16,8,128]{2,1,0:T(8,128)S(1)} %get-tuple-element.30), channel_id=1, replica_groups=mesh['seq'=32,'head'=16] {'head'}, dimensions={0} | all-to-all | bytes 131072 | tf_op jit(solution)/shard_map/all_to_all | solution.py:441
  60.2 1.5 %shard_map.109 = (f32[8,64,128]{2,1,0:T(8,128)}, f32[8,128]{1,0:T(8,128)S(1)}) custom-call(f32[8,512]{1,0:T(8,128)S(1)} %get-tuple-element.26.refs_0_.consts, f32[16,8,128]{2,1,0:T(8,128)S(1)} %all_to_all.27.refs_1_, f32[512,512]{1,0:T(8,128)S(1)} %get-tuple-element.31.refs_2_, bf16[512,512]{1,0:T(8,128)(2,1)S(1)} %copy-done.1, bf16[512,512]{1,0:T(8,128)(2,1)S(1)} %copy-done), custom_call_target="tpu_custom_call" | custom-call | tf_op jit(solution)/shard_map/pallas_call | solution.py:334
  61.8 5.6 %all-to-all-start.3 = ((f32[8,64,128]{2,1,0:T(8,128)}), f32[8,64,128]{2,1,0:T(8,128)S(1)}, u32[]{:S(2)}, u32[]{:S(2)}) async-start(f32[8,64,128]{2,1,0:T(8,128)} %get-tuple-element.34), calls=%async_computation.3 | async-start | bytes 524288 | tf_op jit(solution)/shard_map/all_to_all | solution.py:368
  67.3 5.7 %shard_map.108 = (bf16[512,512]{1,0:T(8,128)(2,1)}, bf16[512,512]{1,0:T(8,128)(2,1)}, f32[512,512]{1,0:T(8,128)S(1)}, f32[512,512]{1,0:T(8,128)S(1)}) custom-call(f32[8,512]{1,0:T(8,128)S(1)} %get-tuple-element.26.refs_0_.consts, f32[16,8,128]{2,1,0:T(8,128)S(1)} %all_to_all.27.refs_1_, f32[512,512]{1,0:T(8,128)} %copy-done.8, bf16[512,512]{1,0:T(8,128)(2,1)} %refs_3_.3, ...), custom_call_target="tpu_custom_call" | custom-call | flops 1610612736 | bytes 6291456 | tf_op jit(solution)/shard_map/pallas_call | solution.py:334
  73.0 3.1 %all-to-all-done.3.refs_1_ = f32[8,64,128]{2,1,0:T(8,128)S(1)} async-done(((f32[8,64,128]{2,1,0:T(8,128)}), f32[8,64,128]{2,1,0:T(8,128)S(1)}, u32[]{:S(2)}, u32[]{:S(2)}) %all-to-all-start.3) | async-done | bytes 262176 | tf_op jit(solution)/shard_map/all_to_all | solution.py:368
  76.1 22.0 %all-gather = f32[288,128]{1,0:T(8,128)S(1)} all-gather(f32[72,128]{1,0:T(8,128)S(1)} %get-tuple-element.38), channel_id=2, replica_groups={{0,128,256,384},{16,144,272,400},{32,160,288,416},{48,176,304,432},{64,..., dimensions={0}, use_global_device_ids=true | all-gather | bytes 184320 | tf_op jit(solution)/shard_map/all_gather | solution.py:372
  98.1 0.1 shard_map.111
  98.1 15.5 %all_to_all.28.back = f32[8,72,128]{2,1,0:T(8,128)S(1)} all-to-all(f32[8,72,128]{2,1,0:T(8,128)S(1)} %get-tuple-element.41), channel_id=1, replica_groups={{0,16,32,48,64,80,96,112},{128,144,160,176,192,208,224,240},{256,272,28..., dimensions={0} | all-to-all | bytes 589824 | tf_op jit(solution)/shard_map/all_to_all | solution.py:376
  113.6 2.0 %shard_map.112 = (bf16[512,512]{1,0:T(8,128)(2,1)}, bf16[512,512]{1,0:T(8,128)(2,1)}, f32[1,512]{1,0:T(1,128)}) custom-call(f32[8,512]{1,0:T(8,128)S(1)} %get-tuple-element.26.refs_0_.consts, f32[8,72,128]{2,1,0:T(8,128)S(1)} %all_to_all.28.back, bf16[512,512]{1,0:T(8,128)(2,1)S(1)} %copy-done.3, bf16[512,512]{1,0:T(8,128)(2,1)S(1)} %copy-done.5, ...), custom_call_target="tpu_custom_call" | custom-call | tf_op jit(solution)/shard_map/pallas_call | solution.py:334
  (19 shorter events, 0.1 us)
Async XLA Ops:
  0.6 29.5 %copy-start.2 = (bf16[512,512]{1,0:T(8,128)(2,1)S(1)}, bf16[512,512]{1,0:T(8,128)(2,1)}, u32[]{:S(2)}) copy-start(bf16[512,512]{1,0:T(8,128)(2,1)} %keys.5) | copy-start | bytes 1572868
  0.6 29.5 %copy-start.4 = (bf16[512,512]{1,0:T(8,128)(2,1)S(1)}, bf16[512,512]{1,0:T(8,128)(2,1)}, u32[]{:S(2)}) copy-start(bf16[512,512]{1,0:T(8,128)(2,1)} %values.5) | copy-start | bytes 1572868
  2.8 27.3 %copy-start = (bf16[512,512]{1,0:T(8,128)(2,1)S(1)}, bf16[512,512]{1,0:T(8,128)(2,1)}, u32[]{:S(2)}) copy-start(bf16[512,512]{1,0:T(8,128)(2,1)} %refs_4_.3) | copy-start | bytes 1572868
  21.0 7.7 %collective-permute-start = (f32[64,128]{1,0:T(8,128)S(1)}, f32[64,128]{1,0:T(8,128)S(1)}, u32[]{:S(2)}, u32[]{:S(2)}) collective-permute-start(f32[64,128]{1,0:T(8,128)S(1)} %shard_map.102.refs_1_), channel_id=1, source_target_pairs={{0,128},{16,144},{32,160},{48,176},{64,192},{80,208},{96,224},{112... | collective-permute-start | bytes 98312 | tf_op jit(solution)/shard_map/ppermute | solution.py:345
  28.7 3.1 %collective-permute-start.1 = (f32[64,128]{1,0:T(8,128)S(1)}, f32[64,128]{1,0:T(8,128)S(1)}, u32[]{:S(2)}, u32[]{:S(2)}) collective-permute-start(f32[64,128]{1,0:T(8,128)S(1)} %shard_map.103.x), channel_id=1, source_target_pairs={{128,256},{144,272},{160,288},{176,304},{192,320},{208,336},{224,3... | collective-permute-start | bytes 98312 | tf_op jit(solution)/shard_map/ppermute | solution.py:345
  29.4 2.4 %collective-permute-start.2 = (f32[64,128]{1,0:T(8,128)S(1)}, f32[64,128]{1,0:T(8,128)S(1)}, u32[]{:S(2)}, u32[]{:S(2)}) collective-permute-start(f32[64,128]{1,0:T(8,128)S(1)} %shard_map.104.total), channel_id=1, source_target_pairs={{128,384},{144,400},{160,416},{176,432},{192,448},{208,464},{224,4... | collective-permute-start | bytes 98312 | tf_op jit(solution)/shard_map/ppermute | solution.py:345
  31.8 14.6 %copy-start.1 = (bf16[512,512]{1,0:T(8,128)(2,1)S(1)}, bf16[512,512]{1,0:T(8,128)(2,1)}, u32[]{:S(2)}) copy-start(bf16[512,512]{1,0:T(8,128)(2,1)} %refs_3_.3) | copy-start | bytes 1572868
  46.4 0.7 copy-start.6
  47.1 14.6 %copy-start.8 = (f32[512,512]{1,0:T(8,128)}, f32[512,512]{1,0:T(8,128)S(1)}, u32[]{:S(2)}) copy-start(f32[512,512]{1,0:T(8,128)S(1)} %get-tuple-element.31.refs_2_) | copy-start | bytes 3145732
  61.8 5.6 %copy-start.7 = (f32[8,64,128]{2,1,0:T(8,128)S(1)}, f32[8,64,128]{2,1,0:T(8,128)}, u32[]{:S(2)}) copy-start(f32[8,64,128]{2,1,0:T(8,128)} %copy-done.6) | copy-start | bytes 786436
  61.8 14.3 %all-to-all-start.3 = ((f32[8,64,128]{2,1,0:T(8,128)}), f32[8,64,128]{2,1,0:T(8,128)S(1)}, u32[]{:S(2)}, u32[]{:S(2)}) async-start(f32[8,64,128]{2,1,0:T(8,128)} %get-tuple-element.34), calls=%async_computation.3 | async-start | bytes 524288 | tf_op jit(solution)/shard_map/all_to_all | solution.py:368
  98.1 15.6 %copy-start.5 = (bf16[512,512]{1,0:T(8,128)(2,1)S(1)}, bf16[512,512]{1,0:T(8,128)(2,1)}, u32[]{:S(2)}) copy-start(bf16[512,512]{1,0:T(8,128)(2,1)} %values.5) | copy-start | bytes 1572868
  98.1 15.5 %copy-start.3 = (bf16[512,512]{1,0:T(8,128)(2,1)S(1)}, bf16[512,512]{1,0:T(8,128)(2,1)}, u32[]{:S(2)}) copy-start(bf16[512,512]{1,0:T(8,128)(2,1)} %keys.5) | copy-start | bytes 1572868

commit v17 on v16

--- a/solution.py
+++ b/solution.py
@@ -155,13 +155,12 @@
     return (inv * (upstream * consts[pl.ds(GAIN, 1), cols]) - value * coef).astype(BF16)
 
 
-def back_sum_kernel(channels, consts, received, mixed, cotangent, queries, sums_out, gains, inv, coef, sums, sent):
+def back_sum_kernel(channels, consts, received, mixed, cotangent, queries, sums_out, inv, coef, sums, sent):
     length = queries.shape[0]
     size = 128
     heads = queries.shape[1] // size
     token_scales(received, channels, inv, coef)
     stores = []
-    gains[...] = jnp.zeros_like(gains)
     for h in range(heads):
         cols = column(h, size)
         shards = pl.ds(2 * h, 2)
@@ -172,17 +171,13 @@
         sums[shards] = dot_split(queries[:, cols], scaled, 0, 0).reshape(2, size // 2, size)
         stores.append(pltpu.make_async_copy(sums.at[shards], sums_out.at[shards], sent.at[h]))
         stores[-1].start()
-    for h in range(heads):
-        cols = column(h, size)
-        products = cotangent[:, cols].astype(F32) * (mixed[:, cols] * inv[...])
-        gains[pl.ds(h, 1), :] = jnp.sum(products, axis=0, keepdims=True)
     for store in stores:
         store.wait()
 
 
 def grads_kernel(
     channels, consts, received, mixed_in, cotangent_in, queries_in, keys_in, values_in, state,
-    attended_out, query_out, key_part, value_part,
+    attended_out, query_out, key_part, value_part, gains,
     inv, coef, mixed, cotangent, queries, keys, values, grad, attended, query_grad, arrived, sent,
 ):
     length = queries.shape[0]
@@ -209,6 +204,7 @@
         )
         for copy in copies[-1]:
             copy.start()
+    gains[...] = jnp.zeros_like(gains)
     token_scales(received, channels, inv, coef)
     for h in range(heads):
         cols = column(h, size)
@@ -219,7 +215,9 @@
             copy.wait()
         value = mixed[:, cols]
         attended[:, cols] = (value * inv[...] * consts[pl.ds(GAIN, 1), cols]).astype(BF16)
-        grad[:, cols] = mixed_grad_of(consts, cols, cotangent[:, cols].astype(F32), value, inv[...], coef[...])
+        upstream = cotangent[:, cols].astype(F32)
+        gains[pl.ds(h, 1), :] = jnp.sum(upstream * (value * inv[...]), axis=0, keepdims=True)
+        grad[:, cols] = mixed_grad_of(consts, cols, upstream, value, inv[...], coef[...])
         q, k, v, g = (ref.at[:, cols] for ref in (queries, keys, values, grad))
         state_part = head_in_of(rate, length) * dot_split(g[...], state_in, 1, 1)
         upper = weighted(g, v, first, first, same)
@@ -440,17 +438,17 @@
     )
     received = lax.all_to_all(stats, "head", 0, 0)
     sums_shape = (2 * heads, size // 2, size)
-    back_sums, gains = whole_call(
-        lambda *refs: back_sum_kernel(total_channels, *refs), [pltpu.HBM(sums_shape, F32), array(F32, EXTRA, size)],
-        [consts, received, mixed, cotangent, queries], out_specs=[anywhere, in_vmem],
+    back_sums = whole_call(
+        lambda *refs: back_sum_kernel(total_channels, *refs), pltpu.HBM(sums_shape, F32),
+        [consts, received, mixed, cotangent, queries], out_specs=anywhere,
         scratch_shapes=[scratch, scratch, pltpu.VMEM(sums_shape, F32), pltpu.SemaphoreType.DMA((heads,))],
     )
     part = pltpu.VMEM((length, channels), F32)
-    attended, query_grad, key_part, value_part = whole_call(
-        lambda *refs: grads_kernel(total_channels, *refs), [narrow, narrow, part, part],
+    attended, query_grad, key_part, value_part, gains = whole_call(
+        lambda *refs: grads_kernel(total_channels, *refs), [narrow, narrow, part, part, array(F32, EXTRA, size)],
         [consts, received, hbm(mixed), hbm(cotangent), hbm(queries), hbm(keys), hbm(values), state_in],
         in_specs=[in_vmem] * 2 + [anywhere] * 5 + [in_vmem],
-        out_specs=[anywhere, anywhere, in_vmem, in_vmem],
+        out_specs=[anywhere, anywhere, in_vmem, in_vmem, in_vmem],
         scratch_shapes=[
             scratch, scratch, pltpu.VMEM((length, channels), F32), rows_scratch, rows_scratch, rows_scratch,
             rows_scratch, rows_scratch, rows_scratch, rows_scratch, pltpu.SemaphoreType.DMA((5 * heads,)), copies,

time: 116 us -> 117 us (level)
  no operation moved by 1% of the time
where the time goes in v17:
time: 117 us; the launch traced here: 116 us
  blocking collectives  83.2 us (71%)
  Pallas kernels  13.7 us (12%)
  starting transfers between devices  13.6 us (12%)
  waiting for transfers between devices  4.08 us (3%)
    all_gather x1, blocking collectives, scan_back(): arrived = lax.all_gather(totals, 'seq', axis_index_groups=across)  21.9 us
    all_to_all x1, blocking collectives, scan_forward(): parts = lax.all_to_all(x, 'seq', 0, 0, axis_index_groups=members)  18.1 us
    all_to_all x1, blocking collectives, scan_back(): return (lax.all_to_all(out, 'seq', 0, 0, axis_index_groups=members), kept)  15.5 us
    all_to_all x1, blocking collectives, scan_forward(): return (lax.all_to_all(out, 'seq', 0, 0, axis_index_groups=members), result)  14.5 us
    pallas_call x12, Pallas kernels, whole_call(): pl.pallas_call(kernel, in_specs=in_specs, out_specs=out_specs, out_shape=...  13.7 us
    all_to_all x1, blocking collectives, body(): received = lax.all_to_all(stats, 'head', 0, 0)  13.1 us
    ppermute x3, starting transfers between devices, send(): lax.ppermute(x, 'seq', [(a * GROUP + j, b * GROUP + j) for a, b in pairs...  8.06 us
    all_to_all x1, starting transfers between devices, scan_back(): parts = lax.all_to_all(x, 'seq', 0, 0, axis_index_groups=members)  5.56 us
  transfers between devices with their start and end apart: 4, of which 2 were waited for; matrix products, arithmetic and copies ran while one was open for 0% of the time, Pallas kernels for 6%

profile of v17, /device:TPU:1, one launch (start us, length us, event | category | flops | bytes accessed | tf_op | source)
XLA Modules:
  0.0 116.5 jit_solution(3762224317379564496)
XLA Ops:
  0.6 0.0 copy-start.2
  0.6 0.0 copy-start.4
  0.7 2.1 %shard_map.101 = (f32[8,64,128]{2,1,0:T(8,128)S(1)}, f32[8,512]{1,0:T(8,128)S(1)}) custom-call(f32[4]{0:T(128)} %rates_in.1, f32[1,512]{1,0:T(1,128)} %bitcast.4, bf16[512,512]{1,0:T(8,128)(2,1)} %keys.5, bf16[512,512]{1,0:T(8,128)(2,1)} %values.5), custom_call_target="tpu_custom_call" | custom-call | tf_op jit(solution)/shard_map/pallas_call | solution.py:332
  2.8 0.0 copy-start
  2.8 18.1 %all_to_all.25.refs_1_ = f32[8,64,128]{2,1,0:T(8,128)S(1)} all-to-all(f32[8,64,128]{2,1,0:T(8,128)S(1)} %get-tuple-element.26), channel_id=1, replica_groups={{0,16,32,48,64,80,96,112},{128,144,160,176,192,208,224,240},{256,272,28..., dimensions={0} | all-to-all | bytes 524288 | tf_op jit(solution)/shard_map/all_to_all | solution.py:349
  21.0 6.7 %collective-permute-start = (f32[64,128]{1,0:T(8,128)S(1)}, f32[64,128]{1,0:T(8,128)S(1)}, u32[]{:S(2)}, u32[]{:S(2)}) collective-permute-start(f32[64,128]{1,0:T(8,128)S(1)} %shard_map.102.refs_1_), channel_id=1, source_target_pairs={{0,128},{16,144},{32,160},{48,176},{64,192},{80,208},{96,224},{112... | collective-permute-start | bytes 98312 | tf_op jit(solution)/shard_map/ppermute | solution.py:343
  27.7 1.0 collective-permute-done.refs_2_
  28.7 0.7 collective-permute-start.1
  29.4 0.7 collective-permute-start.2
  30.1 1.7 %shard_map.105 = (f32[512,512]{1,0:T(8,128)S(1)}, f32[8,128]{1,0:T(8,128)S(1)}) custom-call(f32[8,512]{1,0:T(8,128)S(1)} %get-tuple-element.25.refs_0_.consts, bf16[512,512]{1,0:T(8,128)(2,1)S(1)} %copy-done, bf16[512,512]{1,0:T(8,128)(2,1)S(1)} %copy-done.2, bf16[512,512]{1,0:T(8,128)(2,1)S(1)} %copy-done.4, f32[64,128]{1,0:T(8,128)S(1)} %shard_map.104.total), custom_call_target="tpu_custom_call" | custom-call | flops 536870912 | bytes 6291456 | tf_op jit(solution)/shard_map/pallas_call | solution.py:332
  31.8 0.1 shard_map.106
  31.9 14.5 %all_to_all.26.state.refs_7_ = f32[8,64,128]{2,1,0:T(8,128)S(1)} all-to-all(f32[8,64,128]{2,1,0:T(8,128)S(1)} %shard_map.106), channel_id=1, replica_groups={{0,16,32,48,64,80,96,112},{128,144,160,176,192,208,224,240},{256,272,28..., dimensions={0} | all-to-all | bytes 524288 | tf_op jit(solution)/shard_map/all_to_all | solution.py:359
  46.4 0.6 shard_map.107
  47.0 0.1 copy-done.7
  47.1 13.1 %all_to_all.27.refs_1_ = f32[16,8,128]{2,1,0:T(8,128)S(1)} all-to-all(f32[16,8,128]{2,1,0:T(8,128)S(1)} %get-tuple-element.29), channel_id=1, replica_groups=mesh['seq'=32,'head'=16] {'head'}, dimensions={0} | all-to-all | bytes 131072 | tf_op jit(solution)/shard_map/all_to_all | solution.py:439
  60.2 1.4 %shard_map.109 = f32[8,64,128]{2,1,0:T(8,128)} custom-call(f32[8,512]{1,0:T(8,128)S(1)} %get-tuple-element.25.refs_0_.consts, f32[16,8,128]{2,1,0:T(8,128)S(1)} %all_to_all.27.refs_1_, f32[512,512]{1,0:T(8,128)S(1)} %get-tuple-element.30.refs_2_, bf16[512,512]{1,0:T(8,128)(2,1)S(1)} %copy-done.1, bf16[512,512]{1,0:T(8,128)(2,1)S(1)} %copy-done), custom_call_target="tpu_custom_call" | custom-call | tf_op jit(solution)/shard_map/pallas_call | solution.py:332
  61.6 1.0 copy-done.6
  62.6 5.6 %all-to-all-start.3 = ((f32[8,64,128]{2,1,0:T(8,128)}), f32[8,64,128]{2,1,0:T(8,128)S(1)}, u32[]{:S(2)}, u32[]{:S(2)}) async-start(f32[8,64,128]{2,1,0:T(8,128)} %shard_map.109), calls=%async_computation.3 | async-start | bytes 524288 | tf_op jit(solution)/shard_map/all_to_all | solution.py:366
  68.1 5.6 %shard_map.108 = (bf16[512,512]{1,0:T(8,128)(2,1)}, bf16[512,512]{1,0:T(8,128)(2,1)}, f32[512,512]{1,0:T(8,128)S(1)}, f32[512,512]{1,0:T(8,128)S(1)}, f32[8,128]{1,0:T(8,128)S(1)}) custom-call(f32[8,512]{1,0:T(8,128)S(1)} %get-tuple-element.25.refs_0_.consts, f32[16,8,128]{2,1,0:T(8,128)S(1)} %all_to_all.27.refs_1_, f32[512,512]{1,0:T(8,128)} %copy-done.6, ...), custom_call_target="tpu_custom_call" | custom-call | flops 1610612736 | bytes 6291456 | tf_op jit(solution)/shard_map/pallas_call | solution.py:332
  73.8 3.1 %all-to-all-done.3.refs_1_ = f32[8,64,128]{2,1,0:T(8,128)S(1)} async-done(((f32[8,64,128]{2,1,0:T(8,128)}), f32[8,64,128]{2,1,0:T(8,128)S(1)}, u32[]{:S(2)}, u32[]{:S(2)}) %all-to-all-start.3) | async-done | bytes 262176 | tf_op jit(solution)/shard_map/all_to_all | solution.py:366
  76.9 21.9 %all-gather = f32[288,128]{1,0:T(8,128)S(1)} all-gather(f32[72,128]{1,0:T(8,128)S(1)} %get-tuple-element.36), channel_id=2, replica_groups={{0,128,256,384},{16,144,272,400},{32,160,288,416},{48,176,304,432},{64,..., dimensions={0}, use_global_device_ids=true | all-gather | bytes 184320 | tf_op jit(solution)/shard_map/all_gather | solution.py:370
  98.9 0.1 shard_map.111
  98.9 15.5 %all_to_all.28.back = f32[8,72,128]{2,1,0:T(8,128)S(1)} all-to-all(f32[8,72,128]{2,1,0:T(8,128)S(1)} %get-tuple-element.39), channel_id=1, replica_groups={{0,16,32,48,64,80,96,112},{128,144,160,176,192,208,224,240},{256,272,28..., dimensions={0} | all-to-all | bytes 589824 | tf_op jit(solution)/shard_map/all_to_all | solution.py:374
  114.4 2.0 %shard_map.112 = (bf16[512,512]{1,0:T(8,128)(2,1)}, bf16[512,512]{1,0:T(8,128)(2,1)}, f32[1,512]{1,0:T(1,128)}) custom-call(f32[8,512]{1,0:T(8,128)S(1)} %get-tuple-element.25.refs_0_.consts, f32[8,72,128]{2,1,0:T(8,128)S(1)} %all_to_all.28.back, bf16[512,512]{1,0:T(8,128)(2,1)S(1)} %copy-done.3, bf16[512,512]{1,0:T(8,128)(2,1)S(1)} %copy-done.5, ...), custom_call_target="tpu_custom_call" | custom-call | tf_op jit(solution)/shard_map/pallas_call | solution.py:332
  (19 shorter events, 0.1 us)
Async XLA Ops:
  0.6 29.5 %copy-start.2 = (bf16[512,512]{1,0:T(8,128)(2,1)S(1)}, bf16[512,512]{1,0:T(8,128)(2,1)}, u32[]{:S(2)}) copy-start(bf16[512,512]{1,0:T(8,128)(2,1)} %keys.5) | copy-start | bytes 1572868
  0.6 29.5 %copy-start.4 = (bf16[512,512]{1,0:T(8,128)(2,1)S(1)}, bf16[512,512]{1,0:T(8,128)(2,1)}, u32[]{:S(2)}) copy-start(bf16[512,512]{1,0:T(8,128)(2,1)} %values.5) | copy-start | bytes 1572868
  2.8 27.3 %copy-start = (bf16[512,512]{1,0:T(8,128)(2,1)S(1)}, bf16[512,512]{1,0:T(8,128)(2,1)}, u32[]{:S(2)}) copy-start(bf16[512,512]{1,0:T(8,128)(2,1)} %refs_4_.3) | copy-start | bytes 1572868
  21.0 7.7 %collective-permute-start = (f32[64,128]{1,0:T(8,128)S(1)}, f32[64,128]{1,0:T(8,128)S(1)}, u32[]{:S(2)}, u32[]{:S(2)}) collective-permute-start(f32[64,128]{1,0:T(8,128)S(1)} %shard_map.102.refs_1_), channel_id=1, source_target_pairs={{0,128},{16,144},{32,160},{48,176},{64,192},{80,208},{96,224},{112... | collective-permute-start | bytes 98312 | tf_op jit(solution)/shard_map/ppermute | solution.py:343
  28.7 3.1 %collective-permute-start.1 = (f32[64,128]{1,0:T(8,128)S(1)}, f32[64,128]{1,0:T(8,128)S(1)}, u32[]{:S(2)}, u32[]{:S(2)}) collective-permute-start(f32[64,128]{1,0:T(8,128)S(1)} %shard_map.103.x), channel_id=1, source_target_pairs={{128,256},{144,272},{160,288},{176,304},{192,320},{208,336},{224,3... | collective-permute-start | bytes 98312 | tf_op jit(solution)/shard_map/ppermute | solution.py:343
  29.4 2.4 %collective-permute-start.2 = (f32[64,128]{1,0:T(8,128)S(1)}, f32[64,128]{1,0:T(8,128)S(1)}, u32[]{:S(2)}, u32[]{:S(2)}) collective-permute-start(f32[64,128]{1,0:T(8,128)S(1)} %shard_map.104.total), channel_id=1, source_target_pairs={{128,384},{144,400},{160,416},{176,432},{192,448},{208,464},{224,4... | collective-permute-start | bytes 98312 | tf_op jit(solution)/shard_map/ppermute | solution.py:343
  31.8 14.6 %copy-start.1 = (bf16[512,512]{1,0:T(8,128)(2,1)S(1)}, bf16[512,512]{1,0:T(8,128)(2,1)}, u32[]{:S(2)}) copy-start(bf16[512,512]{1,0:T(8,128)(2,1)} %refs_3_.3) | copy-start | bytes 1572868
  46.4 0.7 copy-start.7
  61.6 1.0 copy-start.6
  62.6 5.6 %copy-start.8 = (f32[8,64,128]{2,1,0:T(8,128)S(1)}, f32[8,64,128]{2,1,0:T(8,128)}, u32[]{:S(2)}) copy-start(f32[8,64,128]{2,1,0:T(8,128)} %copy-done.7) | copy-start | bytes 786436
  62.6 14.3 %all-to-all-start.3 = ((f32[8,64,128]{2,1,0:T(8,128)}), f32[8,64,128]{2,1,0:T(8,128)S(1)}, u32[]{:S(2)}, u32[]{:S(2)}) async-start(f32[8,64,128]{2,1,0:T(8,128)} %shard_map.109), calls=%async_computation.3 | async-start | bytes 524288 | tf_op jit(solution)/shard_map/all_to_all | solution.py:366
  98.9 15.6 %copy-start.5 = (bf16[512,512]{1,0:T(8,128)(2,1)S(1)}, bf16[512,512]{1,0:T(8,128)(2,1)}, u32[]{:S(2)}) copy-start(bf16[512,512]{1,0:T(8,128)(2,1)} %values.5) | copy-start | bytes 1572868
  98.9 15.5 %copy-start.3 = (bf16[512,512]{1,0:T(8,128)(2,1)S(1)}, bf16[512,512]{1,0:T(8,128)(2,1)}, u32[]{:S(2)}) copy-start(bf16[512,512]{1,0:T(8,128)(2,1)} %keys.5) | copy-start | bytes 1572868
